TPU v7x, 128 devices: a whole 4x4x4 slice. The times are simulated.
128 devices in a mesh: dp: 8 (over y, z_lo), tensor: 16 (over z_hi, x, core).
Axes of the slice: x: 4, y: 4, z: 4 (z_hi: 2, z_lo: 2; z = z_hi * 2 + z_lo), core: 2. Of those that a mesh axis runs over, the one named last changes fastest.
Arguments:
- tokens: bfloat16 [12288, 5120], P(('dp', 'tensor')), may hold values from -6 to 6
- codes: bfloat16 [128, 5120, 128], P(('dp', 'tensor')), may hold values from -4 to 4
- block_ids: int32 [128], P(('dp', 'tensor')), may hold values from 0 to 7, as said below
- scale_idx: int32 [128], P(('dp', 'tensor')), may hold values from 0 to 63
- scale_table: float32 [64], replicated, may hold values from 0.006 to 0.03
- down_weight: bfloat16 [8192, 5120], P('tensor'), may hold values from -0.0625 to 0.0625
Outputs:
- mixed: bfloat16 [12288, 5120], P(('dp', 'tensor'))
Inputs may be any that keep to these rules, and one draw needn't show every extreme that they name: `block_ids`: the 8 slots that belong to one tensor rank hold each local column block number exactly once.
All inputs are finite; a program needn't handle non-finite values.
Results may differ from a plain program's by a relative error of at most 0.018.
Values may be sent and summed in bfloat16 or wider, within the bound.
No kernel may reach another device: no remote copies, remote signals or barrier semaphores. Data moves between devices by JAX's collectives and lax.ppermute only.
A program may use at most 128 MiB of HBM per device.

v0:
```python
import jax
import jax.numpy as jnp
from jax import lax
from jax.experimental import pallas as pl
from jax.experimental.pallas import tpu as pltpu
from jax.sharding import PartitionSpec as P

NX, NY, NZL, NZH, NC = 4, 4, 2, 2, 2
AXES = ("dp", "tensor")
BF16, F32 = jnp.bfloat16, jnp.float32
NOTE = 16
STEP = 1024


def place(y, zl, zh, x, c):
    return ((y % NY * NZL + zl % NZL) * NZH + zh % NZH) * NX * NC + x % NX * NC + c % NC


def move(value, dx=0, dy=0, zl=0, zh=0, core=0):
    pairs = []
    for y in range(NY):
        for l in range(NZL):
            for h in range(NZH):
                for x in range(NX):
                    for c in range(NC):
                        pairs.append((place(y, l, h, x, c), place(y + dy, l + zl, h + zh, x + dx, c + core)))
    return lax.ppermute(value, AXES, pairs)


def after(value, *others):
    return lax.optimization_barrier((value,) + others)[0]


def rows_of(*parts):
    return jnp.concatenate(parts, axis=0)


def with_note(codes, block_ids, scale_idx):
    _, depth, width = codes.shape

    def kernel(number, entry, block, out, note, sem):
        big = pltpu.make_async_copy(block.at[0], out.at[pl.ds(0, depth)], sem.at[0])
        big.start()
        line = lax.broadcasted_iota(jnp.int32, (NOTE, width), 0)
        note[...] = jnp.where(line == 0, number[0], entry[0]).astype(F32).astype(BF16)
        small = pltpu.make_async_copy(note, out.at[pl.ds(depth, NOTE)], sem.at[1])
        small.start()
        small.wait()
        big.wait()

    smem = pl.BlockSpec(memory_space=pltpu.SMEM)
    anywhere = pl.BlockSpec(memory_space=pltpu.HBM)
    return pl.pallas_call(
        kernel,
        out_shape=jax.ShapeDtypeStruct((depth + NOTE, width), BF16),
        in_specs=[smem, smem, anywhere],
        out_specs=anywhere,
        scratch_shapes=[pltpu.VMEM((NOTE, width), BF16), pltpu.SemaphoreType.DMA((2,))],
        compiler_params=pltpu.CompilerParams(vmem_limit_bytes=2 * 2**20),
    )(block_ids, scale_idx, codes)


def feed_forward(code_map, row_map, depth, width, local_ff, parts):
    n_codes = 1 + max(m[1] for m in code_map)
    n_rows = 1 + max(m[0] for m in row_map)
    slots = 1 + max(m[0] for m in code_map)
    blocks = slots // 2
    rows = sum(m[2] for m in row_map)
    n_copies = len(code_map) + len(row_map) + 1 + 2 * (1 + parts)
    base = len(code_map) + len(row_map)

    def kernel(ids, sidx, table, *refs):
        sources, refs = refs[:n_codes], refs[n_codes:]
        pieces, refs = refs[:n_rows], refs[n_rows:]
        down, outs, (w, x, dn, proj, hid, out, sem) = refs[0], refs[1 : 2 + parts], refs[2 + parts :]
        at = 0
        first = []
        for i, (src, start, n) in enumerate(row_map):
            first.append(pltpu.make_async_copy(pieces[src].at[pl.ds(start, n)], x.at[pl.ds(at, n)], sem.at[i]))
            at += n
        x_copies = list(first)
        waits = [[] for _ in range(blocks)]
        for i, (slot, src, start, n, to) in enumerate(code_map):
            target = w.at[slot // 2, pl.ds(to, n), pl.ds(slot % 2 * width, width)]
            waits[slot // 2].append(
                pltpu.make_async_copy(sources[src].at[pl.ds(start, n)], target, sem.at[len(row_map) + i])
            )
        down_copy = pltpu.make_async_copy(down, dn, sem.at[n_copies - 1])
        stages = [first + waits[0]] + waits[1:] + [[down_copy]]
        for stage in stages[:2]:
            for c in stage:
                c.start()
        for c in x_copies:
            c.wait()

        @pl.loop(0, blocks)
        def _(pair):
            for q in range(blocks):

                @pl.when(pair == q)
                def _(q=q):
                    for c in waits[q]:
                        c.wait()
                    if q + 2 < len(stages):
                        for c in stages[q + 2]:
                            c.start()

            acc = jnp.dot(x[...], w[pair], preferred_element_type=F32)
            for side in range(2):
                slot = 2 * pair + side
                proj[ids[slot]] = acc[:, side * width : (side + 1) * width] * table[sidx[slot]]

        for b in range(blocks):
            gate, up = proj[b], proj[b + blocks]
            hid[:, b * width : (b + 1) * width] = (gate / (1.0 + jnp.exp(-gate)) * up).astype(BF16)
        down_copy.wait()

        def leave(n, slot):
            cols = pl.ds(pl.multiple_of(n * STEP, STEP), STEP)
            piece = rows // 2 // parts
            ranges = [(0, rows // 2)] + [(rows // 2 + i * piece, piece) for i in range(parts)]
            return [
                pltpu.make_async_copy(
                    out.at[slot, pl.ds(at, n)], outs[i].at[:, cols], sem.at[base + slot * (1 + parts) + i]
                )
                for i, (at, n) in enumerate(ranges)
            ]

        steps = depth // STEP

        @pl.loop(0, steps)
        def _(n):
            slot = lax.rem(n, 2)

            @pl.when(n >= 2)
            def _():
                for c in leave(n - 2, slot):
                    c.wait()

            cols = pl.ds(pl.multiple_of(n * STEP, STEP), STEP)
            out[slot] = jnp.dot(hid[...], dn[:, cols], preferred_element_type=F32).astype(BF16)
            for c in leave(n, slot):
                c.start()

        for n in (steps - 2, steps - 1):
            for c in leave(n, n % 2):
                c.wait()

    anywhere = pl.BlockSpec(memory_space=pltpu.HBM)
    smem = pl.BlockSpec(memory_space=pltpu.SMEM)
    half = jax.ShapeDtypeStruct((rows // 2, depth), BF16)
    piece = jax.ShapeDtypeStruct((rows // 2 // parts, depth), BF16)
    return pl.pallas_call(
        kernel,
        out_shape=(half,) + (piece,) * parts,
        in_specs=[smem] * 3 + [anywhere] * (n_codes + n_rows + 1),
        out_specs=(anywhere,) * (1 + parts),
        scratch_shapes=[
            pltpu.VMEM((blocks, depth, 2 * width), BF16),
            pltpu.VMEM((rows, depth), BF16),
            pltpu.VMEM((local_ff, depth), BF16),
            pltpu.VMEM((slots, rows, width), F32),
            pltpu.VMEM((rows, local_ff), BF16),
            pltpu.VMEM((2, rows, STEP), BF16),
            pltpu.SemaphoreType.DMA((n_copies,)),
        ],
        compiler_params=pltpu.CompilerParams(vmem_limit_bytes=60 * 2**20),
        cost_estimate=pl.CostEstimate(
            flops=2 * rows * depth * local_ff * 3,
            bytes_accessed=2 * (depth * slots * width + local_ff * depth + 2 * rows * depth),
            transcendentals=rows * local_ff,
        ),
    )


def body(tokens, codes, block_ids, scale_idx, scale_table, down_weight):
    count, depth = tokens.shape
    width = codes.shape[2]
    local_ff = down_weight.shape[0]
    h_rows, h_depth = count // 2, depth // 2

    own = with_note(codes, block_ids, scale_idx)
    ca, cb = move(own, dy=1), move(own, dy=-1)
    ta, tb, tz = move(tokens, dx=1), move(tokens, dx=-1), move(tokens, zh=1)
    cz = move(after(own, tz), zl=1)
    y_top = move(rows_of(ca[:h_depth], ca[depth:]), dy=1)
    y_low = move(cb[h_depth:depth], dy=-1)
    taz, tbz = move(tz, dx=1), move(tz, dx=-1)
    cy = rows_of(y_top[:h_depth], y_low, y_top[h_depth:])
    caz, cbz, cyz = move(cz, dy=1), move(cz, dy=-1), move(cy, zl=1)
    x_top = move(rows_of(ta[:h_rows], taz[:h_rows]), dx=1)
    x_low = move(rows_of(tb[h_rows:], tbz[h_rows:]), dx=-1)

    sources = [own, ca, cb, cz, cy, caz, cbz, cyz]
    code_map = [(i, i, 0, depth, 0) for i in range(8)]
    notes = jnp.stack([s[depth : depth + 2, 0] for s in sources]).astype(jnp.int32)
    ids, sidx = notes[:, 0], notes[:, 1]

    def swap(*pieces):
        return [move(piece, core=1) for piece in pieces]

    def sums(ids, pieces, parts=3):
        run = feed_forward(code_map, [(i, 0, count) for i in range(4)], depth, width, local_ff, parts)
        return tuple(run(ids, sidx, scale_table, *sources, *pieces, down_weight))

    def add(mine, siblings):
        return mine.astype(F32) + rows_of(*siblings).astype(F32)

    def towards(p, both, top, low):
        top, low = (v[p * h_rows : (p + 1) * h_rows].astype(F32) for v in (top, low))
        right, left = both[:count], both[count:]
        right = rows_of(right[:h_rows] + top, right[h_rows:])
        left = rows_of(left[:h_rows], left[h_rows:] + low)
        return right.astype(BF16), left.astype(BF16)

    x_top, x_low = after((x_top, x_low), caz, cbz, cyz)
    o_far = swap(x_top, x_low)
    later = after((tbz, taz, tb, ta, tz, tokens), *o_far)
    o_near_z, o_near, o_here = swap(*later[:2]), swap(*later[2:4]), swap(*later[4:])
    far = sums(ids, (x_top, x_low, *o_far))
    far = after(far, *o_near_z, *o_near, *o_here)
    far = add(far[0], swap(*far[1:]))
    far_top, far_low = far[:count].astype(BF16), far[count:].astype(BF16)
    top, low = move(far_top, dx=1), move(far_low, dx=-1)

    ids = after(ids, far_top, far_low)
    near_z = sums(ids, (tbz, taz, *o_near_z))
    ids = after(ids, near_z[0])
    here = sums(ids, (tz, tokens, *o_here), 1)
    near_z, top, low, here = after((near_z[:1] + tuple(swap(*near_z[1:])), top, low, here))
    right, left = towards(1, add(near_z[0], near_z[1:]), top, low)
    z_right, z_left = move(right, dx=1), move(left, dx=-1)

    o_sums = swap(after(here[1], right, left))
    ids = after(ids, right, left, *o_sums)
    near = sums(ids, (tb, ta, *o_near))
    near, z_right, z_left = after((near[:1] + tuple(swap(*near[1:])), z_right, z_left))
    right, left = towards(0, add(near[0], near[1:]), top, low)
    here = add(here[0], o_sums)
    across = (here[:count] + z_right.astype(F32) + z_left.astype(F32)).astype(BF16)
    right, left, across = move(right, dx=1), move(left, dx=-1), move(across, zh=1)
    return (here[count:] + right.astype(F32) + left.astype(F32) + across.astype(F32)).astype(BF16)


def solution(mesh):
    return jax.shard_map(
        body,
        mesh=mesh,
        in_specs=(
            P(("dp", "tensor"), None),
            P(("dp", "tensor"), None, None),
            P(("dp", "tensor")),
            P(("dp", "tensor")),
            P(),
            P("tensor", None),
        ),
        out_specs=P(("dp", "tensor"), None),
        check_vma=False,
    )
```

profile of v0, /device:TPU:1, one launch (start us, length us, event | category | flops | bytes accessed | tf_op | source)
XLA Modules:
  0.0 223.6 jit_solution(5056284311926271846)
XLA Ops:
  0.0 4.4 %collective-permute-start.2 = (bf16[96,5120]{1,0:T(8,128)(2,1)}, bf16[96,5120]{1,0:T(8,128)(2,1)}, u32[]{:S(2)}, u32[]{:S(2)}) collective-permute-start(bf16[96,5120]{1,0:T(8,128)(2,1)} %refs_9_.1), channel_id=1, source_target_pairs={{0,8},{1,9},{2,10},{3,11},{4,12},{5,13},{6,14},{7,15},{8,0},{9,1},... | collective-permute-start | bytes 2949128 | tf_op jit(solution)/shard_map/ppermute | solution.py:27
  5.7 1.3 copy-done.1
  7.2 1.4 collective-permute-start
  8.5 1.5 collective-permute-start.1
  10.1 2.5 %collective-permute-start.12 = (bf16[96,5120]{1,0:T(8,128)(2,1)}, bf16[96,5120]{1,0:T(8,128)(2,1)}, u32[]{:S(2)}, u32[]{:S(2)}) collective-permute-start(bf16[96,5120]{1,0:T(8,128)(2,1)} %refs_9_.1), channel_id=1, source_target_pairs={{0,6},{1,7},{2,0},{3,1},{4,2},{5,3},{6,4},{7,5},{8,14},{9,15},{10,... | collective-permute-start | bytes 2949128 | tf_op jit(solution)/shard_map/ppermute | solution.py:27
  12.5 13.7 %collective-permute-done.2.refs_8_ = bf16[96,5120]{1,0:T(8,128)(2,1)} collective-permute-done((bf16[96,5120]{1,0:T(8,128)(2,1)}, bf16[96,5120]{1,0:T(8,128)(2,1)}, u32[]{:S(2)}, u32[]{:S(2)}) %collective-permute-start.2) | collective-permute-done | bytes 983072 | tf_op jit(solution)/shard_map/ppermute | solution.py:27
  26.2 2.5 %collective-permute-start.13 = (bf16[96,5120]{1,0:T(8,128)(2,1)}, bf16[96,5120]{1,0:T(8,128)(2,1)S(1)}, u32[]{:S(2)}, u32[]{:S(2)}) collective-permute-start(bf16[96,5120]{1,0:T(8,128)(2,1)} %collective-permute-done.2.refs_8_), channel_id=1, source_target_pairs={{0,6},{1,7},{2,0},{3,1},{4,2},{5,3},{6,4},{7,5},{8,14},{9,15},{10,... | collective-permute-start | bytes 2949128 | tf_op jit(solution)/shard_map/ppermute | solution.py:27
  28.7 9.3 %collective-permute-done.refs_1_ = bf16[5136,128]{1,0:T(8,128)(2,1)S(1)} collective-permute-done((bf16[5136,128]{1,0:T(8,128)(2,1)S(1)}, bf16[5136,128]{1,0:T(8,128)(2,1)S(1)}, u32[]{:S(2)}, u32[]{:S(2)}) %collective-permute-start) | collective-permute-done | bytes 1314848 | tf_op jit(solution)/shard_map/ppermute | solution.py:27
  38.0 1.2 collective-permute-start.10
  39.5 2.7 %collective-permute-start.7 = (bf16[2560,128]{1,0:T(8,128)(2,1)S(1)}, bf16[2560,128]{1,0:T(8,128)(2,1)S(1)}, u32[]{:S(2)}, u32[]{:S(2)}) collective-permute-start(bf16[2560,128]{1,0:T(8,128)(2,1)S(1)} %slice.169), channel_id=1, source_target_pairs={{0,96},{1,97},{2,98},{3,99},{4,100},{5,101},{6,102},{7,103},{8,104... | collective-permute-start | bytes 1966088 | tf_op jit(solution)/shard_map/ppermute | solution.py:27
  42.2 0.7 collective-permute-start.3
  43.0 1.1 slice.174
  44.0 9.6 %collective-permute-done.13.refs_8_ = bf16[96,5120]{1,0:T(8,128)(2,1)S(1)} collective-permute-done((bf16[96,5120]{1,0:T(8,128)(2,1)}, bf16[96,5120]{1,0:T(8,128)(2,1)S(1)}, u32[]{:S(2)}, u32[]{:S(2)}) %collective-permute-start.13) | collective-permute-done | bytes 983072 | tf_op jit(solution)/shard_map/ppermute | solution.py:27
  53.7 3.4 %collective-permute-start.14 = (bf16[96,5120]{1,0:T(8,128)(2,1)S(1)}, bf16[96,5120]{1,0:T(8,128)(2,1)S(1)}, u32[]{:S(2)}, u32[]{:S(2)}) collective-permute-start(bf16[96,5120]{1,0:T(8,128)(2,1)S(1)} %pad_maximum_fusion.2), channel_id=1, source_target_pairs={{0,6},{1,7},{2,0},{3,1},{4,2},{5,3},{6,4},{7,5},{8,14},{9,15},{10,... | collective-permute-start | bytes 2949128 | tf_op jit(solution)/shard_map/ppermute | solution.py:27
  57.1 3.9 %collective-permute-done.10.refs_9_ = bf16[96,5120]{1,0:T(8,128)(2,1)} collective-permute-done((bf16[96,5120]{1,0:T(8,128)(2,1)}, bf16[96,5120]{1,0:T(8,128)(2,1)}, u32[]{:S(2)}, u32[]{:S(2)}) %collective-permute-start.10) | collective-permute-done | bytes 983072 | tf_op jit(solution)/shard_map/ppermute | solution.py:27
  61.0 1.1 slice.173
  62.3 0.8 collective-permute-start.8
  63.1 6.9 %collective-permute-done.3.refs_3_ = bf16[5136,128]{1,0:T(8,128)(2,1)S(1)} collective-permute-done((bf16[5136,128]{1,0:T(8,128)(2,1)S(1)}, bf16[5136,128]{1,0:T(8,128)(2,1)S(1)}, u32[]{:S(2)}, u32[]{:S(2)}) %collective-permute-start.3) | collective-permute-done | bytes 1314848 | tf_op jit(solution)/shard_map/ppermute | solution.py:27
  70.1 1.3 collective-permute-start.5
  71.5 1.3 collective-permute-start.11
  72.8 3.1 %collective-permute-done.14.refs_9_ = bf16[96,5120]{1,0:T(8,128)(2,1)S(1)} collective-permute-done((bf16[96,5120]{1,0:T(8,128)(2,1)S(1)}, bf16[96,5120]{1,0:T(8,128)(2,1)S(1)}, u32[]{:S(2)}, u32[]{:S(2)}) %collective-permute-start.14) | collective-permute-done | bytes 983072 | tf_op jit(solution)/shard_map/ppermute | solution.py:27
  75.8 12.9 %collective-permute-done.11.refs_8_ = bf16[96,5120]{1,0:T(8,128)(2,1)S(1)} collective-permute-done((bf16[96,5120]{1,0:T(8,128)(2,1)S(1)}, bf16[96,5120]{1,0:T(8,128)(2,1)S(1)}, u32[]{:S(2)}, u32[]{:S(2)}) %collective-permute-start.11) | collective-permute-done | bytes 983072 | tf_op jit(solution)/shard_map/ppermute | solution.py:27
  88.7 9.4 %collective-permute-done.8.refs_7_ = bf16[5136,128]{1,0:T(8,128)(2,1)S(1)} collective-permute-done((bf16[5136,128]{1,0:T(8,128)(2,1)S(1)}, bf16[5136,128]{1,0:T(8,128)(2,1)S(1)}, u32[]{:S(2)}, u32[]{:S(2)}) %collective-permute-start.8) | collective-permute-done | bytes 1314848 | tf_op jit(solution)/shard_map/ppermute | solution.py:27
  98.1 4.4 %collective-permute-start.15 = (bf16[96,5120]{1,0:T(8,128)(2,1)S(1)}, bf16[96,5120]{1,0:T(8,128)(2,1)S(1)}, u32[]{:S(2)}, u32[]{:S(2)}) collective-permute-start(bf16[96,5120]{1,0:T(8,128)(2,1)S(1)} %collective-permute-done.11.refs_8_), channel_id=1, source_target_pairs={{0,1},{1,0},{2,3},{3,2},{4,5},{5,4},{6,7},{7,6},{8,9},{9,8},{10,11... | collective-permute-start | bytes 2949128 | tf_op jit(solution)/shard_map/ppermute | solution.py:27
  102.6 2.2 collective-permute-done.15.refs_10_
  104.8 1.4 collective-permute-done.16.refs_11_
  106.2 0.4 collective-permute-start.17
  106.8 0.4 collective-permute-start.19
  107.3 0.4 collective-permute-start.21
  107.7 1.1 collective-permute-done.17.refs_10_
  108.7 0.4 collective-permute-start.22
  109.1 0.6 copy-done.22
  109.9 0.6 slice_bitcast_fusion.8
  110.5 13.5 %shard_map.65 = (bf16[192,5120]{1,0:T(8,128)(2,1)}, bf16[64,5120]{1,0:T(8,128)(2,1)}, bf16[64,5120]{1,0:T(8,128)(2,1)}, bf16[64,5120]{1,0:T(8,128)(2,1)}) custom-call(s32[8]{0:T(128)} %get-tuple-element.84.ids, s32[8]{0:T(128)} %get-tuple-element.109.sidx, f32[64]{0:T(128)} %table.7, bf16[5136,128]{1,0:T(8,128)(2,1)} %copy-done, ...), custom_call_target="tpu_custom_call" | custom-call | flops 6039797760 | bytes 23592960 | tf_op jit(solution)/shard_map/pallas_call | solution.py:204
  124.0 0.5 collective-permute-start.23
  124.6 0.4 collective-permute-start.25
  125.0 1.4 collective-permute-done.23
  126.4 0.9 collective-permute-done.24
  127.4 0.9 collective-permute-done.25
  128.3 2.2 add_convert_fusion
  130.5 1.5 fusion.13
  132.0 2.3 %collective-permute-start.30 = (bf16[96,5120]{1,0:T(8,128)(2,1)}, bf16[96,5120]{1,0:T(8,128)(2,1)S(1)}, u32[]{:S(2)}, u32[]{:S(2)}) collective-permute-start(bf16[96,5120]{1,0:T(8,128)(2,1)} %get-tuple-element.107), channel_id=1, source_target_pairs={{0,6},{1,7},{2,0},{3,1},{4,2},{5,3},{6,4},{7,5},{8,14},{9,15},{10,... | collective-permute-start | bytes 2949128 | tf_op jit(solution)/shard_map/ppermute | solution.py:27
  134.4 13.3 %shard_map.66 = (bf16[192,5120]{1,0:T(8,128)(2,1)}, bf16[64,5120]{1,0:T(8,128)(2,1)}, bf16[64,5120]{1,0:T(8,128)(2,1)}, bf16[64,5120]{1,0:T(8,128)(2,1)}) custom-call(s32[8]{0:T(128)} %get-tuple-element.84.ids, s32[8]{0:T(128)} %get-tuple-element.109.sidx, f32[64]{0:T(128)} %table.7, bf16[5136,128]{1,0:T(8,128)(2,1)} %copy-done, ...), custom_call_target="tpu_custom_call" | custom-call | flops 6039797760 | bytes 23592960 | tf_op jit(solution)/shard_map/pallas_call | solution.py:204
  147.7 0.7 collective-permute-start.26
  148.5 0.4 collective-permute-start.28
  148.9 13.5 %shard_map.67 = (bf16[192,5120]{1,0:T(8,128)(2,1)}, bf16[192,5120]{1,0:T(8,128)(2,1)}) custom-call(s32[8]{0:T(128)} %get-tuple-element.84.ids, s32[8]{0:T(128)} %get-tuple-element.109.sidx, f32[64]{0:T(128)} %table.7, bf16[5136,128]{1,0:T(8,128)(2,1)} %copy-done, bf16[5136,128]{1,0:T(8,128)(2,1)} %copy-done.12, bf16[5136,128]{1,0:T(8,128)(2,1)} %copy-done.13, ...), custom_call_target="tpu_custom_call" | custom-call | flops 6039797760 | bytes 23592960 | tf_op jit(solution)/shard_map/pallas_call | solution.py:204
  162.5 2.9 %convert_add_fusion.2 = (f32[192,5120]{1,0:T(8,128)S(1)}, bf16[192,5120]{1,0:T(8,128)(2,1)S(1)}) fusion(bf16[192,5120]{1,0:T(8,128)(2,1)S(1)} %copy-done.3, bf16[64,5120]{1,0:T(8,128)(2,1)} %collective-permute-done.28, bf16[64,5120]{1,0:T(8,128)(2,1)} %collective-permute-done.27, bf16[64,5120]{1,0:T(8,128)(2,1)} %collective-permute-done.26), kind=kLoop, calls=%fused_computation.2 | loop fusion | flops 8847360 | bytes 9830400 | tf_op jit(solution)/shard_map/add | solution.py:207
  165.5 0.2 fusion.7
  165.7 1.0 pad_maximum_fusion.4
  166.7 1.0 pad_maximum_fusion.3
  167.9 0.6 collective-permute-start.35
  168.5 2.4 %collective-permute-start.36 = (bf16[96,5120]{1,0:T(8,128)(2,1)}, bf16[96,5120]{1,0:T(8,128)(2,1)}, u32[]{:S(2)}, u32[]{:S(2)}) collective-permute-start(bf16[96,5120]{1,0:T(8,128)(2,1)} %pad_maximum_fusion.4), channel_id=1, source_target_pairs={{0,6},{1,7},{2,0},{3,1},{4,2},{5,3},{6,4},{7,5},{8,14},{9,15},{10,... | collective-permute-start | bytes 2949128 | tf_op jit(solution)/shard_map/ppermute | solution.py:27
  170.9 0.9 collective-permute-done.31
  171.7 13.4 %shard_map.68 = (bf16[192,5120]{1,0:T(8,128)(2,1)}, bf16[64,5120]{1,0:T(8,128)(2,1)}, bf16[64,5120]{1,0:T(8,128)(2,1)}, bf16[64,5120]{1,0:T(8,128)(2,1)}) custom-call(s32[8]{0:T(128)} %get-tuple-element.84.ids, s32[8]{0:T(128)} %get-tuple-element.109.sidx, f32[64]{0:T(128)} %table.7, bf16[5136,128]{1,0:T(8,128)(2,1)} %copy-done, ...), custom_call_target="tpu_custom_call" | custom-call | flops 6039797760 | bytes 23592960 | tf_op jit(solution)/shard_map/pallas_call | solution.py:204
  185.4 0.4 collective-permute-start.33
  185.9 0.5 convert_add_fusion.1
  186.4 6.5 %collective-permute-done.35 = bf16[96,5120]{1,0:T(8,128)(2,1)} collective-permute-done((bf16[96,5120]{1,0:T(8,128)(2,1)}, bf16[96,5120]{1,0:T(8,128)(2,1)}, u32[]{:S(2)}, u32[]{:S(2)}) %collective-permute-start.35) | collective-permute-done | bytes 983072 | tf_op jit(solution)/shard_map/ppermute | solution.py:27
  192.9 2.0 fusion.1
  195.0 0.7 collective-permute-start.39
  195.7 0.7 fusion.10
  196.8 2.5 %collective-permute-start.38 = (bf16[96,5120]{1,0:T(8,128)(2,1)S(1)}, bf16[96,5120]{1,0:T(8,128)(2,1)S(1)}, u32[]{:S(2)}, u32[]{:S(2)}) collective-permute-start(bf16[96,5120]{1,0:T(8,128)(2,1)S(1)} %pad_maximum_fusion.6), channel_id=1, source_target_pairs={{0,6},{1,7},{2,0},{3,1},{4,2},{5,3},{6,4},{7,5},{8,14},{9,15},{10,... | collective-permute-start | bytes 2949128 | tf_op jit(solution)/shard_map/ppermute | solution.py:27
  199.5 19.4 %collective-permute-done.39 = bf16[96,5120]{1,0:T(8,128)(2,1)S(1)} collective-permute-done((bf16[96,5120]{1,0:T(8,128)(2,1)S(1)}, bf16[96,5120]{1,0:T(8,128)(2,1)S(1)}, u32[]{:S(2)}, u32[]{:S(2)}) %collective-permute-start.39) | collective-permute-done | bytes 983072 | tf_op jit(solution)/shard_map/ppermute | solution.py:27
  219.0 3.3 %collective-permute-done.37 = bf16[96,5120]{1,0:T(8,128)(2,1)S(1)} collective-permute-done((bf16[96,5120]{1,0:T(8,128)(2,1)S(1)}, bf16[96,5120]{1,0:T(8,128)(2,1)S(1)}, u32[]{:S(2)}, u32[]{:S(2)}) %collective-permute-start.37) | collective-permute-done | bytes 983072 | tf_op jit(solution)/shard_map/ppermute | solution.py:27
  222.2 1.4 fusion.4
  (113 shorter events, 2.7 us)
Async XLA Ops:
  0.0 26.2 %collective-permute-start.2 = (bf16[96,5120]{1,0:T(8,128)(2,1)}, bf16[96,5120]{1,0:T(8,128)(2,1)}, u32[]{:S(2)}, u32[]{:S(2)}) collective-permute-start(bf16[96,5120]{1,0:T(8,128)(2,1)} %refs_9_.1), channel_id=1, source_target_pairs={{0,8},{1,9},{2,10},{3,11},{4,12},{5,13},{6,14},{7,15},{8,0},{9,1},... | collective-permute-start | bytes 2949128 | tf_op jit(solution)/shard_map/ppermute | solution.py:27
  7.2 95.4 %copy-start = (bf16[5136,128]{1,0:T(8,128)(2,1)}, bf16[5136,128]{1,0:T(8,128)(2,1)S(1)}, u32[]{:S(2)}) copy-start(bf16[5136,128]{1,0:T(8,128)(2,1)S(1)} %shard_map.64.refs_0_) | copy-start | bytes 3944452
  7.2 30.8 %collective-permute-start = (bf16[5136,128]{1,0:T(8,128)(2,1)S(1)}, bf16[5136,128]{1,0:T(8,128)(2,1)S(1)}, u32[]{:S(2)}, u32[]{:S(2)}) collective-permute-start(bf16[5136,128]{1,0:T(8,128)(2,1)S(1)} %shard_map.64.refs_0_), channel_id=1, source_target_pairs={{0,32},{1,33},{2,34},{3,35},{4,36},{5,37},{6,38},{7,39},{8,40},{9,... | collective-permute-start | bytes 3944456 | tf_op jit(solution)/shard_map/ppermute | solution.py:27
  8.5 30.8 %collective-permute-start.1 = (bf16[5136,128]{1,0:T(8,128)(2,1)S(1)}, bf16[5136,128]{1,0:T(8,128)(2,1)S(1)}, u32[]{:S(2)}, u32[]{:S(2)}) collective-permute-start(bf16[5136,128]{1,0:T(8,128)(2,1)S(1)} %shard_map.64.refs_0_), channel_id=1, source_target_pairs={{0,96},{1,97},{2,98},{3,99},{4,100},{5,101},{6,102},{7,103},{8,104... | collective-permute-start | bytes 3944456 | tf_op jit(solution)/shard_map/ppermute | solution.py:27
  10.1 29.4 %collective-permute-start.12 = (bf16[96,5120]{1,0:T(8,128)(2,1)}, bf16[96,5120]{1,0:T(8,128)(2,1)}, u32[]{:S(2)}, u32[]{:S(2)}) collective-permute-start(bf16[96,5120]{1,0:T(8,128)(2,1)} %refs_9_.1), channel_id=1, source_target_pairs={{0,6},{1,7},{2,0},{3,1},{4,2},{5,3},{6,4},{7,5},{8,14},{9,15},{10,... | collective-permute-start | bytes 2949128 | tf_op jit(solution)/shard_map/ppermute | solution.py:27
  12.5 29.7 %collective-permute-start.9 = (bf16[96,5120]{1,0:T(8,128)(2,1)}, bf16[96,5120]{1,0:T(8,128)(2,1)S(1)}, u32[]{:S(2)}, u32[]{:S(2)}) collective-permute-start(bf16[96,5120]{1,0:T(8,128)(2,1)} %refs_9_.1), channel_id=1, source_target_pairs={{0,2},{1,3},{2,4},{3,5},{4,6},{5,7},{6,0},{7,1},{8,10},{9,11},{10,... | collective-permute-start | bytes 2949128 | tf_op jit(solution)/shard_map/ppermute | solution.py:27
  26.2 27.4 %collective-permute-start.13 = (bf16[96,5120]{1,0:T(8,128)(2,1)}, bf16[96,5120]{1,0:T(8,128)(2,1)S(1)}, u32[]{:S(2)}, u32[]{:S(2)}) collective-permute-start(bf16[96,5120]{1,0:T(8,128)(2,1)} %collective-permute-done.2.refs_8_), channel_id=1, source_target_pairs={{0,6},{1,7},{2,0},{3,1},{4,2},{5,3},{6,4},{7,5},{8,14},{9,15},{10,... | collective-permute-start | bytes 2949128 | tf_op jit(solution)/shard_map/ppermute | solution.py:27
  38.0 68.5 %copy-start.12 = (bf16[5136,128]{1,0:T(8,128)(2,1)}, bf16[5136,128]{1,0:T(8,128)(2,1)S(1)}, u32[]{:S(2)}) copy-start(bf16[5136,128]{1,0:T(8,128)(2,1)S(1)} %collective-permute-done.refs_1_) | copy-start | bytes 3944452
  38.0 23.0 %collective-permute-start.10 = (bf16[96,5120]{1,0:T(8,128)(2,1)}, bf16[96,5120]{1,0:T(8,128)(2,1)}, u32[]{:S(2)}, u32[]{:S(2)}) collective-permute-start(bf16[96,5120]{1,0:T(8,128)(2,1)} %collective-permute-done.2.refs_8_), channel_id=1, source_target_pairs={{0,2},{1,3},{2,4},{3,5},{4,6},{5,7},{6,0},{7,1},{8,10},{9,11},{10,... | collective-permute-start | bytes 2949128 | tf_op jit(solution)/shard_map/ppermute | solution.py:27
  39.3 63.2 %copy-start.13 = (bf16[5136,128]{1,0:T(8,128)(2,1)}, bf16[5136,128]{1,0:T(8,128)(2,1)S(1)}, u32[]{:S(2)}) copy-start(bf16[5136,128]{1,0:T(8,128)(2,1)S(1)} %collective-permute-done.1.refs_2_) | copy-start | bytes 3944452
  39.3 22.7 %collective-permute-start.4 = (bf16[2576,128]{1,0:T(8,128)(2,1)S(1)}, bf16[2576,128]{1,0:T(8,128)(2,1)S(1)}, u32[]{:S(2)}, u32[]{:S(2)}) collective-permute-start(bf16[2576,128]{1,0:T(8,128)(2,1)S(1)} %pad_maximum_fusion.7), channel_id=1, source_target_pairs={{0,32},{1,33},{2,34},{3,35},{4,36},{5,37},{6,38},{7,39},{8,40},{9,... | collective-permute-start | bytes 1978376 | tf_op jit(solution)/shard_map/ppermute | solution.py:27
  39.5 22.7 %collective-permute-start.7 = (bf16[2560,128]{1,0:T(8,128)(2,1)S(1)}, bf16[2560,128]{1,0:T(8,128)(2,1)S(1)}, u32[]{:S(2)}, u32[]{:S(2)}) collective-permute-start(bf16[2560,128]{1,0:T(8,128)(2,1)S(1)} %slice.169), channel_id=1, source_target_pairs={{0,96},{1,97},{2,98},{3,99},{4,100},{5,101},{6,102},{7,103},{8,104... | collective-permute-start | bytes 1966088 | tf_op jit(solution)/shard_map/ppermute | solution.py:27
  42.2 11.5 %copy-start.4 = (bf16[96,5120]{1,0:T(8,128)(2,1)}, bf16[96,5120]{1,0:T(8,128)(2,1)S(1)}, u32[]{:S(2)}) copy-start(bf16[96,5120]{1,0:T(8,128)(2,1)S(1)} %collective-permute-done.9.refs_9_) | copy-start | bytes 2949124
  42.2 27.7 %collective-permute-start.3 = (bf16[5136,128]{1,0:T(8,128)(2,1)S(1)}, bf16[5136,128]{1,0:T(8,128)(2,1)S(1)}, u32[]{:S(2)}, u32[]{:S(2)}) collective-permute-start(bf16[5136,128]{1,0:T(8,128)(2,1)S(1)} %shard_map.64.refs_0_), channel_id=1, source_target_pairs={{0,16},{1,17},{2,18},{3,19},{4,20},{5,21},{6,22},{7,23},{8,24},{9,... | collective-permute-start | bytes 3944456 | tf_op jit(solution)/shard_map/ppermute | solution.py:27
  53.6 52.6 %copy-start.14 = (bf16[96,5120]{1,0:T(8,128)(2,1)}, bf16[96,5120]{1,0:T(8,128)(2,1)S(1)}, u32[]{:S(2)}) copy-start(bf16[96,5120]{1,0:T(8,128)(2,1)S(1)} %collective-permute-done.13.refs_8_) | copy-start | bytes 2949124
  53.7 22.1 %collective-permute-start.14 = (bf16[96,5120]{1,0:T(8,128)(2,1)S(1)}, bf16[96,5120]{1,0:T(8,128)(2,1)S(1)}, u32[]{:S(2)}, u32[]{:S(2)}) collective-permute-start(bf16[96,5120]{1,0:T(8,128)(2,1)S(1)} %pad_maximum_fusion.2), channel_id=1, source_target_pairs={{0,6},{1,7},{2,0},{3,1},{4,2},{5,3},{6,4},{7,5},{8,14},{9,15},{10,... | collective-permute-start | bytes 2949128 | tf_op jit(solution)/shard_map/ppermute | solution.py:27
  62.1 9.3 %slice-start = ((bf16[96,5120]{1,0:T(8,128)(2,1)}), bf16[48,5120]{1,0:T(8,128)(2,1)S(1)}, s32[]{:S(2)}) async-start(bf16[96,5120]{1,0:T(8,128)(2,1)} %copy-done.4), calls=%async_computation | async-start | bytes 983040 | tf_op jit(solution)/shard_map/slice | solution.py:191
  62.1 45.0 %copy-start.5 = (bf16[96,5120]{1,0:T(8,128)(2,1)S(1)}, bf16[96,5120]{1,0:T(8,128)(2,1)}, u32[]{:S(2)}) copy-start(bf16[96,5120]{1,0:T(8,128)(2,1)} %copy-done.4) | copy-start | bytes 2949124
  62.2 45.0 %copy-start.7 = (bf16[5136,128]{1,0:T(8,128)(2,1)}, bf16[5136,128]{1,0:T(8,128)(2,1)S(1)}, u32[]{:S(2)}) copy-start(bf16[5136,128]{1,0:T(8,128)(2,1)S(1)} %pad_maximum_fusion.refs_4_) | copy-start | bytes 3944452
  62.3 35.9 %collective-permute-start.8 = (bf16[5136,128]{1,0:T(8,128)(2,1)S(1)}, bf16[5136,128]{1,0:T(8,128)(2,1)S(1)}, u32[]{:S(2)}, u32[]{:S(2)}) collective-permute-start(bf16[5136,128]{1,0:T(8,128)(2,1)S(1)} %pad_maximum_fusion.refs_4_), channel_id=1, source_target_pairs={{0,16},{1,17},{2,18},{3,19},{4,20},{5,21},{6,22},{7,23},{8,24},{9,... | collective-permute-start | bytes 3944456 | tf_op jit(solution)/shard_map/ppermute | solution.py:27
  69.9 39.2 %copy-start.16 = (bf16[5136,128]{1,0:T(8,128)(2,1)}, bf16[5136,128]{1,0:T(8,128)(2,1)S(1)}, u32[]{:S(2)}) copy-start(bf16[5136,128]{1,0:T(8,128)(2,1)S(1)} %collective-permute-done.3.refs_3_) | copy-start | bytes 3944452
  69.9 28.2 %collective-permute-start.6 = (bf16[5136,128]{1,0:T(8,128)(2,1)S(1)}, bf16[5136,128]{1,0:T(8,128)(2,1)S(1)}, u32[]{:S(2)}, u32[]{:S(2)}) collective-permute-start(bf16[5136,128]{1,0:T(8,128)(2,1)S(1)} %collective-permute-done.3.refs_3_), channel_id=1, source_target_pairs={{0,96},{1,97},{2,98},{3,99},{4,100},{5,101},{6,102},{7,103},{8,104... | collective-permute-start | bytes 3944456 | tf_op jit(solution)/shard_map/ppermute | solution.py:27
  70.1 28.1 %collective-permute-start.5 = (bf16[5136,128]{1,0:T(8,128)(2,1)S(1)}, bf16[5136,128]{1,0:T(8,128)(2,1)S(1)}, u32[]{:S(2)}, u32[]{:S(2)}) collective-permute-start(bf16[5136,128]{1,0:T(8,128)(2,1)S(1)} %collective-permute-done.3.refs_3_), channel_id=1, source_target_pairs={{0,32},{1,33},{2,34},{3,35},{4,36},{5,37},{6,38},{7,39},{8,40},{9,... | collective-permute-start | bytes 3944456 | tf_op jit(solution)/shard_map/ppermute | solution.py:27
  71.5 17.2 %collective-permute-start.11 = (bf16[96,5120]{1,0:T(8,128)(2,1)S(1)}, bf16[96,5120]{1,0:T(8,128)(2,1)S(1)}, u32[]{:S(2)}, u32[]{:S(2)}) collective-permute-start(bf16[96,5120]{1,0:T(8,128)(2,1)S(1)} %pad_maximum_fusion.1), channel_id=1, source_target_pairs={{0,2},{1,3},{2,4},{3,5},{4,6},{5,7},{6,0},{7,1},{8,10},{9,11},{10,... | collective-permute-start | bytes 2949128 | tf_op jit(solution)/shard_map/ppermute | solution.py:27
  75.8 33.3 %copy-start.21 = (bf16[96,5120]{1,0:T(8,128)(2,1)}, bf16[96,5120]{1,0:T(8,128)(2,1)S(1)}, u32[]{:S(2)}) copy-start(bf16[96,5120]{1,0:T(8,128)(2,1)S(1)} %collective-permute-done.14.refs_9_) | copy-start | bytes 2949124
  88.7 16.0 %copy-start.23 = (bf16[96,5120]{1,0:T(8,128)(2,1)}, bf16[96,5120]{1,0:T(8,128)(2,1)S(1)}, u32[]{:S(2)}) copy-start(bf16[96,5120]{1,0:T(8,128)(2,1)S(1)} %collective-permute-done.11.refs_8_) | copy-start | bytes 2949124
  98.1 11.0 %copy-start.17 = (bf16[5136,128]{1,0:T(8,128)(2,1)}, bf16[5136,128]{1,0:T(8,128)(2,1)S(1)}, u32[]{:S(2)}) copy-start(bf16[5136,128]{1,0:T(8,128)(2,1)S(1)} %collective-permute-done.8.refs_7_) | copy-start | bytes 3944452
  98.1 11.0 %copy-start.18 = (bf16[5136,128]{1,0:T(8,128)(2,1)}, bf16[5136,128]{1,0:T(8,128)(2,1)S(1)}, u32[]{:S(2)}) copy-start(bf16[5136,128]{1,0:T(8,128)(2,1)S(1)} %collective-permute-done.6.refs_6_) | copy-start | bytes 3944452
  98.1 11.0 %copy-start.19 = (bf16[5136,128]{1,0:T(8,128)(2,1)}, bf16[5136,128]{1,0:T(8,128)(2,1)S(1)}, u32[]{:S(2)}) copy-start(bf16[5136,128]{1,0:T(8,128)(2,1)S(1)} %collective-permute-done.5.refs_5_) | copy-start | bytes 3944452
  98.1 6.6 %collective-permute-start.15 = (bf16[96,5120]{1,0:T(8,128)(2,1)S(1)}, bf16[96,5120]{1,0:T(8,128)(2,1)S(1)}, u32[]{:S(2)}, u32[]{:S(2)}) collective-permute-start(bf16[96,5120]{1,0:T(8,128)(2,1)S(1)} %collective-permute-done.11.refs_8_), channel_id=1, source_target_pairs={{0,1},{1,0},{2,3},{3,2},{4,5},{5,4},{6,7},{7,6},{8,9},{9,8},{10,11... | collective-permute-start | bytes 2949128 | tf_op jit(solution)/shard_map/ppermute | solution.py:27
  102.6 3.6 %collective-permute-start.16 = (bf16[96,5120]{1,0:T(8,128)(2,1)S(1)}, bf16[96,5120]{1,0:T(8,128)(2,1)S(1)}, u32[]{:S(2)}, u32[]{:S(2)}) collective-permute-start(bf16[96,5120]{1,0:T(8,128)(2,1)S(1)} %collective-permute-done.14.refs_9_), channel_id=1, source_target_pairs={{0,1},{1,0},{2,3},{3,2},{4,5},{5,4},{6,7},{7,6},{8,9},{9,8},{10,11... | collective-permute-start | bytes 2949128 | tf_op jit(solution)/shard_map/ppermute | solution.py:27
  104.7 4.4 %copy-start.24 = (bf16[96,5120]{1,0:T(8,128)(2,1)}, bf16[96,5120]{1,0:T(8,128)(2,1)S(1)}, u32[]{:S(2)}) copy-start(bf16[96,5120]{1,0:T(8,128)(2,1)S(1)} %collective-permute-done.15.refs_10_) | copy-start | bytes 2949124
  106.2 3.0 %copy-start.25 = (bf16[96,5120]{1,0:T(8,128)(2,1)}, bf16[96,5120]{1,0:T(8,128)(2,1)S(1)}, u32[]{:S(2)}) copy-start(bf16[96,5120]{1,0:T(8,128)(2,1)S(1)} %collective-permute-done.16.refs_11_) | copy-start | bytes 2949124
  106.2 2.6 %collective-permute-start.17 = (bf16[96,5120]{1,0:T(8,128)(2,1)S(1)}, bf16[96,5120]{1,0:T(8,128)(2,1)S(1)}, u32[]{:S(2)}, u32[]{:S(2)}) collective-permute-start(bf16[96,5120]{1,0:T(8,128)(2,1)S(1)} %collective-permute-done.13.refs_8_), channel_id=1, source_target_pairs={{0,1},{1,0},{2,3},{3,2},{4,5},{5,4},{6,7},{7,6},{8,9},{9,8},{10,11... | collective-permute-start | bytes 2949128 | tf_op jit(solution)/shard_map/ppermute | solution.py:27
  106.6 17.4 %collective-permute-start.18 = (bf16[96,5120]{1,0:T(8,128)(2,1)}, bf16[96,5120]{1,0:T(8,128)(2,1)}, u32[]{:S(2)}, u32[]{:S(2)}) collective-permute-start(bf16[96,5120]{1,0:T(8,128)(2,1)} %collective-permute-done.10.refs_9_), channel_id=1, source_target_pairs={{0,1},{1,0},{2,3},{3,2},{4,5},{5,4},{6,7},{7,6},{8,9},{9,8},{10,11... | collective-permute-start | bytes 2949128 | tf_op jit(solution)/shard_map/ppermute | solution.py:27
  106.8 17.2 %collective-permute-start.19 = (bf16[96,5120]{1,0:T(8,128)(2,1)}, bf16[96,5120]{1,0:T(8,128)(2,1)S(1)}, u32[]{:S(2)}, u32[]{:S(2)}) collective-permute-start(bf16[96,5120]{1,0:T(8,128)(2,1)} %collective-permute-done.12.refs_8_), channel_id=1, source_target_pairs={{0,1},{1,0},{2,3},{3,2},{4,5},{5,4},{6,7},{7,6},{8,9},{9,8},{10,11... | collective-permute-start | bytes 2949128 | tf_op jit(solution)/shard_map/ppermute | solution.py:27
  107.2 16.8 %collective-permute-start.20 = (bf16[96,5120]{1,0:T(8,128)(2,1)S(1)}, bf16[96,5120]{1,0:T(8,128)(2,1)}, u32[]{:S(2)}, u32[]{:S(2)}) collective-permute-start(bf16[96,5120]{1,0:T(8,128)(2,1)S(1)} %copy-done.5), channel_id=1, source_target_pairs={{0,1},{1,0},{2,3},{3,2},{4,5},{5,4},{6,7},{7,6},{8,9},{9,8},{10,11... | collective-permute-start | bytes 2949128 | tf_op jit(solution)/shard_map/ppermute | solution.py:27
  107.3 16.7 %collective-permute-start.21 = (bf16[96,5120]{1,0:T(8,128)(2,1)}, bf16[96,5120]{1,0:T(8,128)(2,1)}, u32[]{:S(2)}, u32[]{:S(2)}) collective-permute-start(bf16[96,5120]{1,0:T(8,128)(2,1)} %collective-permute-done.2.refs_8_), channel_id=1, source_target_pairs={{0,1},{1,0},{2,3},{3,2},{4,5},{5,4},{6,7},{7,6},{8,9},{9,8},{10,11... | collective-permute-start | bytes 2949128 | tf_op jit(solution)/shard_map/ppermute | solution.py:27
  108.7 15.3 %collective-permute-start.22 = (bf16[96,5120]{1,0:T(8,128)(2,1)}, bf16[96,5120]{1,0:T(8,128)(2,1)}, u32[]{:S(2)}, u32[]{:S(2)}) collective-permute-start(bf16[96,5120]{1,0:T(8,128)(2,1)} %refs_9_.1), channel_id=1, source_target_pairs={{0,1},{1,0},{2,3},{3,2},{4,5},{5,4},{6,7},{7,6},{8,9},{9,8},{10,11... | collective-permute-start | bytes 2949128 | tf_op jit(solution)/shard_map/ppermute | solution.py:27
  124.0 6.5 %copy-start.20 = (bf16[96,5120]{1,0:T(8,128)(2,1)}, bf16[96,5120]{1,0:T(8,128)(2,1)S(1)}, u32[]{:S(2)}) copy-start(bf16[96,5120]{1,0:T(8,128)(2,1)S(1)} %collective-permute-done.19.refs_10_) | copy-start | bytes 2949124
  124.0 2.4 %collective-permute-start.23 = (bf16[64,5120]{1,0:T(8,128)(2,1)}, bf16[64,5120]{1,0:T(8,128)(2,1)S(1)}, u32[]{:S(2)}, u32[]{:S(2)}) collective-permute-start(bf16[64,5120]{1,0:T(8,128)(2,1)} %get-tuple-element.64), channel_id=1, source_target_pairs={{0,1},{1,0},{2,3},{3,2},{4,5},{5,4},{6,7},{7,6},{8,9},{9,8},{10,11... | collective-permute-start | bytes 1966088 | tf_op jit(solution)/shard_map/ppermute | solution.py:27
  124.5 2.9 %collective-permute-start.24 = (bf16[64,5120]{1,0:T(8,128)(2,1)}, bf16[64,5120]{1,0:T(8,128)(2,1)S(1)}, u32[]{:S(2)}, u32[]{:S(2)}) collective-permute-start(bf16[64,5120]{1,0:T(8,128)(2,1)} %get-tuple-element.65), channel_id=1, source_target_pairs={{0,1},{1,0},{2,3},{3,2},{4,5},{5,4},{6,7},{7,6},{8,9},{9,8},{10,11... | collective-permute-start | bytes 1966088 | tf_op jit(solution)/shard_map/ppermute | solution.py:27
  124.6 3.7 %collective-permute-start.25 = (bf16[64,5120]{1,0:T(8,128)(2,1)}, bf16[64,5120]{1,0:T(8,128)(2,1)S(1)}, u32[]{:S(2)}, u32[]{:S(2)}) collective-permute-start(bf16[64,5120]{1,0:T(8,128)(2,1)} %get-tuple-element.66), channel_id=1, source_target_pairs={{0,1},{1,0},{2,3},{3,2},{4,5},{5,4},{6,7},{7,6},{8,9},{9,8},{10,11... | collective-permute-start | bytes 1966088 | tf_op jit(solution)/shard_map/ppermute | solution.py:27
  132.0 30.4 %collective-permute-start.30 = (bf16[96,5120]{1,0:T(8,128)(2,1)}, bf16[96,5120]{1,0:T(8,128)(2,1)S(1)}, u32[]{:S(2)}, u32[]{:S(2)}) collective-permute-start(bf16[96,5120]{1,0:T(8,128)(2,1)} %get-tuple-element.107), channel_id=1, source_target_pairs={{0,6},{1,7},{2,0},{3,1},{4,2},{5,3},{6,4},{7,5},{8,14},{9,15},{10,... | collective-permute-start | bytes 2949128 | tf_op jit(solution)/shard_map/ppermute | solution.py:27
  134.4 28.1 %collective-permute-start.29 = (bf16[96,5120]{1,0:T(8,128)(2,1)}, bf16[96,5120]{1,0:T(8,128)(2,1)S(1)}, u32[]{:S(2)}, u32[]{:S(2)}) collective-permute-start(bf16[96,5120]{1,0:T(8,128)(2,1)} %get-tuple-element.108), channel_id=1, source_target_pairs={{0,2},{1,3},{2,4},{3,5},{4,6},{5,7},{6,0},{7,1},{8,10},{9,11},{10,... | collective-permute-start | bytes 2949128 | tf_op jit(solution)/shard_map/ppermute | solution.py:27
  147.7 14.7 %collective-permute-start.26 = (bf16[64,5120]{1,0:T(8,128)(2,1)}, bf16[64,5120]{1,0:T(8,128)(2,1)}, u32[]{:S(2)}, u32[]{:S(2)}) collective-permute-start(bf16[64,5120]{1,0:T(8,128)(2,1)} %get-tuple-element.69), channel_id=1, source_target_pairs={{0,1},{1,0},{2,3},{3,2},{4,5},{5,4},{6,7},{7,6},{8,9},{9,8},{10,11... | collective-permute-start | bytes 1966088 | tf_op jit(solution)/shard_map/ppermute | solution.py:27
  148.4 14.0 %collective-permute-start.27 = (bf16[64,5120]{1,0:T(8,128)(2,1)}, bf16[64,5120]{1,0:T(8,128)(2,1)}, u32[]{:S(2)}, u32[]{:S(2)}) collective-permute-start(bf16[64,5120]{1,0:T(8,128)(2,1)} %get-tuple-element.70), channel_id=1, source_target_pairs={{0,1},{1,0},{2,3},{3,2},{4,5},{5,4},{6,7},{7,6},{8,9},{9,8},{10,11... | collective-permute-start | bytes 1966088 | tf_op jit(solution)/shard_map/ppermute | solution.py:27
  148.5 13.9 %collective-permute-start.28 = (bf16[64,5120]{1,0:T(8,128)(2,1)}, bf16[64,5120]{1,0:T(8,128)(2,1)}, u32[]{:S(2)}, u32[]{:S(2)}) collective-permute-start(bf16[64,5120]{1,0:T(8,128)(2,1)} %get-tuple-element.71), channel_id=1, source_target_pairs={{0,1},{1,0},{2,3},{3,2},{4,5},{5,4},{6,7},{7,6},{8,9},{9,8},{10,11... | collective-permute-start | bytes 1966088 | tf_op jit(solution)/shard_map/ppermute | solution.py:27
  148.9 13.5 %copy-start.3 = (bf16[192,5120]{1,0:T(8,128)(2,1)S(1)}, bf16[192,5120]{1,0:T(8,128)(2,1)}, u32[]{:S(2)}) copy-start(bf16[192,5120]{1,0:T(8,128)(2,1)} %get-tuple-element.77) | copy-start | bytes 5898244
  162.4 3.0 %copy-start.8 = (bf16[96,5120]{1,0:T(8,128)(2,1)}, bf16[96,5120]{1,0:T(8,128)(2,1)S(1)}, u32[]{:S(2)}) copy-start(bf16[96,5120]{1,0:T(8,128)(2,1)S(1)} %collective-permute-done.30) | copy-start | bytes 2949124
  162.4 3.0 %copy-start.10 = (bf16[96,5120]{1,0:T(8,128)(2,1)}, bf16[96,5120]{1,0:T(8,128)(2,1)S(1)}, u32[]{:S(2)}) copy-start(bf16[96,5120]{1,0:T(8,128)(2,1)S(1)} %collective-permute-done.29) | copy-start | bytes 2949124
  165.7 2.0 copy-start.15
  167.8 18.1 %copy-start.6 = (bf16[192,5120]{1,0:T(8,128)(2,1)S(1)}, bf16[192,5120]{1,0:T(8,128)(2,1)}, u32[]{:S(2)}) copy-start(bf16[192,5120]{1,0:T(8,128)(2,1)} %get-tuple-element.75) | copy-start | bytes 5898244
  167.8 4.0 %collective-permute-start.31 = (bf16[192,5120]{1,0:T(8,128)(2,1)S(1)}, bf16[192,5120]{1,0:T(8,128)(2,1)S(1)}, u32[]{:S(2)}, u32[]{:S(2)}) collective-permute-start(bf16[192,5120]{1,0:T(8,128)(2,1)S(1)} %copy-done.15), channel_id=1, source_target_pairs={{0,1},{1,0},{2,3},{3,2},{4,5},{5,4},{6,7},{7,6},{8,9},{9,8},{10,11... | collective-permute-start | bytes 5898248 | tf_op jit(solution)/shard_map/ppermute | solution.py:27
  167.9 25.0 %collective-permute-start.35 = (bf16[96,5120]{1,0:T(8,128)(2,1)}, bf16[96,5120]{1,0:T(8,128)(2,1)}, u32[]{:S(2)}, u32[]{:S(2)}) collective-permute-start(bf16[96,5120]{1,0:T(8,128)(2,1)} %pad_maximum_fusion.3), channel_id=1, source_target_pairs={{0,2},{1,3},{2,4},{3,5},{4,6},{5,7},{6,0},{7,1},{8,10},{9,11},{10,... | collective-permute-start | bytes 2949128 | tf_op jit(solution)/shard_map/ppermute | solution.py:27
  168.5 24.4 %collective-permute-start.36 = (bf16[96,5120]{1,0:T(8,128)(2,1)}, bf16[96,5120]{1,0:T(8,128)(2,1)}, u32[]{:S(2)}, u32[]{:S(2)}) collective-permute-start(bf16[96,5120]{1,0:T(8,128)(2,1)} %pad_maximum_fusion.4), channel_id=1, source_target_pairs={{0,6},{1,7},{2,0},{3,1},{4,2},{5,3},{6,4},{7,5},{8,14},{9,15},{10,... | collective-permute-start | bytes 2949128 | tf_op jit(solution)/shard_map/ppermute | solution.py:27
  185.2 7.8 %collective-permute-start.32 = (bf16[64,5120]{1,0:T(8,128)(2,1)}, bf16[64,5120]{1,0:T(8,128)(2,1)S(1)}, u32[]{:S(2)}, u32[]{:S(2)}) collective-permute-start(bf16[64,5120]{1,0:T(8,128)(2,1)} %get-tuple-element.86), channel_id=1, source_target_pairs={{0,1},{1,0},{2,3},{3,2},{4,5},{5,4},{6,7},{7,6},{8,9},{9,8},{10,11... | collective-permute-start | bytes 1966088 | tf_op jit(solution)/shard_map/ppermute | solution.py:27
  185.4 7.5 %collective-permute-start.33 = (bf16[64,5120]{1,0:T(8,128)(2,1)}, bf16[64,5120]{1,0:T(8,128)(2,1)S(1)}, u32[]{:S(2)}, u32[]{:S(2)}) collective-permute-start(bf16[64,5120]{1,0:T(8,128)(2,1)} %get-tuple-element.87), channel_id=1, source_target_pairs={{0,1},{1,0},{2,3},{3,2},{4,5},{5,4},{6,7},{7,6},{8,9},{9,8},{10,11... | collective-permute-start | bytes 1966088 | tf_op jit(solution)/shard_map/ppermute | solution.py:27
  185.7 7.2 %collective-permute-start.34 = (bf16[64,5120]{1,0:T(8,128)(2,1)}, bf16[64,5120]{1,0:T(8,128)(2,1)S(1)}, u32[]{:S(2)}, u32[]{:S(2)}) collective-permute-start(bf16[64,5120]{1,0:T(8,128)(2,1)} %get-tuple-element.88), channel_id=1, source_target_pairs={{0,1},{1,0},{2,3},{3,2},{4,5},{5,4},{6,7},{7,6},{8,9},{9,8},{10,11... | collective-permute-start | bytes 1966088 | tf_op jit(solution)/shard_map/ppermute | solution.py:27
  192.9 2.7 %copy-start.2 = (bf16[192,5120]{1,0:T(8,128)(2,1)S(1)}, bf16[192,5120]{1,0:T(8,128)(2,1)}, u32[]{:S(2)}) copy-start(bf16[192,5120]{1,0:T(8,128)(2,1)} %get-tuple-element.89) | copy-start | bytes 5898244
  195.0 1.5 copy-start.11
  195.0 23.9 %collective-permute-start.39 = (bf16[96,5120]{1,0:T(8,128)(2,1)S(1)}, bf16[96,5120]{1,0:T(8,128)(2,1)S(1)}, u32[]{:S(2)}, u32[]{:S(2)}) collective-permute-start(bf16[96,5120]{1,0:T(8,128)(2,1)S(1)} %fusion.1), channel_id=1, source_target_pairs={{0,8},{1,9},{2,10},{3,11},{4,12},{5,13},{6,14},{7,15},{8,0},{9,1},... | collective-permute-start | bytes 2949128 | tf_op jit(solution)/shard_map/ppermute | solution.py:27
  196.8 22.2 %collective-permute-start.38 = (bf16[96,5120]{1,0:T(8,128)(2,1)S(1)}, bf16[96,5120]{1,0:T(8,128)(2,1)S(1)}, u32[]{:S(2)}, u32[]{:S(2)}) collective-permute-start(bf16[96,5120]{1,0:T(8,128)(2,1)S(1)} %pad_maximum_fusion.6), channel_id=1, source_target_pairs={{0,6},{1,7},{2,0},{3,1},{4,2},{5,3},{6,4},{7,5},{8,14},{9,15},{10,... | collective-permute-start | bytes 2949128 | tf_op jit(solution)/shard_map/ppermute | solution.py:27
  199.4 22.8 %collective-permute-start.37 = (bf16[96,5120]{1,0:T(8,128)(2,1)S(1)}, bf16[96,5120]{1,0:T(8,128)(2,1)S(1)}, u32[]{:S(2)}, u32[]{:S(2)}) collective-permute-start(bf16[96,5120]{1,0:T(8,128)(2,1)S(1)} %pad_maximum_fusion.5), channel_id=1, source_target_pairs={{0,2},{1,3},{2,4},{3,5},{4,6},{5,7},{6,0},{7,1},{8,10},{9,11},{10,... | collective-permute-start | bytes 2949128 | tf_op jit(solution)/shard_map/ppermute | solution.py:27
  (3 other events, 3.8 us)
where the time goes:
time: 225 us; the launch traced here: 224 us
  waiting for transfers between devices  107 us (48%)
  Pallas kernels  53.8 us (24%)
  starting transfers between devices  41.9 us (19%)
  other arithmetic  12.6 us (6%)
  local copies, waits for them, and re-layouts  6.72 us (3%)
    ppermute x40, waiting for transfers between devices, move(): return lax.ppermute(value, AXES, pairs)  107 us
    pallas_call x4, Pallas kernels, sums(): return tuple(run(ids, sidx, scale_table, *sources, *pieces, down_weight))  53.7 us
    ppermute x40, starting transfers between devices, move(): return lax.ppermute(value, AXES, pairs)  41.9 us
  transfers between devices with their start and end apart: 40, of which 19 were waited for; matrix products, arithmetic and copies ran while one was open for 2% of the time, Pallas kernels for 24%

commit v1 on v0

--- a/solution.py
+++ b/solution.py
@@ -60,19 +60,21 @@
     )(block_ids, scale_idx, codes)
 
 
-def feed_forward(code_map, row_map, depth, width, local_ff, parts):
+def feed_forward(code_map, row_map, ranges, depth, width, local_ff):
     n_codes = 1 + max(m[1] for m in code_map)
     n_rows = 1 + max(m[0] for m in row_map)
     slots = 1 + max(m[0] for m in code_map)
     blocks = slots // 2
     rows = sum(m[2] for m in row_map)
-    n_copies = len(code_map) + len(row_map) + 1 + 2 * (1 + parts)
+    tile = rows if rows <= 576 else rows // 2
+    n_out = len(ranges)
     base = len(code_map) + len(row_map)
+    n_copies = base + 1 + 2 * n_out
 
     def kernel(ids, sidx, table, *refs):
         sources, refs = refs[:n_codes], refs[n_codes:]
         pieces, refs = refs[:n_rows], refs[n_rows:]
-        down, outs, (w, x, dn, proj, hid, out, sem) = refs[0], refs[1 : 2 + parts], refs[2 + parts :]
+        down, outs, (w, x, dn, proj, hid, out, sem) = refs[0], refs[1 : 1 + n_out], refs[1 + n_out :]
         at = 0
         first = []
         for i, (src, start, n) in enumerate(row_map):
@@ -105,24 +107,27 @@
                         for c in stages[q + 2]:
                             c.start()
 
-            acc = jnp.dot(x[...], w[pair], preferred_element_type=F32)
-            for side in range(2):
-                slot = 2 * pair + side
-                proj[ids[slot]] = acc[:, side * width : (side + 1) * width] * table[sidx[slot]]
-
-        for b in range(blocks):
-            gate, up = proj[b], proj[b + blocks]
-            hid[:, b * width : (b + 1) * width] = (gate / (1.0 + jnp.exp(-gate)) * up).astype(BF16)
+            @pl.loop(0, rows // tile)
+            def _(part):
+                at = pl.ds(pl.multiple_of(part * tile, tile), tile)
+                acc = jnp.dot(x[at, :], w[pair], preferred_element_type=F32)
+                for side in range(2):
+                    slot = 2 * pair + side
+                    proj[ids[slot], at] = acc[:, side * width : (side + 1) * width] * table[sidx[slot]]
+
+        @pl.loop(0, rows // tile)
+        def _(part):
+            at = pl.ds(pl.multiple_of(part * tile, tile), tile)
+            for b in range(blocks):
+                gate, up = proj[b, at], proj[b + blocks, at]
+                hid[at, b * width : (b + 1) * width] = (gate / (1.0 + jnp.exp(-gate)) * up).astype(BF16)
+
         down_copy.wait()
 
         def leave(n, slot):
             cols = pl.ds(pl.multiple_of(n * STEP, STEP), STEP)
-            piece = rows // 2 // parts
-            ranges = [(0, rows // 2)] + [(rows // 2 + i * piece, piece) for i in range(parts)]
             return [
-                pltpu.make_async_copy(
-                    out.at[slot, pl.ds(at, n)], outs[i].at[:, cols], sem.at[base + slot * (1 + parts) + i]
-                )
+                pltpu.make_async_copy(out.at[slot, pl.ds(at, n)], outs[i].at[:, cols], sem.at[base + slot * n_out + i])
                 for i, (at, n) in enumerate(ranges)
             ]
 
@@ -138,7 +143,12 @@
                     c.wait()
 
             cols = pl.ds(pl.multiple_of(n * STEP, STEP), STEP)
-            out[slot] = jnp.dot(hid[...], dn[:, cols], preferred_element_type=F32).astype(BF16)
+
+            @pl.loop(0, rows // tile)
+            def _(part):
+                at = pl.ds(pl.multiple_of(part * tile, tile), tile)
+                out[slot, at] = jnp.dot(hid[at, :], dn[:, cols], preferred_element_type=F32).astype(BF16)
+
             for c in leave(n, slot):
                 c.start()
 
@@ -148,13 +158,11 @@
 
     anywhere = pl.BlockSpec(memory_space=pltpu.HBM)
     smem = pl.BlockSpec(memory_space=pltpu.SMEM)
-    half = jax.ShapeDtypeStruct((rows // 2, depth), BF16)
-    piece = jax.ShapeDtypeStruct((rows // 2 // parts, depth), BF16)
     return pl.pallas_call(
         kernel,
-        out_shape=(half,) + (piece,) * parts,
+        out_shape=tuple(jax.ShapeDtypeStruct((n, depth), BF16) for _, n in ranges),
         in_specs=[smem] * 3 + [anywhere] * (n_codes + n_rows + 1),
-        out_specs=(anywhere,) * (1 + parts),
+        out_specs=(anywhere,) * n_out,
         scratch_shapes=[
             pltpu.VMEM((blocks, depth, 2 * width), BF16),
             pltpu.VMEM((rows, depth), BF16),
@@ -187,9 +195,11 @@
     y_low = move(cb[h_depth:depth], dy=-1)
     taz, tbz = move(tz, dx=1), move(tz, dx=-1)
     cy = rows_of(y_top[:h_depth], y_low, y_top[h_depth:])
+    top_in, low_in = rows_of(ta[:h_rows], taz[:h_rows]), rows_of(tb[h_rows:], tbz[h_rows:])
+    cy = after(cy, cz)
+    top_in, low_in = after((top_in, low_in), cy)
     caz, cbz, cyz = move(cz, dy=1), move(cz, dy=-1), move(cy, zl=1)
-    x_top = move(rows_of(ta[:h_rows], taz[:h_rows]), dx=1)
-    x_low = move(rows_of(tb[h_rows:], tbz[h_rows:]), dx=-1)
+    x_top, x_low = move(top_in, dx=1), move(low_in, dx=-1)
 
     sources = [own, ca, cb, cz, cy, caz, cbz, cyz]
     code_map = [(i, i, 0, depth, 0) for i in range(8)]
@@ -197,49 +207,67 @@
     ids, sidx = notes[:, 0], notes[:, 1]
 
     def swap(*pieces):
-        return [move(piece, core=1) for piece in pieces]
-
-    def sums(ids, pieces, parts=3):
-        run = feed_forward(code_map, [(i, 0, count) for i in range(4)], depth, width, local_ff, parts)
+        return tuple(move(piece, core=1) for piece in pieces)
+
+    def sums(ids, groups, cuts):
+        pieces, row_map = [], []
+        for piece, first, n in [g[0] for g in groups] + [g[1] for g in groups]:
+            held = [i for i, p in enumerate(pieces) if p is piece]
+            if not held:
+                held = [len(pieces)]
+                pieces.append(piece)
+            row_map.append((held[0], first, n))
+        ranges = [(sum(cuts[:i]), n) for i, n in enumerate(cuts)]
+        run = feed_forward(code_map, row_map, ranges, depth, width, local_ff)
         return tuple(run(ids, sidx, scale_table, *sources, *pieces, down_weight))
 
-    def add(mine, siblings):
-        return mine.astype(F32) + rows_of(*siblings).astype(F32)
-
-    def towards(p, both, top, low):
-        top, low = (v[p * h_rows : (p + 1) * h_rows].astype(F32) for v in (top, low))
-        right, left = both[:count], both[count:]
-        right = rows_of(right[:h_rows] + top, right[h_rows:])
-        left = rows_of(left[:h_rows], left[h_rows:] + low)
-        return right.astype(BF16), left.astype(BF16)
-
-    x_top, x_low = after((x_top, x_low), caz, cbz, cyz)
-    o_far = swap(x_top, x_low)
-    later = after((tbz, taz, tb, ta, tz, tokens), *o_far)
-    o_near_z, o_near, o_here = swap(*later[:2]), swap(*later[2:4]), swap(*later[4:])
-    far = sums(ids, (x_top, x_low, *o_far))
-    far = after(far, *o_near_z, *o_near, *o_here)
-    far = add(far[0], swap(*far[1:]))
-    far_top, far_low = far[:count].astype(BF16), far[count:].astype(BF16)
-    top, low = move(far_top, dx=1), move(far_low, dx=-1)
-
-    ids = after(ids, far_top, far_low)
-    near_z = sums(ids, (tbz, taz, *o_near_z))
-    ids = after(ids, near_z[0])
-    here = sums(ids, (tz, tokens, *o_here), 1)
-    near_z, top, low, here = after((near_z[:1] + tuple(swap(*near_z[1:])), top, low, here))
-    right, left = towards(1, add(near_z[0], near_z[1:]), top, low)
-    z_right, z_left = move(right, dx=1), move(left, dx=-1)
-
-    o_sums = swap(after(here[1], right, left))
-    ids = after(ids, right, left, *o_sums)
-    near = sums(ids, (tb, ta, *o_near))
-    near, z_right, z_left = after((near[:1] + tuple(swap(*near[1:])), z_right, z_left))
-    right, left = towards(0, add(near[0], near[1:]), top, low)
-    here = add(here[0], o_sums)
-    across = (here[:count] + z_right.astype(F32) + z_left.astype(F32)).astype(BF16)
-    right, left, across = move(right, dx=1), move(left, dx=-1), move(across, zh=1)
-    return (here[count:] + right.astype(F32) + left.astype(F32) + across.astype(F32)).astype(BF16)
+    def whole(mine, sibling):
+        return (mine, 0, count), (sibling, 0, count)
+
+    def halves(p):
+        return [
+            ((mine, p * h_rows, h_rows), (sibling, p * h_rows, h_rows))
+            for mine, sibling in ((x_top, o_top), (x_low, o_low))
+        ]
+
+    def add(*terms):
+        total = terms[0].astype(F32)
+        for term in terms[1:]:
+            total = total + term.astype(F32)
+        return total
+
+    o_top, o_low, o_right_z, o_left_z = swap(x_top, x_low, tbz, taz)
+    later = after((tb, ta, tz, tokens), o_top, o_low)
+    o_right, o_left, o_z, o_own = swap(*later)
+    part = sums(ids, halves(1) + [whole(tbz, o_right_z), whole(taz, o_left_z)], [count] * 6)
+    part = after(part, o_right, o_left, o_z, o_own)
+    got = swap(*part[3:])
+    far_z, right, left = (add(part[i], got[i]).astype(BF16) for i in range(3))
+    far_in, z_right, z_left = move(far_z, zh=1), move(right, dx=1), move(left, dx=-1)
+
+    ids = after(ids, far_z, right, left)
+    groups = halves(0) + [whole(tb, o_right), whole(ta, o_left), whole(tz, o_z)]
+    part = sums(ids, groups, [count] * 4 + [h_rows] * 2 + [count] * 3)
+    far, near, here_z, near_sib, here_sib = part[0], part[1:3], part[3], part[6:8], part[8]
+    got = swap(*part[4:6])
+    far, got, far_in, z_right, z_left = after((far, got, far_in, z_right, z_left))
+    top = add(far[:h_rows], got[0], far_in[:h_rows]).astype(BF16)
+    low = add(far[h_rows:], got[1], far_in[h_rows:]).astype(BF16)
+    past_top, past_low = move(top, dx=1), move(low, dx=-1)
+
+    near_sib, here_sib = after((near_sib, here_sib), top, low)
+    got = swap(*near_sib, here_sib)
+    ids = after(ids, top, low)
+    here, own_sib = sums(ids, [whole(tokens, o_own)], [count] * 2)
+    near, got, past_top, past_low, here = after((near, got, past_top, past_low, here))
+    zero = jnp.zeros((), BF16)
+    past_top = lax.pad(past_top, zero, ((0, h_rows, 0), (0, 0, 0)))
+    past_low = lax.pad(past_low, zero, ((h_rows, 0, 0), (0, 0, 0)))
+    right, left = (add(near[i], got[i], past).astype(BF16) for i, past in enumerate((past_top, past_low)))
+    across = add(here_z, got[2], z_right, z_left).astype(BF16)
+    right_in, left_in, across_in = move(right, dx=1), move(left, dx=-1), move(across, zh=1)
+    own_sib = after(own_sib, right, left, across)
+    return add(here, *swap(own_sib), right_in, left_in, across_in).astype(BF16)
 
 
 def solution(mesh):

time: 225 us -> 205 us (0.911)
  waiting for transfers between devices: 107 us -> 84.4 us
  starting transfers between devices: 41.9 us -> 50.5 us
  Pallas kernels: 53.8 us -> 50.7 us
    ppermute x40, waiting for transfers between devices: 107 us -> 84.4 us  [move(): return lax.ppermute(value, AXES, pairs)]
    ppermute x40, starting transfers between devices: 41.9 us -> 50.5 us  [move(): return lax.ppermute(value, AXES, pairs)]
    convert_element_type x2 -> x8, other arithmetic: 3.41 us -> 11.4 us  [the longest x2 3.32 us: body(): add(near[i], got[i], past).astype(BF16)]
    add x2 -> x0, other arithmetic: 3.42 us -> none  [add(): return mine.astype(F32) + rows_of(*siblings).astype(F32)]
    another operation x4 -> x0, other arithmetic: 3.36 us -> none
    pallas_call x4 -> x3, Pallas kernels: 53.7 us -> 50.6 us  [sums(): return tuple(run(ids, sidx, scale_table, *sources, *pieces, down_weight))]
  transfers between devices with their start and end apart: 40 -> 40, of which waited for: 19 -> 18; matrix products, arithmetic and copies ran while one was open for 2% -> 3% of each run, Pallas kernels for 24% -> 25%
where the time goes in v1:
time: 205 us
  waiting for transfers between devices  84.4 us (41%)
  Pallas kernels  50.7 us (25%)
  starting transfers between devices  50.5 us (25%)
  other arithmetic  11.6 us (6%)
  local copies, waits for them, and re-layouts  6.04 us (3%)
    ppermute x40, waiting for transfers between devices, move(): return lax.ppermute(value, AXES, pairs)  84.4 us
    pallas_call x3, Pallas kernels, sums(): return tuple(run(ids, sidx, scale_table, *sources, *pieces, down_weight))  50.6 us
    ppermute x40, starting transfers between devices, move(): return lax.ppermute(value, AXES, pairs)  50.5 us
  transfers between devices with their start and end apart: 40, of which 18 were waited for; matrix products, arithmetic and copies ran while one was open for 3% of the time, Pallas kernels for 25%

profile of v1, /device:TPU:1, one launch (start us, length us, event | category | flops | bytes accessed | tf_op | source)
XLA Modules:
  0.0 205.0 jit_solution(14258456075120694503)
XLA Ops:
  0.0 4.4 %collective-permute-start.2 = (bf16[96,5120]{1,0:T(8,128)(2,1)}, bf16[96,5120]{1,0:T(8,128)(2,1)S(1)}, u32[]{:S(2)}, u32[]{:S(2)}) collective-permute-start(bf16[96,5120]{1,0:T(8,128)(2,1)} %refs_8_.1), channel_id=1, source_target_pairs={{0,8},{1,9},{2,10},{3,11},{4,12},{5,13},{6,14},{7,15},{8,0},{9,1},... | collective-permute-start | bytes 2949128 | tf_op jit(solution)/shard_map/ppermute | solution.py:27
  5.7 1.3 copy-done.1
  7.0 0.1 shard_map.64.refs_0_
  7.2 2.8 %collective-permute-start.1 = (bf16[5136,128]{1,0:T(8,128)(2,1)S(1)}, bf16[5136,128]{1,0:T(8,128)(2,1)S(1)}, u32[]{:S(2)}, u32[]{:S(2)}) collective-permute-start(bf16[5136,128]{1,0:T(8,128)(2,1)S(1)} %shard_map.64.refs_0_), channel_id=1, source_target_pairs={{0,96},{1,97},{2,98},{3,99},{4,100},{5,101},{6,102},{7,103},{8,104... | collective-permute-start | bytes 3944456 | tf_op jit(solution)/shard_map/ppermute | solution.py:27
  10.0 2.5 %collective-permute-start.11 = (bf16[96,5120]{1,0:T(8,128)(2,1)S(1)}, bf16[96,5120]{1,0:T(8,128)(2,1)S(1)}, u32[]{:S(2)}, u32[]{:S(2)}) collective-permute-start(bf16[96,5120]{1,0:T(8,128)(2,1)S(1)} %copy-done.17), channel_id=1, source_target_pairs={{0,6},{1,7},{2,0},{3,1},{4,2},{5,3},{6,4},{7,5},{8,14},{9,15},{10,... | collective-permute-start | bytes 2949128 | tf_op jit(solution)/shard_map/ppermute | solution.py:27
  12.5 13.6 %collective-permute-done.2.refs_12_ = bf16[96,5120]{1,0:T(8,128)(2,1)S(1)} collective-permute-done((bf16[96,5120]{1,0:T(8,128)(2,1)}, bf16[96,5120]{1,0:T(8,128)(2,1)S(1)}, u32[]{:S(2)}, u32[]{:S(2)}) %collective-permute-start.2) | collective-permute-done | bytes 983072 | tf_op jit(solution)/shard_map/ppermute | solution.py:27
  26.1 2.5 %collective-permute-start.12 = (bf16[96,5120]{1,0:T(8,128)(2,1)S(1)}, bf16[96,5120]{1,0:T(8,128)(2,1)}, u32[]{:S(2)}, u32[]{:S(2)}) collective-permute-start(bf16[96,5120]{1,0:T(8,128)(2,1)S(1)} %collective-permute-done.2.refs_12_), channel_id=1, source_target_pairs={{0,6},{1,7},{2,0},{3,1},{4,2},{5,3},{6,4},{7,5},{8,14},{9,15},{10,... | collective-permute-start | bytes 2949128 | tf_op jit(solution)/shard_map/ppermute | solution.py:27
  28.6 3.7 %collective-permute-done.11.refs_10_ = bf16[96,5120]{1,0:T(8,128)(2,1)S(1)} collective-permute-done((bf16[96,5120]{1,0:T(8,128)(2,1)S(1)}, bf16[96,5120]{1,0:T(8,128)(2,1)S(1)}, u32[]{:S(2)}, u32[]{:S(2)}) %collective-permute-start.11) | collective-permute-done | bytes 983072 | tf_op jit(solution)/shard_map/ppermute | solution.py:27
  32.3 0.9 collective-permute-start.10
  33.3 2.2 %collective-permute-done.9.refs_11_ = bf16[96,5120]{1,0:T(8,128)(2,1)S(1)} collective-permute-done((bf16[96,5120]{1,0:T(8,128)(2,1)S(1)}, bf16[96,5120]{1,0:T(8,128)(2,1)S(1)}, u32[]{:S(2)}, u32[]{:S(2)}) %collective-permute-start.9) | collective-permute-done | bytes 983072 | tf_op jit(solution)/shard_map/ppermute | solution.py:27
  35.4 0.7 collective-permute-start.3
  36.2 1.0 collective-permute-done.1.refs_2_
  37.2 3.5 %collective-permute-start.5 = (bf16[2560,128]{1,0:T(8,128)(2,1)S(1)}, bf16[2560,128]{1,0:T(8,128)(2,1)S(1)}, u32[]{:S(2)}, u32[]{:S(2)}) collective-permute-start(bf16[2560,128]{1,0:T(8,128)(2,1)S(1)} %slice.99), channel_id=1, source_target_pairs={{0,96},{1,97},{2,98},{3,99},{4,100},{5,101},{6,102},{7,103},{8,104... | collective-permute-start | bytes 1966088 | tf_op jit(solution)/shard_map/ppermute | solution.py:27
  40.9 12.4 %collective-permute-done.12.refs_10_ = bf16[96,5120]{1,0:T(8,128)(2,1)} collective-permute-done((bf16[96,5120]{1,0:T(8,128)(2,1)S(1)}, bf16[96,5120]{1,0:T(8,128)(2,1)}, u32[]{:S(2)}, u32[]{:S(2)}) %collective-permute-start.12) | collective-permute-done | bytes 983072 | tf_op jit(solution)/shard_map/ppermute | solution.py:27
  53.3 1.1 slice.107
  54.5 0.5 collective-permute-done.10.refs_11_
  55.0 1.1 slice.105
  56.1 0.3 collective-permute-done.4
  56.5 6.4 %collective-permute-done.3.refs_3_ = bf16[5136,128]{1,0:T(8,128)(2,1)S(1)} collective-permute-done((bf16[5136,128]{1,0:T(8,128)(2,1)S(1)}, bf16[5136,128]{1,0:T(8,128)(2,1)S(1)}, u32[]{:S(2)}, u32[]{:S(2)}) %collective-permute-start.3) | collective-permute-done | bytes 1314848 | tf_op jit(solution)/shard_map/ppermute | solution.py:27
  62.9 1.8 collective-permute-start.7
  64.9 2.7 %collective-permute-start.14 = (bf16[96,5120]{1,0:T(8,128)(2,1)S(1)}, bf16[96,5120]{1,0:T(8,128)(2,1)}, u32[]{:S(2)}, u32[]{:S(2)}) collective-permute-start(bf16[96,5120]{1,0:T(8,128)(2,1)S(1)} %pad_maximum_fusion.2), channel_id=1, source_target_pairs={{0,6},{1,7},{2,0},{3,1},{4,2},{5,3},{6,4},{7,5},{8,14},{9,15},{10,... | collective-permute-start | bytes 2949128 | tf_op jit(solution)/shard_map/ppermute | solution.py:27
  67.6 0.7 collective-permute-start.8
  68.3 16.5 %collective-permute-done.13.refs_8_ = bf16[96,5120]{1,0:T(8,128)(2,1)} collective-permute-done((bf16[96,5120]{1,0:T(8,128)(2,1)S(1)}, bf16[96,5120]{1,0:T(8,128)(2,1)}, u32[]{:S(2)}, u32[]{:S(2)}) %collective-permute-start.13) | collective-permute-done | bytes 983072 | tf_op jit(solution)/shard_map/ppermute | solution.py:27
  84.8 5.6 %collective-permute-start.17 = (bf16[96,5120]{1,0:T(8,128)(2,1)}, bf16[96,5120]{1,0:T(8,128)(2,1)}, u32[]{:S(2)}, u32[]{:S(2)}) collective-permute-start(bf16[96,5120]{1,0:T(8,128)(2,1)} %collective-permute-done.12.refs_10_), channel_id=1, source_target_pairs={{0,1},{1,0},{2,3},{3,2},{4,5},{5,4},{6,7},{7,6},{8,9},{9,8},{10,11... | collective-permute-start | bytes 2949128 | tf_op jit(solution)/shard_map/ppermute | solution.py:27
  90.4 3.8 %collective-permute-start.16 = (bf16[96,5120]{1,0:T(8,128)(2,1)}, bf16[96,5120]{1,0:T(8,128)(2,1)}, u32[]{:S(2)}, u32[]{:S(2)}) collective-permute-start(bf16[96,5120]{1,0:T(8,128)(2,1)} %collective-permute-done.14.refs_9_), channel_id=1, source_target_pairs={{0,1},{1,0},{2,3},{3,2},{4,5},{5,4},{6,7},{7,6},{8,9},{9,8},{10,11... | collective-permute-start | bytes 2949128 | tf_op jit(solution)/shard_map/ppermute | solution.py:27
  94.2 3.0 %collective-permute-start.18 = (bf16[96,5120]{1,0:T(8,128)(2,1)}, bf16[96,5120]{1,0:T(8,128)(2,1)}, u32[]{:S(2)}, u32[]{:S(2)}) collective-permute-start(bf16[96,5120]{1,0:T(8,128)(2,1)} %collective-permute-done.10.refs_11_), channel_id=1, source_target_pairs={{0,1},{1,0},{2,3},{3,2},{4,5},{5,4},{6,7},{7,6},{8,9},{9,8},{10,11... | collective-permute-start | bytes 2949128 | tf_op jit(solution)/shard_map/ppermute | solution.py:27
  97.3 1.1 copy-done.10
  98.3 0.1 stack.3
  98.4 1.7 collective-permute-start.19
  100.2 0.4 collective-permute-start.21
  100.7 0.1 collective-permute-start.22
  100.8 0.6 slice_bitcast_fusion.7
  101.4 17.2 %shard_map.65 = (bf16[96,5120]{1,0:T(8,128)(2,1)}, bf16[96,5120]{1,0:T(8,128)(2,1)}, bf16[96,5120]{1,0:T(8,128)(2,1)}, bf16[96,5120]{1,0:T(8,128)(2,1)}, bf16[96...) custom-call(s32[8]{0:T(128)} %get-tuple-element.92.ids, s32[8]{0:T(128)} %get-tuple-element.109.sidx, f32[64]{0:T(128)} %table.5, ...), custom_call_target="tpu_custom_call" | custom-call | flops 9059696640 | bytes 27525120 | tf_op jit(solution)/shard_map/pallas_call | solution.py:222
  118.6 0.5 collective-permute-start.23
  119.2 0.4 collective-permute-start.25
  119.6 1.9 collective-permute-done.23
  121.5 1.5 add_convert_fusion.6
  123.0 0.9 collective-permute-start.28
  124.0 0.2 add_convert_fusion.5
  124.3 1.3 add_convert_fusion.4
  125.6 2.6 %collective-permute-start.30 = (bf16[96,5120]{1,0:T(8,128)(2,1)}, bf16[96,5120]{1,0:T(8,128)(2,1)S(1)}, u32[]{:S(2)}, u32[]{:S(2)}) collective-permute-start(bf16[96,5120]{1,0:T(8,128)(2,1)} %add_convert_fusion.4), channel_id=1, source_target_pairs={{0,6},{1,7},{2,0},{3,1},{4,2},{5,3},{6,4},{7,5},{8,14},{9,15},{10,... | collective-permute-start | bytes 2949128 | tf_op jit(solution)/shard_map/ppermute | solution.py:27
  128.2 22.2 %shard_map.66 = (bf16[96,5120]{1,0:T(8,128)(2,1)}, bf16[96,5120]{1,0:T(8,128)(2,1)}, bf16[96,5120]{1,0:T(8,128)(2,1)}, bf16[96,5120]{1,0:T(8,128)(2,1)}, bf16[48...) custom-call(s32[8]{0:T(128)} %get-tuple-element.92.ids, ...), custom_call_target="tpu_custom_call" | custom-call | flops 12079595520 | bytes 31457280 | tf_op jit(solution)/shard_map/pallas_call | solution.py:222
  150.5 1.3 collective-permute-start.26
  151.9 1.6 collective-permute-done.26
  153.5 0.7 collective-permute-done.27
  154.2 2.8 %add_convert_fusion.7 = (bf16[48,5120]{1,0:T(8,128)(2,1)}, bf16[48,5120]{1,0:T(8,128)(2,1)}) fusion(bf16[48,5120]{1,0:T(8,128)(2,1)S(1)} %collective-permute-done.27, bf16[96,5120]{1,0:T(8,128)(2,1)} %collective-permute-done.28, bf16[96,5120]{1,0:T(8,128)(2,1)} %get-tuple-element.85, bf16[48,5120]{1,0:T(8,128)(2,1)S(1)} %collective-permute-done.26), kind=kLoop, calls=%fused_computation.10 | loop fusion | flops 2949120 | bytes 3932160 | tf_op jit(solution)/shard_map/convert_element_type | solution.py:255
  157.0 0.4 collective-permute-start.31
  157.3 0.1 collective-permute-start.32
  157.5 0.4 collective-permute-start.33
  157.8 1.5 collective-permute-start.34
  159.3 11.1 %shard_map.67 = (bf16[96,5120]{1,0:T(8,128)(2,1)}, bf16[96,5120]{1,0:T(8,128)(2,1)}) custom-call(s32[8]{0:T(128)} %get-tuple-element.92.ids, s32[8]{0:T(128)} %get-tuple-element.109.sidx, f32[64]{0:T(128)} %table.5, bf16[5136,128]{1,0:T(8,128)(2,1)} %copy-done, bf16[5136,128]{1,0:T(8,128)(2,1)} %copy-done.3, bf16[5136,128]{1,0:T(8,128)(2,1)} %copy-done.4, ...), custom_call_target="tpu_custom_call" | custom-call | flops 3019898880 | bytes 19660800 | tf_op jit(solution)/shard_map/pallas_call | solution.py:222
  170.5 0.4 collective-permute-done.35
  170.8 1.2 collective-permute-done.34
  172.1 1.6 add_convert_fusion.3
  173.7 1.7 add_convert_fusion.2
  175.5 0.6 add_convert_fusion.1
  176.0 0.6 copy-done.20
  176.6 1.0 collective-permute-start.36
  177.6 1.5 collective-permute-start.37
  179.1 2.3 %collective-permute-start.39 = (bf16[96,5120]{1,0:T(8,128)(2,1)S(1)}, bf16[96,5120]{1,0:T(8,128)(2,1)S(1)}, u32[]{:S(2)}, u32[]{:S(2)}) collective-permute-start(bf16[96,5120]{1,0:T(8,128)(2,1)S(1)} %add_convert_fusion.1), channel_id=1, source_target_pairs={{0,8},{1,9},{2,10},{3,11},{4,12},{5,13},{6,14},{7,15},{8,0},{9,1},... | collective-permute-start | bytes 2949128 | tf_op jit(solution)/shard_map/ppermute | solution.py:27
  181.4 19.6 %collective-permute-done.38 = bf16[96,5120]{1,0:T(8,128)(2,1)S(1)} collective-permute-done((bf16[96,5120]{1,0:T(8,128)(2,1)S(1)}, bf16[96,5120]{1,0:T(8,128)(2,1)S(1)}, u32[]{:S(2)}, u32[]{:S(2)}) %collective-permute-start.38) | collective-permute-done | bytes 983072 | tf_op jit(solution)/shard_map/ppermute | solution.py:27
  201.0 0.9 collective-permute-done.37
  201.9 1.4 collective-permute-done.39
  203.3 1.7 add_convert_fusion
  (95 shorter events, 1.2 us)
Async XLA Ops:
  0.0 26.1 %collective-permute-start.2 = (bf16[96,5120]{1,0:T(8,128)(2,1)}, bf16[96,5120]{1,0:T(8,128)(2,1)S(1)}, u32[]{:S(2)}, u32[]{:S(2)}) collective-permute-start(bf16[96,5120]{1,0:T(8,128)(2,1)} %refs_8_.1), channel_id=1, source_target_pairs={{0,8},{1,9},{2,10},{3,11},{4,12},{5,13},{6,14},{7,15},{8,0},{9,1},... | collective-permute-start | bytes 2949128 | tf_op jit(solution)/shard_map/ppermute | solution.py:27
  5.7 1.3 copy-start.1
  7.0 3.0 %copy-start.17 = (bf16[96,5120]{1,0:T(8,128)(2,1)S(1)}, bf16[96,5120]{1,0:T(8,128)(2,1)}, u32[]{:S(2)}) copy-start(bf16[96,5120]{1,0:T(8,128)(2,1)} %refs_8_.1) | copy-start | bytes 2949124
  7.2 60.4 %copy-start = (bf16[5136,128]{1,0:T(8,128)(2,1)}, bf16[5136,128]{1,0:T(8,128)(2,1)S(1)}, u32[]{:S(2)}) copy-start(bf16[5136,128]{1,0:T(8,128)(2,1)S(1)} %shard_map.64.refs_0_) | copy-start | bytes 3944452
  7.2 30.0 %collective-permute-start.1 = (bf16[5136,128]{1,0:T(8,128)(2,1)S(1)}, bf16[5136,128]{1,0:T(8,128)(2,1)S(1)}, u32[]{:S(2)}, u32[]{:S(2)}) collective-permute-start(bf16[5136,128]{1,0:T(8,128)(2,1)S(1)} %shard_map.64.refs_0_), channel_id=1, source_target_pairs={{0,96},{1,97},{2,98},{3,99},{4,100},{5,101},{6,102},{7,103},{8,104... | collective-permute-start | bytes 3944456 | tf_op jit(solution)/shard_map/ppermute | solution.py:27
  10.0 30.7 %collective-permute-start = (bf16[5136,128]{1,0:T(8,128)(2,1)S(1)}, bf16[5136,128]{1,0:T(8,128)(2,1)S(1)}, u32[]{:S(2)}, u32[]{:S(2)}) collective-permute-start(bf16[5136,128]{1,0:T(8,128)(2,1)S(1)} %shard_map.64.refs_0_), channel_id=1, source_target_pairs={{0,32},{1,33},{2,34},{3,35},{4,36},{5,37},{6,38},{7,39},{8,40},{9,... | collective-permute-start | bytes 3944456 | tf_op jit(solution)/shard_map/ppermute | solution.py:27
  10.0 22.3 %collective-permute-start.11 = (bf16[96,5120]{1,0:T(8,128)(2,1)S(1)}, bf16[96,5120]{1,0:T(8,128)(2,1)S(1)}, u32[]{:S(2)}, u32[]{:S(2)}) collective-permute-start(bf16[96,5120]{1,0:T(8,128)(2,1)S(1)} %copy-done.17), channel_id=1, source_target_pairs={{0,6},{1,7},{2,0},{3,1},{4,2},{5,3},{6,4},{7,5},{8,14},{9,15},{10,... | collective-permute-start | bytes 2949128 | tf_op jit(solution)/shard_map/ppermute | solution.py:27
  12.5 22.9 %collective-permute-start.9 = (bf16[96,5120]{1,0:T(8,128)(2,1)S(1)}, bf16[96,5120]{1,0:T(8,128)(2,1)S(1)}, u32[]{:S(2)}, u32[]{:S(2)}) collective-permute-start(bf16[96,5120]{1,0:T(8,128)(2,1)S(1)} %copy-done.17), channel_id=1, source_target_pairs={{0,2},{1,3},{2,4},{3,5},{4,6},{5,7},{6,0},{7,1},{8,10},{9,11},{10,... | collective-permute-start | bytes 2949128 | tf_op jit(solution)/shard_map/ppermute | solution.py:27
  26.1 28.9 %copy-start.19 = (bf16[96,5120]{1,0:T(8,128)(2,1)}, bf16[96,5120]{1,0:T(8,128)(2,1)S(1)}, u32[]{:S(2)}) copy-start(bf16[96,5120]{1,0:T(8,128)(2,1)S(1)} %collective-permute-done.2.refs_12_) | copy-start | bytes 2949124
  26.1 27.2 %collective-permute-start.12 = (bf16[96,5120]{1,0:T(8,128)(2,1)S(1)}, bf16[96,5120]{1,0:T(8,128)(2,1)}, u32[]{:S(2)}, u32[]{:S(2)}) collective-permute-start(bf16[96,5120]{1,0:T(8,128)(2,1)S(1)} %collective-permute-done.2.refs_12_), channel_id=1, source_target_pairs={{0,6},{1,7},{2,0},{3,1},{4,2},{5,3},{6,4},{7,5},{8,14},{9,15},{10,... | collective-permute-start | bytes 2949128 | tf_op jit(solution)/shard_map/ppermute | solution.py:27
  32.3 3.9 %copy-start.18 = (bf16[96,5120]{1,0:T(8,128)(2,1)}, bf16[96,5120]{1,0:T(8,128)(2,1)S(1)}, u32[]{:S(2)}) copy-start(bf16[96,5120]{1,0:T(8,128)(2,1)S(1)} %collective-permute-done.11.refs_10_) | copy-start | bytes 2949124
  32.3 22.7 %collective-permute-start.10 = (bf16[96,5120]{1,0:T(8,128)(2,1)S(1)}, bf16[96,5120]{1,0:T(8,128)(2,1)}, u32[]{:S(2)}, u32[]{:S(2)}) collective-permute-start(bf16[96,5120]{1,0:T(8,128)(2,1)S(1)} %collective-permute-done.2.refs_12_), channel_id=1, source_target_pairs={{0,2},{1,3},{2,4},{3,5},{4,6},{5,7},{6,0},{7,1},{8,10},{9,11},{10,... | collective-permute-start | bytes 2949128 | tf_op jit(solution)/shard_map/ppermute | solution.py:27
  35.4 5.4 %copy-start.5 = (bf16[96,5120]{1,0:T(8,128)(2,1)}, bf16[96,5120]{1,0:T(8,128)(2,1)S(1)}, u32[]{:S(2)}) copy-start(bf16[96,5120]{1,0:T(8,128)(2,1)S(1)} %collective-permute-done.9.refs_11_) | copy-start | bytes 2949124
  35.4 27.5 %collective-permute-start.3 = (bf16[5136,128]{1,0:T(8,128)(2,1)S(1)}, bf16[5136,128]{1,0:T(8,128)(2,1)S(1)}, u32[]{:S(2)}, u32[]{:S(2)}) collective-permute-start(bf16[5136,128]{1,0:T(8,128)(2,1)S(1)} %shard_map.64.refs_0_), channel_id=1, source_target_pairs={{0,16},{1,17},{2,18},{3,19},{4,20},{5,21},{6,22},{7,23},{8,24},{9,... | collective-permute-start | bytes 3944456 | tf_op jit(solution)/shard_map/ppermute | solution.py:27
  37.2 31.1 %copy-start.4 = (bf16[5136,128]{1,0:T(8,128)(2,1)}, bf16[5136,128]{1,0:T(8,128)(2,1)S(1)}, u32[]{:S(2)}) copy-start(bf16[5136,128]{1,0:T(8,128)(2,1)S(1)} %collective-permute-done.1.refs_2_) | copy-start | bytes 3944452
  37.2 27.5 %collective-permute-start.5 = (bf16[2560,128]{1,0:T(8,128)(2,1)S(1)}, bf16[2560,128]{1,0:T(8,128)(2,1)S(1)}, u32[]{:S(2)}, u32[]{:S(2)}) collective-permute-start(bf16[2560,128]{1,0:T(8,128)(2,1)S(1)} %slice.99), channel_id=1, source_target_pairs={{0,96},{1,97},{2,98},{3,99},{4,100},{5,101},{6,102},{7,103},{8,104... | collective-permute-start | bytes 1966088 | tf_op jit(solution)/shard_map/ppermute | solution.py:27
  40.7 27.6 %copy-start.3 = (bf16[5136,128]{1,0:T(8,128)(2,1)}, bf16[5136,128]{1,0:T(8,128)(2,1)S(1)}, u32[]{:S(2)}) copy-start(bf16[5136,128]{1,0:T(8,128)(2,1)S(1)} %collective-permute-done.refs_1_) | copy-start | bytes 3944452
  40.8 15.6 %collective-permute-start.4 = (bf16[2576,128]{1,0:T(8,128)(2,1)S(1)}, bf16[2576,128]{1,0:T(8,128)(2,1)S(1)}, u32[]{:S(2)}, u32[]{:S(2)}) collective-permute-start(bf16[2576,128]{1,0:T(8,128)(2,1)S(1)} %pad_maximum_fusion.3), channel_id=1, source_target_pairs={{0,32},{1,33},{2,34},{3,35},{4,36},{5,37},{6,38},{7,39},{8,40},{9,... | collective-permute-start | bytes 1978376 | tf_op jit(solution)/shard_map/ppermute | solution.py:27
  40.9 15.1 %slice-start = ((bf16[96,5120]{1,0:T(8,128)(2,1)}), bf16[48,5120]{1,0:T(8,128)(2,1)S(1)}, s32[]{:S(2)}) async-start(bf16[96,5120]{1,0:T(8,128)(2,1)} %copy-done.5), calls=%async_computation | async-start | bytes 983040 | tf_op jit(solution)/shard_map/slice | solution.py:198
  56.4 43.7 %copy-start.6 = (bf16[96,5120]{1,0:T(8,128)(2,1)S(1)}, bf16[96,5120]{1,0:T(8,128)(2,1)}, u32[]{:S(2)}) copy-start(bf16[96,5120]{1,0:T(8,128)(2,1)} %copy-done.5) | copy-start | bytes 2949124
  62.9 34.3 %copy-start.7 = (bf16[5136,128]{1,0:T(8,128)(2,1)}, bf16[5136,128]{1,0:T(8,128)(2,1)S(1)}, u32[]{:S(2)}) copy-start(bf16[5136,128]{1,0:T(8,128)(2,1)S(1)} %collective-permute-done.3.refs_3_) | copy-start | bytes 3944452
  62.9 27.5 %collective-permute-start.7 = (bf16[5136,128]{1,0:T(8,128)(2,1)S(1)}, bf16[5136,128]{1,0:T(8,128)(2,1)S(1)}, u32[]{:S(2)}, u32[]{:S(2)}) collective-permute-start(bf16[5136,128]{1,0:T(8,128)(2,1)S(1)} %collective-permute-done.3.refs_3_), channel_id=1, source_target_pairs={{0,96},{1,97},{2,98},{3,99},{4,100},{5,101},{6,102},{7,103},{8,104... | collective-permute-start | bytes 3944456 | tf_op jit(solution)/shard_map/ppermute | solution.py:27
  64.7 29.5 %collective-permute-start.6 = (bf16[5136,128]{1,0:T(8,128)(2,1)S(1)}, bf16[5136,128]{1,0:T(8,128)(2,1)S(1)}, u32[]{:S(2)}, u32[]{:S(2)}) collective-permute-start(bf16[5136,128]{1,0:T(8,128)(2,1)S(1)} %collective-permute-done.3.refs_3_), channel_id=1, source_target_pairs={{0,32},{1,33},{2,34},{3,35},{4,36},{5,37},{6,38},{7,39},{8,40},{9,... | collective-permute-start | bytes 3944456 | tf_op jit(solution)/shard_map/ppermute | solution.py:27
  64.8 36.5 %copy-start.2 = (bf16[5136,128]{1,0:T(8,128)(2,1)}, bf16[5136,128]{1,0:T(8,128)(2,1)S(1)}, u32[]{:S(2)}) copy-start(bf16[5136,128]{1,0:T(8,128)(2,1)S(1)} %pad_maximum_fusion.refs_4_) | copy-start | bytes 3944452
  64.8 20.0 %collective-permute-start.13 = (bf16[96,5120]{1,0:T(8,128)(2,1)S(1)}, bf16[96,5120]{1,0:T(8,128)(2,1)}, u32[]{:S(2)}, u32[]{:S(2)}) collective-permute-start(bf16[96,5120]{1,0:T(8,128)(2,1)S(1)} %pad_maximum_fusion.1), channel_id=1, source_target_pairs={{0,2},{1,3},{2,4},{3,5},{4,6},{5,7},{6,0},{7,1},{8,10},{9,11},{10,... | collective-permute-start | bytes 2949128 | tf_op jit(solution)/shard_map/ppermute | solution.py:27
  64.9 25.5 %collective-permute-start.14 = (bf16[96,5120]{1,0:T(8,128)(2,1)S(1)}, bf16[96,5120]{1,0:T(8,128)(2,1)}, u32[]{:S(2)}, u32[]{:S(2)}) collective-permute-start(bf16[96,5120]{1,0:T(8,128)(2,1)S(1)} %pad_maximum_fusion.2), channel_id=1, source_target_pairs={{0,6},{1,7},{2,0},{3,1},{4,2},{5,3},{6,4},{7,5},{8,14},{9,15},{10,... | collective-permute-start | bytes 2949128 | tf_op jit(solution)/shard_map/ppermute | solution.py:27
  67.6 29.6 %collective-permute-start.8 = (bf16[5136,128]{1,0:T(8,128)(2,1)S(1)}, bf16[5136,128]{1,0:T(8,128)(2,1)S(1)}, u32[]{:S(2)}, u32[]{:S(2)}) collective-permute-start(bf16[5136,128]{1,0:T(8,128)(2,1)S(1)} %pad_maximum_fusion.refs_4_), channel_id=1, source_target_pairs={{0,16},{1,17},{2,18},{3,19},{4,20},{5,21},{6,22},{7,23},{8,24},{9,... | collective-permute-start | bytes 3944456 | tf_op jit(solution)/shard_map/ppermute | solution.py:27
  84.8 15.8 %collective-permute-start.17 = (bf16[96,5120]{1,0:T(8,128)(2,1)}, bf16[96,5120]{1,0:T(8,128)(2,1)}, u32[]{:S(2)}, u32[]{:S(2)}) collective-permute-start(bf16[96,5120]{1,0:T(8,128)(2,1)} %collective-permute-done.12.refs_10_), channel_id=1, source_target_pairs={{0,1},{1,0},{2,3},{3,2},{4,5},{5,4},{6,7},{7,6},{8,9},{9,8},{10,11... | collective-permute-start | bytes 2949128 | tf_op jit(solution)/shard_map/ppermute | solution.py:27
  90.4 8.1 %collective-permute-start.15 = (bf16[96,5120]{1,0:T(8,128)(2,1)}, bf16[96,5120]{1,0:T(8,128)(2,1)}, u32[]{:S(2)}, u32[]{:S(2)}) collective-permute-start(bf16[96,5120]{1,0:T(8,128)(2,1)} %collective-permute-done.13.refs_8_), channel_id=1, source_target_pairs={{0,1},{1,0},{2,3},{3,2},{4,5},{5,4},{6,7},{7,6},{8,9},{9,8},{10,11... | collective-permute-start | bytes 2949128 | tf_op jit(solution)/shard_map/ppermute | solution.py:27
  90.4 6.8 %copy-start.8 = (bf16[5136,128]{1,0:T(8,128)(2,1)}, bf16[5136,128]{1,0:T(8,128)(2,1)S(1)}, u32[]{:S(2)}) copy-start(bf16[5136,128]{1,0:T(8,128)(2,1)S(1)} %collective-permute-done.7.refs_6_) | copy-start | bytes 3944452
  90.4 8.0 %collective-permute-start.16 = (bf16[96,5120]{1,0:T(8,128)(2,1)}, bf16[96,5120]{1,0:T(8,128)(2,1)}, u32[]{:S(2)}, u32[]{:S(2)}) collective-permute-start(bf16[96,5120]{1,0:T(8,128)(2,1)} %collective-permute-done.14.refs_9_), channel_id=1, source_target_pairs={{0,1},{1,0},{2,3},{3,2},{4,5},{5,4},{6,7},{7,6},{8,9},{9,8},{10,11... | collective-permute-start | bytes 2949128 | tf_op jit(solution)/shard_map/ppermute | solution.py:27
  94.2 3.1 %copy-start.9 = (bf16[5136,128]{1,0:T(8,128)(2,1)}, bf16[5136,128]{1,0:T(8,128)(2,1)S(1)}, u32[]{:S(2)}) copy-start(bf16[5136,128]{1,0:T(8,128)(2,1)S(1)} %collective-permute-done.6.refs_5_) | copy-start | bytes 3944452
  94.2 7.2 %collective-permute-start.18 = (bf16[96,5120]{1,0:T(8,128)(2,1)}, bf16[96,5120]{1,0:T(8,128)(2,1)}, u32[]{:S(2)}, u32[]{:S(2)}) collective-permute-start(bf16[96,5120]{1,0:T(8,128)(2,1)} %collective-permute-done.10.refs_11_), channel_id=1, source_target_pairs={{0,1},{1,0},{2,3},{3,2},{4,5},{5,4},{6,7},{7,6},{8,9},{9,8},{10,11... | collective-permute-start | bytes 2949128 | tf_op jit(solution)/shard_map/ppermute | solution.py:27
  97.3 1.1 copy-start.10
  98.4 20.2 %collective-permute-start.19 = (bf16[96,5120]{1,0:T(8,128)(2,1)}, bf16[96,5120]{1,0:T(8,128)(2,1)}, u32[]{:S(2)}, u32[]{:S(2)}) collective-permute-start(bf16[96,5120]{1,0:T(8,128)(2,1)} %copy-done.18), channel_id=1, source_target_pairs={{0,1},{1,0},{2,3},{3,2},{4,5},{5,4},{6,7},{7,6},{8,9},{9,8},{10,11... | collective-permute-start | bytes 2949128 | tf_op jit(solution)/shard_map/ppermute | solution.py:27
  100.1 18.5 %collective-permute-start.20 = (bf16[96,5120]{1,0:T(8,128)(2,1)S(1)}, bf16[96,5120]{1,0:T(8,128)(2,1)}, u32[]{:S(2)}, u32[]{:S(2)}) collective-permute-start(bf16[96,5120]{1,0:T(8,128)(2,1)S(1)} %copy-done.6), channel_id=1, source_target_pairs={{0,1},{1,0},{2,3},{3,2},{4,5},{5,4},{6,7},{7,6},{8,9},{9,8},{10,11... | collective-permute-start | bytes 2949128 | tf_op jit(solution)/shard_map/ppermute | solution.py:27
  100.2 18.4 %collective-permute-start.21 = (bf16[96,5120]{1,0:T(8,128)(2,1)}, bf16[96,5120]{1,0:T(8,128)(2,1)}, u32[]{:S(2)}, u32[]{:S(2)}) collective-permute-start(bf16[96,5120]{1,0:T(8,128)(2,1)} %copy-done.19), channel_id=1, source_target_pairs={{0,1},{1,0},{2,3},{3,2},{4,5},{5,4},{6,7},{7,6},{8,9},{9,8},{10,11... | collective-permute-start | bytes 2949128 | tf_op jit(solution)/shard_map/ppermute | solution.py:27
  100.7 18.0 %collective-permute-start.22 = (bf16[96,5120]{1,0:T(8,128)(2,1)S(1)}, bf16[96,5120]{1,0:T(8,128)(2,1)}, u32[]{:S(2)}, u32[]{:S(2)}) collective-permute-start(bf16[96,5120]{1,0:T(8,128)(2,1)S(1)} %copy-done.17), channel_id=1, source_target_pairs={{0,1},{1,0},{2,3},{3,2},{4,5},{5,4},{6,7},{7,6},{8,9},{9,8},{10,11... | collective-permute-start | bytes 2949128 | tf_op jit(solution)/shard_map/ppermute | solution.py:27
  118.6 5.4 %copy-start.14 = (bf16[96,5120]{1,0:T(8,128)(2,1)S(1)}, bf16[96,5120]{1,0:T(8,128)(2,1)}, u32[]{:S(2)}) copy-start(bf16[96,5120]{1,0:T(8,128)(2,1)} %get-tuple-element.72) | copy-start | bytes 2949124
  118.6 2.9 %collective-permute-start.23 = (bf16[96,5120]{1,0:T(8,128)(2,1)}, bf16[96,5120]{1,0:T(8,128)(2,1)S(1)}, u32[]{:S(2)}, u32[]{:S(2)}) collective-permute-start(bf16[96,5120]{1,0:T(8,128)(2,1)} %get-tuple-element.71), channel_id=1, source_target_pairs={{0,1},{1,0},{2,3},{3,2},{4,5},{5,4},{6,7},{7,6},{8,9},{9,8},{10,11... | collective-permute-start | bytes 2949128 | tf_op jit(solution)/shard_map/ppermute | solution.py:27
  119.1 4.8 %collective-permute-start.24 = (bf16[96,5120]{1,0:T(8,128)(2,1)}, bf16[96,5120]{1,0:T(8,128)(2,1)S(1)}, u32[]{:S(2)}, u32[]{:S(2)}) collective-permute-start(bf16[96,5120]{1,0:T(8,128)(2,1)} %get-tuple-element.73), channel_id=1, source_target_pairs={{0,1},{1,0},{2,3},{3,2},{4,5},{5,4},{6,7},{7,6},{8,9},{9,8},{10,11... | collective-permute-start | bytes 2949128 | tf_op jit(solution)/shard_map/ppermute | solution.py:27
  119.2 5.1 %collective-permute-start.25 = (bf16[96,5120]{1,0:T(8,128)(2,1)}, bf16[96,5120]{1,0:T(8,128)(2,1)S(1)}, u32[]{:S(2)}, u32[]{:S(2)}) collective-permute-start(bf16[96,5120]{1,0:T(8,128)(2,1)} %get-tuple-element.75), channel_id=1, source_target_pairs={{0,1},{1,0},{2,3},{3,2},{4,5},{5,4},{6,7},{7,6},{8,9},{9,8},{10,11... | collective-permute-start | bytes 2949128 | tf_op jit(solution)/shard_map/ppermute | solution.py:27
  123.0 1.4 copy-start.13
  123.0 31.2 %collective-permute-start.28 = (bf16[96,5120]{1,0:T(8,128)(2,1)S(1)}, bf16[96,5120]{1,0:T(8,128)(2,1)}, u32[]{:S(2)}, u32[]{:S(2)}) collective-permute-start(bf16[96,5120]{1,0:T(8,128)(2,1)S(1)} %add_convert_fusion.6), channel_id=1, source_target_pairs={{0,8},{1,9},{2,10},{3,11},{4,12},{5,13},{6,14},{7,15},{8,0},{9,1},... | collective-permute-start | bytes 2949128 | tf_op jit(solution)/shard_map/ppermute | solution.py:27
  124.2 30.0 %collective-permute-start.29 = (bf16[96,5120]{1,0:T(8,128)(2,1)S(1)}, bf16[96,5120]{1,0:T(8,128)(2,1)S(1)}, u32[]{:S(2)}, u32[]{:S(2)}) collective-permute-start(bf16[96,5120]{1,0:T(8,128)(2,1)S(1)} %add_convert_fusion.5), channel_id=1, source_target_pairs={{0,2},{1,3},{2,4},{3,5},{4,6},{5,7},{6,0},{7,1},{8,10},{9,11},{10,... | collective-permute-start | bytes 2949128 | tf_op jit(solution)/shard_map/ppermute | solution.py:27
  125.6 28.5 %collective-permute-start.30 = (bf16[96,5120]{1,0:T(8,128)(2,1)}, bf16[96,5120]{1,0:T(8,128)(2,1)S(1)}, u32[]{:S(2)}, u32[]{:S(2)}) collective-permute-start(bf16[96,5120]{1,0:T(8,128)(2,1)} %add_convert_fusion.4), channel_id=1, source_target_pairs={{0,6},{1,7},{2,0},{3,1},{4,2},{5,3},{6,4},{7,5},{8,14},{9,15},{10,... | collective-permute-start | bytes 2949128 | tf_op jit(solution)/shard_map/ppermute | solution.py:27
  150.5 3.0 %collective-permute-start.26 = (bf16[48,5120]{1,0:T(8,128)(2,1)}, bf16[48,5120]{1,0:T(8,128)(2,1)S(1)}, u32[]{:S(2)}, u32[]{:S(2)}) collective-permute-start(bf16[48,5120]{1,0:T(8,128)(2,1)} %get-tuple-element.83), channel_id=1, source_target_pairs={{0,1},{1,0},{2,3},{3,2},{4,5},{5,4},{6,7},{7,6},{8,9},{9,8},{10,11... | collective-permute-start | bytes 1474568 | tf_op jit(solution)/shard_map/ppermute | solution.py:27
  151.8 2.4 %collective-permute-start.27 = (bf16[48,5120]{1,0:T(8,128)(2,1)}, bf16[48,5120]{1,0:T(8,128)(2,1)S(1)}, u32[]{:S(2)}, u32[]{:S(2)}) collective-permute-start(bf16[48,5120]{1,0:T(8,128)(2,1)} %get-tuple-element.84), channel_id=1, source_target_pairs={{0,1},{1,0},{2,3},{3,2},{4,5},{5,4},{6,7},{7,6},{8,9},{9,8},{10,11... | collective-permute-start | bytes 1474568 | tf_op jit(solution)/shard_map/ppermute | solution.py:27
  157.0 15.1 %copy-start.16 = (bf16[96,5120]{1,0:T(8,128)(2,1)S(1)}, bf16[96,5120]{1,0:T(8,128)(2,1)}, u32[]{:S(2)}) copy-start(bf16[96,5120]{1,0:T(8,128)(2,1)} %get-tuple-element.96) | copy-start | bytes 2949124
  157.0 15.1 %collective-permute-start.31 = (bf16[96,5120]{1,0:T(8,128)(2,1)}, bf16[96,5120]{1,0:T(8,128)(2,1)}, u32[]{:S(2)}, u32[]{:S(2)}) collective-permute-start(bf16[96,5120]{1,0:T(8,128)(2,1)} %get-tuple-element.89), channel_id=1, source_target_pairs={{0,1},{1,0},{2,3},{3,2},{4,5},{5,4},{6,7},{7,6},{8,9},{9,8},{10,11... | collective-permute-start | bytes 2949128 | tf_op jit(solution)/shard_map/ppermute | solution.py:27
  157.3 14.7 %collective-permute-start.32 = (bf16[96,5120]{1,0:T(8,128)(2,1)}, bf16[96,5120]{1,0:T(8,128)(2,1)}, u32[]{:S(2)}, u32[]{:S(2)}) collective-permute-start(bf16[96,5120]{1,0:T(8,128)(2,1)} %get-tuple-element.90), channel_id=1, source_target_pairs={{0,1},{1,0},{2,3},{3,2},{4,5},{5,4},{6,7},{7,6},{8,9},{9,8},{10,11... | collective-permute-start | bytes 2949128 | tf_op jit(solution)/shard_map/ppermute | solution.py:27
  157.5 14.6 %collective-permute-start.33 = (bf16[96,5120]{1,0:T(8,128)(2,1)}, bf16[96,5120]{1,0:T(8,128)(2,1)S(1)}, u32[]{:S(2)}, u32[]{:S(2)}) collective-permute-start(bf16[96,5120]{1,0:T(8,128)(2,1)} %get-tuple-element.91), channel_id=1, source_target_pairs={{0,1},{1,0},{2,3},{3,2},{4,5},{5,4},{6,7},{7,6},{8,9},{9,8},{10,11... | collective-permute-start | bytes 2949128 | tf_op jit(solution)/shard_map/ppermute | solution.py:27
  157.8 13.0 %collective-permute-start.35 = (bf16[48,5120]{1,0:T(8,128)(2,1)}, bf16[48,5120]{1,0:T(8,128)(2,1)}, u32[]{:S(2)}, u32[]{:S(2)}) collective-permute-start(bf16[48,5120]{1,0:T(8,128)(2,1)} %get-tuple-element.107), channel_id=1, source_target_pairs={{0,6},{1,7},{2,0},{3,1},{4,2},{5,3},{6,4},{7,5},{8,14},{9,15},{10,... | collective-permute-start | bytes 1474568 | tf_op jit(solution)/shard_map/ppermute | solution.py:27
  157.8 14.2 %collective-permute-start.34 = (bf16[48,5120]{1,0:T(8,128)(2,1)}, bf16[48,5120]{1,0:T(8,128)(2,1)}, u32[]{:S(2)}, u32[]{:S(2)}) collective-permute-start(bf16[48,5120]{1,0:T(8,128)(2,1)} %get-tuple-element.108), channel_id=1, source_target_pairs={{0,2},{1,3},{2,4},{3,5},{4,6},{5,7},{6,0},{7,1},{8,10},{9,11},{10,... | collective-permute-start | bytes 1474568 | tf_op jit(solution)/shard_map/ppermute | solution.py:27
  170.5 3.2 %copy-start.15 = (bf16[96,5120]{1,0:T(8,128)(2,1)S(1)}, bf16[96,5120]{1,0:T(8,128)(2,1)}, u32[]{:S(2)}) copy-start(bf16[96,5120]{1,0:T(8,128)(2,1)} %get-tuple-element.99) | copy-start | bytes 2949124
  173.7 1.7 copy-start.11
  175.4 1.2 copy-start.20
  175.4 27.9 %copy-start.12 = (bf16[96,5120]{1,0:T(8,128)(2,1)S(1)}, bf16[96,5120]{1,0:T(8,128)(2,1)}, u32[]{:S(2)}) copy-start(bf16[96,5120]{1,0:T(8,128)(2,1)} %get-tuple-element.94) | copy-start | bytes 2949124
  176.6 4.7 %collective-permute-start.36 = (bf16[96,5120]{1,0:T(8,128)(2,1)S(1)}, bf16[96,5120]{1,0:T(8,128)(2,1)S(1)}, u32[]{:S(2)}, u32[]{:S(2)}) collective-permute-start(bf16[96,5120]{1,0:T(8,128)(2,1)S(1)} %copy-done.20), channel_id=1, source_target_pairs={{0,1},{1,0},{2,3},{3,2},{4,5},{5,4},{6,7},{7,6},{8,9},{9,8},{10,11... | collective-permute-start | bytes 2949128 | tf_op jit(solution)/shard_map/ppermute | solution.py:27
  177.6 23.4 %collective-permute-start.38 = (bf16[96,5120]{1,0:T(8,128)(2,1)S(1)}, bf16[96,5120]{1,0:T(8,128)(2,1)S(1)}, u32[]{:S(2)}, u32[]{:S(2)}) collective-permute-start(bf16[96,5120]{1,0:T(8,128)(2,1)S(1)} %add_convert_fusion.2), channel_id=1, source_target_pairs={{0,6},{1,7},{2,0},{3,1},{4,2},{5,3},{6,4},{7,5},{8,14},{9,15},{10,... | collective-permute-start | bytes 2949128 | tf_op jit(solution)/shard_map/ppermute | solution.py:27
  177.6 24.3 %collective-permute-start.37 = (bf16[96,5120]{1,0:T(8,128)(2,1)S(1)}, bf16[96,5120]{1,0:T(8,128)(2,1)S(1)}, u32[]{:S(2)}, u32[]{:S(2)}) collective-permute-start(bf16[96,5120]{1,0:T(8,128)(2,1)S(1)} %add_convert_fusion.3), channel_id=1, source_target_pairs={{0,2},{1,3},{2,4},{3,5},{4,6},{5,7},{6,0},{7,1},{8,10},{9,11},{10,... | collective-permute-start | bytes 2949128 | tf_op jit(solution)/shard_map/ppermute | solution.py:27
  179.1 24.3 %collective-permute-start.39 = (bf16[96,5120]{1,0:T(8,128)(2,1)S(1)}, bf16[96,5120]{1,0:T(8,128)(2,1)S(1)}, u32[]{:S(2)}, u32[]{:S(2)}) collective-permute-start(bf16[96,5120]{1,0:T(8,128)(2,1)S(1)} %add_convert_fusion.1), channel_id=1, source_target_pairs={{0,8},{1,9},{2,10},{3,11},{4,12},{5,13},{6,14},{7,15},{8,0},{9,1},... | collective-permute-start | bytes 2949128 | tf_op jit(solution)/shard_map/ppermute | solution.py:27

commit v2 on v1

--- a/solution.py
+++ b/solution.py
@@ -60,8 +60,40 @@
     )(block_ids, scale_idx, codes)
 
 
-def feed_forward(code_map, row_map, ranges, depth, width, local_ff):
-    n_codes = 1 + max(m[1] for m in code_map)
+def join(pieces, plans):
+    n_copies = sum(len(plan) for plan in plans)
+
+    def kernel(*refs):
+        sources, outs, sem = refs[: len(pieces)], refs[len(pieces) : -1], refs[-1]
+        copies = []
+        for plan, out in zip(plans, outs):
+            at = 0
+            for src, first, n in plan:
+                copies.append(
+                    pltpu.make_async_copy(sources[src].at[pl.ds(first, n)], out.at[pl.ds(at, n)], sem.at[len(copies)])
+                )
+                at += n
+        for c in copies:
+            c.start()
+        for c in copies:
+            c.wait()
+
+    anywhere = pl.BlockSpec(memory_space=pl.ANY)
+    return pl.pallas_call(
+        kernel,
+        out_shape=tuple(
+            jax.ShapeDtypeStruct((sum(n for _, _, n in plan), pieces[plan[0][0]].shape[1]), BF16) for plan in plans
+        ),
+        in_specs=[anywhere] * len(pieces),
+        out_specs=(anywhere,) * len(plans),
+        scratch_shapes=[pltpu.SemaphoreType.DMA((n_copies,))],
+        compiler_params=pltpu.CompilerParams(vmem_limit_bytes=2 * 2**20),
+        cost_estimate=pl.CostEstimate(flops=1, bytes_accessed=1, transcendentals=0),
+    )(*pieces)
+
+
+def feed_forward(code_map, row_map, ranges, depth, width, local_ff, load):
+    n_codes = 1 + max(m[1] for m in code_map) if load else 0
     n_rows = 1 + max(m[0] for m in row_map)
     slots = 1 + max(m[0] for m in code_map)
     blocks = slots // 2
@@ -74,41 +106,57 @@
     def kernel(ids, sidx, table, *refs):
         sources, refs = refs[:n_codes], refs[n_codes:]
         pieces, refs = refs[:n_rows], refs[n_rows:]
-        down, outs, (w, x, dn, proj, hid, out, sem) = refs[0], refs[1 : 1 + n_out], refs[1 + n_out :]
+        if load:
+            down, outs, (w, dn, x, proj, hid, out, sem) = refs[0], refs[1 : 1 + n_out], refs[1 + n_out :]
+        else:
+            w, dn, outs, (x, proj, hid, out, sem) = refs[0], refs[1], refs[2 : 2 + n_out], refs[2 + n_out :]
         at = 0
-        first = []
+        tiles = [[] for _ in range(rows // tile)]
         for i, (src, start, n) in enumerate(row_map):
-            first.append(pltpu.make_async_copy(pieces[src].at[pl.ds(start, n)], x.at[pl.ds(at, n)], sem.at[i]))
+            copy = pltpu.make_async_copy(pieces[src].at[pl.ds(start, n)], x.at[pl.ds(at, n)], sem.at[i])
+            tiles[at // tile].append(copy)
             at += n
-        x_copies = list(first)
-        waits = [[] for _ in range(blocks)]
-        for i, (slot, src, start, n, to) in enumerate(code_map):
-            target = w.at[slot // 2, pl.ds(to, n), pl.ds(slot % 2 * width, width)]
-            waits[slot // 2].append(
-                pltpu.make_async_copy(sources[src].at[pl.ds(start, n)], target, sem.at[len(row_map) + i])
-            )
-        down_copy = pltpu.make_async_copy(down, dn, sem.at[n_copies - 1])
-        stages = [first + waits[0]] + waits[1:] + [[down_copy]]
-        for stage in stages[:2]:
-            for c in stage:
+        x_copies = [c for copies in tiles for c in copies]
+        if load:
+            waits = [[] for _ in range(blocks)]
+            for i, (slot, src, start, n, to) in enumerate(code_map):
+                target = w.at[slot // 2, pl.ds(to, n), pl.ds(slot % 2 * width, width)]
+                waits[slot // 2].append(
+                    pltpu.make_async_copy(sources[src].at[pl.ds(start, n)], target, sem.at[len(row_map) + i])
+                )
+            down_copy = pltpu.make_async_copy(down, dn, sem.at[n_copies - 1])
+            stages = [x_copies + waits[0]] + waits[1:] + [[down_copy]]
+            for stage in stages[:2]:
+                for c in stage:
+                    c.start()
+        else:
+            for c in x_copies:
                 c.start()
-        for c in x_copies:
+        for c in tiles[0]:
             c.wait()
 
         @pl.loop(0, blocks)
         def _(pair):
-            for q in range(blocks):
-
-                @pl.when(pair == q)
-                def _(q=q):
-                    for c in waits[q]:
-                        c.wait()
-                    if q + 2 < len(stages):
-                        for c in stages[q + 2]:
-                            c.start()
+            if load:
+                for q in range(blocks):
+
+                    @pl.when(pair == q)
+                    def _(q=q):
+                        for c in waits[q]:
+                            c.wait()
+                        if q + 2 < len(stages):
+                            for c in stages[q + 2]:
+                                c.start()
 
             @pl.loop(0, rows // tile)
             def _(part):
+                for t in range(1, rows // tile):
+
+                    @pl.when((pair == 0) & (part == t))
+                    def _(t=t):
+                        for c in tiles[t]:
+                            c.wait()
+
                 at = pl.ds(pl.multiple_of(part * tile, tile), tile)
                 acc = jnp.dot(x[at, :], w[pair], preferred_element_type=F32)
                 for side in range(2):
@@ -122,7 +170,8 @@
                 gate, up = proj[b, at], proj[b + blocks, at]
                 hid[at, b * width : (b + 1) * width] = (gate / (1.0 + jnp.exp(-gate)) * up).astype(BF16)
 
-        down_copy.wait()
+        if load:
+            down_copy.wait()
 
         def leave(n, slot):
             cols = pl.ds(pl.multiple_of(n * STEP, STEP), STEP)
@@ -158,21 +207,22 @@
 
     anywhere = pl.BlockSpec(memory_space=pltpu.HBM)
     smem = pl.BlockSpec(memory_space=pltpu.SMEM)
+    vmem = pl.BlockSpec(memory_space=pltpu.VMEM)
+    results = tuple(jax.ShapeDtypeStruct((n, depth), BF16) for _, n in ranges)
+    kept = (pltpu.VMEM((blocks, depth, 2 * width), BF16), pltpu.VMEM((local_ff, depth), BF16))
     return pl.pallas_call(
         kernel,
-        out_shape=tuple(jax.ShapeDtypeStruct((n, depth), BF16) for _, n in ranges),
-        in_specs=[smem] * 3 + [anywhere] * (n_codes + n_rows + 1),
-        out_specs=(anywhere,) * n_out,
+        out_shape=results + kept if load else results,
+        in_specs=[smem] * 3 + [anywhere] * (n_codes + n_rows) + ([anywhere] if load else [vmem, vmem]),
+        out_specs=(anywhere,) * n_out + ((vmem, vmem) if load else ()),
         scratch_shapes=[
-            pltpu.VMEM((blocks, depth, 2 * width), BF16),
             pltpu.VMEM((rows, depth), BF16),
-            pltpu.VMEM((local_ff, depth), BF16),
             pltpu.VMEM((slots, rows, width), F32),
             pltpu.VMEM((rows, local_ff), BF16),
             pltpu.VMEM((2, rows, STEP), BF16),
             pltpu.SemaphoreType.DMA((n_copies,)),
         ],
-        compiler_params=pltpu.CompilerParams(vmem_limit_bytes=60 * 2**20),
+        compiler_params=pltpu.CompilerParams(vmem_limit_bytes=44 * 2**20),
         cost_estimate=pl.CostEstimate(
             flops=2 * rows * depth * local_ff * 3,
             bytes_accessed=2 * (depth * slots * width + local_ff * depth + 2 * rows * depth),
@@ -194,10 +244,15 @@
     y_top = move(rows_of(ca[:h_depth], ca[depth:]), dy=1)
     y_low = move(cb[h_depth:depth], dy=-1)
     taz, tbz = move(tz, dx=1), move(tz, dx=-1)
-    cy = rows_of(y_top[:h_depth], y_low, y_top[h_depth:])
-    top_in, low_in = rows_of(ta[:h_rows], taz[:h_rows]), rows_of(tb[h_rows:], tbz[h_rows:])
-    cy = after(cy, cz)
-    top_in, low_in = after((top_in, low_in), cy)
+    cy, top_in, low_in = join(
+        (y_top, y_low, ta, taz, tb, tbz),
+        (
+            ((0, 0, h_depth), (1, 0, h_depth), (0, h_depth, NOTE)),
+            ((2, 0, h_rows), (3, 0, h_rows)),
+            ((4, h_rows, h_rows), (5, h_rows, h_rows)),
+        ),
+    )
+    cy, top_in, low_in = after((cy, top_in, low_in), cz)
     caz, cbz, cyz = move(cz, dy=1), move(cz, dy=-1), move(cy, zl=1)
     x_top, x_low = move(top_in, dx=1), move(low_in, dx=-1)
 
@@ -209,7 +264,7 @@
     def swap(*pieces):
         return tuple(move(piece, core=1) for piece in pieces)
 
-    def sums(ids, groups, cuts):
+    def sums(ids, groups, cuts, weights=None):
         pieces, row_map = [], []
         for piece, first, n in [g[0] for g in groups] + [g[1] for g in groups]:
             held = [i for i, p in enumerate(pieces) if p is piece]
@@ -218,8 +273,10 @@
                 pieces.append(piece)
             row_map.append((held[0], first, n))
         ranges = [(sum(cuts[:i]), n) for i, n in enumerate(cuts)]
-        run = feed_forward(code_map, row_map, ranges, depth, width, local_ff)
-        return tuple(run(ids, sidx, scale_table, *sources, *pieces, down_weight))
+        run = feed_forward(code_map, row_map, ranges, depth, width, local_ff, weights is None)
+        if weights is None:
+            return tuple(run(ids, sidx, scale_table, *sources, *pieces, down_weight))
+        return tuple(run(ids, sidx, scale_table, *pieces, *weights))
 
     def whole(mine, sibling):
         return (mine, 0, count), (sibling, 0, count)
@@ -240,6 +297,7 @@
     later = after((tb, ta, tz, tokens), o_top, o_low)
     o_right, o_left, o_z, o_own = swap(*later)
     part = sums(ids, halves(1) + [whole(tbz, o_right_z), whole(taz, o_left_z)], [count] * 6)
+    part, weights = part[:6], part[6:]
     part = after(part, o_right, o_left, o_z, o_own)
     got = swap(*part[3:])
     far_z, right, left = (add(part[i], got[i]).astype(BF16) for i in range(3))
@@ -247,7 +305,7 @@
 
     ids = after(ids, far_z, right, left)
     groups = halves(0) + [whole(tb, o_right), whole(ta, o_left), whole(tz, o_z)]
-    part = sums(ids, groups, [count] * 4 + [h_rows] * 2 + [count] * 3)
+    part = sums(ids, groups, [count] * 4 + [h_rows] * 2 + [count] * 3, weights)
     far, near, here_z, near_sib, here_sib = part[0], part[1:3], part[3], part[6:8], part[8]
     got = swap(*part[4:6])
     far, got, far_in, z_right, z_left = after((far, got, far_in, z_right, z_left))
@@ -258,7 +316,7 @@
     near_sib, here_sib = after((near_sib, here_sib), top, low)
     got = swap(*near_sib, here_sib)
     ids = after(ids, top, low)
-    here, own_sib = sums(ids, [whole(tokens, o_own)], [count] * 2)
+    here, own_sib = sums(ids, [whole(tokens, o_own)], [count] * 2, weights)
     near, got, past_top, past_low, here = after((near, got, past_top, past_low, here))
     zero = jnp.zeros((), BF16)
     past_top = lax.pad(past_top, zero, ((0, h_rows, 0), (0, 0, 0)))

time: 205 us -> 213 us (1.039)
  Pallas kernels: 50.7 us -> 54.3 us
    pallas_call x0 -> x3, Pallas kernels: none -> 37.3 us  [the longest x2 35.1 us: sums(): return tuple(run(ids, sidx, scale_table, *pieces, *weights))]
    pallas_call x3 -> x1, Pallas kernels: 50.6 us -> 16.9 us  [sums(): return tuple(run(ids, sidx, scale_table, *sources, *pieces, down_weight))]
    unnamed x42 -> x44, local copies, waits for them, and re-layouts: 3.03 us -> 6.46 us
    slice x7 -> x0, local copies, waits for them, and re-layouts: 2.21 us -> none  [the longest x1 1.06 us: body(): taz[:h_rows]]
  transfers between devices with their start and end apart: 40 -> 40, of which waited for: 18 -> 12; matrix products, arithmetic and copies ran while one was open for 3% -> 3% of each run, Pallas kernels for 25% -> 26%
where the time goes in v2:
time: 213 us; the launch traced here: 212 us
  waiting for transfers between devices  85.6 us (40%)
  Pallas kernels  54.3 us (25%)
  starting transfers between devices  52.4 us (25%)
  other arithmetic  11.2 us (5%)
  local copies, waits for them, and re-layouts  7.25 us (3%)
    ppermute x40, waiting for transfers between devices, move(): return lax.ppermute(value, AXES, pairs)  85.6 us
    ppermute x40, starting transfers between devices, move(): return lax.ppermute(value, AXES, pairs)  52.4 us
    pallas_call x2, Pallas kernels, sums(): return tuple(run(ids, sidx, scale_table, *pieces, *weights))  35.1 us
    pallas_call x1, Pallas kernels, sums(): return tuple(run(ids, sidx, scale_table, *sources, *pieces, down_weight))  16.9 us
    unnamed x44, local copies, waits for them, and re-layouts  6.46 us
    convert_element_type x3, other arithmetic, body(): far_z, right, left = (add(part[i], got[i]).astype(BF16) for i in range(3))  4.79 us
  transfers between devices with their start and end apart: 40, of which 12 were waited for; matrix products, arithmetic and copies ran while one was open for 3% of the time, Pallas kernels for 26%

profile of v2, /device:TPU:1, one launch (start us, length us, event | category | flops | bytes accessed | tf_op | source)
XLA Modules:
  0.0 212.4 jit_solution(12914482619206969705)
XLA Ops:
  1.3 1.3 copy-done.3
  2.6 0.1 shard_map.64.refs_0_
  2.8 2.2 %collective-permute-start = (bf16[5136,128]{1,0:T(8,128)(2,1)S(1)}, bf16[5136,128]{1,0:T(8,128)(2,1)S(1)}, u32[]{:S(2)}, u32[]{:S(2)}) collective-permute-start(bf16[5136,128]{1,0:T(8,128)(2,1)S(1)} %shard_map.64.refs_0_), channel_id=1, source_target_pairs={{0,32},{1,33},{2,34},{3,35},{4,36},{5,37},{6,38},{7,39},{8,40},{9,... | collective-permute-start | bytes 3944456 | tf_op jit(solution)/shard_map/ppermute | solution.py:27
  5.0 3.6 %collective-permute-start.2 = (bf16[96,5120]{1,0:T(8,128)(2,1)S(1)}, bf16[96,5120]{1,0:T(8,128)(2,1)S(1)}, u32[]{:S(2)}, u32[]{:S(2)}) collective-permute-start(bf16[96,5120]{1,0:T(8,128)(2,1)S(1)} %copy-done.6), channel_id=1, source_target_pairs={{0,8},{1,9},{2,10},{3,11},{4,12},{5,13},{6,14},{7,15},{8,0},{9,1},... | collective-permute-start | bytes 2949128 | tf_op jit(solution)/shard_map/ppermute | solution.py:27
  8.6 1.2 collective-permute-start.6
  9.8 2.7 %collective-permute-start.1 = (bf16[5136,128]{1,0:T(8,128)(2,1)S(1)}, bf16[5136,128]{1,0:T(8,128)(2,1)S(1)}, u32[]{:S(2)}, u32[]{:S(2)}) collective-permute-start(bf16[5136,128]{1,0:T(8,128)(2,1)S(1)} %shard_map.64.refs_0_), channel_id=1, source_target_pairs={{0,96},{1,97},{2,98},{3,99},{4,100},{5,101},{6,102},{7,103},{8,104... | collective-permute-start | bytes 3944456 | tf_op jit(solution)/shard_map/ppermute | solution.py:27
  12.5 1.5 collective-permute-start.8
  14.0 15.8 %collective-permute-done.2.refs_4_ = bf16[96,5120]{1,0:T(8,128)(2,1)S(1)} collective-permute-done((bf16[96,5120]{1,0:T(8,128)(2,1)S(1)}, bf16[96,5120]{1,0:T(8,128)(2,1)S(1)}, u32[]{:S(2)}, u32[]{:S(2)}) %collective-permute-start.2) | collective-permute-done | bytes 983072 | tf_op jit(solution)/shard_map/ppermute | solution.py:27
  29.8 0.7 collective-permute-start.3
  30.5 4.3 %collective-permute-done.refs_1_ = bf16[5136,128]{1,0:T(8,128)(2,1)S(1)} collective-permute-done((bf16[5136,128]{1,0:T(8,128)(2,1)S(1)}, bf16[5136,128]{1,0:T(8,128)(2,1)S(1)}, u32[]{:S(2)}, u32[]{:S(2)}) %collective-permute-start) | collective-permute-done | bytes 1314848 | tf_op jit(solution)/shard_map/ppermute | solution.py:27
  34.8 1.1 collective-permute-start.7
  36.0 1.6 collective-permute-start.9
  37.7 1.8 collective-permute-done.1.refs_2_
  39.5 0.5 collective-permute-start.4
  40.1 3.1 %collective-permute-start.5 = (bf16[2560,128]{1,0:T(8,128)(2,1)S(1)}, bf16[2560,128]{1,0:T(8,128)(2,1)S(1)}, u32[]{:S(2)}, u32[]{:S(2)}) collective-permute-start(bf16[2560,128]{1,0:T(8,128)(2,1)S(1)} %slice.74), channel_id=1, source_target_pairs={{0,96},{1,97},{2,98},{3,99},{4,100},{5,101},{6,102},{7,103},{8,104... | collective-permute-start | bytes 1966088 | tf_op jit(solution)/shard_map/ppermute | solution.py:27
  43.1 14.9 %collective-permute-done.7.refs_3_.refs_11_ = bf16[96,5120]{1,0:T(8,128)(2,1)} collective-permute-done((bf16[96,5120]{1,0:T(8,128)(2,1)S(1)}, bf16[96,5120]{1,0:T(8,128)(2,1)}, u32[]{:S(2)}, u32[]{:S(2)}) %collective-permute-start.7) | collective-permute-done | bytes 983072 | tf_op jit(solution)/shard_map/ppermute | solution.py:27
  58.0 2.2 %shard_map.65 = (bf16[5136,128]{1,0:T(8,128)(2,1)S(1)}, bf16[96,5120]{1,0:T(8,128)(2,1)S(1)}, bf16[96,5120]{1,0:T(8,128)(2,1)S(1)}) custom-call(bf16[2576,128]{1,0:T(8,128)(2,1)S(1)} %collective-permute-done.4.refs_0_, bf16[2560,128]{1,0:T(8,128)(2,1)S(1)} %collective-permute-done.5.refs_1_, bf16[96,5120]{1,0:T(8,128)(2,1)S(1)} %collective-permute-done.6.refs_2_.refs_3_, ...), custom_call_target="tpu_custom_call" | custom-call | flops 1 | bytes 1 | tf_op jit(solution)/shard_map/pallas_call | solution.py:82
  60.2 1.5 collective-permute-start.12
  61.8 1.3 collective-permute-start.11
  63.1 1.1 collective-permute-start.13
  64.2 1.6 collective-permute-start.14
  65.8 0.1 collective-permute-start.10
  65.9 18.6 %collective-permute-done.13.refs_8_.refs_0_ = bf16[96,5120]{1,0:T(8,128)(2,1)} collective-permute-done((bf16[96,5120]{1,0:T(8,128)(2,1)S(1)}, bf16[96,5120]{1,0:T(8,128)(2,1)}, u32[]{:S(2)}, u32[]{:S(2)}) %collective-permute-start.13) | collective-permute-done | bytes 983072 | tf_op jit(solution)/shard_map/ppermute | solution.py:27
  84.5 4.1 %collective-permute-start.17 = (bf16[96,5120]{1,0:T(8,128)(2,1)}, bf16[96,5120]{1,0:T(8,128)(2,1)}, u32[]{:S(2)}, u32[]{:S(2)}) collective-permute-start(bf16[96,5120]{1,0:T(8,128)(2,1)} %collective-permute-done.9.refs_5_.refs_10_), channel_id=1, source_target_pairs={{0,1},{1,0},{2,3},{3,2},{4,5},{5,4},{6,7},{7,6},{8,9},{9,8},{10,11... | collective-permute-start | bytes 2949128 | tf_op jit(solution)/shard_map/ppermute | solution.py:27
  88.6 3.0 %collective-permute-start.16 = (bf16[96,5120]{1,0:T(8,128)(2,1)}, bf16[96,5120]{1,0:T(8,128)(2,1)}, u32[]{:S(2)}, u32[]{:S(2)}) collective-permute-start(bf16[96,5120]{1,0:T(8,128)(2,1)} %collective-permute-done.14.refs_9_.refs_1_), channel_id=1, source_target_pairs={{0,1},{1,0},{2,3},{3,2},{4,5},{5,4},{6,7},{7,6},{8,9},{9,8},{10,11... | collective-permute-start | bytes 2949128 | tf_op jit(solution)/shard_map/ppermute | solution.py:27
  91.6 1.4 collective-permute-start.18
  93.1 0.6 collective-permute-done.10.refs_5_
  93.6 1.1 copy-done.18
  94.7 0.1 stack.3
  94.8 4.7 %collective-permute-start.19 = (bf16[96,5120]{1,0:T(8,128)(2,1)S(1)}, bf16[96,5120]{1,0:T(8,128)(2,1)}, u32[]{:S(2)}, u32[]{:S(2)}) collective-permute-start(bf16[96,5120]{1,0:T(8,128)(2,1)S(1)} %collective-permute-done.8.refs_4_.refs_2_), channel_id=1, source_target_pairs={{0,1},{1,0},{2,3},{3,2},{4,5},{5,4},{6,7},{7,6},{8,9},{9,8},{10,11... | collective-permute-start | bytes 2949128 | tf_op jit(solution)/shard_map/ppermute | solution.py:27
  99.7 0.4 collective-permute-start.21
  100.2 0.6 slice_bitcast_fusion.7
  100.8 16.9 %shard_map.66 = (bf16[96,5120]{1,0:T(8,128)(2,1)}, bf16[96,5120]{1,0:T(8,128)(2,1)}, bf16[96,5120]{1,0:T(8,128)(2,1)}, bf16[96,5120]{1,0:T(8,128)(2,1)}, bf16[96...) custom-call(s32[8]{0:T(128)} %get-tuple-element.102.ids, ...), custom_call_target="tpu_custom_call" | custom-call | flops 9059696640 | bytes 27525120 | tf_op jit(solution)/shard_map/pallas_call | solution.py:278
  117.7 4.0 %copy-done = bf16[4,5120,256]{2,1,0:T(8,128)(2,1)} copy-done((bf16[4,5120,256]{2,1,0:T(8,128)(2,1)}, bf16[4,5120,256]{2,1,0:T(8,128)(2,1)S(1)}, u32[]{:S(2)}) %copy-start) | copy-done | bytes 10485784
  121.8 0.5 collective-permute-start.25
  122.3 0.1 collective-permute-start.24
  122.4 0.4 collective-permute-start.23
  122.8 1.9 collective-permute-done.25
  124.7 2.4 %add_convert_fusion.4 = bf16[96,5120]{1,0:T(8,128)(2,1)} fusion(bf16[96,5120]{1,0:T(8,128)(2,1)S(1)} %collective-permute-done.25, bf16[96,5120]{1,0:T(8,128)(2,1)} %get-tuple-element.82), kind=kLoop, calls=%fused_computation.4 | loop fusion | flops 1966080 | bytes 2949120 | tf_op jit(solution)/shard_map/convert_element_type | solution.py:303
  127.1 1.3 collective-permute-start.30
  128.4 1.2 add_convert_fusion.5
  129.6 0.2 collective-permute-start.29
  129.8 1.2 add_convert_fusion.6
  131.0 3.3 %collective-permute-start.28 = (bf16[96,5120]{1,0:T(8,128)(2,1)}, bf16[96,5120]{1,0:T(8,128)(2,1)}, u32[]{:S(2)}, u32[]{:S(2)}) collective-permute-start(bf16[96,5120]{1,0:T(8,128)(2,1)} %add_convert_fusion.6), channel_id=1, source_target_pairs={{0,8},{1,9},{2,10},{3,11},{4,12},{5,13},{6,14},{7,15},{8,0},{9,1},... | collective-permute-start | bytes 2949128 | tf_op jit(solution)/shard_map/ppermute | solution.py:27
  134.3 25.2 %shard_map.67 = (bf16[96,5120]{1,0:T(8,128)(2,1)S(1)}, bf16[96,5120]{1,0:T(8,128)(2,1)S(1)}, bf16[96,5120]{1,0:T(8,128)(2,1)S(1)}, bf16[96,5120]{1,0:T(8,128)(2,...) custom-call(s32[8]{0:T(128)S(1)} %copy-done.8, ...), custom_call_target="tpu_custom_call" | custom-call | flops 12079595520 | bytes 31457280 | tf_op jit(solution)/shard_map/pallas_call | solution.py:279
  159.5 1.3 collective-permute-start.26
  160.9 1.4 collective-permute-done.26
  162.3 0.7 collective-permute-done.27
  163.0 2.3 %add_convert_fusion.7 = (bf16[48,5120]{1,0:T(8,128)(2,1)S(1)}, bf16[48,5120]{1,0:T(8,128)(2,1)}) fusion(bf16[48,5120]{1,0:T(8,128)(2,1)S(1)} %collective-permute-done.27, bf16[96,5120]{1,0:T(8,128)(2,1)} %collective-permute-done.28, bf16[96,5120]{1,0:T(8,128)(2,1)S(1)} %get-tuple-element.95, bf16[48,5120]{1,0:T(8,128)(2,1)S(1)} %collective-permute-done.26), kind=kLoop, calls=%fused_computation.7 | loop fusion | flops 2949120 | bytes 3932160 | tf_op jit(solution)/shard_map/convert_element_type | solution.py:313
  165.4 0.4 collective-permute-start.31
  165.7 0.1 collective-permute-start.32
  165.9 0.4 collective-permute-start.33
  166.2 2.7 %collective-permute-start.35 = (bf16[48,5120]{1,0:T(8,128)(2,1)S(1)}, bf16[48,5120]{1,0:T(8,128)(2,1)S(1)}, u32[]{:S(2)}, u32[]{:S(2)}) collective-permute-start(bf16[48,5120]{1,0:T(8,128)(2,1)S(1)} %get-tuple-element.117), channel_id=1, source_target_pairs={{0,6},{1,7},{2,0},{3,1},{4,2},{5,3},{6,4},{7,5},{8,14},{9,15},{10,... | collective-permute-start | bytes 1474568 | tf_op jit(solution)/shard_map/ppermute | solution.py:27
  168.9 9.9 %shard_map.68 = (bf16[96,5120]{1,0:T(8,128)(2,1)S(1)}, bf16[96,5120]{1,0:T(8,128)(2,1)S(1)}) custom-call(s32[8]{0:T(128)S(1)} %copy-done.8, s32[8]{0:T(128)S(1)} %copy-done.7, f32[64]{0:T(128)S(1)} %copy-done.9, bf16[96,5120]{1,0:T(8,128)(2,1)S(1)} %copy-done.6, bf16[96,5120]{1,0:T(8,128)(2,1)S(1)} %collective-permute-done.22.refs_1_, ...), custom_call_target="tpu_custom_call" | custom-call | flops 3019898880 | bytes 19660800 | tf_op jit(solution)/shard_map/pallas_call | solution.py:279
  178.8 1.5 collective-permute-done.34
  180.4 0.3 add_convert_fusion.3
  180.7 1.5 add_convert_fusion.2
  182.2 0.6 add_convert_fusion.1
  182.8 1.0 collective-permute-start.36
  183.8 0.5 collective-permute-start.37
  184.3 2.2 %collective-permute-start.38 = (bf16[96,5120]{1,0:T(8,128)(2,1)S(1)}, bf16[96,5120]{1,0:T(8,128)(2,1)S(1)}, u32[]{:S(2)}, u32[]{:S(2)}) collective-permute-start(bf16[96,5120]{1,0:T(8,128)(2,1)S(1)} %add_convert_fusion.2), channel_id=1, source_target_pairs={{0,6},{1,7},{2,0},{3,1},{4,2},{5,3},{6,4},{7,5},{8,14},{9,15},{10,... | collective-permute-start | bytes 2949128 | tf_op jit(solution)/shard_map/ppermute | solution.py:27
  186.6 21.8 %collective-permute-done.37 = bf16[96,5120]{1,0:T(8,128)(2,1)S(1)} collective-permute-done((bf16[96,5120]{1,0:T(8,128)(2,1)S(1)}, bf16[96,5120]{1,0:T(8,128)(2,1)S(1)}, u32[]{:S(2)}, u32[]{:S(2)}) %collective-permute-start.37) | collective-permute-done | bytes 983072 | tf_op jit(solution)/shard_map/ppermute | solution.py:27
  208.4 2.3 %collective-permute-done.39 = bf16[96,5120]{1,0:T(8,128)(2,1)S(1)} collective-permute-done((bf16[96,5120]{1,0:T(8,128)(2,1)S(1)}, bf16[96,5120]{1,0:T(8,128)(2,1)S(1)}, u32[]{:S(2)}, u32[]{:S(2)}) %collective-permute-start.39) | collective-permute-done | bytes 983072 | tf_op jit(solution)/shard_map/ppermute | solution.py:27
  210.7 1.7 add_convert_fusion
  (89 shorter events, 0.7 us)
Async XLA Ops:
  1.3 1.3 copy-start.3
  2.6 2.3 %copy-start.6 = (bf16[96,5120]{1,0:T(8,128)(2,1)S(1)}, bf16[96,5120]{1,0:T(8,128)(2,1)}, u32[]{:S(2)}) copy-start(bf16[96,5120]{1,0:T(8,128)(2,1)} %refs_0_.1) | copy-start | bytes 2949124
  2.7 63.0 %copy-start.2 = (bf16[5136,128]{1,0:T(8,128)(2,1)}, bf16[5136,128]{1,0:T(8,128)(2,1)S(1)}, u32[]{:S(2)}) copy-start(bf16[5136,128]{1,0:T(8,128)(2,1)S(1)} %shard_map.64.refs_0_) | copy-start | bytes 3944452
  2.8 32.1 %collective-permute-start = (bf16[5136,128]{1,0:T(8,128)(2,1)S(1)}, bf16[5136,128]{1,0:T(8,128)(2,1)S(1)}, u32[]{:S(2)}, u32[]{:S(2)}) collective-permute-start(bf16[5136,128]{1,0:T(8,128)(2,1)S(1)} %shard_map.64.refs_0_), channel_id=1, source_target_pairs={{0,32},{1,33},{2,34},{3,35},{4,36},{5,37},{6,38},{7,39},{8,40},{9,... | collective-permute-start | bytes 3944456 | tf_op jit(solution)/shard_map/ppermute | solution.py:27
  5.0 24.9 %collective-permute-start.2 = (bf16[96,5120]{1,0:T(8,128)(2,1)S(1)}, bf16[96,5120]{1,0:T(8,128)(2,1)S(1)}, u32[]{:S(2)}, u32[]{:S(2)}) collective-permute-start(bf16[96,5120]{1,0:T(8,128)(2,1)S(1)} %copy-done.6), channel_id=1, source_target_pairs={{0,8},{1,9},{2,10},{3,11},{4,12},{5,13},{6,14},{7,15},{8,0},{9,1},... | collective-permute-start | bytes 2949128 | tf_op jit(solution)/shard_map/ppermute | solution.py:27
  8.6 27.4 %collective-permute-start.6 = (bf16[96,5120]{1,0:T(8,128)(2,1)S(1)}, bf16[96,5120]{1,0:T(8,128)(2,1)S(1)}, u32[]{:S(2)}, u32[]{:S(2)}) collective-permute-start(bf16[96,5120]{1,0:T(8,128)(2,1)S(1)} %copy-done.6), channel_id=1, source_target_pairs={{0,2},{1,3},{2,4},{3,5},{4,6},{5,7},{6,0},{7,1},{8,10},{9,11},{10,... | collective-permute-start | bytes 2949128 | tf_op jit(solution)/shard_map/ppermute | solution.py:27
  9.8 29.7 %collective-permute-start.1 = (bf16[5136,128]{1,0:T(8,128)(2,1)S(1)}, bf16[5136,128]{1,0:T(8,128)(2,1)S(1)}, u32[]{:S(2)}, u32[]{:S(2)}) collective-permute-start(bf16[5136,128]{1,0:T(8,128)(2,1)S(1)} %shard_map.64.refs_0_), channel_id=1, source_target_pairs={{0,96},{1,97},{2,98},{3,99},{4,100},{5,101},{6,102},{7,103},{8,104... | collective-permute-start | bytes 3944456 | tf_op jit(solution)/shard_map/ppermute | solution.py:27
  12.5 27.5 %collective-permute-start.8 = (bf16[96,5120]{1,0:T(8,128)(2,1)S(1)}, bf16[96,5120]{1,0:T(8,128)(2,1)S(1)}, u32[]{:S(2)}, u32[]{:S(2)}) collective-permute-start(bf16[96,5120]{1,0:T(8,128)(2,1)S(1)} %copy-done.6), channel_id=1, source_target_pairs={{0,6},{1,7},{2,0},{3,1},{4,2},{5,3},{6,4},{7,5},{8,14},{9,15},{10,... | collective-permute-start | bytes 2949128 | tf_op jit(solution)/shard_map/ppermute | solution.py:27
  29.8 30.4 %copy-start.19 = (bf16[96,5120]{1,0:T(8,128)(2,1)}, bf16[96,5120]{1,0:T(8,128)(2,1)S(1)}, u32[]{:S(2)}) copy-start(bf16[96,5120]{1,0:T(8,128)(2,1)S(1)} %collective-permute-done.2.refs_4_) | copy-start | bytes 2949124
  29.8 30.4 %collective-permute-start.3 = (bf16[5136,128]{1,0:T(8,128)(2,1)S(1)}, bf16[5136,128]{1,0:T(8,128)(2,1)S(1)}, u32[]{:S(2)}, u32[]{:S(2)}) collective-permute-start(bf16[5136,128]{1,0:T(8,128)(2,1)S(1)} %shard_map.64.refs_0_), channel_id=1, source_target_pairs={{0,16},{1,17},{2,18},{3,19},{4,20},{5,21},{6,22},{7,23},{8,24},{9,... | collective-permute-start | bytes 3944456 | tf_op jit(solution)/shard_map/ppermute | solution.py:27
  34.8 31.1 %copy-start.13 = (bf16[5136,128]{1,0:T(8,128)(2,1)}, bf16[5136,128]{1,0:T(8,128)(2,1)S(1)}, u32[]{:S(2)}) copy-start(bf16[5136,128]{1,0:T(8,128)(2,1)S(1)} %collective-permute-done.refs_1_) | copy-start | bytes 3944452
  34.8 23.2 %collective-permute-start.7 = (bf16[96,5120]{1,0:T(8,128)(2,1)S(1)}, bf16[96,5120]{1,0:T(8,128)(2,1)}, u32[]{:S(2)}, u32[]{:S(2)}) collective-permute-start(bf16[96,5120]{1,0:T(8,128)(2,1)S(1)} %collective-permute-done.2.refs_4_), channel_id=1, source_target_pairs={{0,2},{1,3},{2,4},{3,5},{4,6},{5,7},{6,0},{7,1},{8,10},{9,11},{10,... | collective-permute-start | bytes 2949128 | tf_op jit(solution)/shard_map/ppermute | solution.py:27
  36.0 63.5 %copy-start.4 = (bf16[96,5120]{1,0:T(8,128)(2,1)}, bf16[96,5120]{1,0:T(8,128)(2,1)S(1)}, u32[]{:S(2)}) copy-start(bf16[96,5120]{1,0:T(8,128)(2,1)S(1)} %collective-permute-done.6.refs_2_.refs_3_) | copy-start | bytes 2949124
  36.0 22.0 %collective-permute-start.9 = (bf16[96,5120]{1,0:T(8,128)(2,1)S(1)}, bf16[96,5120]{1,0:T(8,128)(2,1)}, u32[]{:S(2)}, u32[]{:S(2)}) collective-permute-start(bf16[96,5120]{1,0:T(8,128)(2,1)S(1)} %collective-permute-done.2.refs_4_), channel_id=1, source_target_pairs={{0,6},{1,7},{2,0},{3,1},{4,2},{5,3},{6,4},{7,5},{8,14},{9,15},{10,... | collective-permute-start | bytes 2949128 | tf_op jit(solution)/shard_map/ppermute | solution.py:27
  39.5 26.5 %copy-start.14 = (bf16[5136,128]{1,0:T(8,128)(2,1)}, bf16[5136,128]{1,0:T(8,128)(2,1)S(1)}, u32[]{:S(2)}) copy-start(bf16[5136,128]{1,0:T(8,128)(2,1)S(1)} %collective-permute-done.1.refs_2_) | copy-start | bytes 3944452
  39.5 18.6 %collective-permute-start.4 = (bf16[2576,128]{1,0:T(8,128)(2,1)S(1)}, bf16[2576,128]{1,0:T(8,128)(2,1)S(1)}, u32[]{:S(2)}, u32[]{:S(2)}) collective-permute-start(bf16[2576,128]{1,0:T(8,128)(2,1)S(1)} %pad_maximum_fusion), channel_id=1, source_target_pairs={{0,32},{1,33},{2,34},{3,35},{4,36},{5,37},{6,38},{7,39},{8,40},{9,... | collective-permute-start | bytes 1978376 | tf_op jit(solution)/shard_map/ppermute | solution.py:27
  40.1 54.8 %copy-start.5 = (bf16[96,5120]{1,0:T(8,128)(2,1)}, bf16[96,5120]{1,0:T(8,128)(2,1)S(1)}, u32[]{:S(2)}) copy-start(bf16[96,5120]{1,0:T(8,128)(2,1)S(1)} %collective-permute-done.8.refs_4_.refs_2_) | copy-start | bytes 2949124
  40.1 18.0 %collective-permute-start.5 = (bf16[2560,128]{1,0:T(8,128)(2,1)S(1)}, bf16[2560,128]{1,0:T(8,128)(2,1)S(1)}, u32[]{:S(2)}, u32[]{:S(2)}) collective-permute-start(bf16[2560,128]{1,0:T(8,128)(2,1)S(1)} %slice.74), channel_id=1, source_target_pairs={{0,96},{1,97},{2,98},{3,99},{4,100},{5,101},{6,102},{7,103},{8,104... | collective-permute-start | bytes 1966088 | tf_op jit(solution)/shard_map/ppermute | solution.py:27
  60.2 31.4 %copy-start.10 = (bf16[5136,128]{1,0:T(8,128)(2,1)}, bf16[5136,128]{1,0:T(8,128)(2,1)S(1)}, u32[]{:S(2)}) copy-start(bf16[5136,128]{1,0:T(8,128)(2,1)S(1)} %get-tuple-element.65.refs_4_) | copy-start | bytes 3944452
  60.2 33.4 %copy-start.15 = (bf16[5136,128]{1,0:T(8,128)(2,1)}, bf16[5136,128]{1,0:T(8,128)(2,1)S(1)}, u32[]{:S(2)}) copy-start(bf16[5136,128]{1,0:T(8,128)(2,1)S(1)} %collective-permute-done.3.refs_3_) | copy-start | bytes 3944452
  60.2 28.3 %collective-permute-start.12 = (bf16[5136,128]{1,0:T(8,128)(2,1)S(1)}, bf16[5136,128]{1,0:T(8,128)(2,1)S(1)}, u32[]{:S(2)}, u32[]{:S(2)}) collective-permute-start(bf16[5136,128]{1,0:T(8,128)(2,1)S(1)} %get-tuple-element.65.refs_4_), channel_id=1, source_target_pairs={{0,16},{1,17},{2,18},{3,19},{4,20},{5,21},{6,22},{7,23},{8,24},{9,... | collective-permute-start | bytes 3944456 | tf_op jit(solution)/shard_map/ppermute | solution.py:27
  61.8 29.8 %collective-permute-start.11 = (bf16[5136,128]{1,0:T(8,128)(2,1)S(1)}, bf16[5136,128]{1,0:T(8,128)(2,1)S(1)}, u32[]{:S(2)}, u32[]{:S(2)}) collective-permute-start(bf16[5136,128]{1,0:T(8,128)(2,1)S(1)} %collective-permute-done.3.refs_3_), channel_id=1, source_target_pairs={{0,96},{1,97},{2,98},{3,99},{4,100},{5,101},{6,102},{7,103},{8,104... | collective-permute-start | bytes 3944456 | tf_op jit(solution)/shard_map/ppermute | solution.py:27
  63.1 21.4 %collective-permute-start.13 = (bf16[96,5120]{1,0:T(8,128)(2,1)S(1)}, bf16[96,5120]{1,0:T(8,128)(2,1)}, u32[]{:S(2)}, u32[]{:S(2)}) collective-permute-start(bf16[96,5120]{1,0:T(8,128)(2,1)S(1)} %get-tuple-element.66), channel_id=1, source_target_pairs={{0,2},{1,3},{2,4},{3,5},{4,6},{5,7},{6,0},{7,1},{8,10},{9,11},{10,... | collective-permute-start | bytes 2949128 | tf_op jit(solution)/shard_map/ppermute | solution.py:27
  64.2 24.4 %collective-permute-start.14 = (bf16[96,5120]{1,0:T(8,128)(2,1)S(1)}, bf16[96,5120]{1,0:T(8,128)(2,1)}, u32[]{:S(2)}, u32[]{:S(2)}) collective-permute-start(bf16[96,5120]{1,0:T(8,128)(2,1)S(1)} %get-tuple-element.67), channel_id=1, source_target_pairs={{0,6},{1,7},{2,0},{3,1},{4,2},{5,3},{6,4},{7,5},{8,14},{9,15},{10,... | collective-permute-start | bytes 2949128 | tf_op jit(solution)/shard_map/ppermute | solution.py:27
  65.8 27.8 %collective-permute-start.10 = (bf16[5136,128]{1,0:T(8,128)(2,1)S(1)}, bf16[5136,128]{1,0:T(8,128)(2,1)S(1)}, u32[]{:S(2)}, u32[]{:S(2)}) collective-permute-start(bf16[5136,128]{1,0:T(8,128)(2,1)S(1)} %collective-permute-done.3.refs_3_), channel_id=1, source_target_pairs={{0,32},{1,33},{2,34},{3,35},{4,36},{5,37},{6,38},{7,39},{8,40},{9,... | collective-permute-start | bytes 3944456 | tf_op jit(solution)/shard_map/ppermute | solution.py:27
  84.5 15.6 %collective-permute-start.17 = (bf16[96,5120]{1,0:T(8,128)(2,1)}, bf16[96,5120]{1,0:T(8,128)(2,1)}, u32[]{:S(2)}, u32[]{:S(2)}) collective-permute-start(bf16[96,5120]{1,0:T(8,128)(2,1)} %collective-permute-done.9.refs_5_.refs_10_), channel_id=1, source_target_pairs={{0,1},{1,0},{2,3},{3,2},{4,5},{5,4},{6,7},{7,6},{8,9},{9,8},{10,11... | collective-permute-start | bytes 2949128 | tf_op jit(solution)/shard_map/ppermute | solution.py:27
  88.6 6.2 %collective-permute-start.15 = (bf16[96,5120]{1,0:T(8,128)(2,1)}, bf16[96,5120]{1,0:T(8,128)(2,1)}, u32[]{:S(2)}, u32[]{:S(2)}) collective-permute-start(bf16[96,5120]{1,0:T(8,128)(2,1)} %collective-permute-done.13.refs_8_.refs_0_), channel_id=1, source_target_pairs={{0,1},{1,0},{2,3},{3,2},{4,5},{5,4},{6,7},{7,6},{8,9},{9,8},{10,11... | collective-permute-start | bytes 2949128 | tf_op jit(solution)/shard_map/ppermute | solution.py:27
  88.6 5.0 %copy-start.16 = (bf16[5136,128]{1,0:T(8,128)(2,1)}, bf16[5136,128]{1,0:T(8,128)(2,1)S(1)}, u32[]{:S(2)}) copy-start(bf16[5136,128]{1,0:T(8,128)(2,1)S(1)} %collective-permute-done.12.refs_7_) | copy-start | bytes 3944452
  88.6 6.2 %collective-permute-start.16 = (bf16[96,5120]{1,0:T(8,128)(2,1)}, bf16[96,5120]{1,0:T(8,128)(2,1)}, u32[]{:S(2)}, u32[]{:S(2)}) collective-permute-start(bf16[96,5120]{1,0:T(8,128)(2,1)} %collective-permute-done.14.refs_9_.refs_1_), channel_id=1, source_target_pairs={{0,1},{1,0},{2,3},{3,2},{4,5},{5,4},{6,7},{7,6},{8,9},{9,8},{10,11... | collective-permute-start | bytes 2949128 | tf_op jit(solution)/shard_map/ppermute | solution.py:27
  91.6 2.0 copy-start.17
  91.6 9.1 %collective-permute-start.18 = (bf16[96,5120]{1,0:T(8,128)(2,1)}, bf16[96,5120]{1,0:T(8,128)(2,1)}, u32[]{:S(2)}, u32[]{:S(2)}) collective-permute-start(bf16[96,5120]{1,0:T(8,128)(2,1)} %collective-permute-done.7.refs_3_.refs_11_), channel_id=1, source_target_pairs={{0,1},{1,0},{2,3},{3,2},{4,5},{5,4},{6,7},{7,6},{8,9},{9,8},{10,11... | collective-permute-start | bytes 2949128 | tf_op jit(solution)/shard_map/ppermute | solution.py:27
  93.6 1.1 copy-start.18
  94.8 26.9 %collective-permute-start.19 = (bf16[96,5120]{1,0:T(8,128)(2,1)S(1)}, bf16[96,5120]{1,0:T(8,128)(2,1)}, u32[]{:S(2)}, u32[]{:S(2)}) collective-permute-start(bf16[96,5120]{1,0:T(8,128)(2,1)S(1)} %collective-permute-done.8.refs_4_.refs_2_), channel_id=1, source_target_pairs={{0,1},{1,0},{2,3},{3,2},{4,5},{5,4},{6,7},{7,6},{8,9},{9,8},{10,11... | collective-permute-start | bytes 2949128 | tf_op jit(solution)/shard_map/ppermute | solution.py:27
  99.6 22.2 %collective-permute-start.20 = (bf16[96,5120]{1,0:T(8,128)(2,1)S(1)}, bf16[96,5120]{1,0:T(8,128)(2,1)}, u32[]{:S(2)}, u32[]{:S(2)}) collective-permute-start(bf16[96,5120]{1,0:T(8,128)(2,1)S(1)} %collective-permute-done.6.refs_2_.refs_3_), channel_id=1, source_target_pairs={{0,1},{1,0},{2,3},{3,2},{4,5},{5,4},{6,7},{7,6},{8,9},{9,8},{10,11... | collective-permute-start | bytes 2949128 | tf_op jit(solution)/shard_map/ppermute | solution.py:27
  99.7 22.1 %collective-permute-start.21 = (bf16[96,5120]{1,0:T(8,128)(2,1)}, bf16[96,5120]{1,0:T(8,128)(2,1)}, u32[]{:S(2)}, u32[]{:S(2)}) collective-permute-start(bf16[96,5120]{1,0:T(8,128)(2,1)} %copy-done.19), channel_id=1, source_target_pairs={{0,1},{1,0},{2,3},{3,2},{4,5},{5,4},{6,7},{7,6},{8,9},{9,8},{10,11... | collective-permute-start | bytes 2949128 | tf_op jit(solution)/shard_map/ppermute | solution.py:27
  100.1 21.7 %collective-permute-start.22 = (bf16[96,5120]{1,0:T(8,128)(2,1)S(1)}, bf16[96,5120]{1,0:T(8,128)(2,1)S(1)}, u32[]{:S(2)}, u32[]{:S(2)}) collective-permute-start(bf16[96,5120]{1,0:T(8,128)(2,1)S(1)} %copy-done.6), channel_id=1, source_target_pairs={{0,1},{1,0},{2,3},{3,2},{4,5},{5,4},{6,7},{7,6},{8,9},{9,8},{10,11... | collective-permute-start | bytes 2949128 | tf_op jit(solution)/shard_map/ppermute | solution.py:27
  117.7 4.0 %copy-start = (bf16[4,5120,256]{2,1,0:T(8,128)(2,1)}, bf16[4,5120,256]{2,1,0:T(8,128)(2,1)S(1)}, u32[]{:S(2)}) copy-start(bf16[4,5120,256]{2,1,0:T(8,128)(2,1)S(1)} %get-tuple-element.85.refs_10_.refs_2_) | copy-start | bytes 31457284
  121.7 7.9 %copy-start.1 = (bf16[512,5120]{1,0:T(8,128)(2,1)}, bf16[512,5120]{1,0:T(8,128)(2,1)S(1)}, u32[]{:S(2)}) copy-start(bf16[512,5120]{1,0:T(8,128)(2,1)S(1)} %get-tuple-element.86.refs_11_.refs_3_) | copy-start | bytes 15728644
  121.7 6.7 %copy-start.12 = (bf16[96,5120]{1,0:T(8,128)(2,1)S(1)}, bf16[96,5120]{1,0:T(8,128)(2,1)}, u32[]{:S(2)}) copy-start(bf16[96,5120]{1,0:T(8,128)(2,1)} %get-tuple-element.80) | copy-start | bytes 2949124
  121.8 2.9 %collective-permute-start.25 = (bf16[96,5120]{1,0:T(8,128)(2,1)}, bf16[96,5120]{1,0:T(8,128)(2,1)S(1)}, u32[]{:S(2)}, u32[]{:S(2)}) collective-permute-start(bf16[96,5120]{1,0:T(8,128)(2,1)} %get-tuple-element.83), channel_id=1, source_target_pairs={{0,1},{1,0},{2,3},{3,2},{4,5},{5,4},{6,7},{7,6},{8,9},{9,8},{10,11... | collective-permute-start | bytes 2949128 | tf_op jit(solution)/shard_map/ppermute | solution.py:27
  122.3 6.1 %collective-permute-start.24 = (bf16[96,5120]{1,0:T(8,128)(2,1)}, bf16[96,5120]{1,0:T(8,128)(2,1)S(1)}, u32[]{:S(2)}, u32[]{:S(2)}) collective-permute-start(bf16[96,5120]{1,0:T(8,128)(2,1)} %get-tuple-element.81), channel_id=1, source_target_pairs={{0,1},{1,0},{2,3},{3,2},{4,5},{5,4},{6,7},{7,6},{8,9},{9,8},{10,11... | collective-permute-start | bytes 2949128 | tf_op jit(solution)/shard_map/ppermute | solution.py:27
  122.4 7.5 %collective-permute-start.23 = (bf16[96,5120]{1,0:T(8,128)(2,1)}, bf16[96,5120]{1,0:T(8,128)(2,1)S(1)}, u32[]{:S(2)}, u32[]{:S(2)}) collective-permute-start(bf16[96,5120]{1,0:T(8,128)(2,1)} %get-tuple-element.79), channel_id=1, source_target_pairs={{0,1},{1,0},{2,3},{3,2},{4,5},{5,4},{6,7},{7,6},{8,9},{9,8},{10,11... | collective-permute-start | bytes 2949128 | tf_op jit(solution)/shard_map/ppermute | solution.py:27
  127.1 2.8 %copy-start.11 = (bf16[96,5120]{1,0:T(8,128)(2,1)S(1)}, bf16[96,5120]{1,0:T(8,128)(2,1)}, u32[]{:S(2)}) copy-start(bf16[96,5120]{1,0:T(8,128)(2,1)} %get-tuple-element.78) | copy-start | bytes 2949124
  127.1 36.0 %collective-permute-start.30 = (bf16[96,5120]{1,0:T(8,128)(2,1)}, bf16[96,5120]{1,0:T(8,128)(2,1)S(1)}, u32[]{:S(2)}, u32[]{:S(2)}) collective-permute-start(bf16[96,5120]{1,0:T(8,128)(2,1)} %add_convert_fusion.4), channel_id=1, source_target_pairs={{0,6},{1,7},{2,0},{3,1},{4,2},{5,3},{6,4},{7,5},{8,14},{9,15},{10,... | collective-permute-start | bytes 2949128 | tf_op jit(solution)/shard_map/ppermute | solution.py:27
  129.6 4.7 %copy-start.7 = (s32[8]{0:T(128)S(1)}, s32[8]{0:T(128)}, u32[]{:S(2)}) copy-start(s32[8]{0:T(128)} %get-tuple-element.119.sidx) | copy-start | bytes 100
  129.6 4.7 %copy-start.8 = (s32[8]{0:T(128)S(1)}, s32[8]{0:T(128)}, u32[]{:S(2)}) copy-start(s32[8]{0:T(128)} %get-tuple-element.102.ids) | copy-start | bytes 100
  129.6 4.7 %copy-start.9 = (f32[64]{0:T(128)S(1)}, f32[64]{0:T(128)}, u32[]{:S(2)}) copy-start(f32[64]{0:T(128)} %table.5) | copy-start | bytes 772
  129.6 33.4 %collective-permute-start.29 = (bf16[96,5120]{1,0:T(8,128)(2,1)}, bf16[96,5120]{1,0:T(8,128)(2,1)S(1)}, u32[]{:S(2)}, u32[]{:S(2)}) collective-permute-start(bf16[96,5120]{1,0:T(8,128)(2,1)} %add_convert_fusion.5), channel_id=1, source_target_pairs={{0,2},{1,3},{2,4},{3,5},{4,6},{5,7},{6,0},{7,1},{8,10},{9,11},{10,... | collective-permute-start | bytes 2949128 | tf_op jit(solution)/shard_map/ppermute | solution.py:27
  129.8 39.1 %slice-start = ((s8[5242880]{0:T(1024)(128)(4,1)}), s8[4194304]{0:T(1024)(128)(4,1)S(1)}, s32[]{:S(2)}) async-start(s8[5242880]{0:T(1024)(128)(4,1)} %bitcast.20), calls=%async_computation | async-start | bytes 8388608
  131.0 32.0 %collective-permute-start.28 = (bf16[96,5120]{1,0:T(8,128)(2,1)}, bf16[96,5120]{1,0:T(8,128)(2,1)}, u32[]{:S(2)}, u32[]{:S(2)}) collective-permute-start(bf16[96,5120]{1,0:T(8,128)(2,1)} %add_convert_fusion.6), channel_id=1, source_target_pairs={{0,8},{1,9},{2,10},{3,11},{4,12},{5,13},{6,14},{7,15},{8,0},{9,1},... | collective-permute-start | bytes 2949128 | tf_op jit(solution)/shard_map/ppermute | solution.py:27
  134.3 34.6 %slice-start.1 = ((s8[5242880]{0:T(1024)(128)(4,1)}), s8[1048576]{0:T(1024)(128)(4,1)S(1)}, s32[]{:S(2)}) async-start(s8[5242880]{0:T(1024)(128)(4,1)} %bitcast.20), calls=%async_computation.1 | async-start | bytes 2097152
  159.5 2.8 %collective-permute-start.26 = (bf16[48,5120]{1,0:T(8,128)(2,1)S(1)}, bf16[48,5120]{1,0:T(8,128)(2,1)S(1)}, u32[]{:S(2)}, u32[]{:S(2)}) collective-permute-start(bf16[48,5120]{1,0:T(8,128)(2,1)S(1)} %get-tuple-element.93), channel_id=1, source_target_pairs={{0,1},{1,0},{2,3},{3,2},{4,5},{5,4},{6,7},{7,6},{8,9},{9,8},{10,11... | collective-permute-start | bytes 1474568 | tf_op jit(solution)/shard_map/ppermute | solution.py:27
  160.8 2.2 %collective-permute-start.27 = (bf16[48,5120]{1,0:T(8,128)(2,1)S(1)}, bf16[48,5120]{1,0:T(8,128)(2,1)S(1)}, u32[]{:S(2)}, u32[]{:S(2)}) collective-permute-start(bf16[48,5120]{1,0:T(8,128)(2,1)S(1)} %get-tuple-element.94), channel_id=1, source_target_pairs={{0,1},{1,0},{2,3},{3,2},{4,5},{5,4},{6,7},{7,6},{8,9},{9,8},{10,11... | collective-permute-start | bytes 1474568 | tf_op jit(solution)/shard_map/ppermute | solution.py:27
  165.4 15.0 %collective-permute-start.31 = (bf16[96,5120]{1,0:T(8,128)(2,1)S(1)}, bf16[96,5120]{1,0:T(8,128)(2,1)S(1)}, u32[]{:S(2)}, u32[]{:S(2)}) collective-permute-start(bf16[96,5120]{1,0:T(8,128)(2,1)S(1)} %get-tuple-element.99), channel_id=1, source_target_pairs={{0,1},{1,0},{2,3},{3,2},{4,5},{5,4},{6,7},{7,6},{8,9},{9,8},{10,11... | collective-permute-start | bytes 2949128 | tf_op jit(solution)/shard_map/ppermute | solution.py:27
  165.7 14.6 %collective-permute-start.32 = (bf16[96,5120]{1,0:T(8,128)(2,1)S(1)}, bf16[96,5120]{1,0:T(8,128)(2,1)}, u32[]{:S(2)}, u32[]{:S(2)}) collective-permute-start(bf16[96,5120]{1,0:T(8,128)(2,1)S(1)} %get-tuple-element.100), channel_id=1, source_target_pairs={{0,1},{1,0},{2,3},{3,2},{4,5},{5,4},{6,7},{7,6},{8,9},{9,8},{10,11... | collective-permute-start | bytes 2949128 | tf_op jit(solution)/shard_map/ppermute | solution.py:27
  165.9 14.5 %collective-permute-start.33 = (bf16[96,5120]{1,0:T(8,128)(2,1)S(1)}, bf16[96,5120]{1,0:T(8,128)(2,1)S(1)}, u32[]{:S(2)}, u32[]{:S(2)}) collective-permute-start(bf16[96,5120]{1,0:T(8,128)(2,1)S(1)} %get-tuple-element.101), channel_id=1, source_target_pairs={{0,1},{1,0},{2,3},{3,2},{4,5},{5,4},{6,7},{7,6},{8,9},{9,8},{10,11... | collective-permute-start | bytes 2949128 | tf_op jit(solution)/shard_map/ppermute | solution.py:27
  166.2 14.1 %collective-permute-start.34 = (bf16[48,5120]{1,0:T(8,128)(2,1)}, bf16[48,5120]{1,0:T(8,128)(2,1)S(1)}, u32[]{:S(2)}, u32[]{:S(2)}) collective-permute-start(bf16[48,5120]{1,0:T(8,128)(2,1)} %get-tuple-element.118), channel_id=1, source_target_pairs={{0,2},{1,3},{2,4},{3,5},{4,6},{5,7},{6,0},{7,1},{8,10},{9,11},{10,... | collective-permute-start | bytes 1474568 | tf_op jit(solution)/shard_map/ppermute | solution.py:27
  166.2 14.1 %collective-permute-start.35 = (bf16[48,5120]{1,0:T(8,128)(2,1)S(1)}, bf16[48,5120]{1,0:T(8,128)(2,1)S(1)}, u32[]{:S(2)}, u32[]{:S(2)}) collective-permute-start(bf16[48,5120]{1,0:T(8,128)(2,1)S(1)} %get-tuple-element.117), channel_id=1, source_target_pairs={{0,6},{1,7},{2,0},{3,1},{4,2},{5,3},{6,4},{7,5},{8,14},{9,15},{10,... | collective-permute-start | bytes 1474568 | tf_op jit(solution)/shard_map/ppermute | solution.py:27
  182.8 3.8 %collective-permute-start.36 = (bf16[96,5120]{1,0:T(8,128)(2,1)S(1)}, bf16[96,5120]{1,0:T(8,128)(2,1)S(1)}, u32[]{:S(2)}, u32[]{:S(2)}) collective-permute-start(bf16[96,5120]{1,0:T(8,128)(2,1)S(1)} %get-tuple-element.116), channel_id=1, source_target_pairs={{0,1},{1,0},{2,3},{3,2},{4,5},{5,4},{6,7},{7,6},{8,9},{9,8},{10,11... | collective-permute-start | bytes 2949128 | tf_op jit(solution)/shard_map/ppermute | solution.py:27
  183.8 24.5 %collective-permute-start.37 = (bf16[96,5120]{1,0:T(8,128)(2,1)S(1)}, bf16[96,5120]{1,0:T(8,128)(2,1)S(1)}, u32[]{:S(2)}, u32[]{:S(2)}) collective-permute-start(bf16[96,5120]{1,0:T(8,128)(2,1)S(1)} %add_convert_fusion.3), channel_id=1, source_target_pairs={{0,2},{1,3},{2,4},{3,5},{4,6},{5,7},{6,0},{7,1},{8,10},{9,11},{10,... | collective-permute-start | bytes 2949128 | tf_op jit(solution)/shard_map/ppermute | solution.py:27
  184.3 24.0 %collective-permute-start.38 = (bf16[96,5120]{1,0:T(8,128)(2,1)S(1)}, bf16[96,5120]{1,0:T(8,128)(2,1)S(1)}, u32[]{:S(2)}, u32[]{:S(2)}) collective-permute-start(bf16[96,5120]{1,0:T(8,128)(2,1)S(1)} %add_convert_fusion.2), channel_id=1, source_target_pairs={{0,6},{1,7},{2,0},{3,1},{4,2},{5,3},{6,4},{7,5},{8,14},{9,15},{10,... | collective-permute-start | bytes 2949128 | tf_op jit(solution)/shard_map/ppermute | solution.py:27
  186.5 24.2 %collective-permute-start.39 = (bf16[96,5120]{1,0:T(8,128)(2,1)S(1)}, bf16[96,5120]{1,0:T(8,128)(2,1)S(1)}, u32[]{:S(2)}, u32[]{:S(2)}) collective-permute-start(bf16[96,5120]{1,0:T(8,128)(2,1)S(1)} %add_convert_fusion.1), channel_id=1, source_target_pairs={{0,8},{1,9},{2,10},{3,11},{4,12},{5,13},{6,14},{7,15},{8,0},{9,1},... | collective-permute-start | bytes 2949128 | tf_op jit(solution)/shard_map/ppermute | solution.py:27

commit v3 on v2

--- a/solution.py
+++ b/solution.py
@@ -109,7 +109,7 @@
         if load:
             down, outs, (w, dn, x, proj, hid, out, sem) = refs[0], refs[1 : 1 + n_out], refs[1 + n_out :]
         else:
-            w, dn, outs, (x, proj, hid, out, sem) = refs[0], refs[1], refs[2 : 2 + n_out], refs[2 + n_out :]
+            w, dn, outs, (_, _, x, proj, hid, out, sem) = refs[0], refs[1], refs[2 : 2 + n_out], refs[2 + n_out :]
         at = 0
         tiles = [[] for _ in range(rows // tile)]
         for i, (src, start, n) in enumerate(row_map):
@@ -212,9 +212,10 @@
     kept = (pltpu.VMEM((blocks, depth, 2 * width), BF16), pltpu.VMEM((local_ff, depth), BF16))
     return pl.pallas_call(
         kernel,
-        out_shape=results + kept if load else results,
+        out_shape=results + kept,
         in_specs=[smem] * 3 + [anywhere] * (n_codes + n_rows) + ([anywhere] if load else [vmem, vmem]),
-        out_specs=(anywhere,) * n_out + ((vmem, vmem) if load else ()),
+        out_specs=(anywhere,) * n_out + (vmem, vmem),
+        input_output_aliases={} if load else {3 + n_rows: n_out, 4 + n_rows: n_out + 1},
         scratch_shapes=[
             pltpu.VMEM((rows, depth), BF16),
             pltpu.VMEM((slots, rows, width), F32),
@@ -306,6 +307,7 @@
     ids = after(ids, far_z, right, left)
     groups = halves(0) + [whole(tb, o_right), whole(ta, o_left), whole(tz, o_z)]
     part = sums(ids, groups, [count] * 4 + [h_rows] * 2 + [count] * 3, weights)
+    part, weights = part[:9], part[9:]
     far, near, here_z, near_sib, here_sib = part[0], part[1:3], part[3], part[6:8], part[8]
     got = swap(*part[4:6])
     far, got, far_in, z_right, z_left = after((far, got, far_in, z_right, z_left))
@@ -316,7 +318,7 @@
     near_sib, here_sib = after((near_sib, here_sib), top, low)
     got = swap(*near_sib, here_sib)
     ids = after(ids, top, low)
-    here, own_sib = sums(ids, [whole(tokens, o_own)], [count] * 2, weights)
+    here, own_sib = sums(ids, [whole(tokens, o_own)], [count] * 2, weights)[:2]
     near, got, past_top, past_low, here = after((near, got, past_top, past_low, here))
     zero = jnp.zeros((), BF16)
     past_top = lax.pad(past_top, zero, ((0, h_rows, 0), (0, 0, 0)))

time: 213 us -> 214 us (level)
  waiting for transfers between devices: 85.6 us -> 101 us
  Pallas kernels: 54.3 us -> 48.2 us
  starting transfers between devices: 52.4 us -> 48.2 us
  local copies, waits for them, and re-layouts: 7.25 us -> 3.81 us
    ppermute x40, waiting for transfers between devices: 85.6 us -> 101 us  [move(): return lax.ppermute(value, AXES, pairs)]
    pallas_call x2, Pallas kernels: 35.1 us -> 28.9 us  [sums(): return tuple(run(ids, sidx, scale_table, *pieces, *weights))]
    ppermute x40, starting transfers between devices: 52.4 us -> 48.2 us  [move(): return lax.ppermute(value, AXES, pairs)]
    unnamed x44 -> x40, local copies, waits for them, and re-layouts: 6.46 us -> 3.06 us
    convert_element_type x3, other arithmetic: 4.79 us -> 1.96 us  [body(): far_z, right, left = (add(part[i], got[i]).astype(BF16) for i in range(3))]
  transfers between devices with their start and end apart: 40 -> 40, of which waited for: 12 -> 17; matrix products, arithmetic and copies ran while one was open for 3% -> 1% of each run, Pallas kernels for 26% -> 23%
where the time goes in v3:
time: 214 us; the launch traced here: 213 us
  waiting for transfers between devices  101 us (47%)
  starting transfers between devices  48.2 us (23%)
  Pallas kernels  48.2 us (23%)
  other arithmetic  10.1 us (5%)
  local copies, waits for them, and re-layouts  3.81 us (2%)
    ppermute x40, waiting for transfers between devices, move(): return lax.ppermute(value, AXES, pairs)  101 us
    ppermute x40, starting transfers between devices, move(): return lax.ppermute(value, AXES, pairs)  48.2 us
    pallas_call x2, Pallas kernels, sums(): return tuple(run(ids, sidx, scale_table, *pieces, *weights))  28.9 us
    pallas_call x1, Pallas kernels, sums(): return tuple(run(ids, sidx, scale_table, *sources, *pieces, down_weight))  17 us
  transfers between devices with their start and end apart: 40, of which 17 were waited for; matrix products, arithmetic and copies ran while one was open for 1% of the time, Pallas kernels for 23%

profile of v3, /device:TPU:1, one launch (start us, length us, event | category | flops | bytes accessed | tf_op | source)
XLA Modules:
  0.0 213.1 jit_solution(7060591341658215789)
XLA Ops:
  0.0 4.4 %collective-permute-start.2 = (bf16[96,5120]{1,0:T(8,128)(2,1)}, bf16[96,5120]{1,0:T(8,128)(2,1)S(1)}, u32[]{:S(2)}, u32[]{:S(2)}) collective-permute-start(bf16[96,5120]{1,0:T(8,128)(2,1)} %refs_0_.1), channel_id=1, source_target_pairs={{0,8},{1,9},{2,10},{3,11},{4,12},{5,13},{6,14},{7,15},{8,0},{9,1},... | collective-permute-start | bytes 2949128 | tf_op jit(solution)/shard_map/ppermute | solution.py:27
  5.7 1.3 copy-done.1
  7.0 0.1 shard_map.64.refs_0_
  7.2 1.4 collective-permute-start
  8.6 2.5 %collective-permute-start.8 = (bf16[96,5120]{1,0:T(8,128)(2,1)S(1)}, bf16[96,5120]{1,0:T(8,128)(2,1)S(1)}, u32[]{:S(2)}, u32[]{:S(2)}) collective-permute-start(bf16[96,5120]{1,0:T(8,128)(2,1)S(1)} %copy-done.11), channel_id=1, source_target_pairs={{0,6},{1,7},{2,0},{3,1},{4,2},{5,3},{6,4},{7,5},{8,14},{9,15},{10,... | collective-permute-start | bytes 2949128 | tf_op jit(solution)/shard_map/ppermute | solution.py:27
  11.1 2.7 %collective-permute-start.1 = (bf16[5136,128]{1,0:T(8,128)(2,1)S(1)}, bf16[5136,128]{1,0:T(8,128)(2,1)S(1)}, u32[]{:S(2)}, u32[]{:S(2)}) collective-permute-start(bf16[5136,128]{1,0:T(8,128)(2,1)S(1)} %shard_map.64.refs_0_), channel_id=1, source_target_pairs={{0,96},{1,97},{2,98},{3,99},{4,100},{5,101},{6,102},{7,103},{8,104... | collective-permute-start | bytes 3944456 | tf_op jit(solution)/shard_map/ppermute | solution.py:27
  13.8 12.3 %collective-permute-done.2.refs_4_ = bf16[96,5120]{1,0:T(8,128)(2,1)S(1)} collective-permute-done((bf16[96,5120]{1,0:T(8,128)(2,1)}, bf16[96,5120]{1,0:T(8,128)(2,1)S(1)}, u32[]{:S(2)}, u32[]{:S(2)}) %collective-permute-start.2) | collective-permute-done | bytes 983072 | tf_op jit(solution)/shard_map/ppermute | solution.py:27
  26.1 0.7 collective-permute-start.3
  26.8 1.2 collective-permute-start.6
  28.0 10.0 %collective-permute-done.refs_1_ = bf16[5136,128]{1,0:T(8,128)(2,1)S(1)} collective-permute-done((bf16[5136,128]{1,0:T(8,128)(2,1)S(1)}, bf16[5136,128]{1,0:T(8,128)(2,1)S(1)}, u32[]{:S(2)}, u32[]{:S(2)}) %collective-permute-start) | collective-permute-done | bytes 1314848 | tf_op jit(solution)/shard_map/ppermute | solution.py:27
  38.0 2.5 %collective-permute-start.9 = (bf16[96,5120]{1,0:T(8,128)(2,1)S(1)}, bf16[96,5120]{1,0:T(8,128)(2,1)}, u32[]{:S(2)}, u32[]{:S(2)}) collective-permute-start(bf16[96,5120]{1,0:T(8,128)(2,1)S(1)} %collective-permute-done.2.refs_4_), channel_id=1, source_target_pairs={{0,6},{1,7},{2,0},{3,1},{4,2},{5,3},{6,4},{7,5},{8,14},{9,15},{10,... | collective-permute-start | bytes 2949128 | tf_op jit(solution)/shard_map/ppermute | solution.py:27
  40.7 0.5 collective-permute-start.4
  41.3 8.1 %collective-permute-done.6.refs_2_.refs_3_ = bf16[96,5120]{1,0:T(8,128)(2,1)S(1)} collective-permute-done((bf16[96,5120]{1,0:T(8,128)(2,1)S(1)}, bf16[96,5120]{1,0:T(8,128)(2,1)S(1)}, u32[]{:S(2)}, u32[]{:S(2)}) %collective-permute-start.6) | collective-permute-done | bytes 983072 | tf_op jit(solution)/shard_map/ppermute | solution.py:27
  49.4 2.7 %collective-permute-start.5 = (bf16[2560,128]{1,0:T(8,128)(2,1)S(1)}, bf16[2560,128]{1,0:T(8,128)(2,1)S(1)}, u32[]{:S(2)}, u32[]{:S(2)}) collective-permute-start(bf16[2560,128]{1,0:T(8,128)(2,1)S(1)} %slice.74), channel_id=1, source_target_pairs={{0,96},{1,97},{2,98},{3,99},{4,100},{5,101},{6,102},{7,103},{8,104... | collective-permute-start | bytes 1966088 | tf_op jit(solution)/shard_map/ppermute | solution.py:27
  52.2 3.2 %collective-permute-done.3.refs_3_ = bf16[5136,128]{1,0:T(8,128)(2,1)S(1)} collective-permute-done((bf16[5136,128]{1,0:T(8,128)(2,1)S(1)}, bf16[5136,128]{1,0:T(8,128)(2,1)S(1)}, u32[]{:S(2)}, u32[]{:S(2)}) %collective-permute-start.3) | collective-permute-done | bytes 1314848 | tf_op jit(solution)/shard_map/ppermute | solution.py:27
  55.4 2.7 %collective-permute-start.11 = (bf16[5136,128]{1,0:T(8,128)(2,1)S(1)}, bf16[5136,128]{1,0:T(8,128)(2,1)S(1)}, u32[]{:S(2)}, u32[]{:S(2)}) collective-permute-start(bf16[5136,128]{1,0:T(8,128)(2,1)S(1)} %collective-permute-done.3.refs_3_), channel_id=1, source_target_pairs={{0,96},{1,97},{2,98},{3,99},{4,100},{5,101},{6,102},{7,103},{8,104... | collective-permute-start | bytes 3944456 | tf_op jit(solution)/shard_map/ppermute | solution.py:27
  58.1 1.6 collective-permute-done.9.refs_5_.refs_10_
  59.7 10.9 %collective-permute-done.7.refs_3_.refs_11_ = bf16[96,5120]{1,0:T(8,128)(2,1)} collective-permute-done((bf16[96,5120]{1,0:T(8,128)(2,1)S(1)}, bf16[96,5120]{1,0:T(8,128)(2,1)}, u32[]{:S(2)}, u32[]{:S(2)}) %collective-permute-start.7) | collective-permute-done | bytes 983072 | tf_op jit(solution)/shard_map/ppermute | solution.py:27
  70.6 2.2 %shard_map.65 = (bf16[5136,128]{1,0:T(8,128)(2,1)S(1)}, bf16[96,5120]{1,0:T(8,128)(2,1)S(1)}, bf16[96,5120]{1,0:T(8,128)(2,1)S(1)}) custom-call(bf16[2576,128]{1,0:T(8,128)(2,1)S(1)} %collective-permute-done.4.refs_0_, bf16[2560,128]{1,0:T(8,128)(2,1)S(1)} %collective-permute-done.5.refs_1_, bf16[96,5120]{1,0:T(8,128)(2,1)S(1)} %collective-permute-done.6.refs_2_.refs_3_, ...), custom_call_target="tpu_custom_call" | custom-call | flops 1 | bytes 1 | tf_op jit(solution)/shard_map/pallas_call | solution.py:82
  72.9 2.7 %collective-permute-start.14 = (bf16[96,5120]{1,0:T(8,128)(2,1)S(1)}, bf16[96,5120]{1,0:T(8,128)(2,1)}, u32[]{:S(2)}, u32[]{:S(2)}) collective-permute-start(bf16[96,5120]{1,0:T(8,128)(2,1)S(1)} %get-tuple-element.69), channel_id=1, source_target_pairs={{0,6},{1,7},{2,0},{3,1},{4,2},{5,3},{6,4},{7,5},{8,14},{9,15},{10,... | collective-permute-start | bytes 2949128 | tf_op jit(solution)/shard_map/ppermute | solution.py:27
  75.6 1.1 collective-permute-start.12
  76.7 18.0 %collective-permute-done.13.refs_8_.refs_0_ = bf16[96,5120]{1,0:T(8,128)(2,1)} collective-permute-done((bf16[96,5120]{1,0:T(8,128)(2,1)S(1)}, bf16[96,5120]{1,0:T(8,128)(2,1)}, u32[]{:S(2)}, u32[]{:S(2)}) %collective-permute-start.13) | collective-permute-done | bytes 983072 | tf_op jit(solution)/shard_map/ppermute | solution.py:27
  94.7 3.7 %collective-permute-start.17 = (bf16[96,5120]{1,0:T(8,128)(2,1)}, bf16[96,5120]{1,0:T(8,128)(2,1)}, u32[]{:S(2)}, u32[]{:S(2)}) collective-permute-start(bf16[96,5120]{1,0:T(8,128)(2,1)} %collective-permute-done.9.refs_5_.refs_10_), channel_id=1, source_target_pairs={{0,1},{1,0},{2,3},{3,2},{4,5},{5,4},{6,7},{7,6},{8,9},{9,8},{10,11... | collective-permute-start | bytes 2949128 | tf_op jit(solution)/shard_map/ppermute | solution.py:27
  98.4 0.5 collective-permute-start.16
  98.9 0.2 collective-permute-start.18
  99.1 3.5 %collective-permute-done.12.refs_7_ = bf16[5136,128]{1,0:T(8,128)(2,1)S(1)} collective-permute-done((bf16[5136,128]{1,0:T(8,128)(2,1)S(1)}, bf16[5136,128]{1,0:T(8,128)(2,1)S(1)}, u32[]{:S(2)}, u32[]{:S(2)}) %collective-permute-start.12) | collective-permute-done | bytes 1314848 | tf_op jit(solution)/shard_map/ppermute | solution.py:27
  102.6 1.1 copy-done.17
  103.8 4.3 %collective-permute-start.19 = (bf16[96,5120]{1,0:T(8,128)(2,1)S(1)}, bf16[96,5120]{1,0:T(8,128)(2,1)}, u32[]{:S(2)}, u32[]{:S(2)}) collective-permute-start(bf16[96,5120]{1,0:T(8,128)(2,1)S(1)} %collective-permute-done.8.refs_4_.refs_2_), channel_id=1, source_target_pairs={{0,1},{1,0},{2,3},{3,2},{4,5},{5,4},{6,7},{7,6},{8,9},{9,8},{10,11... | collective-permute-start | bytes 2949128 | tf_op jit(solution)/shard_map/ppermute | solution.py:27
  108.2 0.4 collective-permute-start.21
  108.7 0.5 slice_bitcast_fusion.7
  109.3 17.0 %shard_map.66 = (bf16[96,5120]{1,0:T(8,128)(2,1)}, bf16[96,5120]{1,0:T(8,128)(2,1)}, bf16[96,5120]{1,0:T(8,128)(2,1)}, bf16[96,5120]{1,0:T(8,128)(2,1)}, bf16[96...) custom-call(s32[8]{0:T(128)} %get-tuple-element.104.ids, ...), custom_call_target="tpu_custom_call" | custom-call | flops 9059696640 | bytes 27525120 | tf_op jit(solution)/shard_map/pallas_call | solution.py:279
  126.3 0.5 collective-permute-start.23
  126.9 0.4 collective-permute-start.25
  127.3 1.9 collective-permute-done.23
  129.2 1.5 add_convert_fusion.6
  130.7 3.4 %collective-permute-start.28 = (bf16[96,5120]{1,0:T(8,128)(2,1)S(1)}, bf16[96,5120]{1,0:T(8,128)(2,1)}, u32[]{:S(2)}, u32[]{:S(2)}) collective-permute-start(bf16[96,5120]{1,0:T(8,128)(2,1)S(1)} %add_convert_fusion.6), channel_id=1, source_target_pairs={{0,8},{1,9},{2,10},{3,11},{4,12},{5,13},{6,14},{7,15},{8,0},{9,1},... | collective-permute-start | bytes 2949128 | tf_op jit(solution)/shard_map/ppermute | solution.py:27
  134.1 0.3 add_convert_fusion.5
  134.3 0.3 collective-permute-start.29
  134.6 0.3 add_convert_fusion.4
  134.9 2.7 %collective-permute-start.30 = (bf16[96,5120]{1,0:T(8,128)(2,1)S(1)}, bf16[96,5120]{1,0:T(8,128)(2,1)S(1)}, u32[]{:S(2)}, u32[]{:S(2)}) collective-permute-start(bf16[96,5120]{1,0:T(8,128)(2,1)S(1)} %add_convert_fusion.4), channel_id=1, source_target_pairs={{0,6},{1,7},{2,0},{3,1},{4,2},{5,3},{6,4},{7,5},{8,14},{9,15},{10,... | collective-permute-start | bytes 2949128 | tf_op jit(solution)/shard_map/ppermute | solution.py:27
  137.6 20.1 %shard_map.67 = (bf16[96,5120]{1,0:T(8,128)(2,1)}, bf16[96,5120]{1,0:T(8,128)(2,1)}, bf16[96,5120]{1,0:T(8,128)(2,1)}, bf16[96,5120]{1,0:T(8,128)(2,1)}, bf16[48...) custom-call(s32[8]{0:T(128)} %get-tuple-element.104.ids, ...), custom_call_target="tpu_custom_call", output_to_operand_aliasing={{9}: (13, {}), {10}: (14, {})} | custom-call | flops 12079595520 | bytes 31457280 | tf_op jit(solution)/shard_map/pallas_call | solution.py:280
  157.7 1.3 collective-permute-start.26
  159.1 1.6 collective-permute-done.26
  160.7 0.7 collective-permute-done.27
  161.4 2.8 %add_convert_fusion.7 = (bf16[48,5120]{1,0:T(8,128)(2,1)}, bf16[48,5120]{1,0:T(8,128)(2,1)}) fusion(bf16[48,5120]{1,0:T(8,128)(2,1)S(1)} %collective-permute-done.27, bf16[96,5120]{1,0:T(8,128)(2,1)} %collective-permute-done.28, bf16[96,5120]{1,0:T(8,128)(2,1)} %get-tuple-element.97, bf16[48,5120]{1,0:T(8,128)(2,1)S(1)} %collective-permute-done.26), kind=kLoop, calls=%fused_computation.7 | loop fusion | flops 2949120 | bytes 3932160 | tf_op jit(solution)/shard_map/convert_element_type | solution.py:315
  164.2 0.4 collective-permute-start.31
  164.6 0.1 collective-permute-start.32
  164.8 0.4 collective-permute-start.33
  165.1 1.1 collective-permute-start.35
  166.3 0.3 collective-permute-start.34
  166.6 8.8 %shard_map.68 = (bf16[96,5120]{1,0:T(8,128)(2,1)}, bf16[96,5120]{1,0:T(8,128)(2,1)}, bf16[4,5120,256]{2,1,0:T(8,128)(2,1)S(1)}, bf16[512,5120]{1,0:T(8,128)(2,1)S(1)}) custom-call(s32[8]{0:T(128)} %get-tuple-element.104.ids, s32[8]{0:T(128)} %get-tuple-element.123.sidx, f32[64]{0:T(128)} %table.5, ...), custom_call_target="tpu_custom_call", output_to_operand_aliasing={{2}: (5, {}), {3}: (6, {})} | custom-call | flops 3019898880 | bytes 19660800 | tf_op jit(solution)/shard_map/pallas_call | solution.py:280
  175.4 2.7 %collective-permute-done.35 = bf16[48,5120]{1,0:T(8,128)(2,1)} collective-permute-done((bf16[48,5120]{1,0:T(8,128)(2,1)}, bf16[48,5120]{1,0:T(8,128)(2,1)}, u32[]{:S(2)}, u32[]{:S(2)}) %collective-permute-start.35) | collective-permute-done | bytes 491552 | tf_op jit(solution)/shard_map/ppermute | solution.py:27
  178.1 2.2 %collective-permute-done.34 = bf16[48,5120]{1,0:T(8,128)(2,1)} collective-permute-done((bf16[48,5120]{1,0:T(8,128)(2,1)}, bf16[48,5120]{1,0:T(8,128)(2,1)}, u32[]{:S(2)}, u32[]{:S(2)}) %collective-permute-start.34) | collective-permute-done | bytes 491552 | tf_op jit(solution)/shard_map/ppermute | solution.py:27
  180.3 1.3 add_convert_fusion.3
  181.7 1.7 add_convert_fusion.2
  183.4 0.6 add_convert_fusion.1
  184.0 0.6 copy-done.19
  184.6 1.1 collective-permute-start.36
  185.7 1.5 collective-permute-start.37
  187.2 0.7 collective-permute-done.36
  187.9 21.2 %collective-permute-done.38 = bf16[96,5120]{1,0:T(8,128)(2,1)S(1)} collective-permute-done((bf16[96,5120]{1,0:T(8,128)(2,1)S(1)}, bf16[96,5120]{1,0:T(8,128)(2,1)S(1)}, u32[]{:S(2)}, u32[]{:S(2)}) %collective-permute-start.38) | collective-permute-done | bytes 983072 | tf_op jit(solution)/shard_map/ppermute | solution.py:27
  209.1 0.9 collective-permute-done.37
  210.0 1.4 collective-permute-done.39
  211.4 1.7 add_convert_fusion
  (84 shorter events, 1.1 us)
Async XLA Ops:
  0.0 26.1 %collective-permute-start.2 = (bf16[96,5120]{1,0:T(8,128)(2,1)}, bf16[96,5120]{1,0:T(8,128)(2,1)S(1)}, u32[]{:S(2)}, u32[]{:S(2)}) collective-permute-start(bf16[96,5120]{1,0:T(8,128)(2,1)} %refs_0_.1), channel_id=1, source_target_pairs={{0,8},{1,9},{2,10},{3,11},{4,12},{5,13},{6,14},{7,15},{8,0},{9,1},... | collective-permute-start | bytes 2949128 | tf_op jit(solution)/shard_map/ppermute | solution.py:27
  5.7 1.3 copy-start.1
  7.0 1.6 copy-start.11
  7.2 68.4 %copy-start = (bf16[5136,128]{1,0:T(8,128)(2,1)}, bf16[5136,128]{1,0:T(8,128)(2,1)S(1)}, u32[]{:S(2)}) copy-start(bf16[5136,128]{1,0:T(8,128)(2,1)S(1)} %shard_map.64.refs_0_) | copy-start | bytes 3944452
  7.2 30.8 %collective-permute-start = (bf16[5136,128]{1,0:T(8,128)(2,1)S(1)}, bf16[5136,128]{1,0:T(8,128)(2,1)S(1)}, u32[]{:S(2)}, u32[]{:S(2)}) collective-permute-start(bf16[5136,128]{1,0:T(8,128)(2,1)S(1)} %shard_map.64.refs_0_), channel_id=1, source_target_pairs={{0,32},{1,33},{2,34},{3,35},{4,36},{5,37},{6,38},{7,39},{8,40},{9,... | collective-permute-start | bytes 3944456 | tf_op jit(solution)/shard_map/ppermute | solution.py:27
  8.6 31.9 %collective-permute-start.8 = (bf16[96,5120]{1,0:T(8,128)(2,1)S(1)}, bf16[96,5120]{1,0:T(8,128)(2,1)S(1)}, u32[]{:S(2)}, u32[]{:S(2)}) collective-permute-start(bf16[96,5120]{1,0:T(8,128)(2,1)S(1)} %copy-done.11), channel_id=1, source_target_pairs={{0,6},{1,7},{2,0},{3,1},{4,2},{5,3},{6,4},{7,5},{8,14},{9,15},{10,... | collective-permute-start | bytes 2949128 | tf_op jit(solution)/shard_map/ppermute | solution.py:27
  11.1 29.7 %collective-permute-start.1 = (bf16[5136,128]{1,0:T(8,128)(2,1)S(1)}, bf16[5136,128]{1,0:T(8,128)(2,1)S(1)}, u32[]{:S(2)}, u32[]{:S(2)}) collective-permute-start(bf16[5136,128]{1,0:T(8,128)(2,1)S(1)} %shard_map.64.refs_0_), channel_id=1, source_target_pairs={{0,96},{1,97},{2,98},{3,99},{4,100},{5,101},{6,102},{7,103},{8,104... | collective-permute-start | bytes 3944456 | tf_op jit(solution)/shard_map/ppermute | solution.py:27
  26.1 15.2 %copy-start.18 = (bf16[96,5120]{1,0:T(8,128)(2,1)}, bf16[96,5120]{1,0:T(8,128)(2,1)S(1)}, u32[]{:S(2)}) copy-start(bf16[96,5120]{1,0:T(8,128)(2,1)S(1)} %collective-permute-done.2.refs_4_) | copy-start | bytes 2949124
  26.1 29.2 %collective-permute-start.3 = (bf16[5136,128]{1,0:T(8,128)(2,1)S(1)}, bf16[5136,128]{1,0:T(8,128)(2,1)S(1)}, u32[]{:S(2)}, u32[]{:S(2)}) collective-permute-start(bf16[5136,128]{1,0:T(8,128)(2,1)S(1)} %shard_map.64.refs_0_), channel_id=1, source_target_pairs={{0,16},{1,17},{2,18},{3,19},{4,20},{5,21},{6,22},{7,23},{8,24},{9,... | collective-permute-start | bytes 3944456 | tf_op jit(solution)/shard_map/ppermute | solution.py:27
  26.8 22.6 %collective-permute-start.6 = (bf16[96,5120]{1,0:T(8,128)(2,1)S(1)}, bf16[96,5120]{1,0:T(8,128)(2,1)S(1)}, u32[]{:S(2)}, u32[]{:S(2)}) collective-permute-start(bf16[96,5120]{1,0:T(8,128)(2,1)S(1)} %copy-done.11), channel_id=1, source_target_pairs={{0,2},{1,3},{2,4},{3,5},{4,6},{5,7},{6,0},{7,1},{8,10},{9,11},{10,... | collective-permute-start | bytes 2949128 | tf_op jit(solution)/shard_map/ppermute | solution.py:27
  38.0 38.6 %copy-start.12 = (bf16[5136,128]{1,0:T(8,128)(2,1)}, bf16[5136,128]{1,0:T(8,128)(2,1)S(1)}, u32[]{:S(2)}) copy-start(bf16[5136,128]{1,0:T(8,128)(2,1)S(1)} %collective-permute-done.refs_1_) | copy-start | bytes 3944452
  38.0 21.7 %collective-permute-start.9 = (bf16[96,5120]{1,0:T(8,128)(2,1)S(1)}, bf16[96,5120]{1,0:T(8,128)(2,1)}, u32[]{:S(2)}, u32[]{:S(2)}) collective-permute-start(bf16[96,5120]{1,0:T(8,128)(2,1)S(1)} %collective-permute-done.2.refs_4_), channel_id=1, source_target_pairs={{0,6},{1,7},{2,0},{3,1},{4,2},{5,3},{6,4},{7,5},{8,14},{9,15},{10,... | collective-permute-start | bytes 2949128 | tf_op jit(solution)/shard_map/ppermute | solution.py:27
  40.5 63.2 %copy-start.2 = (bf16[96,5120]{1,0:T(8,128)(2,1)}, bf16[96,5120]{1,0:T(8,128)(2,1)S(1)}, u32[]{:S(2)}) copy-start(bf16[96,5120]{1,0:T(8,128)(2,1)S(1)} %collective-permute-done.8.refs_4_.refs_2_) | copy-start | bytes 2949124
  40.6 30.1 %collective-permute-start.7 = (bf16[96,5120]{1,0:T(8,128)(2,1)S(1)}, bf16[96,5120]{1,0:T(8,128)(2,1)}, u32[]{:S(2)}, u32[]{:S(2)}) collective-permute-start(bf16[96,5120]{1,0:T(8,128)(2,1)S(1)} %collective-permute-done.2.refs_4_), channel_id=1, source_target_pairs={{0,2},{1,3},{2,4},{3,5},{4,6},{5,7},{6,0},{7,1},{8,10},{9,11},{10,... | collective-permute-start | bytes 2949128 | tf_op jit(solution)/shard_map/ppermute | solution.py:27
  40.7 35.9 %copy-start.13 = (bf16[5136,128]{1,0:T(8,128)(2,1)}, bf16[5136,128]{1,0:T(8,128)(2,1)S(1)}, u32[]{:S(2)}) copy-start(bf16[5136,128]{1,0:T(8,128)(2,1)S(1)} %collective-permute-done.1.refs_2_) | copy-start | bytes 3944452
  40.7 29.9 %collective-permute-start.4 = (bf16[2576,128]{1,0:T(8,128)(2,1)S(1)}, bf16[2576,128]{1,0:T(8,128)(2,1)S(1)}, u32[]{:S(2)}, u32[]{:S(2)}) collective-permute-start(bf16[2576,128]{1,0:T(8,128)(2,1)S(1)} %pad_maximum_fusion), channel_id=1, source_target_pairs={{0,32},{1,33},{2,34},{3,35},{4,36},{5,37},{6,38},{7,39},{8,40},{9,... | collective-permute-start | bytes 1978376 | tf_op jit(solution)/shard_map/ppermute | solution.py:27
  49.4 58.7 %copy-start.3 = (bf16[96,5120]{1,0:T(8,128)(2,1)}, bf16[96,5120]{1,0:T(8,128)(2,1)S(1)}, u32[]{:S(2)}) copy-start(bf16[96,5120]{1,0:T(8,128)(2,1)S(1)} %collective-permute-done.6.refs_2_.refs_3_) | copy-start | bytes 2949124
  49.4 21.2 %collective-permute-start.5 = (bf16[2560,128]{1,0:T(8,128)(2,1)S(1)}, bf16[2560,128]{1,0:T(8,128)(2,1)S(1)}, u32[]{:S(2)}, u32[]{:S(2)}) collective-permute-start(bf16[2560,128]{1,0:T(8,128)(2,1)S(1)} %slice.74), channel_id=1, source_target_pairs={{0,96},{1,97},{2,98},{3,99},{4,100},{5,101},{6,102},{7,103},{8,104... | collective-permute-start | bytes 1966088 | tf_op jit(solution)/shard_map/ppermute | solution.py:27
  55.4 43.7 %copy-start.14 = (bf16[5136,128]{1,0:T(8,128)(2,1)}, bf16[5136,128]{1,0:T(8,128)(2,1)S(1)}, u32[]{:S(2)}) copy-start(bf16[5136,128]{1,0:T(8,128)(2,1)S(1)} %collective-permute-done.3.refs_3_) | copy-start | bytes 3944452
  55.4 43.0 %collective-permute-start.11 = (bf16[5136,128]{1,0:T(8,128)(2,1)S(1)}, bf16[5136,128]{1,0:T(8,128)(2,1)S(1)}, u32[]{:S(2)}, u32[]{:S(2)}) collective-permute-start(bf16[5136,128]{1,0:T(8,128)(2,1)S(1)} %collective-permute-done.3.refs_3_), channel_id=1, source_target_pairs={{0,96},{1,97},{2,98},{3,99},{4,100},{5,101},{6,102},{7,103},{8,104... | collective-permute-start | bytes 3944456 | tf_op jit(solution)/shard_map/ppermute | solution.py:27
  59.7 39.1 %collective-permute-start.10 = (bf16[5136,128]{1,0:T(8,128)(2,1)S(1)}, bf16[5136,128]{1,0:T(8,128)(2,1)S(1)}, u32[]{:S(2)}, u32[]{:S(2)}) collective-permute-start(bf16[5136,128]{1,0:T(8,128)(2,1)S(1)} %collective-permute-done.3.refs_3_), channel_id=1, source_target_pairs={{0,32},{1,33},{2,34},{3,35},{4,36},{5,37},{6,38},{7,39},{8,40},{9,... | collective-permute-start | bytes 3944456 | tf_op jit(solution)/shard_map/ppermute | solution.py:27
  72.8 26.1 %copy-start.4 = (bf16[5136,128]{1,0:T(8,128)(2,1)}, bf16[5136,128]{1,0:T(8,128)(2,1)S(1)}, u32[]{:S(2)}) copy-start(bf16[5136,128]{1,0:T(8,128)(2,1)S(1)} %get-tuple-element.67.refs_4_) | copy-start | bytes 3944452
  72.8 21.9 %collective-permute-start.13 = (bf16[96,5120]{1,0:T(8,128)(2,1)S(1)}, bf16[96,5120]{1,0:T(8,128)(2,1)}, u32[]{:S(2)}, u32[]{:S(2)}) collective-permute-start(bf16[96,5120]{1,0:T(8,128)(2,1)S(1)} %get-tuple-element.68), channel_id=1, source_target_pairs={{0,2},{1,3},{2,4},{3,5},{4,6},{5,7},{6,0},{7,1},{8,10},{9,11},{10,... | collective-permute-start | bytes 2949128 | tf_op jit(solution)/shard_map/ppermute | solution.py:27
  72.9 25.5 %collective-permute-start.14 = (bf16[96,5120]{1,0:T(8,128)(2,1)S(1)}, bf16[96,5120]{1,0:T(8,128)(2,1)}, u32[]{:S(2)}, u32[]{:S(2)}) collective-permute-start(bf16[96,5120]{1,0:T(8,128)(2,1)S(1)} %get-tuple-element.69), channel_id=1, source_target_pairs={{0,6},{1,7},{2,0},{3,1},{4,2},{5,3},{6,4},{7,5},{8,14},{9,15},{10,... | collective-permute-start | bytes 2949128 | tf_op jit(solution)/shard_map/ppermute | solution.py:27
  75.6 27.1 %collective-permute-start.12 = (bf16[5136,128]{1,0:T(8,128)(2,1)S(1)}, bf16[5136,128]{1,0:T(8,128)(2,1)S(1)}, u32[]{:S(2)}, u32[]{:S(2)}) collective-permute-start(bf16[5136,128]{1,0:T(8,128)(2,1)S(1)} %get-tuple-element.67.refs_4_), channel_id=1, source_target_pairs={{0,16},{1,17},{2,18},{3,19},{4,20},{5,21},{6,22},{7,23},{8,24},{9,... | collective-permute-start | bytes 3944456 | tf_op jit(solution)/shard_map/ppermute | solution.py:27
  94.7 13.9 %collective-permute-start.17 = (bf16[96,5120]{1,0:T(8,128)(2,1)}, bf16[96,5120]{1,0:T(8,128)(2,1)}, u32[]{:S(2)}, u32[]{:S(2)}) collective-permute-start(bf16[96,5120]{1,0:T(8,128)(2,1)} %collective-permute-done.9.refs_5_.refs_10_), channel_id=1, source_target_pairs={{0,1},{1,0},{2,3},{3,2},{4,5},{5,4},{6,7},{7,6},{8,9},{9,8},{10,11... | collective-permute-start | bytes 2949128 | tf_op jit(solution)/shard_map/ppermute | solution.py:27
  98.4 5.4 %collective-permute-start.15 = (bf16[96,5120]{1,0:T(8,128)(2,1)}, bf16[96,5120]{1,0:T(8,128)(2,1)}, u32[]{:S(2)}, u32[]{:S(2)}) collective-permute-start(bf16[96,5120]{1,0:T(8,128)(2,1)} %collective-permute-done.13.refs_8_.refs_0_), channel_id=1, source_target_pairs={{0,1},{1,0},{2,3},{3,2},{4,5},{5,4},{6,7},{7,6},{8,9},{9,8},{10,11... | collective-permute-start | bytes 2949128 | tf_op jit(solution)/shard_map/ppermute | solution.py:27
  98.4 4.2 %copy-start.15 = (bf16[5136,128]{1,0:T(8,128)(2,1)}, bf16[5136,128]{1,0:T(8,128)(2,1)S(1)}, u32[]{:S(2)}) copy-start(bf16[5136,128]{1,0:T(8,128)(2,1)S(1)} %collective-permute-done.11.refs_6_) | copy-start | bytes 3944452
  98.4 5.4 %collective-permute-start.16 = (bf16[96,5120]{1,0:T(8,128)(2,1)}, bf16[96,5120]{1,0:T(8,128)(2,1)}, u32[]{:S(2)}, u32[]{:S(2)}) collective-permute-start(bf16[96,5120]{1,0:T(8,128)(2,1)} %collective-permute-done.14.refs_9_.refs_1_), channel_id=1, source_target_pairs={{0,1},{1,0},{2,3},{3,2},{4,5},{5,4},{6,7},{7,6},{8,9},{9,8},{10,11... | collective-permute-start | bytes 2949128 | tf_op jit(solution)/shard_map/ppermute | solution.py:27
  98.9 3.7 %copy-start.16 = (bf16[5136,128]{1,0:T(8,128)(2,1)}, bf16[5136,128]{1,0:T(8,128)(2,1)S(1)}, u32[]{:S(2)}) copy-start(bf16[5136,128]{1,0:T(8,128)(2,1)S(1)} %collective-permute-done.10.refs_5_) | copy-start | bytes 3944452
  98.9 10.4 %collective-permute-start.18 = (bf16[96,5120]{1,0:T(8,128)(2,1)}, bf16[96,5120]{1,0:T(8,128)(2,1)}, u32[]{:S(2)}, u32[]{:S(2)}) collective-permute-start(bf16[96,5120]{1,0:T(8,128)(2,1)} %collective-permute-done.7.refs_3_.refs_11_), channel_id=1, source_target_pairs={{0,1},{1,0},{2,3},{3,2},{4,5},{5,4},{6,7},{7,6},{8,9},{9,8},{10,11... | collective-permute-start | bytes 2949128 | tf_op jit(solution)/shard_map/ppermute | solution.py:27
  102.6 1.1 copy-start.17
  103.8 22.5 %collective-permute-start.19 = (bf16[96,5120]{1,0:T(8,128)(2,1)S(1)}, bf16[96,5120]{1,0:T(8,128)(2,1)}, u32[]{:S(2)}, u32[]{:S(2)}) collective-permute-start(bf16[96,5120]{1,0:T(8,128)(2,1)S(1)} %collective-permute-done.8.refs_4_.refs_2_), channel_id=1, source_target_pairs={{0,1},{1,0},{2,3},{3,2},{4,5},{5,4},{6,7},{7,6},{8,9},{9,8},{10,11... | collective-permute-start | bytes 2949128 | tf_op jit(solution)/shard_map/ppermute | solution.py:27
  108.1 18.2 %collective-permute-start.20 = (bf16[96,5120]{1,0:T(8,128)(2,1)S(1)}, bf16[96,5120]{1,0:T(8,128)(2,1)}, u32[]{:S(2)}, u32[]{:S(2)}) collective-permute-start(bf16[96,5120]{1,0:T(8,128)(2,1)S(1)} %collective-permute-done.6.refs_2_.refs_3_), channel_id=1, source_target_pairs={{0,1},{1,0},{2,3},{3,2},{4,5},{5,4},{6,7},{7,6},{8,9},{9,8},{10,11... | collective-permute-start | bytes 2949128 | tf_op jit(solution)/shard_map/ppermute | solution.py:27
  108.2 18.1 %collective-permute-start.21 = (bf16[96,5120]{1,0:T(8,128)(2,1)}, bf16[96,5120]{1,0:T(8,128)(2,1)}, u32[]{:S(2)}, u32[]{:S(2)}) collective-permute-start(bf16[96,5120]{1,0:T(8,128)(2,1)} %copy-done.18), channel_id=1, source_target_pairs={{0,1},{1,0},{2,3},{3,2},{4,5},{5,4},{6,7},{7,6},{8,9},{9,8},{10,11... | collective-permute-start | bytes 2949128 | tf_op jit(solution)/shard_map/ppermute | solution.py:27
  108.6 17.7 %collective-permute-start.22 = (bf16[96,5120]{1,0:T(8,128)(2,1)S(1)}, bf16[96,5120]{1,0:T(8,128)(2,1)}, u32[]{:S(2)}, u32[]{:S(2)}) collective-permute-start(bf16[96,5120]{1,0:T(8,128)(2,1)S(1)} %copy-done.11), channel_id=1, source_target_pairs={{0,1},{1,0},{2,3},{3,2},{4,5},{5,4},{6,7},{7,6},{8,9},{9,8},{10,11... | collective-permute-start | bytes 2949128 | tf_op jit(solution)/shard_map/ppermute | solution.py:27
  126.2 7.8 %copy-start.8 = (bf16[96,5120]{1,0:T(8,128)(2,1)S(1)}, bf16[96,5120]{1,0:T(8,128)(2,1)}, u32[]{:S(2)}) copy-start(bf16[96,5120]{1,0:T(8,128)(2,1)} %get-tuple-element.82) | copy-start | bytes 2949124
  126.3 2.9 %collective-permute-start.23 = (bf16[96,5120]{1,0:T(8,128)(2,1)}, bf16[96,5120]{1,0:T(8,128)(2,1)S(1)}, u32[]{:S(2)}, u32[]{:S(2)}) collective-permute-start(bf16[96,5120]{1,0:T(8,128)(2,1)} %get-tuple-element.81), channel_id=1, source_target_pairs={{0,1},{1,0},{2,3},{3,2},{4,5},{5,4},{6,7},{7,6},{8,9},{9,8},{10,11... | collective-permute-start | bytes 2949128 | tf_op jit(solution)/shard_map/ppermute | solution.py:27
  126.8 7.3 %collective-permute-start.24 = (bf16[96,5120]{1,0:T(8,128)(2,1)}, bf16[96,5120]{1,0:T(8,128)(2,1)S(1)}, u32[]{:S(2)}, u32[]{:S(2)}) collective-permute-start(bf16[96,5120]{1,0:T(8,128)(2,1)} %get-tuple-element.83), channel_id=1, source_target_pairs={{0,1},{1,0},{2,3},{3,2},{4,5},{5,4},{6,7},{7,6},{8,9},{9,8},{10,11... | collective-permute-start | bytes 2949128 | tf_op jit(solution)/shard_map/ppermute | solution.py:27
  126.9 7.7 %collective-permute-start.25 = (bf16[96,5120]{1,0:T(8,128)(2,1)}, bf16[96,5120]{1,0:T(8,128)(2,1)S(1)}, u32[]{:S(2)}, u32[]{:S(2)}) collective-permute-start(bf16[96,5120]{1,0:T(8,128)(2,1)} %get-tuple-element.85), channel_id=1, source_target_pairs={{0,1},{1,0},{2,3},{3,2},{4,5},{5,4},{6,7},{7,6},{8,9},{9,8},{10,11... | collective-permute-start | bytes 2949128 | tf_op jit(solution)/shard_map/ppermute | solution.py:27
  130.7 3.9 %copy-start.7 = (bf16[96,5120]{1,0:T(8,128)(2,1)S(1)}, bf16[96,5120]{1,0:T(8,128)(2,1)}, u32[]{:S(2)}) copy-start(bf16[96,5120]{1,0:T(8,128)(2,1)} %get-tuple-element.84) | copy-start | bytes 2949124
  130.7 30.8 %collective-permute-start.28 = (bf16[96,5120]{1,0:T(8,128)(2,1)S(1)}, bf16[96,5120]{1,0:T(8,128)(2,1)}, u32[]{:S(2)}, u32[]{:S(2)}) collective-permute-start(bf16[96,5120]{1,0:T(8,128)(2,1)S(1)} %add_convert_fusion.6), channel_id=1, source_target_pairs={{0,8},{1,9},{2,10},{3,11},{4,12},{5,13},{6,14},{7,15},{8,0},{9,1},... | collective-permute-start | bytes 2949128 | tf_op jit(solution)/shard_map/ppermute | solution.py:27
  134.3 27.1 %collective-permute-start.29 = (bf16[96,5120]{1,0:T(8,128)(2,1)S(1)}, bf16[96,5120]{1,0:T(8,128)(2,1)S(1)}, u32[]{:S(2)}, u32[]{:S(2)}) collective-permute-start(bf16[96,5120]{1,0:T(8,128)(2,1)S(1)} %add_convert_fusion.5), channel_id=1, source_target_pairs={{0,2},{1,3},{2,4},{3,5},{4,6},{5,7},{6,0},{7,1},{8,10},{9,11},{10,... | collective-permute-start | bytes 2949128 | tf_op jit(solution)/shard_map/ppermute | solution.py:27
  134.9 26.6 %collective-permute-start.30 = (bf16[96,5120]{1,0:T(8,128)(2,1)S(1)}, bf16[96,5120]{1,0:T(8,128)(2,1)S(1)}, u32[]{:S(2)}, u32[]{:S(2)}) collective-permute-start(bf16[96,5120]{1,0:T(8,128)(2,1)S(1)} %add_convert_fusion.4), channel_id=1, source_target_pairs={{0,6},{1,7},{2,0},{3,1},{4,2},{5,3},{6,4},{7,5},{8,14},{9,15},{10,... | collective-permute-start | bytes 2949128 | tf_op jit(solution)/shard_map/ppermute | solution.py:27
  157.7 3.0 %collective-permute-start.26 = (bf16[48,5120]{1,0:T(8,128)(2,1)}, bf16[48,5120]{1,0:T(8,128)(2,1)S(1)}, u32[]{:S(2)}, u32[]{:S(2)}) collective-permute-start(bf16[48,5120]{1,0:T(8,128)(2,1)} %get-tuple-element.95), channel_id=1, source_target_pairs={{0,1},{1,0},{2,3},{3,2},{4,5},{5,4},{6,7},{7,6},{8,9},{9,8},{10,11... | collective-permute-start | bytes 1474568 | tf_op jit(solution)/shard_map/ppermute | solution.py:27
  159.0 2.4 %collective-permute-start.27 = (bf16[48,5120]{1,0:T(8,128)(2,1)}, bf16[48,5120]{1,0:T(8,128)(2,1)S(1)}, u32[]{:S(2)}, u32[]{:S(2)}) collective-permute-start(bf16[48,5120]{1,0:T(8,128)(2,1)} %get-tuple-element.96), channel_id=1, source_target_pairs={{0,1},{1,0},{2,3},{3,2},{4,5},{5,4},{6,7},{7,6},{8,9},{9,8},{10,11... | collective-permute-start | bytes 1474568 | tf_op jit(solution)/shard_map/ppermute | solution.py:27
  164.2 16.1 %collective-permute-start.31 = (bf16[96,5120]{1,0:T(8,128)(2,1)}, bf16[96,5120]{1,0:T(8,128)(2,1)S(1)}, u32[]{:S(2)}, u32[]{:S(2)}) collective-permute-start(bf16[96,5120]{1,0:T(8,128)(2,1)} %get-tuple-element.101), channel_id=1, source_target_pairs={{0,1},{1,0},{2,3},{3,2},{4,5},{5,4},{6,7},{7,6},{8,9},{9,8},{10,11... | collective-permute-start | bytes 2949128 | tf_op jit(solution)/shard_map/ppermute | solution.py:27
  164.6 15.7 %collective-permute-start.32 = (bf16[96,5120]{1,0:T(8,128)(2,1)}, bf16[96,5120]{1,0:T(8,128)(2,1)}, u32[]{:S(2)}, u32[]{:S(2)}) collective-permute-start(bf16[96,5120]{1,0:T(8,128)(2,1)} %get-tuple-element.102), channel_id=1, source_target_pairs={{0,1},{1,0},{2,3},{3,2},{4,5},{5,4},{6,7},{7,6},{8,9},{9,8},{10,11... | collective-permute-start | bytes 2949128 | tf_op jit(solution)/shard_map/ppermute | solution.py:27
  164.8 15.6 %collective-permute-start.33 = (bf16[96,5120]{1,0:T(8,128)(2,1)}, bf16[96,5120]{1,0:T(8,128)(2,1)S(1)}, u32[]{:S(2)}, u32[]{:S(2)}) collective-permute-start(bf16[96,5120]{1,0:T(8,128)(2,1)} %get-tuple-element.103), channel_id=1, source_target_pairs={{0,1},{1,0},{2,3},{3,2},{4,5},{5,4},{6,7},{7,6},{8,9},{9,8},{10,11... | collective-permute-start | bytes 2949128 | tf_op jit(solution)/shard_map/ppermute | solution.py:27
  165.1 13.0 %collective-permute-start.35 = (bf16[48,5120]{1,0:T(8,128)(2,1)}, bf16[48,5120]{1,0:T(8,128)(2,1)}, u32[]{:S(2)}, u32[]{:S(2)}) collective-permute-start(bf16[48,5120]{1,0:T(8,128)(2,1)} %get-tuple-element.121), channel_id=1, source_target_pairs={{0,6},{1,7},{2,0},{3,1},{4,2},{5,3},{6,4},{7,5},{8,14},{9,15},{10,... | collective-permute-start | bytes 1474568 | tf_op jit(solution)/shard_map/ppermute | solution.py:27
  166.3 14.1 %collective-permute-start.34 = (bf16[48,5120]{1,0:T(8,128)(2,1)}, bf16[48,5120]{1,0:T(8,128)(2,1)}, u32[]{:S(2)}, u32[]{:S(2)}) collective-permute-start(bf16[48,5120]{1,0:T(8,128)(2,1)} %get-tuple-element.122), channel_id=1, source_target_pairs={{0,2},{1,3},{2,4},{3,5},{4,6},{5,7},{6,0},{7,1},{8,10},{9,11},{10,... | collective-permute-start | bytes 1474568 | tf_op jit(solution)/shard_map/ppermute | solution.py:27
  166.6 13.7 %copy-start.10 = (bf16[96,5120]{1,0:T(8,128)(2,1)S(1)}, bf16[96,5120]{1,0:T(8,128)(2,1)}, u32[]{:S(2)}) copy-start(bf16[96,5120]{1,0:T(8,128)(2,1)} %get-tuple-element.110) | copy-start | bytes 2949124
  175.4 6.3 %copy-start.9 = (bf16[96,5120]{1,0:T(8,128)(2,1)S(1)}, bf16[96,5120]{1,0:T(8,128)(2,1)}, u32[]{:S(2)}) copy-start(bf16[96,5120]{1,0:T(8,128)(2,1)} %get-tuple-element.113) | copy-start | bytes 2949124
  181.7 1.7 copy-start.5
  183.4 1.2 copy-start.19
  183.4 28.0 %copy-start.6 = (bf16[96,5120]{1,0:T(8,128)(2,1)S(1)}, bf16[96,5120]{1,0:T(8,128)(2,1)}, u32[]{:S(2)}) copy-start(bf16[96,5120]{1,0:T(8,128)(2,1)} %get-tuple-element.108) | copy-start | bytes 2949124
  184.6 3.3 %collective-permute-start.36 = (bf16[96,5120]{1,0:T(8,128)(2,1)S(1)}, bf16[96,5120]{1,0:T(8,128)(2,1)S(1)}, u32[]{:S(2)}, u32[]{:S(2)}) collective-permute-start(bf16[96,5120]{1,0:T(8,128)(2,1)S(1)} %copy-done.19), channel_id=1, source_target_pairs={{0,1},{1,0},{2,3},{3,2},{4,5},{5,4},{6,7},{7,6},{8,9},{9,8},{10,11... | collective-permute-start | bytes 2949128 | tf_op jit(solution)/shard_map/ppermute | solution.py:27
  185.7 23.4 %collective-permute-start.38 = (bf16[96,5120]{1,0:T(8,128)(2,1)S(1)}, bf16[96,5120]{1,0:T(8,128)(2,1)S(1)}, u32[]{:S(2)}, u32[]{:S(2)}) collective-permute-start(bf16[96,5120]{1,0:T(8,128)(2,1)S(1)} %add_convert_fusion.2), channel_id=1, source_target_pairs={{0,6},{1,7},{2,0},{3,1},{4,2},{5,3},{6,4},{7,5},{8,14},{9,15},{10,... | collective-permute-start | bytes 2949128 | tf_op jit(solution)/shard_map/ppermute | solution.py:27
  185.7 24.3 %collective-permute-start.37 = (bf16[96,5120]{1,0:T(8,128)(2,1)S(1)}, bf16[96,5120]{1,0:T(8,128)(2,1)S(1)}, u32[]{:S(2)}, u32[]{:S(2)}) collective-permute-start(bf16[96,5120]{1,0:T(8,128)(2,1)S(1)} %add_convert_fusion.3), channel_id=1, source_target_pairs={{0,2},{1,3},{2,4},{3,5},{4,6},{5,7},{6,0},{7,1},{8,10},{9,11},{10,... | collective-permute-start | bytes 2949128 | tf_op jit(solution)/shard_map/ppermute | solution.py:27
  187.2 24.3 %collective-permute-start.39 = (bf16[96,5120]{1,0:T(8,128)(2,1)S(1)}, bf16[96,5120]{1,0:T(8,128)(2,1)S(1)}, u32[]{:S(2)}, u32[]{:S(2)}) collective-permute-start(bf16[96,5120]{1,0:T(8,128)(2,1)S(1)} %add_convert_fusion.1), channel_id=1, source_target_pairs={{0,8},{1,9},{2,10},{3,11},{4,12},{5,13},{6,14},{7,15},{8,0},{9,1},... | collective-permute-start | bytes 2949128 | tf_op jit(solution)/shard_map/ppermute | solution.py:27

commit v4 on v3

--- a/solution.py
+++ b/solution.py
@@ -244,7 +244,8 @@
     cz = move(after(own, tz), zl=1)
     y_top = move(rows_of(ca[:h_depth], ca[depth:]), dy=1)
     y_low = move(cb[h_depth:depth], dy=-1)
-    taz, tbz = move(tz, dx=1), move(tz, dx=-1)
+    tz_x = after(tz, ta, tb)
+    taz, tbz = move(tz_x, dx=1), move(tz_x, dx=-1)
     cy, top_in, low_in = join(
         (y_top, y_low, ta, taz, tb, tbz),
         (
@@ -253,8 +254,8 @@
             ((4, h_rows, h_rows), (5, h_rows, h_rows)),
         ),
     )
-    cy, top_in, low_in = after((cy, top_in, low_in), cz)
-    caz, cbz, cyz = move(cz, dy=1), move(cz, dy=-1), move(cy, zl=1)
+    cy, cz_y = after((cy, cz), top_in)
+    caz, cbz, cyz = move(cz_y, dy=1), move(cz_y, dy=-1), move(cy, zl=1)
     x_top, x_low = move(top_in, dx=1), move(low_in, dx=-1)
 
     sources = [own, ca, cb, cz, cy, caz, cbz, cyz]

time: 214 us -> 202 us (0.944)
  waiting for transfers between devices: 101 us -> 85.5 us
  starting transfers between devices: 48.2 us -> 52.2 us
    ppermute x40, waiting for transfers between devices: 101 us -> 85.5 us  [move(): return lax.ppermute(value, AXES, pairs)]
    ppermute x40, starting transfers between devices: 48.2 us -> 52.2 us  [move(): return lax.ppermute(value, AXES, pairs)]
  transfers between devices with their start and end apart: 40 -> 40, of which waited for: 17 -> 16; matrix products, arithmetic and copies ran while one was open for 1% -> 1% of each run, Pallas kernels for 23% -> 24%
where the time goes in v4:
time: 202 us; the launch traced here: 201 us
  waiting for transfers between devices  85.5 us (42%)
  starting transfers between devices  52.2 us (26%)
  Pallas kernels  48.2 us (24%)
  other arithmetic  10.1 us (5%)
  local copies, waits for them, and re-layouts  3.75 us (2%)
    ppermute x40, waiting for transfers between devices, move(): return lax.ppermute(value, AXES, pairs)  85.5 us
    ppermute x40, starting transfers between devices, move(): return lax.ppermute(value, AXES, pairs)  52.2 us
    pallas_call x2, Pallas kernels, sums(): return tuple(run(ids, sidx, scale_table, *pieces, *weights))  28.9 us
    pallas_call x1, Pallas kernels, sums(): return tuple(run(ids, sidx, scale_table, *sources, *pieces, down_weight))  17 us
  transfers between devices with their start and end apart: 40, of which 16 were waited for; matrix products, arithmetic and copies ran while one was open for 1% of the time, Pallas kernels for 24%

profile of v4, /device:TPU:1, one launch (start us, length us, event | category | flops | bytes accessed | tf_op | source)
XLA Modules:
  0.0 201.4 jit_solution(6881976107419065736)
XLA Ops:
  1.3 1.3 copy-done.1
  2.6 0.1 shard_map.64.refs_0_
  2.8 2.2 %collective-permute-start = (bf16[5136,128]{1,0:T(8,128)(2,1)S(1)}, bf16[5136,128]{1,0:T(8,128)(2,1)S(1)}, u32[]{:S(2)}, u32[]{:S(2)}) collective-permute-start(bf16[5136,128]{1,0:T(8,128)(2,1)S(1)} %shard_map.64.refs_0_), channel_id=1, source_target_pairs={{0,32},{1,33},{2,34},{3,35},{4,36},{5,37},{6,38},{7,39},{8,40},{9,... | collective-permute-start | bytes 3944456 | tf_op jit(solution)/shard_map/ppermute | solution.py:27
  5.0 3.6 %collective-permute-start.2 = (bf16[96,5120]{1,0:T(8,128)(2,1)S(1)}, bf16[96,5120]{1,0:T(8,128)(2,1)S(1)}, u32[]{:S(2)}, u32[]{:S(2)}) collective-permute-start(bf16[96,5120]{1,0:T(8,128)(2,1)S(1)} %copy-done.11), channel_id=1, source_target_pairs={{0,8},{1,9},{2,10},{3,11},{4,12},{5,13},{6,14},{7,15},{8,0},{9,1},... | collective-permute-start | bytes 2949128 | tf_op jit(solution)/shard_map/ppermute | solution.py:27
  8.6 2.5 %collective-permute-start.7 = (bf16[96,5120]{1,0:T(8,128)(2,1)S(1)}, bf16[96,5120]{1,0:T(8,128)(2,1)S(1)}, u32[]{:S(2)}, u32[]{:S(2)}) collective-permute-start(bf16[96,5120]{1,0:T(8,128)(2,1)S(1)} %copy-done.11), channel_id=1, source_target_pairs={{0,6},{1,7},{2,0},{3,1},{4,2},{5,3},{6,4},{7,5},{8,14},{9,15},{10,... | collective-permute-start | bytes 2949128 | tf_op jit(solution)/shard_map/ppermute | solution.py:27
  11.1 2.7 %collective-permute-start.1 = (bf16[5136,128]{1,0:T(8,128)(2,1)S(1)}, bf16[5136,128]{1,0:T(8,128)(2,1)S(1)}, u32[]{:S(2)}, u32[]{:S(2)}) collective-permute-start(bf16[5136,128]{1,0:T(8,128)(2,1)S(1)} %shard_map.64.refs_0_), channel_id=1, source_target_pairs={{0,96},{1,97},{2,98},{3,99},{4,100},{5,101},{6,102},{7,103},{8,104... | collective-permute-start | bytes 3944456 | tf_op jit(solution)/shard_map/ppermute | solution.py:27
  13.8 16.0 %collective-permute-done.2.refs_4_ = bf16[96,5120]{1,0:T(8,128)(2,1)S(1)} collective-permute-done((bf16[96,5120]{1,0:T(8,128)(2,1)S(1)}, bf16[96,5120]{1,0:T(8,128)(2,1)S(1)}, u32[]{:S(2)}, u32[]{:S(2)}) %collective-permute-start.2) | collective-permute-done | bytes 983072 | tf_op jit(solution)/shard_map/ppermute | solution.py:27
  29.8 0.7 collective-permute-start.3
  30.5 0.4 collective-permute-done.7.refs_4_.refs_2_
  30.9 3.1 %collective-permute-done.6.refs_2_.refs_3_ = bf16[96,5120]{1,0:T(8,128)(2,1)S(1)} collective-permute-done((bf16[96,5120]{1,0:T(8,128)(2,1)S(1)}, bf16[96,5120]{1,0:T(8,128)(2,1)S(1)}, u32[]{:S(2)}, u32[]{:S(2)}) %collective-permute-start.6) | collective-permute-done | bytes 983072 | tf_op jit(solution)/shard_map/ppermute | solution.py:27
  34.1 0.3 collective-permute-start.9
  34.4 1.1 collective-permute-start.8
  35.6 1.4 collective-permute-start.4
  37.0 3.7 %collective-permute-done.1.refs_2_ = bf16[5136,128]{1,0:T(8,128)(2,1)S(1)} collective-permute-done((bf16[5136,128]{1,0:T(8,128)(2,1)S(1)}, bf16[5136,128]{1,0:T(8,128)(2,1)S(1)}, u32[]{:S(2)}, u32[]{:S(2)}) %collective-permute-start.1) | collective-permute-done | bytes 1314848 | tf_op jit(solution)/shard_map/ppermute | solution.py:27
  40.8 3.6 %collective-permute-start.5 = (bf16[2560,128]{1,0:T(8,128)(2,1)S(1)}, bf16[2560,128]{1,0:T(8,128)(2,1)S(1)}, u32[]{:S(2)}, u32[]{:S(2)}) collective-permute-start(bf16[2560,128]{1,0:T(8,128)(2,1)S(1)} %slice.74), channel_id=1, source_target_pairs={{0,96},{1,97},{2,98},{3,99},{4,100},{5,101},{6,102},{7,103},{8,104... | collective-permute-start | bytes 1966088 | tf_op jit(solution)/shard_map/ppermute | solution.py:27
  44.4 10.7 %collective-permute-done.9.refs_5_.refs_10_ = bf16[96,5120]{1,0:T(8,128)(2,1)} collective-permute-done((bf16[96,5120]{1,0:T(8,128)(2,1)S(1)}, bf16[96,5120]{1,0:T(8,128)(2,1)}, u32[]{:S(2)}, u32[]{:S(2)}) %collective-permute-start.9) | collective-permute-done | bytes 983072 | tf_op jit(solution)/shard_map/ppermute | solution.py:27
  55.0 1.6 collective-permute-done.8.refs_3_.refs_11_
  56.6 2.2 %shard_map.65 = (bf16[5136,128]{1,0:T(8,128)(2,1)S(1)}, bf16[96,5120]{1,0:T(8,128)(2,1)S(1)}, bf16[96,5120]{1,0:T(8,128)(2,1)S(1)}) custom-call(bf16[2576,128]{1,0:T(8,128)(2,1)S(1)} %collective-permute-done.4.refs_0_, bf16[2560,128]{1,0:T(8,128)(2,1)S(1)} %collective-permute-done.5.refs_1_, bf16[96,5120]{1,0:T(8,128)(2,1)S(1)} %collective-permute-done.6.refs_2_.refs_3_, ...), custom_call_target="tpu_custom_call" | custom-call | flops 1 | bytes 1 | tf_op jit(solution)/shard_map/pallas_call | solution.py:82
  58.8 3.3 %collective-permute-start.11 = (bf16[5136,128]{1,0:T(8,128)(2,1)S(1)}, bf16[5136,128]{1,0:T(8,128)(2,1)S(1)}, u32[]{:S(2)}, u32[]{:S(2)}) collective-permute-start(bf16[5136,128]{1,0:T(8,128)(2,1)S(1)} %collective-permute-done.3.refs_3_), channel_id=1, source_target_pairs={{0,96},{1,97},{2,98},{3,99},{4,100},{5,101},{6,102},{7,103},{8,104... | collective-permute-start | bytes 3944456 | tf_op jit(solution)/shard_map/ppermute | solution.py:27
  62.1 2.3 %collective-permute-start.14 = (bf16[96,5120]{1,0:T(8,128)(2,1)S(1)}, bf16[96,5120]{1,0:T(8,128)(2,1)}, u32[]{:S(2)}, u32[]{:S(2)}) collective-permute-start(bf16[96,5120]{1,0:T(8,128)(2,1)S(1)} %get-tuple-element.69), channel_id=1, source_target_pairs={{0,6},{1,7},{2,0},{3,1},{4,2},{5,3},{6,4},{7,5},{8,14},{9,15},{10,... | collective-permute-start | bytes 2949128 | tf_op jit(solution)/shard_map/ppermute | solution.py:27
  64.4 0.6 collective-permute-start.12
  65.1 17.1 %collective-permute-done.14.refs_9_.refs_1_ = bf16[96,5120]{1,0:T(8,128)(2,1)} collective-permute-done((bf16[96,5120]{1,0:T(8,128)(2,1)S(1)}, bf16[96,5120]{1,0:T(8,128)(2,1)}, u32[]{:S(2)}, u32[]{:S(2)}) %collective-permute-start.14) | collective-permute-done | bytes 983072 | tf_op jit(solution)/shard_map/ppermute | solution.py:27
  82.2 4.2 %collective-permute-start.17 = (bf16[96,5120]{1,0:T(8,128)(2,1)}, bf16[96,5120]{1,0:T(8,128)(2,1)}, u32[]{:S(2)}, u32[]{:S(2)}) collective-permute-start(bf16[96,5120]{1,0:T(8,128)(2,1)} %collective-permute-done.9.refs_5_.refs_10_), channel_id=1, source_target_pairs={{0,1},{1,0},{2,3},{3,2},{4,5},{5,4},{6,7},{7,6},{8,9},{9,8},{10,11... | collective-permute-start | bytes 2949128 | tf_op jit(solution)/shard_map/ppermute | solution.py:27
  86.4 3.5 %collective-permute-start.16 = (bf16[96,5120]{1,0:T(8,128)(2,1)}, bf16[96,5120]{1,0:T(8,128)(2,1)}, u32[]{:S(2)}, u32[]{:S(2)}) collective-permute-start(bf16[96,5120]{1,0:T(8,128)(2,1)} %collective-permute-done.14.refs_9_.refs_1_), channel_id=1, source_target_pairs={{0,1},{1,0},{2,3},{3,2},{4,5},{5,4},{6,7},{7,6},{8,9},{9,8},{10,11... | collective-permute-start | bytes 2949128 | tf_op jit(solution)/shard_map/ppermute | solution.py:27
  89.9 1.3 collective-permute-start.15
  91.2 3.4 %collective-permute-start.18 = (bf16[96,5120]{1,0:T(8,128)(2,1)}, bf16[96,5120]{1,0:T(8,128)(2,1)}, u32[]{:S(2)}, u32[]{:S(2)}) collective-permute-start(bf16[96,5120]{1,0:T(8,128)(2,1)} %collective-permute-done.8.refs_3_.refs_11_), channel_id=1, source_target_pairs={{0,1},{1,0},{2,3},{3,2},{4,5},{5,4},{6,7},{7,6},{8,9},{9,8},{10,11... | collective-permute-start | bytes 2949128 | tf_op jit(solution)/shard_map/ppermute | solution.py:27
  94.7 1.0 copy-done.17
  95.7 0.1 stack.3
  95.9 1.2 collective-permute-start.19
  97.2 0.4 collective-permute-start.21
  97.7 0.5 slice_bitcast_fusion.7
  98.2 17.0 %shard_map.66 = (bf16[96,5120]{1,0:T(8,128)(2,1)}, bf16[96,5120]{1,0:T(8,128)(2,1)}, bf16[96,5120]{1,0:T(8,128)(2,1)}, bf16[96,5120]{1,0:T(8,128)(2,1)}, bf16[96...) custom-call(s32[8]{0:T(128)} %get-tuple-element.104.ids, ...), custom_call_target="tpu_custom_call" | custom-call | flops 9059696640 | bytes 27525120 | tf_op jit(solution)/shard_map/pallas_call | solution.py:280
  115.3 0.5 collective-permute-start.23
  115.8 0.4 collective-permute-start.25
  116.3 1.9 collective-permute-done.23
  118.2 1.5 add_convert_fusion.6
  119.6 2.4 %collective-permute-start.28 = (bf16[96,5120]{1,0:T(8,128)(2,1)S(1)}, bf16[96,5120]{1,0:T(8,128)(2,1)}, u32[]{:S(2)}, u32[]{:S(2)}) collective-permute-start(bf16[96,5120]{1,0:T(8,128)(2,1)S(1)} %add_convert_fusion.6), channel_id=1, source_target_pairs={{0,8},{1,9},{2,10},{3,11},{4,12},{5,13},{6,14},{7,15},{8,0},{9,1},... | collective-permute-start | bytes 2949128 | tf_op jit(solution)/shard_map/ppermute | solution.py:27
  122.0 0.3 add_convert_fusion.5
  122.3 1.2 collective-permute-start.29
  123.5 0.3 add_convert_fusion.4
  123.7 1.8 collective-permute-start.30
  125.6 20.2 %shard_map.67 = (bf16[96,5120]{1,0:T(8,128)(2,1)}, bf16[96,5120]{1,0:T(8,128)(2,1)}, bf16[96,5120]{1,0:T(8,128)(2,1)}, bf16[96,5120]{1,0:T(8,128)(2,1)}, bf16[48...) custom-call(s32[8]{0:T(128)} %get-tuple-element.104.ids, ...), custom_call_target="tpu_custom_call", output_to_operand_aliasing={{9}: (13, {}), {10}: (14, {})} | custom-call | flops 12079595520 | bytes 31457280 | tf_op jit(solution)/shard_map/pallas_call | solution.py:281
  145.7 1.3 collective-permute-start.26
  147.1 1.6 collective-permute-done.26
  148.7 0.7 collective-permute-done.27
  149.4 2.8 %add_convert_fusion.7 = (bf16[48,5120]{1,0:T(8,128)(2,1)}, bf16[48,5120]{1,0:T(8,128)(2,1)}) fusion(bf16[48,5120]{1,0:T(8,128)(2,1)S(1)} %collective-permute-done.27, bf16[96,5120]{1,0:T(8,128)(2,1)} %collective-permute-done.28, bf16[96,5120]{1,0:T(8,128)(2,1)} %get-tuple-element.97, bf16[48,5120]{1,0:T(8,128)(2,1)S(1)} %collective-permute-done.26), kind=kLoop, calls=%fused_computation.7 | loop fusion | flops 2949120 | bytes 3932160 | tf_op jit(solution)/shard_map/convert_element_type | solution.py:316
  152.2 0.4 collective-permute-start.31
  152.6 0.1 collective-permute-start.32
  152.7 0.4 collective-permute-start.33
  153.1 1.4 collective-permute-start.35
  154.6 8.8 %shard_map.68 = (bf16[96,5120]{1,0:T(8,128)(2,1)}, bf16[96,5120]{1,0:T(8,128)(2,1)}, bf16[4,5120,256]{2,1,0:T(8,128)(2,1)S(1)}, bf16[512,5120]{1,0:T(8,128)(2,1)S(1)}) custom-call(s32[8]{0:T(128)} %get-tuple-element.104.ids, s32[8]{0:T(128)} %get-tuple-element.123.sidx, f32[64]{0:T(128)} %table.5, ...), custom_call_target="tpu_custom_call", output_to_operand_aliasing={{2}: (5, {}), {3}: (6, {})} | custom-call | flops 3019898880 | bytes 19660800 | tf_op jit(solution)/shard_map/pallas_call | solution.py:281
  163.4 2.7 %collective-permute-done.35 = bf16[48,5120]{1,0:T(8,128)(2,1)} collective-permute-done((bf16[48,5120]{1,0:T(8,128)(2,1)}, bf16[48,5120]{1,0:T(8,128)(2,1)}, u32[]{:S(2)}, u32[]{:S(2)}) %collective-permute-start.35) | collective-permute-done | bytes 491552 | tf_op jit(solution)/shard_map/ppermute | solution.py:27
  166.1 2.3 %collective-permute-done.34 = bf16[48,5120]{1,0:T(8,128)(2,1)} collective-permute-done((bf16[48,5120]{1,0:T(8,128)(2,1)}, bf16[48,5120]{1,0:T(8,128)(2,1)}, u32[]{:S(2)}, u32[]{:S(2)}) %collective-permute-start.34) | collective-permute-done | bytes 491552 | tf_op jit(solution)/shard_map/ppermute | solution.py:27
  168.4 1.3 add_convert_fusion.3
  169.8 1.7 add_convert_fusion.2
  171.5 0.6 add_convert_fusion.1
  172.1 0.6 copy-done.19
  172.7 1.3 collective-permute-start.36
  174.0 1.5 collective-permute-start.37
  175.4 0.6 collective-permute-start.39
  176.2 21.2 %collective-permute-done.38 = bf16[96,5120]{1,0:T(8,128)(2,1)S(1)} collective-permute-done((bf16[96,5120]{1,0:T(8,128)(2,1)S(1)}, bf16[96,5120]{1,0:T(8,128)(2,1)S(1)}, u32[]{:S(2)}, u32[]{:S(2)}) %collective-permute-start.38) | collective-permute-done | bytes 983072 | tf_op jit(solution)/shard_map/ppermute | solution.py:27
  197.3 0.9 collective-permute-done.37
  198.3 1.4 collective-permute-done.39
  199.7 1.7 add_convert_fusion
  (84 shorter events, 0.9 us)
Async XLA Ops:
  1.3 1.3 copy-start.1
  2.6 2.3 %copy-start.11 = (bf16[96,5120]{1,0:T(8,128)(2,1)S(1)}, bf16[96,5120]{1,0:T(8,128)(2,1)}, u32[]{:S(2)}) copy-start(bf16[96,5120]{1,0:T(8,128)(2,1)} %refs_0_.1) | copy-start | bytes 2949124
  2.7 61.7 %copy-start = (bf16[5136,128]{1,0:T(8,128)(2,1)}, bf16[5136,128]{1,0:T(8,128)(2,1)S(1)}, u32[]{:S(2)}) copy-start(bf16[5136,128]{1,0:T(8,128)(2,1)S(1)} %shard_map.64.refs_0_) | copy-start | bytes 3944452
  2.8 32.8 %collective-permute-start = (bf16[5136,128]{1,0:T(8,128)(2,1)S(1)}, bf16[5136,128]{1,0:T(8,128)(2,1)S(1)}, u32[]{:S(2)}, u32[]{:S(2)}) collective-permute-start(bf16[5136,128]{1,0:T(8,128)(2,1)S(1)} %shard_map.64.refs_0_), channel_id=1, source_target_pairs={{0,32},{1,33},{2,34},{3,35},{4,36},{5,37},{6,38},{7,39},{8,40},{9,... | collective-permute-start | bytes 3944456 | tf_op jit(solution)/shard_map/ppermute | solution.py:27
  5.0 24.9 %collective-permute-start.2 = (bf16[96,5120]{1,0:T(8,128)(2,1)S(1)}, bf16[96,5120]{1,0:T(8,128)(2,1)S(1)}, u32[]{:S(2)}, u32[]{:S(2)}) collective-permute-start(bf16[96,5120]{1,0:T(8,128)(2,1)S(1)} %copy-done.11), channel_id=1, source_target_pairs={{0,8},{1,9},{2,10},{3,11},{4,12},{5,13},{6,14},{7,15},{8,0},{9,1},... | collective-permute-start | bytes 2949128 | tf_op jit(solution)/shard_map/ppermute | solution.py:27
  8.6 22.3 %collective-permute-start.7 = (bf16[96,5120]{1,0:T(8,128)(2,1)S(1)}, bf16[96,5120]{1,0:T(8,128)(2,1)S(1)}, u32[]{:S(2)}, u32[]{:S(2)}) collective-permute-start(bf16[96,5120]{1,0:T(8,128)(2,1)S(1)} %copy-done.11), channel_id=1, source_target_pairs={{0,6},{1,7},{2,0},{3,1},{4,2},{5,3},{6,4},{7,5},{8,14},{9,15},{10,... | collective-permute-start | bytes 2949128 | tf_op jit(solution)/shard_map/ppermute | solution.py:27
  11.1 23.0 %collective-permute-start.6 = (bf16[96,5120]{1,0:T(8,128)(2,1)S(1)}, bf16[96,5120]{1,0:T(8,128)(2,1)S(1)}, u32[]{:S(2)}, u32[]{:S(2)}) collective-permute-start(bf16[96,5120]{1,0:T(8,128)(2,1)S(1)} %copy-done.11), channel_id=1, source_target_pairs={{0,2},{1,3},{2,4},{3,5},{4,6},{5,7},{6,0},{7,1},{8,10},{9,11},{10,... | collective-permute-start | bytes 2949128 | tf_op jit(solution)/shard_map/ppermute | solution.py:27
  11.1 29.7 %collective-permute-start.1 = (bf16[5136,128]{1,0:T(8,128)(2,1)S(1)}, bf16[5136,128]{1,0:T(8,128)(2,1)S(1)}, u32[]{:S(2)}, u32[]{:S(2)}) collective-permute-start(bf16[5136,128]{1,0:T(8,128)(2,1)S(1)} %shard_map.64.refs_0_), channel_id=1, source_target_pairs={{0,96},{1,97},{2,98},{3,99},{4,100},{5,101},{6,102},{7,103},{8,104... | collective-permute-start | bytes 3944456 | tf_op jit(solution)/shard_map/ppermute | solution.py:27
  29.8 11.0 %copy-start.18 = (bf16[96,5120]{1,0:T(8,128)(2,1)}, bf16[96,5120]{1,0:T(8,128)(2,1)S(1)}, u32[]{:S(2)}) copy-start(bf16[96,5120]{1,0:T(8,128)(2,1)S(1)} %collective-permute-done.2.refs_4_) | copy-start | bytes 2949124
  29.8 29.0 %collective-permute-start.3 = (bf16[5136,128]{1,0:T(8,128)(2,1)S(1)}, bf16[5136,128]{1,0:T(8,128)(2,1)S(1)}, u32[]{:S(2)}, u32[]{:S(2)}) collective-permute-start(bf16[5136,128]{1,0:T(8,128)(2,1)S(1)} %shard_map.64.refs_0_), channel_id=1, source_target_pairs={{0,16},{1,17},{2,18},{3,19},{4,20},{5,21},{6,22},{7,23},{8,24},{9,... | collective-permute-start | bytes 3944456 | tf_op jit(solution)/shard_map/ppermute | solution.py:27
  30.9 64.9 %copy-start.2 = (bf16[96,5120]{1,0:T(8,128)(2,1)}, bf16[96,5120]{1,0:T(8,128)(2,1)S(1)}, u32[]{:S(2)}) copy-start(bf16[96,5120]{1,0:T(8,128)(2,1)S(1)} %collective-permute-done.7.refs_4_.refs_2_) | copy-start | bytes 2949124
  34.1 63.0 %copy-start.3 = (bf16[96,5120]{1,0:T(8,128)(2,1)}, bf16[96,5120]{1,0:T(8,128)(2,1)S(1)}, u32[]{:S(2)}) copy-start(bf16[96,5120]{1,0:T(8,128)(2,1)S(1)} %collective-permute-done.6.refs_2_.refs_3_) | copy-start | bytes 2949124
  34.1 21.0 %collective-permute-start.9 = (bf16[96,5120]{1,0:T(8,128)(2,1)S(1)}, bf16[96,5120]{1,0:T(8,128)(2,1)}, u32[]{:S(2)}, u32[]{:S(2)}) collective-permute-start(bf16[96,5120]{1,0:T(8,128)(2,1)S(1)} %collective-permute-done.2.refs_4_), channel_id=1, source_target_pairs={{0,6},{1,7},{2,0},{3,1},{4,2},{5,3},{6,4},{7,5},{8,14},{9,15},{10,... | collective-permute-start | bytes 2949128 | tf_op jit(solution)/shard_map/ppermute | solution.py:27
  34.4 22.2 %collective-permute-start.8 = (bf16[96,5120]{1,0:T(8,128)(2,1)S(1)}, bf16[96,5120]{1,0:T(8,128)(2,1)}, u32[]{:S(2)}, u32[]{:S(2)}) collective-permute-start(bf16[96,5120]{1,0:T(8,128)(2,1)S(1)} %collective-permute-done.2.refs_4_), channel_id=1, source_target_pairs={{0,2},{1,3},{2,4},{3,5},{4,6},{5,7},{6,0},{7,1},{8,10},{9,11},{10,... | collective-permute-start | bytes 2949128 | tf_op jit(solution)/shard_map/ppermute | solution.py:27
  35.5 29.5 %copy-start.12 = (bf16[5136,128]{1,0:T(8,128)(2,1)}, bf16[5136,128]{1,0:T(8,128)(2,1)S(1)}, u32[]{:S(2)}) copy-start(bf16[5136,128]{1,0:T(8,128)(2,1)S(1)} %collective-permute-done.refs_1_) | copy-start | bytes 3944452
  35.6 21.0 %collective-permute-start.4 = (bf16[2576,128]{1,0:T(8,128)(2,1)S(1)}, bf16[2576,128]{1,0:T(8,128)(2,1)S(1)}, u32[]{:S(2)}, u32[]{:S(2)}) collective-permute-start(bf16[2576,128]{1,0:T(8,128)(2,1)S(1)} %pad_maximum_fusion), channel_id=1, source_target_pairs={{0,32},{1,33},{2,34},{3,35},{4,36},{5,37},{6,38},{7,39},{8,40},{9,... | collective-permute-start | bytes 1978376 | tf_op jit(solution)/shard_map/ppermute | solution.py:27
  40.7 24.3 %copy-start.13 = (bf16[5136,128]{1,0:T(8,128)(2,1)}, bf16[5136,128]{1,0:T(8,128)(2,1)S(1)}, u32[]{:S(2)}) copy-start(bf16[5136,128]{1,0:T(8,128)(2,1)S(1)} %collective-permute-done.1.refs_2_) | copy-start | bytes 3944452
  40.8 15.8 %collective-permute-start.5 = (bf16[2560,128]{1,0:T(8,128)(2,1)S(1)}, bf16[2560,128]{1,0:T(8,128)(2,1)S(1)}, u32[]{:S(2)}, u32[]{:S(2)}) collective-permute-start(bf16[2560,128]{1,0:T(8,128)(2,1)S(1)} %slice.74), channel_id=1, source_target_pairs={{0,96},{1,97},{2,98},{3,99},{4,100},{5,101},{6,102},{7,103},{8,104... | collective-permute-start | bytes 1966088 | tf_op jit(solution)/shard_map/ppermute | solution.py:27
  58.8 32.5 %copy-start.4 = (bf16[5136,128]{1,0:T(8,128)(2,1)}, bf16[5136,128]{1,0:T(8,128)(2,1)S(1)}, u32[]{:S(2)}) copy-start(bf16[5136,128]{1,0:T(8,128)(2,1)S(1)} %get-tuple-element.67.refs_4_) | copy-start | bytes 3944452
  58.8 35.9 %copy-start.14 = (bf16[5136,128]{1,0:T(8,128)(2,1)}, bf16[5136,128]{1,0:T(8,128)(2,1)S(1)}, u32[]{:S(2)}) copy-start(bf16[5136,128]{1,0:T(8,128)(2,1)S(1)} %collective-permute-done.3.refs_3_) | copy-start | bytes 3944452
  58.8 31.1 %collective-permute-start.11 = (bf16[5136,128]{1,0:T(8,128)(2,1)S(1)}, bf16[5136,128]{1,0:T(8,128)(2,1)S(1)}, u32[]{:S(2)}, u32[]{:S(2)}) collective-permute-start(bf16[5136,128]{1,0:T(8,128)(2,1)S(1)} %collective-permute-done.3.refs_3_), channel_id=1, source_target_pairs={{0,96},{1,97},{2,98},{3,99},{4,100},{5,101},{6,102},{7,103},{8,104... | collective-permute-start | bytes 3944456 | tf_op jit(solution)/shard_map/ppermute | solution.py:27
  62.1 29.1 %collective-permute-start.10 = (bf16[5136,128]{1,0:T(8,128)(2,1)S(1)}, bf16[5136,128]{1,0:T(8,128)(2,1)S(1)}, u32[]{:S(2)}, u32[]{:S(2)}) collective-permute-start(bf16[5136,128]{1,0:T(8,128)(2,1)S(1)} %collective-permute-done.3.refs_3_), channel_id=1, source_target_pairs={{0,32},{1,33},{2,34},{3,35},{4,36},{5,37},{6,38},{7,39},{8,40},{9,... | collective-permute-start | bytes 3944456 | tf_op jit(solution)/shard_map/ppermute | solution.py:27
  62.1 20.1 %collective-permute-start.14 = (bf16[96,5120]{1,0:T(8,128)(2,1)S(1)}, bf16[96,5120]{1,0:T(8,128)(2,1)}, u32[]{:S(2)}, u32[]{:S(2)}) collective-permute-start(bf16[96,5120]{1,0:T(8,128)(2,1)S(1)} %get-tuple-element.69), channel_id=1, source_target_pairs={{0,6},{1,7},{2,0},{3,1},{4,2},{5,3},{6,4},{7,5},{8,14},{9,15},{10,... | collective-permute-start | bytes 2949128 | tf_op jit(solution)/shard_map/ppermute | solution.py:27
  64.4 22.0 %collective-permute-start.13 = (bf16[96,5120]{1,0:T(8,128)(2,1)S(1)}, bf16[96,5120]{1,0:T(8,128)(2,1)}, u32[]{:S(2)}, u32[]{:S(2)}) collective-permute-start(bf16[96,5120]{1,0:T(8,128)(2,1)S(1)} %get-tuple-element.66), channel_id=1, source_target_pairs={{0,2},{1,3},{2,4},{3,5},{4,6},{5,7},{6,0},{7,1},{8,10},{9,11},{10,... | collective-permute-start | bytes 2949128 | tf_op jit(solution)/shard_map/ppermute | solution.py:27
  64.4 30.2 %collective-permute-start.12 = (bf16[5136,128]{1,0:T(8,128)(2,1)S(1)}, bf16[5136,128]{1,0:T(8,128)(2,1)S(1)}, u32[]{:S(2)}, u32[]{:S(2)}) collective-permute-start(bf16[5136,128]{1,0:T(8,128)(2,1)S(1)} %get-tuple-element.67.refs_4_), channel_id=1, source_target_pairs={{0,16},{1,17},{2,18},{3,19},{4,20},{5,21},{6,22},{7,23},{8,24},{9,... | collective-permute-start | bytes 3944456 | tf_op jit(solution)/shard_map/ppermute | solution.py:27
  82.2 15.4 %collective-permute-start.17 = (bf16[96,5120]{1,0:T(8,128)(2,1)}, bf16[96,5120]{1,0:T(8,128)(2,1)}, u32[]{:S(2)}, u32[]{:S(2)}) collective-permute-start(bf16[96,5120]{1,0:T(8,128)(2,1)} %collective-permute-done.9.refs_5_.refs_10_), channel_id=1, source_target_pairs={{0,1},{1,0},{2,3},{3,2},{4,5},{5,4},{6,7},{7,6},{8,9},{9,8},{10,11... | collective-permute-start | bytes 2949128 | tf_op jit(solution)/shard_map/ppermute | solution.py:27
  86.4 9.4 %collective-permute-start.16 = (bf16[96,5120]{1,0:T(8,128)(2,1)}, bf16[96,5120]{1,0:T(8,128)(2,1)}, u32[]{:S(2)}, u32[]{:S(2)}) collective-permute-start(bf16[96,5120]{1,0:T(8,128)(2,1)} %collective-permute-done.14.refs_9_.refs_1_), channel_id=1, source_target_pairs={{0,1},{1,0},{2,3},{3,2},{4,5},{5,4},{6,7},{7,6},{8,9},{9,8},{10,11... | collective-permute-start | bytes 2949128 | tf_op jit(solution)/shard_map/ppermute | solution.py:27
  89.9 4.7 %copy-start.15 = (bf16[5136,128]{1,0:T(8,128)(2,1)}, bf16[5136,128]{1,0:T(8,128)(2,1)S(1)}, u32[]{:S(2)}) copy-start(bf16[5136,128]{1,0:T(8,128)(2,1)S(1)} %collective-permute-done.11.refs_6_) | copy-start | bytes 3944452
  89.9 5.9 %collective-permute-start.15 = (bf16[96,5120]{1,0:T(8,128)(2,1)}, bf16[96,5120]{1,0:T(8,128)(2,1)}, u32[]{:S(2)}, u32[]{:S(2)}) collective-permute-start(bf16[96,5120]{1,0:T(8,128)(2,1)} %collective-permute-done.13.refs_8_.refs_0_), channel_id=1, source_target_pairs={{0,1},{1,0},{2,3},{3,2},{4,5},{5,4},{6,7},{7,6},{8,9},{9,8},{10,11... | collective-permute-start | bytes 2949128 | tf_op jit(solution)/shard_map/ppermute | solution.py:27
  91.2 3.4 %copy-start.16 = (bf16[5136,128]{1,0:T(8,128)(2,1)}, bf16[5136,128]{1,0:T(8,128)(2,1)S(1)}, u32[]{:S(2)}) copy-start(bf16[5136,128]{1,0:T(8,128)(2,1)S(1)} %collective-permute-done.10.refs_5_) | copy-start | bytes 3944452
  91.2 7.0 %collective-permute-start.18 = (bf16[96,5120]{1,0:T(8,128)(2,1)}, bf16[96,5120]{1,0:T(8,128)(2,1)}, u32[]{:S(2)}, u32[]{:S(2)}) collective-permute-start(bf16[96,5120]{1,0:T(8,128)(2,1)} %collective-permute-done.8.refs_3_.refs_11_), channel_id=1, source_target_pairs={{0,1},{1,0},{2,3},{3,2},{4,5},{5,4},{6,7},{7,6},{8,9},{9,8},{10,11... | collective-permute-start | bytes 2949128 | tf_op jit(solution)/shard_map/ppermute | solution.py:27
  94.7 1.1 copy-start.17
  95.9 19.4 %collective-permute-start.19 = (bf16[96,5120]{1,0:T(8,128)(2,1)S(1)}, bf16[96,5120]{1,0:T(8,128)(2,1)}, u32[]{:S(2)}, u32[]{:S(2)}) collective-permute-start(bf16[96,5120]{1,0:T(8,128)(2,1)S(1)} %collective-permute-done.7.refs_4_.refs_2_), channel_id=1, source_target_pairs={{0,1},{1,0},{2,3},{3,2},{4,5},{5,4},{6,7},{7,6},{8,9},{9,8},{10,11... | collective-permute-start | bytes 2949128 | tf_op jit(solution)/shard_map/ppermute | solution.py:27
  97.1 18.2 %collective-permute-start.20 = (bf16[96,5120]{1,0:T(8,128)(2,1)S(1)}, bf16[96,5120]{1,0:T(8,128)(2,1)}, u32[]{:S(2)}, u32[]{:S(2)}) collective-permute-start(bf16[96,5120]{1,0:T(8,128)(2,1)S(1)} %collective-permute-done.6.refs_2_.refs_3_), channel_id=1, source_target_pairs={{0,1},{1,0},{2,3},{3,2},{4,5},{5,4},{6,7},{7,6},{8,9},{9,8},{10,11... | collective-permute-start | bytes 2949128 | tf_op jit(solution)/shard_map/ppermute | solution.py:27
  97.2 18.1 %collective-permute-start.21 = (bf16[96,5120]{1,0:T(8,128)(2,1)}, bf16[96,5120]{1,0:T(8,128)(2,1)}, u32[]{:S(2)}, u32[]{:S(2)}) collective-permute-start(bf16[96,5120]{1,0:T(8,128)(2,1)} %copy-done.18), channel_id=1, source_target_pairs={{0,1},{1,0},{2,3},{3,2},{4,5},{5,4},{6,7},{7,6},{8,9},{9,8},{10,11... | collective-permute-start | bytes 2949128 | tf_op jit(solution)/shard_map/ppermute | solution.py:27
  97.6 17.7 %collective-permute-start.22 = (bf16[96,5120]{1,0:T(8,128)(2,1)S(1)}, bf16[96,5120]{1,0:T(8,128)(2,1)}, u32[]{:S(2)}, u32[]{:S(2)}) collective-permute-start(bf16[96,5120]{1,0:T(8,128)(2,1)S(1)} %copy-done.11), channel_id=1, source_target_pairs={{0,1},{1,0},{2,3},{3,2},{4,5},{5,4},{6,7},{7,6},{8,9},{9,8},{10,11... | collective-permute-start | bytes 2949128 | tf_op jit(solution)/shard_map/ppermute | solution.py:27
  115.2 6.8 %copy-start.8 = (bf16[96,5120]{1,0:T(8,128)(2,1)S(1)}, bf16[96,5120]{1,0:T(8,128)(2,1)}, u32[]{:S(2)}) copy-start(bf16[96,5120]{1,0:T(8,128)(2,1)} %get-tuple-element.82) | copy-start | bytes 2949124
  115.3 2.9 %collective-permute-start.23 = (bf16[96,5120]{1,0:T(8,128)(2,1)}, bf16[96,5120]{1,0:T(8,128)(2,1)S(1)}, u32[]{:S(2)}, u32[]{:S(2)}) collective-permute-start(bf16[96,5120]{1,0:T(8,128)(2,1)} %get-tuple-element.81), channel_id=1, source_target_pairs={{0,1},{1,0},{2,3},{3,2},{4,5},{5,4},{6,7},{7,6},{8,9},{9,8},{10,11... | collective-permute-start | bytes 2949128 | tf_op jit(solution)/shard_map/ppermute | solution.py:27
  115.7 6.3 %collective-permute-start.24 = (bf16[96,5120]{1,0:T(8,128)(2,1)}, bf16[96,5120]{1,0:T(8,128)(2,1)S(1)}, u32[]{:S(2)}, u32[]{:S(2)}) collective-permute-start(bf16[96,5120]{1,0:T(8,128)(2,1)} %get-tuple-element.83), channel_id=1, source_target_pairs={{0,1},{1,0},{2,3},{3,2},{4,5},{5,4},{6,7},{7,6},{8,9},{9,8},{10,11... | collective-permute-start | bytes 2949128 | tf_op jit(solution)/shard_map/ppermute | solution.py:27
  115.8 7.6 %collective-permute-start.25 = (bf16[96,5120]{1,0:T(8,128)(2,1)}, bf16[96,5120]{1,0:T(8,128)(2,1)S(1)}, u32[]{:S(2)}, u32[]{:S(2)}) collective-permute-start(bf16[96,5120]{1,0:T(8,128)(2,1)} %get-tuple-element.85), channel_id=1, source_target_pairs={{0,1},{1,0},{2,3},{3,2},{4,5},{5,4},{6,7},{7,6},{8,9},{9,8},{10,11... | collective-permute-start | bytes 2949128 | tf_op jit(solution)/shard_map/ppermute | solution.py:27
  119.6 3.9 %copy-start.7 = (bf16[96,5120]{1,0:T(8,128)(2,1)S(1)}, bf16[96,5120]{1,0:T(8,128)(2,1)}, u32[]{:S(2)}) copy-start(bf16[96,5120]{1,0:T(8,128)(2,1)} %get-tuple-element.84) | copy-start | bytes 2949124
  119.6 29.8 %collective-permute-start.28 = (bf16[96,5120]{1,0:T(8,128)(2,1)S(1)}, bf16[96,5120]{1,0:T(8,128)(2,1)}, u32[]{:S(2)}, u32[]{:S(2)}) collective-permute-start(bf16[96,5120]{1,0:T(8,128)(2,1)S(1)} %add_convert_fusion.6), channel_id=1, source_target_pairs={{0,8},{1,9},{2,10},{3,11},{4,12},{5,13},{6,14},{7,15},{8,0},{9,1},... | collective-permute-start | bytes 2949128 | tf_op jit(solution)/shard_map/ppermute | solution.py:27
  122.3 27.1 %collective-permute-start.29 = (bf16[96,5120]{1,0:T(8,128)(2,1)S(1)}, bf16[96,5120]{1,0:T(8,128)(2,1)S(1)}, u32[]{:S(2)}, u32[]{:S(2)}) collective-permute-start(bf16[96,5120]{1,0:T(8,128)(2,1)S(1)} %add_convert_fusion.5), channel_id=1, source_target_pairs={{0,2},{1,3},{2,4},{3,5},{4,6},{5,7},{6,0},{7,1},{8,10},{9,11},{10,... | collective-permute-start | bytes 2949128 | tf_op jit(solution)/shard_map/ppermute | solution.py:27
  123.7 25.7 %collective-permute-start.30 = (bf16[96,5120]{1,0:T(8,128)(2,1)S(1)}, bf16[96,5120]{1,0:T(8,128)(2,1)S(1)}, u32[]{:S(2)}, u32[]{:S(2)}) collective-permute-start(bf16[96,5120]{1,0:T(8,128)(2,1)S(1)} %add_convert_fusion.4), channel_id=1, source_target_pairs={{0,6},{1,7},{2,0},{3,1},{4,2},{5,3},{6,4},{7,5},{8,14},{9,15},{10,... | collective-permute-start | bytes 2949128 | tf_op jit(solution)/shard_map/ppermute | solution.py:27
  145.7 3.0 %collective-permute-start.26 = (bf16[48,5120]{1,0:T(8,128)(2,1)}, bf16[48,5120]{1,0:T(8,128)(2,1)S(1)}, u32[]{:S(2)}, u32[]{:S(2)}) collective-permute-start(bf16[48,5120]{1,0:T(8,128)(2,1)} %get-tuple-element.95), channel_id=1, source_target_pairs={{0,1},{1,0},{2,3},{3,2},{4,5},{5,4},{6,7},{7,6},{8,9},{9,8},{10,11... | collective-permute-start | bytes 1474568 | tf_op jit(solution)/shard_map/ppermute | solution.py:27
  147.0 2.4 %collective-permute-start.27 = (bf16[48,5120]{1,0:T(8,128)(2,1)}, bf16[48,5120]{1,0:T(8,128)(2,1)S(1)}, u32[]{:S(2)}, u32[]{:S(2)}) collective-permute-start(bf16[48,5120]{1,0:T(8,128)(2,1)} %get-tuple-element.96), channel_id=1, source_target_pairs={{0,1},{1,0},{2,3},{3,2},{4,5},{5,4},{6,7},{7,6},{8,9},{9,8},{10,11... | collective-permute-start | bytes 1474568 | tf_op jit(solution)/shard_map/ppermute | solution.py:27
  152.2 16.2 %collective-permute-start.31 = (bf16[96,5120]{1,0:T(8,128)(2,1)}, bf16[96,5120]{1,0:T(8,128)(2,1)S(1)}, u32[]{:S(2)}, u32[]{:S(2)}) collective-permute-start(bf16[96,5120]{1,0:T(8,128)(2,1)} %get-tuple-element.101), channel_id=1, source_target_pairs={{0,1},{1,0},{2,3},{3,2},{4,5},{5,4},{6,7},{7,6},{8,9},{9,8},{10,11... | collective-permute-start | bytes 2949128 | tf_op jit(solution)/shard_map/ppermute | solution.py:27
  152.6 15.8 %collective-permute-start.32 = (bf16[96,5120]{1,0:T(8,128)(2,1)}, bf16[96,5120]{1,0:T(8,128)(2,1)}, u32[]{:S(2)}, u32[]{:S(2)}) collective-permute-start(bf16[96,5120]{1,0:T(8,128)(2,1)} %get-tuple-element.102), channel_id=1, source_target_pairs={{0,1},{1,0},{2,3},{3,2},{4,5},{5,4},{6,7},{7,6},{8,9},{9,8},{10,11... | collective-permute-start | bytes 2949128 | tf_op jit(solution)/shard_map/ppermute | solution.py:27
  152.7 15.7 %collective-permute-start.33 = (bf16[96,5120]{1,0:T(8,128)(2,1)}, bf16[96,5120]{1,0:T(8,128)(2,1)S(1)}, u32[]{:S(2)}, u32[]{:S(2)}) collective-permute-start(bf16[96,5120]{1,0:T(8,128)(2,1)} %get-tuple-element.103), channel_id=1, source_target_pairs={{0,1},{1,0},{2,3},{3,2},{4,5},{5,4},{6,7},{7,6},{8,9},{9,8},{10,11... | collective-permute-start | bytes 2949128 | tf_op jit(solution)/shard_map/ppermute | solution.py:27
  153.1 13.0 %collective-permute-start.35 = (bf16[48,5120]{1,0:T(8,128)(2,1)}, bf16[48,5120]{1,0:T(8,128)(2,1)}, u32[]{:S(2)}, u32[]{:S(2)}) collective-permute-start(bf16[48,5120]{1,0:T(8,128)(2,1)} %get-tuple-element.121), channel_id=1, source_target_pairs={{0,6},{1,7},{2,0},{3,1},{4,2},{5,3},{6,4},{7,5},{8,14},{9,15},{10,... | collective-permute-start | bytes 1474568 | tf_op jit(solution)/shard_map/ppermute | solution.py:27
  154.5 13.9 %collective-permute-start.34 = (bf16[48,5120]{1,0:T(8,128)(2,1)}, bf16[48,5120]{1,0:T(8,128)(2,1)}, u32[]{:S(2)}, u32[]{:S(2)}) collective-permute-start(bf16[48,5120]{1,0:T(8,128)(2,1)} %get-tuple-element.122), channel_id=1, source_target_pairs={{0,2},{1,3},{2,4},{3,5},{4,6},{5,7},{6,0},{7,1},{8,10},{9,11},{10,... | collective-permute-start | bytes 1474568 | tf_op jit(solution)/shard_map/ppermute | solution.py:27
  154.6 13.8 %copy-start.10 = (bf16[96,5120]{1,0:T(8,128)(2,1)S(1)}, bf16[96,5120]{1,0:T(8,128)(2,1)}, u32[]{:S(2)}) copy-start(bf16[96,5120]{1,0:T(8,128)(2,1)} %get-tuple-element.110) | copy-start | bytes 2949124
  163.4 6.4 %copy-start.9 = (bf16[96,5120]{1,0:T(8,128)(2,1)S(1)}, bf16[96,5120]{1,0:T(8,128)(2,1)}, u32[]{:S(2)}) copy-start(bf16[96,5120]{1,0:T(8,128)(2,1)} %get-tuple-element.113) | copy-start | bytes 2949124
  169.8 1.7 copy-start.5
  171.5 1.2 copy-start.19
  171.5 28.2 %copy-start.6 = (bf16[96,5120]{1,0:T(8,128)(2,1)S(1)}, bf16[96,5120]{1,0:T(8,128)(2,1)}, u32[]{:S(2)}) copy-start(bf16[96,5120]{1,0:T(8,128)(2,1)} %get-tuple-element.108) | copy-start | bytes 2949124
  172.7 3.5 %collective-permute-start.36 = (bf16[96,5120]{1,0:T(8,128)(2,1)S(1)}, bf16[96,5120]{1,0:T(8,128)(2,1)S(1)}, u32[]{:S(2)}, u32[]{:S(2)}) collective-permute-start(bf16[96,5120]{1,0:T(8,128)(2,1)S(1)} %copy-done.19), channel_id=1, source_target_pairs={{0,1},{1,0},{2,3},{3,2},{4,5},{5,4},{6,7},{7,6},{8,9},{9,8},{10,11... | collective-permute-start | bytes 2949128 | tf_op jit(solution)/shard_map/ppermute | solution.py:27
  174.0 23.4 %collective-permute-start.38 = (bf16[96,5120]{1,0:T(8,128)(2,1)S(1)}, bf16[96,5120]{1,0:T(8,128)(2,1)S(1)}, u32[]{:S(2)}, u32[]{:S(2)}) collective-permute-start(bf16[96,5120]{1,0:T(8,128)(2,1)S(1)} %add_convert_fusion.2), channel_id=1, source_target_pairs={{0,6},{1,7},{2,0},{3,1},{4,2},{5,3},{6,4},{7,5},{8,14},{9,15},{10,... | collective-permute-start | bytes 2949128 | tf_op jit(solution)/shard_map/ppermute | solution.py:27
  174.0 24.3 %collective-permute-start.37 = (bf16[96,5120]{1,0:T(8,128)(2,1)S(1)}, bf16[96,5120]{1,0:T(8,128)(2,1)S(1)}, u32[]{:S(2)}, u32[]{:S(2)}) collective-permute-start(bf16[96,5120]{1,0:T(8,128)(2,1)S(1)} %add_convert_fusion.3), channel_id=1, source_target_pairs={{0,2},{1,3},{2,4},{3,5},{4,6},{5,7},{6,0},{7,1},{8,10},{9,11},{10,... | collective-permute-start | bytes 2949128 | tf_op jit(solution)/shard_map/ppermute | solution.py:27
  175.4 24.3 %collective-permute-start.39 = (bf16[96,5120]{1,0:T(8,128)(2,1)S(1)}, bf16[96,5120]{1,0:T(8,128)(2,1)S(1)}, u32[]{:S(2)}, u32[]{:S(2)}) collective-permute-start(bf16[96,5120]{1,0:T(8,128)(2,1)S(1)} %add_convert_fusion.1), channel_id=1, source_target_pairs={{0,8},{1,9},{2,10},{3,11},{4,12},{5,13},{6,14},{7,15},{8,0},{9,1},... | collective-permute-start | bytes 2949128 | tf_op jit(solution)/shard_map/ppermute | solution.py:27

commit v5 on v4

--- a/solution.py
+++ b/solution.py
@@ -307,28 +307,32 @@
 
     ids = after(ids, far_z, right, left)
     groups = halves(0) + [whole(tb, o_right), whole(ta, o_left), whole(tz, o_z)]
-    part = sums(ids, groups, [count] * 4 + [h_rows] * 2 + [count] * 3, weights)
-    part, weights = part[:9], part[9:]
-    far, near, here_z, near_sib, here_sib = part[0], part[1:3], part[3], part[6:8], part[8]
-    got = swap(*part[4:6])
-    far, got, far_in, z_right, z_left = after((far, got, far_in, z_right, z_left))
+    part = sums(ids, groups, [count] + [h_rows] * 4 + [count] + [h_rows] * 6 + [count], weights)
+    part, weights = part[:13], part[13:]
+    got = swap(*part[6:8])
+    part, got, far_in, z_right, z_left = after((part, got, far_in, z_right, z_left))
+    far, near, here_z, near_sib, z_sib = part[0], part[1:5], part[5], part[8:12], part[12]
     top = add(far[:h_rows], got[0], far_in[:h_rows]).astype(BF16)
     low = add(far[h_rows:], got[1], far_in[h_rows:]).astype(BF16)
     past_top, past_low = move(top, dx=1), move(low, dx=-1)
-
-    near_sib, here_sib = after((near_sib, here_sib), top, low)
-    got = swap(*near_sib, here_sib)
-    ids = after(ids, top, low)
+    got = swap(near_sib[1], near_sib[2], z_sib)
+    right, left = add(near[1], got[0]).astype(BF16), add(near[2], got[1]).astype(BF16)
+    across = add(here_z, got[2], z_right, z_left).astype(BF16)
+    right_bottom, left_top, across_in = move(right, dx=1), move(left, dx=-1), move(across, zh=1)
+
+    ids = after(ids, top, low, right, left, across)
     here, own_sib = sums(ids, [whole(tokens, o_own)], [count] * 2, weights)[:2]
-    near, got, past_top, past_low, here = after((near, got, past_top, past_low, here))
+    held = after((here, near, near_sib, past_top, past_low, right_bottom, left_top, across_in))
+    here, near, near_sib, past_top, past_low, right_bottom, left_top, across_in = held
+    got = swap(near_sib[0], near_sib[3])
+    right, left = add(near[0], got[0], past_top).astype(BF16), add(near[3], got[1], past_low).astype(BF16)
+    right_top, left_bottom = move(right, dx=1), move(left, dx=-1)
+    own_sib = after(own_sib, right, left)
+    total = add(here, *swap(own_sib), across_in)
     zero = jnp.zeros((), BF16)
-    past_top = lax.pad(past_top, zero, ((0, h_rows, 0), (0, 0, 0)))
-    past_low = lax.pad(past_low, zero, ((h_rows, 0, 0), (0, 0, 0)))
-    right, left = (add(near[i], got[i], past).astype(BF16) for i, past in enumerate((past_top, past_low)))
-    across = add(here_z, got[2], z_right, z_left).astype(BF16)
-    right_in, left_in, across_in = move(right, dx=1), move(left, dx=-1), move(across, zh=1)
-    own_sib = after(own_sib, right, left, across)
-    return add(here, *swap(own_sib), right_in, left_in, across_in).astype(BF16)
+    for first, piece in ((0, right_top), (h_rows, right_bottom), (0, left_top), (h_rows, left_bottom)):
+        total = total + lax.pad(piece, zero, ((first, h_rows - first, 0), (0, 0, 0))).astype(F32)
+    return total.astype(BF16)
 
 
 def solution(mesh):

time: 202 us -> 204 us (level)
  starting transfers between devices: 52.2 us -> 57 us
    ppermute x40 -> x44, starting transfers between devices: 52.2 us -> 57 us  [move(): return lax.ppermute(value, AXES, pairs)]
    ppermute x40 -> x44, waiting for transfers between devices: 85.5 us -> 84.7 us  [move(): return lax.ppermute(value, AXES, pairs)]
    convert_element_type x3 -> x5, other arithmetic: 4.73 us -> 4.5 us  [the longest x1 1.7 us: body(): return total.astype(BF16)]
  transfers between devices with their start and end apart: 40 -> 44, of which waited for: 16 -> 15; matrix products, arithmetic and copies ran while one was open for 1% -> 3% of each run, Pallas kernels for 24% -> 24%
where the time goes in v5:
time: 204 us
  waiting for transfers between devices  84.7 us (42%)
  starting transfers between devices  57 us (28%)
  Pallas kernels  48.2 us (24%)
  other arithmetic  9.17 us (4%)
  local copies, waits for them, and re-layouts  3.26 us (2%)
    ppermute x44, waiting for transfers between devices, move(): return lax.ppermute(value, AXES, pairs)  84.7 us
    ppermute x44, starting transfers between devices, move(): return lax.ppermute(value, AXES, pairs)  57 us
    pallas_call x2, Pallas kernels, sums(): return tuple(run(ids, sidx, scale_table, *pieces, *weights))  28.9 us
    pallas_call x1, Pallas kernels, sums(): return tuple(run(ids, sidx, scale_table, *sources, *pieces, down_weight))  17 us
  transfers between devices with their start and end apart: 44, of which 15 were waited for; matrix products, arithmetic and copies ran while one was open for 3% of the time, Pallas kernels for 24%

profile of v5, /device:TPU:1, one launch (start us, length us, event | category | flops | bytes accessed | tf_op | source)
XLA Modules:
  0.0 203.9 jit_solution(7154268094418042747)
XLA Ops:
  1.3 1.3 copy-done.1
  2.6 0.1 shard_map.64.refs_0_
  2.8 2.2 %collective-permute-start = (bf16[5136,128]{1,0:T(8,128)(2,1)S(1)}, bf16[5136,128]{1,0:T(8,128)(2,1)S(1)}, u32[]{:S(2)}, u32[]{:S(2)}) collective-permute-start(bf16[5136,128]{1,0:T(8,128)(2,1)S(1)} %shard_map.64.refs_0_), channel_id=1, source_target_pairs={{0,32},{1,33},{2,34},{3,35},{4,36},{5,37},{6,38},{7,39},{8,40},{9,... | collective-permute-start | bytes 3944456 | tf_op jit(solution)/shard_map/ppermute | solution.py:27
  5.0 3.6 %collective-permute-start.2 = (bf16[96,5120]{1,0:T(8,128)(2,1)S(1)}, bf16[96,5120]{1,0:T(8,128)(2,1)S(1)}, u32[]{:S(2)}, u32[]{:S(2)}) collective-permute-start(bf16[96,5120]{1,0:T(8,128)(2,1)S(1)} %copy-done.9), channel_id=1, source_target_pairs={{0,8},{1,9},{2,10},{3,11},{4,12},{5,13},{6,14},{7,15},{8,0},{9,1},... | collective-permute-start | bytes 2949128 | tf_op jit(solution)/shard_map/ppermute | solution.py:27
  8.6 2.5 %collective-permute-start.7 = (bf16[96,5120]{1,0:T(8,128)(2,1)S(1)}, bf16[96,5120]{1,0:T(8,128)(2,1)S(1)}, u32[]{:S(2)}, u32[]{:S(2)}) collective-permute-start(bf16[96,5120]{1,0:T(8,128)(2,1)S(1)} %copy-done.9), channel_id=1, source_target_pairs={{0,6},{1,7},{2,0},{3,1},{4,2},{5,3},{6,4},{7,5},{8,14},{9,15},{10,... | collective-permute-start | bytes 2949128 | tf_op jit(solution)/shard_map/ppermute | solution.py:27
  11.1 2.7 %collective-permute-start.1 = (bf16[5136,128]{1,0:T(8,128)(2,1)S(1)}, bf16[5136,128]{1,0:T(8,128)(2,1)S(1)}, u32[]{:S(2)}, u32[]{:S(2)}) collective-permute-start(bf16[5136,128]{1,0:T(8,128)(2,1)S(1)} %shard_map.64.refs_0_), channel_id=1, source_target_pairs={{0,96},{1,97},{2,98},{3,99},{4,100},{5,101},{6,102},{7,103},{8,104... | collective-permute-start | bytes 3944456 | tf_op jit(solution)/shard_map/ppermute | solution.py:27
  13.8 16.0 %collective-permute-done.2.refs_4_ = bf16[96,5120]{1,0:T(8,128)(2,1)S(1)} collective-permute-done((bf16[96,5120]{1,0:T(8,128)(2,1)S(1)}, bf16[96,5120]{1,0:T(8,128)(2,1)S(1)}, u32[]{:S(2)}, u32[]{:S(2)}) %collective-permute-start.2) | collective-permute-done | bytes 983072 | tf_op jit(solution)/shard_map/ppermute | solution.py:27
  29.8 0.7 collective-permute-start.3
  30.5 0.4 collective-permute-done.7.refs_4_.refs_2_
  30.9 3.1 %collective-permute-done.6.refs_2_.refs_3_ = bf16[96,5120]{1,0:T(8,128)(2,1)S(1)} collective-permute-done((bf16[96,5120]{1,0:T(8,128)(2,1)S(1)}, bf16[96,5120]{1,0:T(8,128)(2,1)S(1)}, u32[]{:S(2)}, u32[]{:S(2)}) %collective-permute-start.6) | collective-permute-done | bytes 983072 | tf_op jit(solution)/shard_map/ppermute | solution.py:27
  34.1 0.3 collective-permute-start.9
  34.4 1.1 collective-permute-start.8
  35.6 1.4 collective-permute-start.4
  37.0 3.7 %collective-permute-done.1.refs_2_ = bf16[5136,128]{1,0:T(8,128)(2,1)S(1)} collective-permute-done((bf16[5136,128]{1,0:T(8,128)(2,1)S(1)}, bf16[5136,128]{1,0:T(8,128)(2,1)S(1)}, u32[]{:S(2)}, u32[]{:S(2)}) %collective-permute-start.1) | collective-permute-done | bytes 1314848 | tf_op jit(solution)/shard_map/ppermute | solution.py:27
  40.8 3.6 %collective-permute-start.5 = (bf16[2560,128]{1,0:T(8,128)(2,1)S(1)}, bf16[2560,128]{1,0:T(8,128)(2,1)S(1)}, u32[]{:S(2)}, u32[]{:S(2)}) collective-permute-start(bf16[2560,128]{1,0:T(8,128)(2,1)S(1)} %slice.74), channel_id=1, source_target_pairs={{0,96},{1,97},{2,98},{3,99},{4,100},{5,101},{6,102},{7,103},{8,104... | collective-permute-start | bytes 1966088 | tf_op jit(solution)/shard_map/ppermute | solution.py:27
  44.4 10.7 %collective-permute-done.9.refs_5_.refs_10_ = bf16[96,5120]{1,0:T(8,128)(2,1)} collective-permute-done((bf16[96,5120]{1,0:T(8,128)(2,1)S(1)}, bf16[96,5120]{1,0:T(8,128)(2,1)}, u32[]{:S(2)}, u32[]{:S(2)}) %collective-permute-start.9) | collective-permute-done | bytes 983072 | tf_op jit(solution)/shard_map/ppermute | solution.py:27
  55.0 1.6 collective-permute-done.8.refs_3_.refs_11_
  56.6 2.2 %shard_map.65 = (bf16[5136,128]{1,0:T(8,128)(2,1)S(1)}, bf16[96,5120]{1,0:T(8,128)(2,1)S(1)}, bf16[96,5120]{1,0:T(8,128)(2,1)S(1)}) custom-call(bf16[2576,128]{1,0:T(8,128)(2,1)S(1)} %collective-permute-done.4.refs_0_, bf16[2560,128]{1,0:T(8,128)(2,1)S(1)} %collective-permute-done.5.refs_1_, bf16[96,5120]{1,0:T(8,128)(2,1)S(1)} %collective-permute-done.6.refs_2_.refs_3_, ...), custom_call_target="tpu_custom_call" | custom-call | flops 1 | bytes 1 | tf_op jit(solution)/shard_map/pallas_call | solution.py:82
  58.8 3.3 %collective-permute-start.11 = (bf16[5136,128]{1,0:T(8,128)(2,1)S(1)}, bf16[5136,128]{1,0:T(8,128)(2,1)S(1)}, u32[]{:S(2)}, u32[]{:S(2)}) collective-permute-start(bf16[5136,128]{1,0:T(8,128)(2,1)S(1)} %collective-permute-done.3.refs_3_), channel_id=1, source_target_pairs={{0,96},{1,97},{2,98},{3,99},{4,100},{5,101},{6,102},{7,103},{8,104... | collective-permute-start | bytes 3944456 | tf_op jit(solution)/shard_map/ppermute | solution.py:27
  62.1 2.3 %collective-permute-start.14 = (bf16[96,5120]{1,0:T(8,128)(2,1)S(1)}, bf16[96,5120]{1,0:T(8,128)(2,1)}, u32[]{:S(2)}, u32[]{:S(2)}) collective-permute-start(bf16[96,5120]{1,0:T(8,128)(2,1)S(1)} %get-tuple-element.82), channel_id=1, source_target_pairs={{0,6},{1,7},{2,0},{3,1},{4,2},{5,3},{6,4},{7,5},{8,14},{9,15},{10,... | collective-permute-start | bytes 2949128 | tf_op jit(solution)/shard_map/ppermute | solution.py:27
  64.4 0.6 collective-permute-start.12
  65.1 17.1 %collective-permute-done.14.refs_9_.refs_1_ = bf16[96,5120]{1,0:T(8,128)(2,1)} collective-permute-done((bf16[96,5120]{1,0:T(8,128)(2,1)S(1)}, bf16[96,5120]{1,0:T(8,128)(2,1)}, u32[]{:S(2)}, u32[]{:S(2)}) %collective-permute-start.14) | collective-permute-done | bytes 983072 | tf_op jit(solution)/shard_map/ppermute | solution.py:27
  82.2 4.2 %collective-permute-start.17 = (bf16[96,5120]{1,0:T(8,128)(2,1)}, bf16[96,5120]{1,0:T(8,128)(2,1)}, u32[]{:S(2)}, u32[]{:S(2)}) collective-permute-start(bf16[96,5120]{1,0:T(8,128)(2,1)} %collective-permute-done.9.refs_5_.refs_10_), channel_id=1, source_target_pairs={{0,1},{1,0},{2,3},{3,2},{4,5},{5,4},{6,7},{7,6},{8,9},{9,8},{10,11... | collective-permute-start | bytes 2949128 | tf_op jit(solution)/shard_map/ppermute | solution.py:27
  86.4 3.5 %collective-permute-start.16 = (bf16[96,5120]{1,0:T(8,128)(2,1)}, bf16[96,5120]{1,0:T(8,128)(2,1)}, u32[]{:S(2)}, u32[]{:S(2)}) collective-permute-start(bf16[96,5120]{1,0:T(8,128)(2,1)} %collective-permute-done.14.refs_9_.refs_1_), channel_id=1, source_target_pairs={{0,1},{1,0},{2,3},{3,2},{4,5},{5,4},{6,7},{7,6},{8,9},{9,8},{10,11... | collective-permute-start | bytes 2949128 | tf_op jit(solution)/shard_map/ppermute | solution.py:27
  89.9 1.3 collective-permute-start.15
  91.2 3.4 %collective-permute-start.18 = (bf16[96,5120]{1,0:T(8,128)(2,1)}, bf16[96,5120]{1,0:T(8,128)(2,1)}, u32[]{:S(2)}, u32[]{:S(2)}) collective-permute-start(bf16[96,5120]{1,0:T(8,128)(2,1)} %collective-permute-done.8.refs_3_.refs_11_), channel_id=1, source_target_pairs={{0,1},{1,0},{2,3},{3,2},{4,5},{5,4},{6,7},{7,6},{8,9},{9,8},{10,11... | collective-permute-start | bytes 2949128 | tf_op jit(solution)/shard_map/ppermute | solution.py:27
  94.7 1.1 copy-done.18
  95.9 1.2 collective-permute-start.19
  97.2 0.4 collective-permute-start.21
  97.7 0.6 slice_bitcast_fusion.7
  98.3 17.0 %shard_map.66 = (bf16[96,5120]{1,0:T(8,128)(2,1)}, bf16[96,5120]{1,0:T(8,128)(2,1)}, bf16[96,5120]{1,0:T(8,128)(2,1)}, bf16[96,5120]{1,0:T(8,128)(2,1)}, bf16[96...) custom-call(s32[8]{0:T(128)} %get-tuple-element.127.ids, ...), custom_call_target="tpu_custom_call" | custom-call | flops 9059696640 | bytes 27525120 | tf_op jit(solution)/shard_map/pallas_call | solution.py:280
  115.3 0.5 collective-permute-start.23
  115.9 0.4 collective-permute-start.25
  116.3 1.9 collective-permute-done.23
  118.2 1.5 add_convert_fusion.4
  119.7 2.4 %collective-permute-start.28 = (bf16[96,5120]{1,0:T(8,128)(2,1)S(1)}, bf16[96,5120]{1,0:T(8,128)(2,1)}, u32[]{:S(2)}, u32[]{:S(2)}) collective-permute-start(bf16[96,5120]{1,0:T(8,128)(2,1)S(1)} %add_convert_fusion.4), channel_id=1, source_target_pairs={{0,8},{1,9},{2,10},{3,11},{4,12},{5,13},{6,14},{7,15},{8,0},{9,1},... | collective-permute-start | bytes 2949128 | tf_op jit(solution)/shard_map/ppermute | solution.py:27
  122.1 0.3 add_convert_fusion.3
  122.4 1.2 collective-permute-start.29
  123.5 0.3 add_convert_fusion.2
  123.8 1.8 collective-permute-start.30
  125.6 20.3 %shard_map.67 = (bf16[96,5120]{1,0:T(8,128)(2,1)}, bf16[48,5120]{1,0:T(8,128)(2,1)}, bf16[48,5120]{1,0:T(8,128)(2,1)}, bf16[48,5120]{1,0:T(8,128)(2,1)}, bf16[48...) custom-call(s32[8]{0:T(128)} %get-tuple-element.127.ids, ...), custom_call_target="tpu_custom_call", output_to_operand_aliasing={{13}: (13, {}), {14}: (14, {})} | custom-call | flops 12079595520 | bytes 31457280 | tf_op jit(solution)/shard_map/pallas_call | solution.py:281
  145.9 1.3 collective-permute-start.26
  147.3 1.6 collective-permute-done.26
  148.9 0.7 collective-permute-done.27
  149.7 0.5 collective-permute-start.31
  150.1 2.1 %add_convert_fusion.9 = (bf16[48,5120]{1,0:T(8,128)(2,1)S(1)}, bf16[48,5120]{1,0:T(8,128)(2,1)S(1)}) fusion(bf16[48,5120]{1,0:T(8,128)(2,1)S(1)} %collective-permute-done.27, bf16[96,5120]{1,0:T(8,128)(2,1)} %collective-permute-done.28, bf16[96,5120]{1,0:T(8,128)(2,1)} %get-tuple-element.115, bf16[48,5120]{1,0:T(8,128)(2,1)S(1)} %collective-permute-done.26), kind=kLoop, calls=%fused_computation.9 | loop fusion | flops 2949120 | bytes 3932160 | tf_op jit(solution)/shard_map/convert_element_type | solution.py:316
  152.2 1.5 collective-permute-start.35
  153.7 0.6 collective-permute-start.32
  154.4 0.1 add_convert_fusion.8
  154.6 2.6 %collective-permute-done.33 = bf16[96,5120]{1,0:T(8,128)(2,1)S(1)} collective-permute-done((bf16[96,5120]{1,0:T(8,128)(2,1)S(1)}, bf16[96,5120]{1,0:T(8,128)(2,1)S(1)}, u32[]{:S(2)}, u32[]{:S(2)}) %collective-permute-start.33) | collective-permute-done | bytes 983072 | tf_op jit(solution)/shard_map/ppermute | solution.py:27
  157.2 0.6 add_convert_fusion.1
  157.8 0.7 collective-permute-start.38
  158.7 2.7 %collective-permute-start.37 = (bf16[48,5120]{1,0:T(8,128)(2,1)S(1)}, bf16[48,5120]{1,0:T(8,128)(2,1)S(1)}, u32[]{:S(2)}, u32[]{:S(2)}) collective-permute-start(bf16[48,5120]{1,0:T(8,128)(2,1)S(1)} %add_convert_fusion.7), channel_id=1, source_target_pairs={{0,6},{1,7},{2,0},{3,1},{4,2},{5,3},{6,4},{7,5},{8,14},{9,15},{10,... | collective-permute-start | bytes 1474568 | tf_op jit(solution)/shard_map/ppermute | solution.py:27
  161.3 8.6 %shard_map.68 = (bf16[96,5120]{1,0:T(8,128)(2,1)}, bf16[96,5120]{1,0:T(8,128)(2,1)}, bf16[4,5120,256]{2,1,0:T(8,128)(2,1)S(1)}, bf16[512,5120]{1,0:T(8,128)(2,1)S(1)}) custom-call(s32[8]{0:T(128)} %get-tuple-element.127.ids, s32[8]{0:T(128)} %get-tuple-element.149.sidx, f32[64]{0:T(128)} %table.5, ...), custom_call_target="tpu_custom_call", output_to_operand_aliasing={{2}: (5, {}), {3}: (6, {})} | custom-call | flops 3019898880 | bytes 19660800 | tf_op jit(solution)/shard_map/pallas_call | solution.py:281
  170.0 7.8 %collective-permute-done.36 = bf16[48,5120]{1,0:T(8,128)(2,1)S(1)} collective-permute-done((bf16[48,5120]{1,0:T(8,128)(2,1)S(1)}, bf16[48,5120]{1,0:T(8,128)(2,1)S(1)}, u32[]{:S(2)}, u32[]{:S(2)}) %collective-permute-start.36) | collective-permute-done | bytes 491552 | tf_op jit(solution)/shard_map/ppermute | solution.py:27
  177.9 4.5 %collective-permute-done.38 = bf16[96,5120]{1,0:T(8,128)(2,1)S(1)} collective-permute-done((bf16[96,5120]{1,0:T(8,128)(2,1)S(1)}, bf16[96,5120]{1,0:T(8,128)(2,1)S(1)}, u32[]{:S(2)}, u32[]{:S(2)}) %collective-permute-start.38) | collective-permute-done | bytes 983072 | tf_op jit(solution)/shard_map/ppermute | solution.py:27
  182.4 1.2 collective-permute-start.39
  183.7 1.6 collective-permute-done.39
  185.3 1.4 add_convert_fusion.6
  186.7 1.2 add_convert_fusion.5
  187.9 0.5 collective-permute-start.41
  188.4 2.7 %collective-permute-start.43 = (bf16[48,5120]{1,0:T(8,128)(2,1)S(1)}, bf16[48,5120]{1,0:T(8,128)(2,1)S(1)}, u32[]{:S(2)}, u32[]{:S(2)}) collective-permute-start(bf16[48,5120]{1,0:T(8,128)(2,1)S(1)} %add_convert_fusion.5), channel_id=1, source_target_pairs={{0,6},{1,7},{2,0},{3,1},{4,2},{5,3},{6,4},{7,5},{8,14},{9,15},{10,... | collective-permute-start | bytes 1474568 | tf_op jit(solution)/shard_map/ppermute | solution.py:27
  191.0 11.2 %collective-permute-done.42 = bf16[48,5120]{1,0:T(8,128)(2,1)S(1)} collective-permute-done((bf16[48,5120]{1,0:T(8,128)(2,1)S(1)}, bf16[48,5120]{1,0:T(8,128)(2,1)S(1)}, u32[]{:S(2)}, u32[]{:S(2)}) %collective-permute-start.42) | collective-permute-done | bytes 491552 | tf_op jit(solution)/shard_map/ppermute | solution.py:27
  202.3 1.7 add_convert_fusion
  (100 shorter events, 1.3 us)
Async XLA Ops:
  2.7 61.7 %copy-start = (bf16[5136,128]{1,0:T(8,128)(2,1)}, bf16[5136,128]{1,0:T(8,128)(2,1)S(1)}, u32[]{:S(2)}) copy-start(bf16[5136,128]{1,0:T(8,128)(2,1)S(1)} %shard_map.64.refs_0_) | copy-start | bytes 3944452
  2.8 32.8 %collective-permute-start = (bf16[5136,128]{1,0:T(8,128)(2,1)S(1)}, bf16[5136,128]{1,0:T(8,128)(2,1)S(1)}, u32[]{:S(2)}, u32[]{:S(2)}) collective-permute-start(bf16[5136,128]{1,0:T(8,128)(2,1)S(1)} %shard_map.64.refs_0_), channel_id=1, source_target_pairs={{0,32},{1,33},{2,34},{3,35},{4,36},{5,37},{6,38},{7,39},{8,40},{9,... | collective-permute-start | bytes 3944456 | tf_op jit(solution)/shard_map/ppermute | solution.py:27
  5.0 24.9 %collective-permute-start.2 = (bf16[96,5120]{1,0:T(8,128)(2,1)S(1)}, bf16[96,5120]{1,0:T(8,128)(2,1)S(1)}, u32[]{:S(2)}, u32[]{:S(2)}) collective-permute-start(bf16[96,5120]{1,0:T(8,128)(2,1)S(1)} %copy-done.9), channel_id=1, source_target_pairs={{0,8},{1,9},{2,10},{3,11},{4,12},{5,13},{6,14},{7,15},{8,0},{9,1},... | collective-permute-start | bytes 2949128 | tf_op jit(solution)/shard_map/ppermute | solution.py:27
  8.6 22.3 %collective-permute-start.7 = (bf16[96,5120]{1,0:T(8,128)(2,1)S(1)}, bf16[96,5120]{1,0:T(8,128)(2,1)S(1)}, u32[]{:S(2)}, u32[]{:S(2)}) collective-permute-start(bf16[96,5120]{1,0:T(8,128)(2,1)S(1)} %copy-done.9), channel_id=1, source_target_pairs={{0,6},{1,7},{2,0},{3,1},{4,2},{5,3},{6,4},{7,5},{8,14},{9,15},{10,... | collective-permute-start | bytes 2949128 | tf_op jit(solution)/shard_map/ppermute | solution.py:27
  11.1 23.0 %collective-permute-start.6 = (bf16[96,5120]{1,0:T(8,128)(2,1)S(1)}, bf16[96,5120]{1,0:T(8,128)(2,1)S(1)}, u32[]{:S(2)}, u32[]{:S(2)}) collective-permute-start(bf16[96,5120]{1,0:T(8,128)(2,1)S(1)} %copy-done.9), channel_id=1, source_target_pairs={{0,2},{1,3},{2,4},{3,5},{4,6},{5,7},{6,0},{7,1},{8,10},{9,11},{10,... | collective-permute-start | bytes 2949128 | tf_op jit(solution)/shard_map/ppermute | solution.py:27
  11.1 29.7 %collective-permute-start.1 = (bf16[5136,128]{1,0:T(8,128)(2,1)S(1)}, bf16[5136,128]{1,0:T(8,128)(2,1)S(1)}, u32[]{:S(2)}, u32[]{:S(2)}) collective-permute-start(bf16[5136,128]{1,0:T(8,128)(2,1)S(1)} %shard_map.64.refs_0_), channel_id=1, source_target_pairs={{0,96},{1,97},{2,98},{3,99},{4,100},{5,101},{6,102},{7,103},{8,104... | collective-permute-start | bytes 3944456 | tf_op jit(solution)/shard_map/ppermute | solution.py:27
  29.8 64.8 %copy-start.19 = (bf16[96,5120]{1,0:T(8,128)(2,1)}, bf16[96,5120]{1,0:T(8,128)(2,1)S(1)}, u32[]{:S(2)}) copy-start(bf16[96,5120]{1,0:T(8,128)(2,1)S(1)} %collective-permute-done.2.refs_4_) | copy-start | bytes 2949124
  29.8 29.0 %collective-permute-start.3 = (bf16[5136,128]{1,0:T(8,128)(2,1)S(1)}, bf16[5136,128]{1,0:T(8,128)(2,1)S(1)}, u32[]{:S(2)}, u32[]{:S(2)}) collective-permute-start(bf16[5136,128]{1,0:T(8,128)(2,1)S(1)} %shard_map.64.refs_0_), channel_id=1, source_target_pairs={{0,16},{1,17},{2,18},{3,19},{4,20},{5,21},{6,22},{7,23},{8,24},{9,... | collective-permute-start | bytes 3944456 | tf_op jit(solution)/shard_map/ppermute | solution.py:27
  30.9 64.9 %copy-start.2 = (bf16[96,5120]{1,0:T(8,128)(2,1)}, bf16[96,5120]{1,0:T(8,128)(2,1)S(1)}, u32[]{:S(2)}) copy-start(bf16[96,5120]{1,0:T(8,128)(2,1)S(1)} %collective-permute-done.7.refs_4_.refs_2_) | copy-start | bytes 2949124
  34.1 63.0 %copy-start.3 = (bf16[96,5120]{1,0:T(8,128)(2,1)}, bf16[96,5120]{1,0:T(8,128)(2,1)S(1)}, u32[]{:S(2)}) copy-start(bf16[96,5120]{1,0:T(8,128)(2,1)S(1)} %collective-permute-done.6.refs_2_.refs_3_) | copy-start | bytes 2949124
  34.1 21.0 %collective-permute-start.9 = (bf16[96,5120]{1,0:T(8,128)(2,1)S(1)}, bf16[96,5120]{1,0:T(8,128)(2,1)}, u32[]{:S(2)}, u32[]{:S(2)}) collective-permute-start(bf16[96,5120]{1,0:T(8,128)(2,1)S(1)} %collective-permute-done.2.refs_4_), channel_id=1, source_target_pairs={{0,6},{1,7},{2,0},{3,1},{4,2},{5,3},{6,4},{7,5},{8,14},{9,15},{10,... | collective-permute-start | bytes 2949128 | tf_op jit(solution)/shard_map/ppermute | solution.py:27
  34.4 22.2 %collective-permute-start.8 = (bf16[96,5120]{1,0:T(8,128)(2,1)S(1)}, bf16[96,5120]{1,0:T(8,128)(2,1)}, u32[]{:S(2)}, u32[]{:S(2)}) collective-permute-start(bf16[96,5120]{1,0:T(8,128)(2,1)S(1)} %collective-permute-done.2.refs_4_), channel_id=1, source_target_pairs={{0,2},{1,3},{2,4},{3,5},{4,6},{5,7},{6,0},{7,1},{8,10},{9,11},{10,... | collective-permute-start | bytes 2949128 | tf_op jit(solution)/shard_map/ppermute | solution.py:27
  35.5 29.5 %copy-start.13 = (bf16[5136,128]{1,0:T(8,128)(2,1)}, bf16[5136,128]{1,0:T(8,128)(2,1)S(1)}, u32[]{:S(2)}) copy-start(bf16[5136,128]{1,0:T(8,128)(2,1)S(1)} %collective-permute-done.refs_1_) | copy-start | bytes 3944452
  35.6 21.0 %collective-permute-start.4 = (bf16[2576,128]{1,0:T(8,128)(2,1)S(1)}, bf16[2576,128]{1,0:T(8,128)(2,1)S(1)}, u32[]{:S(2)}, u32[]{:S(2)}) collective-permute-start(bf16[2576,128]{1,0:T(8,128)(2,1)S(1)} %pad_maximum_fusion), channel_id=1, source_target_pairs={{0,32},{1,33},{2,34},{3,35},{4,36},{5,37},{6,38},{7,39},{8,40},{9,... | collective-permute-start | bytes 1978376 | tf_op jit(solution)/shard_map/ppermute | solution.py:27
  40.7 24.3 %copy-start.14 = (bf16[5136,128]{1,0:T(8,128)(2,1)}, bf16[5136,128]{1,0:T(8,128)(2,1)S(1)}, u32[]{:S(2)}) copy-start(bf16[5136,128]{1,0:T(8,128)(2,1)S(1)} %collective-permute-done.1.refs_2_) | copy-start | bytes 3944452
  40.8 15.8 %collective-permute-start.5 = (bf16[2560,128]{1,0:T(8,128)(2,1)S(1)}, bf16[2560,128]{1,0:T(8,128)(2,1)S(1)}, u32[]{:S(2)}, u32[]{:S(2)}) collective-permute-start(bf16[2560,128]{1,0:T(8,128)(2,1)S(1)} %slice.74), channel_id=1, source_target_pairs={{0,96},{1,97},{2,98},{3,99},{4,100},{5,101},{6,102},{7,103},{8,104... | collective-permute-start | bytes 1966088 | tf_op jit(solution)/shard_map/ppermute | solution.py:27
  58.8 32.4 %copy-start.4 = (bf16[5136,128]{1,0:T(8,128)(2,1)}, bf16[5136,128]{1,0:T(8,128)(2,1)S(1)}, u32[]{:S(2)}) copy-start(bf16[5136,128]{1,0:T(8,128)(2,1)S(1)} %get-tuple-element.80.refs_4_) | copy-start | bytes 3944452
  58.8 35.9 %copy-start.15 = (bf16[5136,128]{1,0:T(8,128)(2,1)}, bf16[5136,128]{1,0:T(8,128)(2,1)S(1)}, u32[]{:S(2)}) copy-start(bf16[5136,128]{1,0:T(8,128)(2,1)S(1)} %collective-permute-done.3.refs_3_) | copy-start | bytes 3944452
  58.8 31.1 %collective-permute-start.11 = (bf16[5136,128]{1,0:T(8,128)(2,1)S(1)}, bf16[5136,128]{1,0:T(8,128)(2,1)S(1)}, u32[]{:S(2)}, u32[]{:S(2)}) collective-permute-start(bf16[5136,128]{1,0:T(8,128)(2,1)S(1)} %collective-permute-done.3.refs_3_), channel_id=1, source_target_pairs={{0,96},{1,97},{2,98},{3,99},{4,100},{5,101},{6,102},{7,103},{8,104... | collective-permute-start | bytes 3944456 | tf_op jit(solution)/shard_map/ppermute | solution.py:27
  62.1 29.1 %collective-permute-start.10 = (bf16[5136,128]{1,0:T(8,128)(2,1)S(1)}, bf16[5136,128]{1,0:T(8,128)(2,1)S(1)}, u32[]{:S(2)}, u32[]{:S(2)}) collective-permute-start(bf16[5136,128]{1,0:T(8,128)(2,1)S(1)} %collective-permute-done.3.refs_3_), channel_id=1, source_target_pairs={{0,32},{1,33},{2,34},{3,35},{4,36},{5,37},{6,38},{7,39},{8,40},{9,... | collective-permute-start | bytes 3944456 | tf_op jit(solution)/shard_map/ppermute | solution.py:27
  62.1 20.1 %collective-permute-start.14 = (bf16[96,5120]{1,0:T(8,128)(2,1)S(1)}, bf16[96,5120]{1,0:T(8,128)(2,1)}, u32[]{:S(2)}, u32[]{:S(2)}) collective-permute-start(bf16[96,5120]{1,0:T(8,128)(2,1)S(1)} %get-tuple-element.82), channel_id=1, source_target_pairs={{0,6},{1,7},{2,0},{3,1},{4,2},{5,3},{6,4},{7,5},{8,14},{9,15},{10,... | collective-permute-start | bytes 2949128 | tf_op jit(solution)/shard_map/ppermute | solution.py:27
  64.4 22.0 %collective-permute-start.13 = (bf16[96,5120]{1,0:T(8,128)(2,1)S(1)}, bf16[96,5120]{1,0:T(8,128)(2,1)}, u32[]{:S(2)}, u32[]{:S(2)}) collective-permute-start(bf16[96,5120]{1,0:T(8,128)(2,1)S(1)} %get-tuple-element.79), channel_id=1, source_target_pairs={{0,2},{1,3},{2,4},{3,5},{4,6},{5,7},{6,0},{7,1},{8,10},{9,11},{10,... | collective-permute-start | bytes 2949128 | tf_op jit(solution)/shard_map/ppermute | solution.py:27
  64.4 30.2 %collective-permute-start.12 = (bf16[5136,128]{1,0:T(8,128)(2,1)S(1)}, bf16[5136,128]{1,0:T(8,128)(2,1)S(1)}, u32[]{:S(2)}, u32[]{:S(2)}) collective-permute-start(bf16[5136,128]{1,0:T(8,128)(2,1)S(1)} %get-tuple-element.80.refs_4_), channel_id=1, source_target_pairs={{0,16},{1,17},{2,18},{3,19},{4,20},{5,21},{6,22},{7,23},{8,24},{9,... | collective-permute-start | bytes 3944456 | tf_op jit(solution)/shard_map/ppermute | solution.py:27
  82.2 15.4 %collective-permute-start.17 = (bf16[96,5120]{1,0:T(8,128)(2,1)}, bf16[96,5120]{1,0:T(8,128)(2,1)}, u32[]{:S(2)}, u32[]{:S(2)}) collective-permute-start(bf16[96,5120]{1,0:T(8,128)(2,1)} %collective-permute-done.9.refs_5_.refs_10_), channel_id=1, source_target_pairs={{0,1},{1,0},{2,3},{3,2},{4,5},{5,4},{6,7},{7,6},{8,9},{9,8},{10,11... | collective-permute-start | bytes 2949128 | tf_op jit(solution)/shard_map/ppermute | solution.py:27
  86.4 9.5 %collective-permute-start.16 = (bf16[96,5120]{1,0:T(8,128)(2,1)}, bf16[96,5120]{1,0:T(8,128)(2,1)}, u32[]{:S(2)}, u32[]{:S(2)}) collective-permute-start(bf16[96,5120]{1,0:T(8,128)(2,1)} %collective-permute-done.14.refs_9_.refs_1_), channel_id=1, source_target_pairs={{0,1},{1,0},{2,3},{3,2},{4,5},{5,4},{6,7},{7,6},{8,9},{9,8},{10,11... | collective-permute-start | bytes 2949128 | tf_op jit(solution)/shard_map/ppermute | solution.py:27
  89.9 4.7 %copy-start.16 = (bf16[5136,128]{1,0:T(8,128)(2,1)}, bf16[5136,128]{1,0:T(8,128)(2,1)S(1)}, u32[]{:S(2)}) copy-start(bf16[5136,128]{1,0:T(8,128)(2,1)S(1)} %collective-permute-done.11.refs_6_) | copy-start | bytes 3944452
  89.9 6.0 %collective-permute-start.15 = (bf16[96,5120]{1,0:T(8,128)(2,1)}, bf16[96,5120]{1,0:T(8,128)(2,1)}, u32[]{:S(2)}, u32[]{:S(2)}) collective-permute-start(bf16[96,5120]{1,0:T(8,128)(2,1)} %collective-permute-done.13.refs_8_.refs_0_), channel_id=1, source_target_pairs={{0,1},{1,0},{2,3},{3,2},{4,5},{5,4},{6,7},{7,6},{8,9},{9,8},{10,11... | collective-permute-start | bytes 2949128 | tf_op jit(solution)/shard_map/ppermute | solution.py:27
  91.2 3.4 %copy-start.17 = (bf16[5136,128]{1,0:T(8,128)(2,1)}, bf16[5136,128]{1,0:T(8,128)(2,1)S(1)}, u32[]{:S(2)}) copy-start(bf16[5136,128]{1,0:T(8,128)(2,1)S(1)} %collective-permute-done.10.refs_5_) | copy-start | bytes 3944452
  91.2 7.1 %collective-permute-start.18 = (bf16[96,5120]{1,0:T(8,128)(2,1)}, bf16[96,5120]{1,0:T(8,128)(2,1)}, u32[]{:S(2)}, u32[]{:S(2)}) collective-permute-start(bf16[96,5120]{1,0:T(8,128)(2,1)} %collective-permute-done.8.refs_3_.refs_11_), channel_id=1, source_target_pairs={{0,1},{1,0},{2,3},{3,2},{4,5},{5,4},{6,7},{7,6},{8,9},{9,8},{10,11... | collective-permute-start | bytes 2949128 | tf_op jit(solution)/shard_map/ppermute | solution.py:27
  95.9 19.4 %collective-permute-start.19 = (bf16[96,5120]{1,0:T(8,128)(2,1)S(1)}, bf16[96,5120]{1,0:T(8,128)(2,1)}, u32[]{:S(2)}, u32[]{:S(2)}) collective-permute-start(bf16[96,5120]{1,0:T(8,128)(2,1)S(1)} %collective-permute-done.7.refs_4_.refs_2_), channel_id=1, source_target_pairs={{0,1},{1,0},{2,3},{3,2},{4,5},{5,4},{6,7},{7,6},{8,9},{9,8},{10,11... | collective-permute-start | bytes 2949128 | tf_op jit(solution)/shard_map/ppermute | solution.py:27
  97.1 18.2 %collective-permute-start.20 = (bf16[96,5120]{1,0:T(8,128)(2,1)S(1)}, bf16[96,5120]{1,0:T(8,128)(2,1)}, u32[]{:S(2)}, u32[]{:S(2)}) collective-permute-start(bf16[96,5120]{1,0:T(8,128)(2,1)S(1)} %collective-permute-done.6.refs_2_.refs_3_), channel_id=1, source_target_pairs={{0,1},{1,0},{2,3},{3,2},{4,5},{5,4},{6,7},{7,6},{8,9},{9,8},{10,11... | collective-permute-start | bytes 2949128 | tf_op jit(solution)/shard_map/ppermute | solution.py:27
  97.2 18.1 %collective-permute-start.21 = (bf16[96,5120]{1,0:T(8,128)(2,1)}, bf16[96,5120]{1,0:T(8,128)(2,1)}, u32[]{:S(2)}, u32[]{:S(2)}) collective-permute-start(bf16[96,5120]{1,0:T(8,128)(2,1)} %copy-done.19), channel_id=1, source_target_pairs={{0,1},{1,0},{2,3},{3,2},{4,5},{5,4},{6,7},{7,6},{8,9},{9,8},{10,11... | collective-permute-start | bytes 2949128 | tf_op jit(solution)/shard_map/ppermute | solution.py:27
  97.6 17.7 %collective-permute-start.22 = (bf16[96,5120]{1,0:T(8,128)(2,1)S(1)}, bf16[96,5120]{1,0:T(8,128)(2,1)}, u32[]{:S(2)}, u32[]{:S(2)}) collective-permute-start(bf16[96,5120]{1,0:T(8,128)(2,1)S(1)} %copy-done.9), channel_id=1, source_target_pairs={{0,1},{1,0},{2,3},{3,2},{4,5},{5,4},{6,7},{7,6},{8,9},{9,8},{10,11... | collective-permute-start | bytes 2949128 | tf_op jit(solution)/shard_map/ppermute | solution.py:27
  115.3 6.8 %copy-start.8 = (bf16[96,5120]{1,0:T(8,128)(2,1)S(1)}, bf16[96,5120]{1,0:T(8,128)(2,1)}, u32[]{:S(2)}) copy-start(bf16[96,5120]{1,0:T(8,128)(2,1)} %get-tuple-element.95) | copy-start | bytes 2949124
  115.3 2.9 %collective-permute-start.23 = (bf16[96,5120]{1,0:T(8,128)(2,1)}, bf16[96,5120]{1,0:T(8,128)(2,1)S(1)}, u32[]{:S(2)}, u32[]{:S(2)}) collective-permute-start(bf16[96,5120]{1,0:T(8,128)(2,1)} %get-tuple-element.94), channel_id=1, source_target_pairs={{0,1},{1,0},{2,3},{3,2},{4,5},{5,4},{6,7},{7,6},{8,9},{9,8},{10,11... | collective-permute-start | bytes 2949128 | tf_op jit(solution)/shard_map/ppermute | solution.py:27
  115.8 6.3 %collective-permute-start.24 = (bf16[96,5120]{1,0:T(8,128)(2,1)}, bf16[96,5120]{1,0:T(8,128)(2,1)S(1)}, u32[]{:S(2)}, u32[]{:S(2)}) collective-permute-start(bf16[96,5120]{1,0:T(8,128)(2,1)} %get-tuple-element.96), channel_id=1, source_target_pairs={{0,1},{1,0},{2,3},{3,2},{4,5},{5,4},{6,7},{7,6},{8,9},{9,8},{10,11... | collective-permute-start | bytes 2949128 | tf_op jit(solution)/shard_map/ppermute | solution.py:27
  115.9 7.6 %collective-permute-start.25 = (bf16[96,5120]{1,0:T(8,128)(2,1)}, bf16[96,5120]{1,0:T(8,128)(2,1)S(1)}, u32[]{:S(2)}, u32[]{:S(2)}) collective-permute-start(bf16[96,5120]{1,0:T(8,128)(2,1)} %get-tuple-element.98), channel_id=1, source_target_pairs={{0,1},{1,0},{2,3},{3,2},{4,5},{5,4},{6,7},{7,6},{8,9},{9,8},{10,11... | collective-permute-start | bytes 2949128 | tf_op jit(solution)/shard_map/ppermute | solution.py:27
  119.7 3.8 %copy-start.7 = (bf16[96,5120]{1,0:T(8,128)(2,1)S(1)}, bf16[96,5120]{1,0:T(8,128)(2,1)}, u32[]{:S(2)}) copy-start(bf16[96,5120]{1,0:T(8,128)(2,1)} %get-tuple-element.97) | copy-start | bytes 2949124
  119.7 29.9 %collective-permute-start.28 = (bf16[96,5120]{1,0:T(8,128)(2,1)S(1)}, bf16[96,5120]{1,0:T(8,128)(2,1)}, u32[]{:S(2)}, u32[]{:S(2)}) collective-permute-start(bf16[96,5120]{1,0:T(8,128)(2,1)S(1)} %add_convert_fusion.4), channel_id=1, source_target_pairs={{0,8},{1,9},{2,10},{3,11},{4,12},{5,13},{6,14},{7,15},{8,0},{9,1},... | collective-permute-start | bytes 2949128 | tf_op jit(solution)/shard_map/ppermute | solution.py:27
  122.4 27.2 %collective-permute-start.29 = (bf16[96,5120]{1,0:T(8,128)(2,1)S(1)}, bf16[96,5120]{1,0:T(8,128)(2,1)S(1)}, u32[]{:S(2)}, u32[]{:S(2)}) collective-permute-start(bf16[96,5120]{1,0:T(8,128)(2,1)S(1)} %add_convert_fusion.3), channel_id=1, source_target_pairs={{0,2},{1,3},{2,4},{3,5},{4,6},{5,7},{6,0},{7,1},{8,10},{9,11},{10,... | collective-permute-start | bytes 2949128 | tf_op jit(solution)/shard_map/ppermute | solution.py:27
  123.8 25.8 %collective-permute-start.30 = (bf16[96,5120]{1,0:T(8,128)(2,1)S(1)}, bf16[96,5120]{1,0:T(8,128)(2,1)S(1)}, u32[]{:S(2)}, u32[]{:S(2)}) collective-permute-start(bf16[96,5120]{1,0:T(8,128)(2,1)S(1)} %add_convert_fusion.2), channel_id=1, source_target_pairs={{0,6},{1,7},{2,0},{3,1},{4,2},{5,3},{6,4},{7,5},{8,14},{9,15},{10,... | collective-permute-start | bytes 2949128 | tf_op jit(solution)/shard_map/ppermute | solution.py:27
  145.9 3.0 %collective-permute-start.26 = (bf16[48,5120]{1,0:T(8,128)(2,1)}, bf16[48,5120]{1,0:T(8,128)(2,1)S(1)}, u32[]{:S(2)}, u32[]{:S(2)}) collective-permute-start(bf16[48,5120]{1,0:T(8,128)(2,1)} %get-tuple-element.108), channel_id=1, source_target_pairs={{0,1},{1,0},{2,3},{3,2},{4,5},{5,4},{6,7},{7,6},{8,9},{9,8},{10,11... | collective-permute-start | bytes 1474568 | tf_op jit(solution)/shard_map/ppermute | solution.py:27
  147.2 2.4 %collective-permute-start.27 = (bf16[48,5120]{1,0:T(8,128)(2,1)}, bf16[48,5120]{1,0:T(8,128)(2,1)S(1)}, u32[]{:S(2)}, u32[]{:S(2)}) collective-permute-start(bf16[48,5120]{1,0:T(8,128)(2,1)} %get-tuple-element.109), channel_id=1, source_target_pairs={{0,1},{1,0},{2,3},{3,2},{4,5},{5,4},{6,7},{7,6},{8,9},{9,8},{10,11... | collective-permute-start | bytes 1474568 | tf_op jit(solution)/shard_map/ppermute | solution.py:27
  149.6 4.1 %copy-start.22 = (bf16[48,5120]{1,0:T(8,128)(2,1)S(1)}, bf16[48,5120]{1,0:T(8,128)(2,1)}, u32[]{:S(2)}) copy-start(bf16[48,5120]{1,0:T(8,128)(2,1)} %get-tuple-element.122) | copy-start | bytes 1474564
  149.6 4.7 %copy-start.20 = (bf16[96,5120]{1,0:T(8,128)(2,1)S(1)}, bf16[96,5120]{1,0:T(8,128)(2,1)}, u32[]{:S(2)}) copy-start(bf16[96,5120]{1,0:T(8,128)(2,1)} %get-tuple-element.124) | copy-start | bytes 2949124
  149.6 4.8 %copy-start.11 = (bf16[48,5120]{1,0:T(8,128)(2,1)S(1)}, bf16[48,5120]{1,0:T(8,128)(2,1)}, u32[]{:S(2)}) copy-start(bf16[48,5120]{1,0:T(8,128)(2,1)} %get-tuple-element.119) | copy-start | bytes 1474564
  149.7 7.6 %copy-start.5 = (bf16[96,5120]{1,0:T(8,128)(2,1)S(1)}, bf16[96,5120]{1,0:T(8,128)(2,1)}, u32[]{:S(2)}) copy-start(bf16[96,5120]{1,0:T(8,128)(2,1)} %get-tuple-element.123) | copy-start | bytes 2949124
  149.7 4.8 %collective-permute-start.31 = (bf16[48,5120]{1,0:T(8,128)(2,1)}, bf16[48,5120]{1,0:T(8,128)(2,1)S(1)}, u32[]{:S(2)}, u32[]{:S(2)}) collective-permute-start(bf16[48,5120]{1,0:T(8,128)(2,1)} %get-tuple-element.120), channel_id=1, source_target_pairs={{0,1},{1,0},{2,3},{3,2},{4,5},{5,4},{6,7},{7,6},{8,9},{9,8},{10,11... | collective-permute-start | bytes 1474568 | tf_op jit(solution)/shard_map/ppermute | solution.py:27
  152.2 17.8 %collective-permute-start.35 = (bf16[48,5120]{1,0:T(8,128)(2,1)S(1)}, bf16[48,5120]{1,0:T(8,128)(2,1)}, u32[]{:S(2)}, u32[]{:S(2)}) collective-permute-start(bf16[48,5120]{1,0:T(8,128)(2,1)S(1)} %get-tuple-element.147), channel_id=1, source_target_pairs={{0,6},{1,7},{2,0},{3,1},{4,2},{5,3},{6,4},{7,5},{8,14},{9,15},{10,... | collective-permute-start | bytes 1474568 | tf_op jit(solution)/shard_map/ppermute | solution.py:27
  153.7 16.4 %collective-permute-start.34 = (bf16[48,5120]{1,0:T(8,128)(2,1)S(1)}, bf16[48,5120]{1,0:T(8,128)(2,1)}, u32[]{:S(2)}, u32[]{:S(2)}) collective-permute-start(bf16[48,5120]{1,0:T(8,128)(2,1)S(1)} %get-tuple-element.148), channel_id=1, source_target_pairs={{0,2},{1,3},{2,4},{3,5},{4,6},{5,7},{6,0},{7,1},{8,10},{9,11},{10,... | collective-permute-start | bytes 1474568 | tf_op jit(solution)/shard_map/ppermute | solution.py:27
  153.7 4.8 %collective-permute-start.32 = (bf16[48,5120]{1,0:T(8,128)(2,1)S(1)}, bf16[48,5120]{1,0:T(8,128)(2,1)S(1)}, u32[]{:S(2)}, u32[]{:S(2)}) collective-permute-start(bf16[48,5120]{1,0:T(8,128)(2,1)S(1)} %copy-done.22), channel_id=1, source_target_pairs={{0,1},{1,0},{2,3},{3,2},{4,5},{5,4},{6,7},{7,6},{8,9},{9,8},{10,11... | collective-permute-start | bytes 1474568 | tf_op jit(solution)/shard_map/ppermute | solution.py:27
  154.3 2.9 %collective-permute-start.33 = (bf16[96,5120]{1,0:T(8,128)(2,1)S(1)}, bf16[96,5120]{1,0:T(8,128)(2,1)S(1)}, u32[]{:S(2)}, u32[]{:S(2)}) collective-permute-start(bf16[96,5120]{1,0:T(8,128)(2,1)S(1)} %copy-done.20), channel_id=1, source_target_pairs={{0,1},{1,0},{2,3},{3,2},{4,5},{5,4},{6,7},{7,6},{8,9},{9,8},{10,11... | collective-permute-start | bytes 2949128 | tf_op jit(solution)/shard_map/ppermute | solution.py:27
  154.6 4.0 %copy-start.10 = (bf16[48,5120]{1,0:T(8,128)(2,1)S(1)}, bf16[48,5120]{1,0:T(8,128)(2,1)}, u32[]{:S(2)}) copy-start(bf16[48,5120]{1,0:T(8,128)(2,1)} %get-tuple-element.121) | copy-start | bytes 1474564
  154.6 23.3 %collective-permute-start.36 = (bf16[48,5120]{1,0:T(8,128)(2,1)S(1)}, bf16[48,5120]{1,0:T(8,128)(2,1)S(1)}, u32[]{:S(2)}, u32[]{:S(2)}) collective-permute-start(bf16[48,5120]{1,0:T(8,128)(2,1)S(1)} %add_convert_fusion.8), channel_id=1, source_target_pairs={{0,2},{1,3},{2,4},{3,5},{4,6},{5,7},{6,0},{7,1},{8,10},{9,11},{10,... | collective-permute-start | bytes 1474568 | tf_op jit(solution)/shard_map/ppermute | solution.py:27
  157.8 24.6 %collective-permute-start.38 = (bf16[96,5120]{1,0:T(8,128)(2,1)S(1)}, bf16[96,5120]{1,0:T(8,128)(2,1)S(1)}, u32[]{:S(2)}, u32[]{:S(2)}) collective-permute-start(bf16[96,5120]{1,0:T(8,128)(2,1)S(1)} %add_convert_fusion.1), channel_id=1, source_target_pairs={{0,8},{1,9},{2,10},{3,11},{4,12},{5,13},{6,14},{7,15},{8,0},{9,1},... | collective-permute-start | bytes 2949128 | tf_op jit(solution)/shard_map/ppermute | solution.py:27
  158.7 19.2 %collective-permute-start.37 = (bf16[48,5120]{1,0:T(8,128)(2,1)S(1)}, bf16[48,5120]{1,0:T(8,128)(2,1)S(1)}, u32[]{:S(2)}, u32[]{:S(2)}) collective-permute-start(bf16[48,5120]{1,0:T(8,128)(2,1)S(1)} %add_convert_fusion.7), channel_id=1, source_target_pairs={{0,6},{1,7},{2,0},{3,1},{4,2},{5,3},{6,4},{7,5},{8,14},{9,15},{10,... | collective-permute-start | bytes 1474568 | tf_op jit(solution)/shard_map/ppermute | solution.py:27
  170.0 16.7 %copy-start.12 = (bf16[48,5120]{1,0:T(8,128)(2,1)S(1)}, bf16[48,5120]{1,0:T(8,128)(2,1)}, u32[]{:S(2)}) copy-start(bf16[48,5120]{1,0:T(8,128)(2,1)} %get-tuple-element.140) | copy-start | bytes 1474564
  182.4 5.5 %copy-start.21 = (bf16[96,5120]{1,0:T(8,128)(2,1)S(1)}, bf16[96,5120]{1,0:T(8,128)(2,1)}, u32[]{:S(2)}) copy-start(bf16[96,5120]{1,0:T(8,128)(2,1)} %get-tuple-element.143) | copy-start | bytes 2949124
  182.4 19.9 %copy-start.6 = (bf16[96,5120]{1,0:T(8,128)(2,1)S(1)}, bf16[96,5120]{1,0:T(8,128)(2,1)}, u32[]{:S(2)}) copy-start(bf16[96,5120]{1,0:T(8,128)(2,1)} %get-tuple-element.135) | copy-start | bytes 2949124
  182.4 2.9 %collective-permute-start.39 = (bf16[48,5120]{1,0:T(8,128)(2,1)}, bf16[48,5120]{1,0:T(8,128)(2,1)S(1)}, u32[]{:S(2)}, u32[]{:S(2)}) collective-permute-start(bf16[48,5120]{1,0:T(8,128)(2,1)} %get-tuple-element.138), channel_id=1, source_target_pairs={{0,1},{1,0},{2,3},{3,2},{4,5},{5,4},{6,7},{7,6},{8,9},{9,8},{10,11... | collective-permute-start | bytes 1474568 | tf_op jit(solution)/shard_map/ppermute | solution.py:27
  183.6 3.1 %collective-permute-start.40 = (bf16[48,5120]{1,0:T(8,128)(2,1)}, bf16[48,5120]{1,0:T(8,128)(2,1)S(1)}, u32[]{:S(2)}, u32[]{:S(2)}) collective-permute-start(bf16[48,5120]{1,0:T(8,128)(2,1)} %get-tuple-element.141), channel_id=1, source_target_pairs={{0,1},{1,0},{2,3},{3,2},{4,5},{5,4},{6,7},{7,6},{8,9},{9,8},{10,11... | collective-permute-start | bytes 1474568 | tf_op jit(solution)/shard_map/ppermute | solution.py:27
  187.9 14.4 %collective-permute-start.41 = (bf16[96,5120]{1,0:T(8,128)(2,1)S(1)}, bf16[96,5120]{1,0:T(8,128)(2,1)S(1)}, u32[]{:S(2)}, u32[]{:S(2)}) collective-permute-start(bf16[96,5120]{1,0:T(8,128)(2,1)S(1)} %copy-done.21), channel_id=1, source_target_pairs={{0,1},{1,0},{2,3},{3,2},{4,5},{5,4},{6,7},{7,6},{8,9},{9,8},{10,11... | collective-permute-start | bytes 2949128 | tf_op jit(solution)/shard_map/ppermute | solution.py:27
  188.3 13.9 %collective-permute-start.42 = (bf16[48,5120]{1,0:T(8,128)(2,1)S(1)}, bf16[48,5120]{1,0:T(8,128)(2,1)S(1)}, u32[]{:S(2)}, u32[]{:S(2)}) collective-permute-start(bf16[48,5120]{1,0:T(8,128)(2,1)S(1)} %add_convert_fusion.6), channel_id=1, source_target_pairs={{0,2},{1,3},{2,4},{3,5},{4,6},{5,7},{6,0},{7,1},{8,10},{9,11},{10,... | collective-permute-start | bytes 1474568 | tf_op jit(solution)/shard_map/ppermute | solution.py:27
  188.4 13.9 %collective-permute-start.43 = (bf16[48,5120]{1,0:T(8,128)(2,1)S(1)}, bf16[48,5120]{1,0:T(8,128)(2,1)S(1)}, u32[]{:S(2)}, u32[]{:S(2)}) collective-permute-start(bf16[48,5120]{1,0:T(8,128)(2,1)S(1)} %add_convert_fusion.5), channel_id=1, source_target_pairs={{0,6},{1,7},{2,0},{3,1},{4,2},{5,3},{6,4},{7,5},{8,14},{9,15},{10,... | collective-permute-start | bytes 1474568 | tf_op jit(solution)/shard_map/ppermute | solution.py:27
  (3 other events, 4.7 us)

commit v6 on v4

--- a/solution.py
+++ b/solution.py
@@ -302,30 +302,32 @@
     part, weights = part[:6], part[6:]
     part = after(part, o_right, o_left, o_z, o_own)
     got = swap(*part[3:])
-    far_z, right, left = (add(part[i], got[i]).astype(BF16) for i in range(3))
+    right, left = (add(part[i], got[i]).astype(BF16) for i in (1, 2))
+    far_z = add(after(part[0], right, left), got[0]).astype(BF16)
     far_in, z_right, z_left = move(far_z, zh=1), move(right, dx=1), move(left, dx=-1)
 
     ids = after(ids, far_z, right, left)
-    groups = halves(0) + [whole(tb, o_right), whole(ta, o_left), whole(tz, o_z)]
-    part = sums(ids, groups, [count] * 4 + [h_rows] * 2 + [count] * 3, weights)
-    part, weights = part[:9], part[9:]
-    far, near, here_z, near_sib, here_sib = part[0], part[1:3], part[3], part[6:8], part[8]
-    got = swap(*part[4:6])
-    far, got, far_in, z_right, z_left = after((far, got, far_in, z_right, z_left))
+    groups = halves(0) + [whole(tb, o_right), whole(ta, o_left)]
+    part = sums(ids, groups, [count] * 3 + [h_rows] * 2 + [count] * 2, weights)
+    part, weights = part[:7], part[7:]
+    far, near, near_sib = part[0], part[1:3], part[5:7]
+    got = swap(*part[3:5])
+    far, got, z_right, z_left, far_in = after((far, got, z_right, z_left, far_in))
     top = add(far[:h_rows], got[0], far_in[:h_rows]).astype(BF16)
     low = add(far[h_rows:], got[1], far_in[h_rows:]).astype(BF16)
     past_top, past_low = move(top, dx=1), move(low, dx=-1)
 
-    near_sib, here_sib = after((near_sib, here_sib), top, low)
-    got = swap(*near_sib, here_sib)
+    near_sib = after(near_sib, top, low)
+    got = swap(*near_sib)
     ids = after(ids, top, low)
-    here, own_sib = sums(ids, [whole(tokens, o_own)], [count] * 2, weights)[:2]
-    near, got, past_top, past_low, here = after((near, got, past_top, past_low, here))
+    here_z, here, z_sib, own_sib = sums(ids, [whole(tz, o_z), whole(tokens, o_own)], [count] * 4, weights)[:4]
+    near, got, past_top, past_low, here_z = after((near, got, past_top, past_low, here_z))
     zero = jnp.zeros((), BF16)
     past_top = lax.pad(past_top, zero, ((0, h_rows, 0), (0, 0, 0)))
     past_low = lax.pad(past_low, zero, ((h_rows, 0, 0), (0, 0, 0)))
     right, left = (add(near[i], got[i], past).astype(BF16) for i, past in enumerate((past_top, past_low)))
-    across = add(here_z, got[2], z_right, z_left).astype(BF16)
+    z_sib, own_sib = after((z_sib, own_sib), near, past_top, past_low)
+    across = add(here_z, *swap(z_sib), z_right, z_left).astype(BF16)
     right_in, left_in, across_in = move(right, dx=1), move(left, dx=-1), move(across, zh=1)
     own_sib = after(own_sib, right, left, across)
     return add(here, *swap(own_sib), right_in, left_in, across_in).astype(BF16)

time: 202 us -> 202 us (level)
  starting transfers between devices: 52.2 us -> 56 us
  waiting for transfers between devices: 85.5 us -> 82.5 us
    ppermute x40, starting transfers between devices: 52.2 us -> 56 us  [move(): return lax.ppermute(value, AXES, pairs)]
    ppermute x40, waiting for transfers between devices: 85.5 us -> 82.5 us  [move(): return lax.ppermute(value, AXES, pairs)]
  transfers between devices with their start and end apart: 40 -> 40, of which waited for: 16 -> 16; matrix products, arithmetic and copies ran while one was open for 1% -> 2% of each run, Pallas kernels for 24% -> 24%
where the time goes in v6:
time: 202 us
  waiting for transfers between devices  82.5 us (41%)
  starting transfers between devices  56 us (28%)
  Pallas kernels  47.9 us (24%)
  other arithmetic  9.74 us (5%)
  local copies, waits for them, and re-layouts  4.19 us (2%)
    ppermute x40, waiting for transfers between devices, move(): return lax.ppermute(value, AXES, pairs)  82.5 us
    ppermute x40, starting transfers between devices, move(): return lax.ppermute(value, AXES, pairs)  56 us
    pallas_call x2, Pallas kernels, sums(): return tuple(run(ids, sidx, scale_table, *pieces, *weights))  28.6 us
    pallas_call x1, Pallas kernels, sums(): return tuple(run(ids, sidx, scale_table, *sources, *pieces, down_weight))  16.9 us
  transfers between devices with their start and end apart: 40, of which 16 were waited for; matrix products, arithmetic and copies ran while one was open for 2% of the time, Pallas kernels for 24%

profile of v6, /device:TPU:1, one launch (start us, length us, event | category | flops | bytes accessed | tf_op | source)
XLA Modules:
  0.0 201.9 jit_solution(12053742827011433421)
XLA Ops:
  1.3 1.3 copy-done.1
  2.6 0.1 shard_map.64.refs_0_
  2.8 2.2 %collective-permute-start = (bf16[5136,128]{1,0:T(8,128)(2,1)S(1)}, bf16[5136,128]{1,0:T(8,128)(2,1)S(1)}, u32[]{:S(2)}, u32[]{:S(2)}) collective-permute-start(bf16[5136,128]{1,0:T(8,128)(2,1)S(1)} %shard_map.64.refs_0_), channel_id=1, source_target_pairs={{0,32},{1,33},{2,34},{3,35},{4,36},{5,37},{6,38},{7,39},{8,40},{9,... | collective-permute-start | bytes 3944456 | tf_op jit(solution)/shard_map/ppermute | solution.py:27
  5.0 3.6 %collective-permute-start.2 = (bf16[96,5120]{1,0:T(8,128)(2,1)S(1)}, bf16[96,5120]{1,0:T(8,128)(2,1)S(1)}, u32[]{:S(2)}, u32[]{:S(2)}) collective-permute-start(bf16[96,5120]{1,0:T(8,128)(2,1)S(1)} %copy-done.17), channel_id=1, source_target_pairs={{0,8},{1,9},{2,10},{3,11},{4,12},{5,13},{6,14},{7,15},{8,0},{9,1},... | collective-permute-start | bytes 2949128 | tf_op jit(solution)/shard_map/ppermute | solution.py:27
  8.6 2.5 %collective-permute-start.7 = (bf16[96,5120]{1,0:T(8,128)(2,1)S(1)}, bf16[96,5120]{1,0:T(8,128)(2,1)S(1)}, u32[]{:S(2)}, u32[]{:S(2)}) collective-permute-start(bf16[96,5120]{1,0:T(8,128)(2,1)S(1)} %copy-done.17), channel_id=1, source_target_pairs={{0,6},{1,7},{2,0},{3,1},{4,2},{5,3},{6,4},{7,5},{8,14},{9,15},{10,... | collective-permute-start | bytes 2949128 | tf_op jit(solution)/shard_map/ppermute | solution.py:27
  11.1 2.7 %collective-permute-start.1 = (bf16[5136,128]{1,0:T(8,128)(2,1)S(1)}, bf16[5136,128]{1,0:T(8,128)(2,1)S(1)}, u32[]{:S(2)}, u32[]{:S(2)}) collective-permute-start(bf16[5136,128]{1,0:T(8,128)(2,1)S(1)} %shard_map.64.refs_0_), channel_id=1, source_target_pairs={{0,96},{1,97},{2,98},{3,99},{4,100},{5,101},{6,102},{7,103},{8,104... | collective-permute-start | bytes 3944456 | tf_op jit(solution)/shard_map/ppermute | solution.py:27
  13.8 16.0 %collective-permute-done.2.refs_0_ = bf16[96,5120]{1,0:T(8,128)(2,1)S(1)} collective-permute-done((bf16[96,5120]{1,0:T(8,128)(2,1)S(1)}, bf16[96,5120]{1,0:T(8,128)(2,1)S(1)}, u32[]{:S(2)}, u32[]{:S(2)}) %collective-permute-start.2) | collective-permute-done | bytes 983072 | tf_op jit(solution)/shard_map/ppermute | solution.py:27
  29.8 0.7 collective-permute-start.3
  30.5 0.4 collective-permute-done.7.refs_4_.refs_2_
  30.9 3.1 %collective-permute-done.6.refs_2_.refs_3_ = bf16[96,5120]{1,0:T(8,128)(2,1)S(1)} collective-permute-done((bf16[96,5120]{1,0:T(8,128)(2,1)S(1)}, bf16[96,5120]{1,0:T(8,128)(2,1)S(1)}, u32[]{:S(2)}, u32[]{:S(2)}) %collective-permute-start.6) | collective-permute-done | bytes 983072 | tf_op jit(solution)/shard_map/ppermute | solution.py:27
  34.1 0.3 collective-permute-start.9
  34.4 1.1 collective-permute-start.8
  35.6 1.4 collective-permute-start.4
  37.0 3.7 %collective-permute-done.1.refs_2_ = bf16[5136,128]{1,0:T(8,128)(2,1)S(1)} collective-permute-done((bf16[5136,128]{1,0:T(8,128)(2,1)S(1)}, bf16[5136,128]{1,0:T(8,128)(2,1)S(1)}, u32[]{:S(2)}, u32[]{:S(2)}) %collective-permute-start.1) | collective-permute-done | bytes 1314848 | tf_op jit(solution)/shard_map/ppermute | solution.py:27
  40.8 3.6 %collective-permute-start.5 = (bf16[2560,128]{1,0:T(8,128)(2,1)S(1)}, bf16[2560,128]{1,0:T(8,128)(2,1)S(1)}, u32[]{:S(2)}, u32[]{:S(2)}) collective-permute-start(bf16[2560,128]{1,0:T(8,128)(2,1)S(1)} %slice.74), channel_id=1, source_target_pairs={{0,96},{1,97},{2,98},{3,99},{4,100},{5,101},{6,102},{7,103},{8,104... | collective-permute-start | bytes 1966088 | tf_op jit(solution)/shard_map/ppermute | solution.py:27
  44.4 10.7 %collective-permute-done.9.refs_5_.refs_10_ = bf16[96,5120]{1,0:T(8,128)(2,1)} collective-permute-done((bf16[96,5120]{1,0:T(8,128)(2,1)S(1)}, bf16[96,5120]{1,0:T(8,128)(2,1)}, u32[]{:S(2)}, u32[]{:S(2)}) %collective-permute-start.9) | collective-permute-done | bytes 983072 | tf_op jit(solution)/shard_map/ppermute | solution.py:27
  55.0 1.6 collective-permute-done.8.refs_3_.refs_11_
  56.6 2.2 %shard_map.65 = (bf16[5136,128]{1,0:T(8,128)(2,1)S(1)}, bf16[96,5120]{1,0:T(8,128)(2,1)S(1)}, bf16[96,5120]{1,0:T(8,128)(2,1)S(1)}) custom-call(bf16[2576,128]{1,0:T(8,128)(2,1)S(1)} %collective-permute-done.4.refs_0_, bf16[2560,128]{1,0:T(8,128)(2,1)S(1)} %collective-permute-done.5.refs_1_, bf16[96,5120]{1,0:T(8,128)(2,1)S(1)} %collective-permute-done.6.refs_2_.refs_3_, ...), custom_call_target="tpu_custom_call" | custom-call | flops 1 | bytes 1 | tf_op jit(solution)/shard_map/pallas_call | solution.py:82
  58.8 3.3 %collective-permute-start.11 = (bf16[5136,128]{1,0:T(8,128)(2,1)S(1)}, bf16[5136,128]{1,0:T(8,128)(2,1)S(1)}, u32[]{:S(2)}, u32[]{:S(2)}) collective-permute-start(bf16[5136,128]{1,0:T(8,128)(2,1)S(1)} %collective-permute-done.3.refs_3_), channel_id=1, source_target_pairs={{0,96},{1,97},{2,98},{3,99},{4,100},{5,101},{6,102},{7,103},{8,104... | collective-permute-start | bytes 3944456 | tf_op jit(solution)/shard_map/ppermute | solution.py:27
  62.1 2.3 %collective-permute-start.14 = (bf16[96,5120]{1,0:T(8,128)(2,1)S(1)}, bf16[96,5120]{1,0:T(8,128)(2,1)}, u32[]{:S(2)}, u32[]{:S(2)}) collective-permute-start(bf16[96,5120]{1,0:T(8,128)(2,1)S(1)} %get-tuple-element.70), channel_id=1, source_target_pairs={{0,6},{1,7},{2,0},{3,1},{4,2},{5,3},{6,4},{7,5},{8,14},{9,15},{10,... | collective-permute-start | bytes 2949128 | tf_op jit(solution)/shard_map/ppermute | solution.py:27
  64.4 0.6 collective-permute-start.12
  65.1 17.1 %collective-permute-done.14.refs_9_.refs_1_ = bf16[96,5120]{1,0:T(8,128)(2,1)} collective-permute-done((bf16[96,5120]{1,0:T(8,128)(2,1)S(1)}, bf16[96,5120]{1,0:T(8,128)(2,1)}, u32[]{:S(2)}, u32[]{:S(2)}) %collective-permute-start.14) | collective-permute-done | bytes 983072 | tf_op jit(solution)/shard_map/ppermute | solution.py:27
  82.2 4.2 %collective-permute-start.17 = (bf16[96,5120]{1,0:T(8,128)(2,1)}, bf16[96,5120]{1,0:T(8,128)(2,1)}, u32[]{:S(2)}, u32[]{:S(2)}) collective-permute-start(bf16[96,5120]{1,0:T(8,128)(2,1)} %collective-permute-done.9.refs_5_.refs_10_), channel_id=1, source_target_pairs={{0,1},{1,0},{2,3},{3,2},{4,5},{5,4},{6,7},{7,6},{8,9},{9,8},{10,11... | collective-permute-start | bytes 2949128 | tf_op jit(solution)/shard_map/ppermute | solution.py:27
  86.4 3.5 %collective-permute-start.16 = (bf16[96,5120]{1,0:T(8,128)(2,1)}, bf16[96,5120]{1,0:T(8,128)(2,1)}, u32[]{:S(2)}, u32[]{:S(2)}) collective-permute-start(bf16[96,5120]{1,0:T(8,128)(2,1)} %collective-permute-done.14.refs_9_.refs_1_), channel_id=1, source_target_pairs={{0,1},{1,0},{2,3},{3,2},{4,5},{5,4},{6,7},{7,6},{8,9},{9,8},{10,11... | collective-permute-start | bytes 2949128 | tf_op jit(solution)/shard_map/ppermute | solution.py:27
  89.9 1.3 collective-permute-start.15
  91.2 3.4 %collective-permute-start.18 = (bf16[96,5120]{1,0:T(8,128)(2,1)}, bf16[96,5120]{1,0:T(8,128)(2,1)}, u32[]{:S(2)}, u32[]{:S(2)}) collective-permute-start(bf16[96,5120]{1,0:T(8,128)(2,1)} %collective-permute-done.8.refs_3_.refs_11_), channel_id=1, source_target_pairs={{0,1},{1,0},{2,3},{3,2},{4,5},{5,4},{6,7},{7,6},{8,9},{9,8},{10,11... | collective-permute-start | bytes 2949128 | tf_op jit(solution)/shard_map/ppermute | solution.py:27
  94.7 1.1 copy-done.16
  95.9 1.2 collective-permute-start.19
  97.2 0.4 collective-permute-start.21
  97.7 0.5 slice_bitcast_fusion.7
  98.2 16.9 %shard_map.66 = (bf16[96,5120]{1,0:T(8,128)(2,1)}, bf16[96,5120]{1,0:T(8,128)(2,1)}, bf16[96,5120]{1,0:T(8,128)(2,1)}, bf16[96,5120]{1,0:T(8,128)(2,1)}, bf16[96...) custom-call(s32[8]{0:T(128)} %get-tuple-element.98.ids, ...), custom_call_target="tpu_custom_call" | custom-call | flops 9059696640 | bytes 27525120 | tf_op jit(solution)/shard_map/pallas_call | solution.py:280
  115.3 1.0 copy-done.19
  116.3 0.4 collective-permute-start.23
  116.8 0.4 collective-permute-start.25
  117.2 1.9 collective-permute-done.23
  119.1 1.4 add_convert_fusion.6
  120.5 1.2 collective-permute-start.28
  121.7 0.3 add_convert_fusion.5
  122.0 1.8 collective-permute-start.29
  123.8 0.2 add_convert_fusion.4
  124.1 2.4 %collective-permute-start.30 = (bf16[96,5120]{1,0:T(8,128)(2,1)S(1)}, bf16[96,5120]{1,0:T(8,128)(2,1)}, u32[]{:S(2)}, u32[]{:S(2)}) collective-permute-start(bf16[96,5120]{1,0:T(8,128)(2,1)S(1)} %add_convert_fusion.4), channel_id=1, source_target_pairs={{0,8},{1,9},{2,10},{3,11},{4,12},{5,13},{6,14},{7,15},{8,0},{9,1},... | collective-permute-start | bytes 2949128 | tf_op jit(solution)/shard_map/ppermute | solution.py:27
  126.5 16.1 %shard_map.67 = (bf16[96,5120]{1,0:T(8,128)(2,1)}, bf16[96,5120]{1,0:T(8,128)(2,1)}, bf16[96,5120]{1,0:T(8,128)(2,1)}, bf16[48,5120]{1,0:T(8,128)(2,1)}, bf16[48...) custom-call(s32[8]{0:T(128)} %get-tuple-element.98.ids, ...), custom_call_target="tpu_custom_call", output_to_operand_aliasing={{7}: (11, {}), {8}: (12, {})} | custom-call | flops 9059696640 | bytes 27525120 | tf_op jit(solution)/shard_map/pallas_call | solution.py:281
  142.6 1.3 collective-permute-start.26
  144.0 1.6 collective-permute-done.26
  145.6 0.7 collective-permute-done.27
  146.3 1.7 collective-permute-done.30
  148.1 2.8 %add_convert_fusion.7 = (bf16[48,5120]{1,0:T(8,128)(2,1)}, bf16[48,5120]{1,0:T(8,128)(2,1)}) fusion(bf16[48,5120]{1,0:T(8,128)(2,1)S(1)} %collective-permute-done.27, bf16[96,5120]{1,0:T(8,128)(2,1)} %collective-permute-done.30, bf16[96,5120]{1,0:T(8,128)(2,1)} %get-tuple-element.94, bf16[48,5120]{1,0:T(8,128)(2,1)S(1)} %collective-permute-done.26), kind=kLoop, calls=%fused_computation.7 | loop fusion | flops 2949120 | bytes 3932160 | tf_op jit(solution)/shard_map/convert_element_type | solution.py:317
  150.9 1.8 collective-permute-start.31
  152.7 1.4 collective-permute-start.34
  154.2 12.5 %shard_map.68 = (bf16[96,5120]{1,0:T(8,128)(2,1)}, bf16[96,5120]{1,0:T(8,128)(2,1)}, bf16[96,5120]{1,0:T(8,128)(2,1)}, bf16[96,5120]{1,0:T(8,128)(2,1)}, bf16[4,...) custom-call(s32[8]{0:T(128)} %get-tuple-element.98.ids, ...), custom_call_target="tpu_custom_call", output_to_operand_aliasing={{4}: (7, {}), {5}: (8, {})} | custom-call | flops 6039797760 | bytes 23592960 | tf_op jit(solution)/shard_map/pallas_call | solution.py:281
  166.7 0.9 collective-permute-done.33
  167.6 1.3 add_convert_fusion.2
  168.9 2.0 collective-permute-start.38
  170.9 1.3 collective-permute-start.35
  172.2 1.3 add_convert_fusion.3
  173.6 0.3 collective-permute-start.37
  173.9 0.6 collective-permute-done.35
  174.4 0.6 add_convert_fusion.1
  175.1 0.5 collective-permute-start.36
  175.5 2.3 %collective-permute-start.39 = (bf16[96,5120]{1,0:T(8,128)(2,1)S(1)}, bf16[96,5120]{1,0:T(8,128)(2,1)S(1)}, u32[]{:S(2)}, u32[]{:S(2)}) collective-permute-start(bf16[96,5120]{1,0:T(8,128)(2,1)S(1)} %add_convert_fusion.1), channel_id=1, source_target_pairs={{0,8},{1,9},{2,10},{3,11},{4,12},{5,13},{6,14},{7,15},{8,0},{9,1},... | collective-permute-start | bytes 2949128 | tf_op jit(solution)/shard_map/ppermute | solution.py:27
  177.8 13.0 %collective-permute-done.38 = bf16[96,5120]{1,0:T(8,128)(2,1)S(1)} collective-permute-done((bf16[96,5120]{1,0:T(8,128)(2,1)S(1)}, bf16[96,5120]{1,0:T(8,128)(2,1)S(1)}, u32[]{:S(2)}, u32[]{:S(2)}) %collective-permute-start.38) | collective-permute-done | bytes 983072 | tf_op jit(solution)/shard_map/ppermute | solution.py:27
  190.9 7.4 %collective-permute-done.37 = bf16[96,5120]{1,0:T(8,128)(2,1)S(1)} collective-permute-done((bf16[96,5120]{1,0:T(8,128)(2,1)S(1)}, bf16[96,5120]{1,0:T(8,128)(2,1)S(1)}, u32[]{:S(2)}, u32[]{:S(2)}) %collective-permute-start.37) | collective-permute-done | bytes 983072 | tf_op jit(solution)/shard_map/ppermute | solution.py:27
  198.3 2.0 collective-permute-done.39
  200.2 1.7 add_convert_fusion
  (88 shorter events, 0.9 us)
Async XLA Ops:
  1.3 1.3 copy-start.1
  2.6 2.3 %copy-start.17 = (bf16[96,5120]{1,0:T(8,128)(2,1)S(1)}, bf16[96,5120]{1,0:T(8,128)(2,1)}, u32[]{:S(2)}) copy-start(bf16[96,5120]{1,0:T(8,128)(2,1)} %refs_1_.1) | copy-start | bytes 2949124
  2.7 61.7 %copy-start = (bf16[5136,128]{1,0:T(8,128)(2,1)}, bf16[5136,128]{1,0:T(8,128)(2,1)S(1)}, u32[]{:S(2)}) copy-start(bf16[5136,128]{1,0:T(8,128)(2,1)S(1)} %shard_map.64.refs_0_) | copy-start | bytes 3944452
  2.8 32.8 %collective-permute-start = (bf16[5136,128]{1,0:T(8,128)(2,1)S(1)}, bf16[5136,128]{1,0:T(8,128)(2,1)S(1)}, u32[]{:S(2)}, u32[]{:S(2)}) collective-permute-start(bf16[5136,128]{1,0:T(8,128)(2,1)S(1)} %shard_map.64.refs_0_), channel_id=1, source_target_pairs={{0,32},{1,33},{2,34},{3,35},{4,36},{5,37},{6,38},{7,39},{8,40},{9,... | collective-permute-start | bytes 3944456 | tf_op jit(solution)/shard_map/ppermute | solution.py:27
  5.0 24.9 %collective-permute-start.2 = (bf16[96,5120]{1,0:T(8,128)(2,1)S(1)}, bf16[96,5120]{1,0:T(8,128)(2,1)S(1)}, u32[]{:S(2)}, u32[]{:S(2)}) collective-permute-start(bf16[96,5120]{1,0:T(8,128)(2,1)S(1)} %copy-done.17), channel_id=1, source_target_pairs={{0,8},{1,9},{2,10},{3,11},{4,12},{5,13},{6,14},{7,15},{8,0},{9,1},... | collective-permute-start | bytes 2949128 | tf_op jit(solution)/shard_map/ppermute | solution.py:27
  8.6 22.3 %collective-permute-start.7 = (bf16[96,5120]{1,0:T(8,128)(2,1)S(1)}, bf16[96,5120]{1,0:T(8,128)(2,1)S(1)}, u32[]{:S(2)}, u32[]{:S(2)}) collective-permute-start(bf16[96,5120]{1,0:T(8,128)(2,1)S(1)} %copy-done.17), channel_id=1, source_target_pairs={{0,6},{1,7},{2,0},{3,1},{4,2},{5,3},{6,4},{7,5},{8,14},{9,15},{10,... | collective-permute-start | bytes 2949128 | tf_op jit(solution)/shard_map/ppermute | solution.py:27
  11.1 23.0 %collective-permute-start.6 = (bf16[96,5120]{1,0:T(8,128)(2,1)S(1)}, bf16[96,5120]{1,0:T(8,128)(2,1)S(1)}, u32[]{:S(2)}, u32[]{:S(2)}) collective-permute-start(bf16[96,5120]{1,0:T(8,128)(2,1)S(1)} %copy-done.17), channel_id=1, source_target_pairs={{0,2},{1,3},{2,4},{3,5},{4,6},{5,7},{6,0},{7,1},{8,10},{9,11},{10,... | collective-permute-start | bytes 2949128 | tf_op jit(solution)/shard_map/ppermute | solution.py:27
  11.1 29.7 %collective-permute-start.1 = (bf16[5136,128]{1,0:T(8,128)(2,1)S(1)}, bf16[5136,128]{1,0:T(8,128)(2,1)S(1)}, u32[]{:S(2)}, u32[]{:S(2)}) collective-permute-start(bf16[5136,128]{1,0:T(8,128)(2,1)S(1)} %shard_map.64.refs_0_), channel_id=1, source_target_pairs={{0,96},{1,97},{2,98},{3,99},{4,100},{5,101},{6,102},{7,103},{8,104... | collective-permute-start | bytes 3944456 | tf_op jit(solution)/shard_map/ppermute | solution.py:27
  29.8 11.0 %copy-start.18 = (bf16[96,5120]{1,0:T(8,128)(2,1)}, bf16[96,5120]{1,0:T(8,128)(2,1)S(1)}, u32[]{:S(2)}) copy-start(bf16[96,5120]{1,0:T(8,128)(2,1)S(1)} %collective-permute-done.2.refs_0_) | copy-start | bytes 2949124
  29.8 29.0 %collective-permute-start.3 = (bf16[5136,128]{1,0:T(8,128)(2,1)S(1)}, bf16[5136,128]{1,0:T(8,128)(2,1)S(1)}, u32[]{:S(2)}, u32[]{:S(2)}) collective-permute-start(bf16[5136,128]{1,0:T(8,128)(2,1)S(1)} %shard_map.64.refs_0_), channel_id=1, source_target_pairs={{0,16},{1,17},{2,18},{3,19},{4,20},{5,21},{6,22},{7,23},{8,24},{9,... | collective-permute-start | bytes 3944456 | tf_op jit(solution)/shard_map/ppermute | solution.py:27
  30.9 64.9 %copy-start.2 = (bf16[96,5120]{1,0:T(8,128)(2,1)}, bf16[96,5120]{1,0:T(8,128)(2,1)S(1)}, u32[]{:S(2)}) copy-start(bf16[96,5120]{1,0:T(8,128)(2,1)S(1)} %collective-permute-done.7.refs_4_.refs_2_) | copy-start | bytes 2949124
  34.1 63.0 %copy-start.3 = (bf16[96,5120]{1,0:T(8,128)(2,1)}, bf16[96,5120]{1,0:T(8,128)(2,1)S(1)}, u32[]{:S(2)}) copy-start(bf16[96,5120]{1,0:T(8,128)(2,1)S(1)} %collective-permute-done.6.refs_2_.refs_3_) | copy-start | bytes 2949124
  34.1 21.0 %collective-permute-start.9 = (bf16[96,5120]{1,0:T(8,128)(2,1)S(1)}, bf16[96,5120]{1,0:T(8,128)(2,1)}, u32[]{:S(2)}, u32[]{:S(2)}) collective-permute-start(bf16[96,5120]{1,0:T(8,128)(2,1)S(1)} %collective-permute-done.2.refs_0_), channel_id=1, source_target_pairs={{0,6},{1,7},{2,0},{3,1},{4,2},{5,3},{6,4},{7,5},{8,14},{9,15},{10,... | collective-permute-start | bytes 2949128 | tf_op jit(solution)/shard_map/ppermute | solution.py:27
  34.4 22.2 %collective-permute-start.8 = (bf16[96,5120]{1,0:T(8,128)(2,1)S(1)}, bf16[96,5120]{1,0:T(8,128)(2,1)}, u32[]{:S(2)}, u32[]{:S(2)}) collective-permute-start(bf16[96,5120]{1,0:T(8,128)(2,1)S(1)} %collective-permute-done.2.refs_0_), channel_id=1, source_target_pairs={{0,2},{1,3},{2,4},{3,5},{4,6},{5,7},{6,0},{7,1},{8,10},{9,11},{10,... | collective-permute-start | bytes 2949128 | tf_op jit(solution)/shard_map/ppermute | solution.py:27
  35.5 29.5 %copy-start.11 = (bf16[5136,128]{1,0:T(8,128)(2,1)}, bf16[5136,128]{1,0:T(8,128)(2,1)S(1)}, u32[]{:S(2)}) copy-start(bf16[5136,128]{1,0:T(8,128)(2,1)S(1)} %collective-permute-done.refs_1_) | copy-start | bytes 3944452
  35.6 21.0 %collective-permute-start.4 = (bf16[2576,128]{1,0:T(8,128)(2,1)S(1)}, bf16[2576,128]{1,0:T(8,128)(2,1)S(1)}, u32[]{:S(2)}, u32[]{:S(2)}) collective-permute-start(bf16[2576,128]{1,0:T(8,128)(2,1)S(1)} %pad_maximum_fusion), channel_id=1, source_target_pairs={{0,32},{1,33},{2,34},{3,35},{4,36},{5,37},{6,38},{7,39},{8,40},{9,... | collective-permute-start | bytes 1978376 | tf_op jit(solution)/shard_map/ppermute | solution.py:27
  40.7 24.3 %copy-start.12 = (bf16[5136,128]{1,0:T(8,128)(2,1)}, bf16[5136,128]{1,0:T(8,128)(2,1)S(1)}, u32[]{:S(2)}) copy-start(bf16[5136,128]{1,0:T(8,128)(2,1)S(1)} %collective-permute-done.1.refs_2_) | copy-start | bytes 3944452
  40.8 15.8 %collective-permute-start.5 = (bf16[2560,128]{1,0:T(8,128)(2,1)S(1)}, bf16[2560,128]{1,0:T(8,128)(2,1)S(1)}, u32[]{:S(2)}, u32[]{:S(2)}) collective-permute-start(bf16[2560,128]{1,0:T(8,128)(2,1)S(1)} %slice.74), channel_id=1, source_target_pairs={{0,96},{1,97},{2,98},{3,99},{4,100},{5,101},{6,102},{7,103},{8,104... | collective-permute-start | bytes 1966088 | tf_op jit(solution)/shard_map/ppermute | solution.py:27
  58.8 32.5 %copy-start.4 = (bf16[5136,128]{1,0:T(8,128)(2,1)}, bf16[5136,128]{1,0:T(8,128)(2,1)S(1)}, u32[]{:S(2)}) copy-start(bf16[5136,128]{1,0:T(8,128)(2,1)S(1)} %get-tuple-element.68.refs_4_) | copy-start | bytes 3944452
  58.8 35.9 %copy-start.13 = (bf16[5136,128]{1,0:T(8,128)(2,1)}, bf16[5136,128]{1,0:T(8,128)(2,1)S(1)}, u32[]{:S(2)}) copy-start(bf16[5136,128]{1,0:T(8,128)(2,1)S(1)} %collective-permute-done.3.refs_3_) | copy-start | bytes 3944452
  58.8 31.1 %collective-permute-start.11 = (bf16[5136,128]{1,0:T(8,128)(2,1)S(1)}, bf16[5136,128]{1,0:T(8,128)(2,1)S(1)}, u32[]{:S(2)}, u32[]{:S(2)}) collective-permute-start(bf16[5136,128]{1,0:T(8,128)(2,1)S(1)} %collective-permute-done.3.refs_3_), channel_id=1, source_target_pairs={{0,96},{1,97},{2,98},{3,99},{4,100},{5,101},{6,102},{7,103},{8,104... | collective-permute-start | bytes 3944456 | tf_op jit(solution)/shard_map/ppermute | solution.py:27
  62.1 29.1 %collective-permute-start.10 = (bf16[5136,128]{1,0:T(8,128)(2,1)S(1)}, bf16[5136,128]{1,0:T(8,128)(2,1)S(1)}, u32[]{:S(2)}, u32[]{:S(2)}) collective-permute-start(bf16[5136,128]{1,0:T(8,128)(2,1)S(1)} %collective-permute-done.3.refs_3_), channel_id=1, source_target_pairs={{0,32},{1,33},{2,34},{3,35},{4,36},{5,37},{6,38},{7,39},{8,40},{9,... | collective-permute-start | bytes 3944456 | tf_op jit(solution)/shard_map/ppermute | solution.py:27
  62.1 20.1 %collective-permute-start.14 = (bf16[96,5120]{1,0:T(8,128)(2,1)S(1)}, bf16[96,5120]{1,0:T(8,128)(2,1)}, u32[]{:S(2)}, u32[]{:S(2)}) collective-permute-start(bf16[96,5120]{1,0:T(8,128)(2,1)S(1)} %get-tuple-element.70), channel_id=1, source_target_pairs={{0,6},{1,7},{2,0},{3,1},{4,2},{5,3},{6,4},{7,5},{8,14},{9,15},{10,... | collective-permute-start | bytes 2949128 | tf_op jit(solution)/shard_map/ppermute | solution.py:27
  64.4 22.0 %collective-permute-start.13 = (bf16[96,5120]{1,0:T(8,128)(2,1)S(1)}, bf16[96,5120]{1,0:T(8,128)(2,1)}, u32[]{:S(2)}, u32[]{:S(2)}) collective-permute-start(bf16[96,5120]{1,0:T(8,128)(2,1)S(1)} %get-tuple-element.67), channel_id=1, source_target_pairs={{0,2},{1,3},{2,4},{3,5},{4,6},{5,7},{6,0},{7,1},{8,10},{9,11},{10,... | collective-permute-start | bytes 2949128 | tf_op jit(solution)/shard_map/ppermute | solution.py:27
  64.4 30.2 %collective-permute-start.12 = (bf16[5136,128]{1,0:T(8,128)(2,1)S(1)}, bf16[5136,128]{1,0:T(8,128)(2,1)S(1)}, u32[]{:S(2)}, u32[]{:S(2)}) collective-permute-start(bf16[5136,128]{1,0:T(8,128)(2,1)S(1)} %get-tuple-element.68.refs_4_), channel_id=1, source_target_pairs={{0,16},{1,17},{2,18},{3,19},{4,20},{5,21},{6,22},{7,23},{8,24},{9,... | collective-permute-start | bytes 3944456 | tf_op jit(solution)/shard_map/ppermute | solution.py:27
  82.2 15.4 %collective-permute-start.17 = (bf16[96,5120]{1,0:T(8,128)(2,1)}, bf16[96,5120]{1,0:T(8,128)(2,1)}, u32[]{:S(2)}, u32[]{:S(2)}) collective-permute-start(bf16[96,5120]{1,0:T(8,128)(2,1)} %collective-permute-done.9.refs_5_.refs_10_), channel_id=1, source_target_pairs={{0,1},{1,0},{2,3},{3,2},{4,5},{5,4},{6,7},{7,6},{8,9},{9,8},{10,11... | collective-permute-start | bytes 2949128 | tf_op jit(solution)/shard_map/ppermute | solution.py:27
  86.4 9.4 %collective-permute-start.16 = (bf16[96,5120]{1,0:T(8,128)(2,1)}, bf16[96,5120]{1,0:T(8,128)(2,1)}, u32[]{:S(2)}, u32[]{:S(2)}) collective-permute-start(bf16[96,5120]{1,0:T(8,128)(2,1)} %collective-permute-done.14.refs_9_.refs_1_), channel_id=1, source_target_pairs={{0,1},{1,0},{2,3},{3,2},{4,5},{5,4},{6,7},{7,6},{8,9},{9,8},{10,11... | collective-permute-start | bytes 2949128 | tf_op jit(solution)/shard_map/ppermute | solution.py:27
  89.9 4.7 %copy-start.14 = (bf16[5136,128]{1,0:T(8,128)(2,1)}, bf16[5136,128]{1,0:T(8,128)(2,1)S(1)}, u32[]{:S(2)}) copy-start(bf16[5136,128]{1,0:T(8,128)(2,1)S(1)} %collective-permute-done.11.refs_6_) | copy-start | bytes 3944452
  89.9 5.9 %collective-permute-start.15 = (bf16[96,5120]{1,0:T(8,128)(2,1)}, bf16[96,5120]{1,0:T(8,128)(2,1)}, u32[]{:S(2)}, u32[]{:S(2)}) collective-permute-start(bf16[96,5120]{1,0:T(8,128)(2,1)} %collective-permute-done.13.refs_8_.refs_0_), channel_id=1, source_target_pairs={{0,1},{1,0},{2,3},{3,2},{4,5},{5,4},{6,7},{7,6},{8,9},{9,8},{10,11... | collective-permute-start | bytes 2949128 | tf_op jit(solution)/shard_map/ppermute | solution.py:27
  91.2 3.4 %copy-start.15 = (bf16[5136,128]{1,0:T(8,128)(2,1)}, bf16[5136,128]{1,0:T(8,128)(2,1)S(1)}, u32[]{:S(2)}) copy-start(bf16[5136,128]{1,0:T(8,128)(2,1)S(1)} %collective-permute-done.10.refs_5_) | copy-start | bytes 3944452
  91.2 7.0 %collective-permute-start.18 = (bf16[96,5120]{1,0:T(8,128)(2,1)}, bf16[96,5120]{1,0:T(8,128)(2,1)}, u32[]{:S(2)}, u32[]{:S(2)}) collective-permute-start(bf16[96,5120]{1,0:T(8,128)(2,1)} %collective-permute-done.8.refs_3_.refs_11_), channel_id=1, source_target_pairs={{0,1},{1,0},{2,3},{3,2},{4,5},{5,4},{6,7},{7,6},{8,9},{9,8},{10,11... | collective-permute-start | bytes 2949128 | tf_op jit(solution)/shard_map/ppermute | solution.py:27
  94.7 1.1 copy-start.16
  95.9 19.3 %collective-permute-start.19 = (bf16[96,5120]{1,0:T(8,128)(2,1)S(1)}, bf16[96,5120]{1,0:T(8,128)(2,1)}, u32[]{:S(2)}, u32[]{:S(2)}) collective-permute-start(bf16[96,5120]{1,0:T(8,128)(2,1)S(1)} %collective-permute-done.7.refs_4_.refs_2_), channel_id=1, source_target_pairs={{0,1},{1,0},{2,3},{3,2},{4,5},{5,4},{6,7},{7,6},{8,9},{9,8},{10,11... | collective-permute-start | bytes 2949128 | tf_op jit(solution)/shard_map/ppermute | solution.py:27
  97.1 18.1 %collective-permute-start.20 = (bf16[96,5120]{1,0:T(8,128)(2,1)S(1)}, bf16[96,5120]{1,0:T(8,128)(2,1)}, u32[]{:S(2)}, u32[]{:S(2)}) collective-permute-start(bf16[96,5120]{1,0:T(8,128)(2,1)S(1)} %collective-permute-done.6.refs_2_.refs_3_), channel_id=1, source_target_pairs={{0,1},{1,0},{2,3},{3,2},{4,5},{5,4},{6,7},{7,6},{8,9},{9,8},{10,11... | collective-permute-start | bytes 2949128 | tf_op jit(solution)/shard_map/ppermute | solution.py:27
  97.2 18.1 %collective-permute-start.21 = (bf16[96,5120]{1,0:T(8,128)(2,1)}, bf16[96,5120]{1,0:T(8,128)(2,1)S(1)}, u32[]{:S(2)}, u32[]{:S(2)}) collective-permute-start(bf16[96,5120]{1,0:T(8,128)(2,1)} %copy-done.18), channel_id=1, source_target_pairs={{0,1},{1,0},{2,3},{3,2},{4,5},{5,4},{6,7},{7,6},{8,9},{9,8},{10,11... | collective-permute-start | bytes 2949128 | tf_op jit(solution)/shard_map/ppermute | solution.py:27
  97.6 17.7 %collective-permute-start.22 = (bf16[96,5120]{1,0:T(8,128)(2,1)S(1)}, bf16[96,5120]{1,0:T(8,128)(2,1)}, u32[]{:S(2)}, u32[]{:S(2)}) collective-permute-start(bf16[96,5120]{1,0:T(8,128)(2,1)S(1)} %copy-done.17), channel_id=1, source_target_pairs={{0,1},{1,0},{2,3},{3,2},{4,5},{5,4},{6,7},{7,6},{8,9},{9,8},{10,11... | collective-permute-start | bytes 2949128 | tf_op jit(solution)/shard_map/ppermute | solution.py:27
  115.2 6.5 %copy-start.8 = (bf16[96,5120]{1,0:T(8,128)(2,1)S(1)}, bf16[96,5120]{1,0:T(8,128)(2,1)}, u32[]{:S(2)}) copy-start(bf16[96,5120]{1,0:T(8,128)(2,1)} %get-tuple-element.84) | copy-start | bytes 2949124
  115.2 1.0 copy-start.19
  116.3 2.8 %collective-permute-start.23 = (bf16[96,5120]{1,0:T(8,128)(2,1)}, bf16[96,5120]{1,0:T(8,128)(2,1)S(1)}, u32[]{:S(2)}, u32[]{:S(2)}) collective-permute-start(bf16[96,5120]{1,0:T(8,128)(2,1)} %get-tuple-element.83), channel_id=1, source_target_pairs={{0,1},{1,0},{2,3},{3,2},{4,5},{5,4},{6,7},{7,6},{8,9},{9,8},{10,11... | collective-permute-start | bytes 2949128 | tf_op jit(solution)/shard_map/ppermute | solution.py:27
  116.7 5.0 %collective-permute-start.24 = (bf16[96,5120]{1,0:T(8,128)(2,1)}, bf16[96,5120]{1,0:T(8,128)(2,1)S(1)}, u32[]{:S(2)}, u32[]{:S(2)}) collective-permute-start(bf16[96,5120]{1,0:T(8,128)(2,1)} %get-tuple-element.85), channel_id=1, source_target_pairs={{0,1},{1,0},{2,3},{3,2},{4,5},{5,4},{6,7},{7,6},{8,9},{9,8},{10,11... | collective-permute-start | bytes 2949128 | tf_op jit(solution)/shard_map/ppermute | solution.py:27
  116.8 7.0 %collective-permute-start.25 = (bf16[96,5120]{1,0:T(8,128)(2,1)}, bf16[96,5120]{1,0:T(8,128)(2,1)S(1)}, u32[]{:S(2)}, u32[]{:S(2)}) collective-permute-start(bf16[96,5120]{1,0:T(8,128)(2,1)} %get-tuple-element.87), channel_id=1, source_target_pairs={{0,1},{1,0},{2,3},{3,2},{4,5},{5,4},{6,7},{7,6},{8,9},{9,8},{10,11... | collective-permute-start | bytes 2949128 | tf_op jit(solution)/shard_map/ppermute | solution.py:27
  120.5 3.3 %copy-start.7 = (bf16[96,5120]{1,0:T(8,128)(2,1)S(1)}, bf16[96,5120]{1,0:T(8,128)(2,1)}, u32[]{:S(2)}) copy-start(bf16[96,5120]{1,0:T(8,128)(2,1)} %get-tuple-element.86) | copy-start | bytes 2949124
  120.5 25.8 %collective-permute-start.28 = (bf16[96,5120]{1,0:T(8,128)(2,1)S(1)}, bf16[96,5120]{1,0:T(8,128)(2,1)S(1)}, u32[]{:S(2)}, u32[]{:S(2)}) collective-permute-start(bf16[96,5120]{1,0:T(8,128)(2,1)S(1)} %add_convert_fusion.6), channel_id=1, source_target_pairs={{0,2},{1,3},{2,4},{3,5},{4,6},{5,7},{6,0},{7,1},{8,10},{9,11},{10,... | collective-permute-start | bytes 2949128 | tf_op jit(solution)/shard_map/ppermute | solution.py:27
  122.0 24.4 %collective-permute-start.29 = (bf16[96,5120]{1,0:T(8,128)(2,1)S(1)}, bf16[96,5120]{1,0:T(8,128)(2,1)S(1)}, u32[]{:S(2)}, u32[]{:S(2)}) collective-permute-start(bf16[96,5120]{1,0:T(8,128)(2,1)S(1)} %add_convert_fusion.5), channel_id=1, source_target_pairs={{0,6},{1,7},{2,0},{3,1},{4,2},{5,3},{6,4},{7,5},{8,14},{9,15},{10,... | collective-permute-start | bytes 2949128 | tf_op jit(solution)/shard_map/ppermute | solution.py:27
  124.1 24.0 %collective-permute-start.30 = (bf16[96,5120]{1,0:T(8,128)(2,1)S(1)}, bf16[96,5120]{1,0:T(8,128)(2,1)}, u32[]{:S(2)}, u32[]{:S(2)}) collective-permute-start(bf16[96,5120]{1,0:T(8,128)(2,1)S(1)} %add_convert_fusion.4), channel_id=1, source_target_pairs={{0,8},{1,9},{2,10},{3,11},{4,12},{5,13},{6,14},{7,15},{8,0},{9,1},... | collective-permute-start | bytes 2949128 | tf_op jit(solution)/shard_map/ppermute | solution.py:27
  142.6 3.0 %collective-permute-start.26 = (bf16[48,5120]{1,0:T(8,128)(2,1)}, bf16[48,5120]{1,0:T(8,128)(2,1)S(1)}, u32[]{:S(2)}, u32[]{:S(2)}) collective-permute-start(bf16[48,5120]{1,0:T(8,128)(2,1)} %get-tuple-element.92), channel_id=1, source_target_pairs={{0,1},{1,0},{2,3},{3,2},{4,5},{5,4},{6,7},{7,6},{8,9},{9,8},{10,11... | collective-permute-start | bytes 1474568 | tf_op jit(solution)/shard_map/ppermute | solution.py:27
  143.9 2.4 %collective-permute-start.27 = (bf16[48,5120]{1,0:T(8,128)(2,1)}, bf16[48,5120]{1,0:T(8,128)(2,1)S(1)}, u32[]{:S(2)}, u32[]{:S(2)}) collective-permute-start(bf16[48,5120]{1,0:T(8,128)(2,1)} %get-tuple-element.93), channel_id=1, source_target_pairs={{0,1},{1,0},{2,3},{3,2},{4,5},{5,4},{6,7},{7,6},{8,9},{9,8},{10,11... | collective-permute-start | bytes 1474568 | tf_op jit(solution)/shard_map/ppermute | solution.py:27
  150.9 16.7 %collective-permute-start.31 = (bf16[96,5120]{1,0:T(8,128)(2,1)}, bf16[96,5120]{1,0:T(8,128)(2,1)S(1)}, u32[]{:S(2)}, u32[]{:S(2)}) collective-permute-start(bf16[96,5120]{1,0:T(8,128)(2,1)} %get-tuple-element.108), channel_id=1, source_target_pairs={{0,1},{1,0},{2,3},{3,2},{4,5},{5,4},{6,7},{7,6},{8,9},{9,8},{10,11... | collective-permute-start | bytes 2949128 | tf_op jit(solution)/shard_map/ppermute | solution.py:27
  152.7 14.9 %collective-permute-start.32 = (bf16[96,5120]{1,0:T(8,128)(2,1)}, bf16[96,5120]{1,0:T(8,128)(2,1)S(1)}, u32[]{:S(2)}, u32[]{:S(2)}) collective-permute-start(bf16[96,5120]{1,0:T(8,128)(2,1)} %get-tuple-element.109), channel_id=1, source_target_pairs={{0,1},{1,0},{2,3},{3,2},{4,5},{5,4},{6,7},{7,6},{8,9},{9,8},{10,11... | collective-permute-start | bytes 2949128 | tf_op jit(solution)/shard_map/ppermute | solution.py:27
  152.7 14.0 %collective-permute-start.34 = (bf16[48,5120]{1,0:T(8,128)(2,1)}, bf16[48,5120]{1,0:T(8,128)(2,1)}, u32[]{:S(2)}, u32[]{:S(2)}) collective-permute-start(bf16[48,5120]{1,0:T(8,128)(2,1)} %get-tuple-element.123), channel_id=1, source_target_pairs={{0,6},{1,7},{2,0},{3,1},{4,2},{5,3},{6,4},{7,5},{8,14},{9,15},{10,... | collective-permute-start | bytes 1474568 | tf_op jit(solution)/shard_map/ppermute | solution.py:27
  154.1 13.5 %collective-permute-start.33 = (bf16[48,5120]{1,0:T(8,128)(2,1)}, bf16[48,5120]{1,0:T(8,128)(2,1)}, u32[]{:S(2)}, u32[]{:S(2)}) collective-permute-start(bf16[48,5120]{1,0:T(8,128)(2,1)} %get-tuple-element.124), channel_id=1, source_target_pairs={{0,2},{1,3},{2,4},{3,5},{4,6},{5,7},{6,0},{7,1},{8,10},{9,11},{10,... | collective-permute-start | bytes 1474568 | tf_op jit(solution)/shard_map/ppermute | solution.py:27
  154.2 13.4 %copy-start.10 = (bf16[96,5120]{1,0:T(8,128)(2,1)S(1)}, bf16[96,5120]{1,0:T(8,128)(2,1)}, u32[]{:S(2)}) copy-start(bf16[96,5120]{1,0:T(8,128)(2,1)} %get-tuple-element.112) | copy-start | bytes 2949124
  166.7 4.2 %copy-start.21 = (bf16[96,5120]{1,0:T(8,128)(2,1)S(1)}, bf16[96,5120]{1,0:T(8,128)(2,1)}, u32[]{:S(2)}) copy-start(bf16[96,5120]{1,0:T(8,128)(2,1)} %get-tuple-element.119) | copy-start | bytes 2949124
  166.7 5.5 %copy-start.9 = (bf16[96,5120]{1,0:T(8,128)(2,1)S(1)}, bf16[96,5120]{1,0:T(8,128)(2,1)}, u32[]{:S(2)}) copy-start(bf16[96,5120]{1,0:T(8,128)(2,1)} %get-tuple-element.111) | copy-start | bytes 2949124
  168.9 5.5 %copy-start.5 = (bf16[96,5120]{1,0:T(8,128)(2,1)S(1)}, bf16[96,5120]{1,0:T(8,128)(2,1)}, u32[]{:S(2)}) copy-start(bf16[96,5120]{1,0:T(8,128)(2,1)} %get-tuple-element.118) | copy-start | bytes 2949124
  168.9 21.9 %collective-permute-start.38 = (bf16[96,5120]{1,0:T(8,128)(2,1)S(1)}, bf16[96,5120]{1,0:T(8,128)(2,1)S(1)}, u32[]{:S(2)}, u32[]{:S(2)}) collective-permute-start(bf16[96,5120]{1,0:T(8,128)(2,1)S(1)} %add_convert_fusion.2), channel_id=1, source_target_pairs={{0,6},{1,7},{2,0},{3,1},{4,2},{5,3},{6,4},{7,5},{8,14},{9,15},{10,... | collective-permute-start | bytes 2949128 | tf_op jit(solution)/shard_map/ppermute | solution.py:27
  170.9 3.5 %collective-permute-start.35 = (bf16[96,5120]{1,0:T(8,128)(2,1)S(1)}, bf16[96,5120]{1,0:T(8,128)(2,1)S(1)}, u32[]{:S(2)}, u32[]{:S(2)}) collective-permute-start(bf16[96,5120]{1,0:T(8,128)(2,1)S(1)} %copy-done.21), channel_id=1, source_target_pairs={{0,1},{1,0},{2,3},{3,2},{4,5},{5,4},{6,7},{7,6},{8,9},{9,8},{10,11... | collective-permute-start | bytes 2949128 | tf_op jit(solution)/shard_map/ppermute | solution.py:27
  173.6 1.5 copy-start.20
  173.6 26.6 %copy-start.6 = (bf16[96,5120]{1,0:T(8,128)(2,1)S(1)}, bf16[96,5120]{1,0:T(8,128)(2,1)}, u32[]{:S(2)}) copy-start(bf16[96,5120]{1,0:T(8,128)(2,1)} %get-tuple-element.101) | copy-start | bytes 2949124
  173.6 24.7 %collective-permute-start.37 = (bf16[96,5120]{1,0:T(8,128)(2,1)S(1)}, bf16[96,5120]{1,0:T(8,128)(2,1)S(1)}, u32[]{:S(2)}, u32[]{:S(2)}) collective-permute-start(bf16[96,5120]{1,0:T(8,128)(2,1)S(1)} %add_convert_fusion.3), channel_id=1, source_target_pairs={{0,2},{1,3},{2,4},{3,5},{4,6},{5,7},{6,0},{7,1},{8,10},{9,11},{10,... | collective-permute-start | bytes 2949128 | tf_op jit(solution)/shard_map/ppermute | solution.py:27
  175.1 23.2 %collective-permute-start.36 = (bf16[96,5120]{1,0:T(8,128)(2,1)S(1)}, bf16[96,5120]{1,0:T(8,128)(2,1)S(1)}, u32[]{:S(2)}, u32[]{:S(2)}) collective-permute-start(bf16[96,5120]{1,0:T(8,128)(2,1)S(1)} %copy-done.20), channel_id=1, source_target_pairs={{0,1},{1,0},{2,3},{3,2},{4,5},{5,4},{6,7},{7,6},{8,9},{9,8},{10,11... | collective-permute-start | bytes 2949128 | tf_op jit(solution)/shard_map/ppermute | solution.py:27
  175.5 24.7 %collective-permute-start.39 = (bf16[96,5120]{1,0:T(8,128)(2,1)S(1)}, bf16[96,5120]{1,0:T(8,128)(2,1)S(1)}, u32[]{:S(2)}, u32[]{:S(2)}) collective-permute-start(bf16[96,5120]{1,0:T(8,128)(2,1)S(1)} %add_convert_fusion.1), channel_id=1, source_target_pairs={{0,8},{1,9},{2,10},{3,11},{4,12},{5,13},{6,14},{7,15},{8,0},{9,1},... | collective-permute-start | bytes 2949128 | tf_op jit(solution)/shard_map/ppermute | solution.py:27

commit v7 on v4

--- a/solution.py
+++ b/solution.py
@@ -307,28 +307,30 @@
 
     ids = after(ids, far_z, right, left)
     groups = halves(0) + [whole(tb, o_right), whole(ta, o_left), whole(tz, o_z)]
-    part = sums(ids, groups, [count] * 4 + [h_rows] * 2 + [count] * 3, weights)
-    part, weights = part[:9], part[9:]
-    far, near, here_z, near_sib, here_sib = part[0], part[1:3], part[3], part[6:8], part[8]
-    got = swap(*part[4:6])
+    part = sums(ids, groups, [h_rows] * 2 + [count] * 3 + [h_rows] * 2 + [count] * 3, weights)
+    part, weights = part[:10], part[10:]
+    far, near, here_z, near_sib, z_sib = part[:2], part[2:4], part[4], part[7:9], part[9]
+    got = swap(*part[5:7])
     far, got, far_in, z_right, z_left = after((far, got, far_in, z_right, z_left))
-    top = add(far[:h_rows], got[0], far_in[:h_rows]).astype(BF16)
-    low = add(far[h_rows:], got[1], far_in[h_rows:]).astype(BF16)
+    top = add(far[0], got[0], far_in[:h_rows]).astype(BF16)
+    low = add(far[1], got[1], far_in[h_rows:]).astype(BF16)
     past_top, past_low = move(top, dx=1), move(low, dx=-1)
 
-    near_sib, here_sib = after((near_sib, here_sib), top, low)
-    got = swap(*near_sib, here_sib)
-    ids = after(ids, top, low)
+    near_sib, z_sib = after((near_sib, z_sib), top, low)
+    got = swap(*near_sib, z_sib)
+    right, left = add(near[0], got[0]), add(near[1], got[1])
+    across = add(here_z, got[2], z_right, z_left).astype(BF16)
+    ids = after(ids, top, low, right, left, across)
     here, own_sib = sums(ids, [whole(tokens, o_own)], [count] * 2, weights)[:2]
-    near, got, past_top, past_low, here = after((near, got, past_top, past_low, here))
+    right, left, across, past_top, past_low, here = after((right, left, across, past_top, past_low, here))
     zero = jnp.zeros((), BF16)
     past_top = lax.pad(past_top, zero, ((0, h_rows, 0), (0, 0, 0)))
     past_low = lax.pad(past_low, zero, ((h_rows, 0, 0), (0, 0, 0)))
-    right, left = (add(near[i], got[i], past).astype(BF16) for i, past in enumerate((past_top, past_low)))
-    across = add(here_z, got[2], z_right, z_left).astype(BF16)
+    right, left = add(right, past_top).astype(BF16), add(left, past_low).astype(BF16)
     right_in, left_in, across_in = move(right, dx=1), move(left, dx=-1), move(across, zh=1)
     own_sib = after(own_sib, right, left, across)
-    return add(here, *swap(own_sib), right_in, left_in, across_in).astype(BF16)
+    base = after(add(here, *swap(own_sib), across_in))
+    return add(base, right_in, left_in).astype(BF16)
 
 
 def solution(mesh):

time: 202 us -> 200 us (0.990)
  waiting for transfers between devices: 85.5 us -> 83.2 us
    ppermute x40, waiting for transfers between devices: 85.5 us -> 83.2 us  [move(): return lax.ppermute(value, AXES, pairs)]
  transfers between devices with their start and end apart: 40 -> 40, of which waited for: 16 -> 16; matrix products, arithmetic and copies ran while one was open for 1% -> 2% of each run, Pallas kernels for 24% -> 24%
where the time goes in v7:
time: 200 us; the launch traced here: 199 us
  waiting for transfers between devices  83.2 us (42%)
  starting transfers between devices  52.5 us (26%)
  Pallas kernels  48.3 us (24%)
  other arithmetic  10 us (5%)
  local copies, waits for them, and re-layouts  3.26 us (2%)
    ppermute x40, waiting for transfers between devices, move(): return lax.ppermute(value, AXES, pairs)  83.2 us
    ppermute x40, starting transfers between devices, move(): return lax.ppermute(value, AXES, pairs)  52.5 us
    pallas_call x2, Pallas kernels, sums(): return tuple(run(ids, sidx, scale_table, *pieces, *weights))  28.9 us
    pallas_call x1, Pallas kernels, sums(): return tuple(run(ids, sidx, scale_table, *sources, *pieces, down_weight))  17.1 us
  transfers between devices with their start and end apart: 40, of which 16 were waited for; matrix products, arithmetic and copies ran while one was open for 2% of the time, Pallas kernels for 24%

profile of v7, /device:TPU:1, one launch (start us, length us, event | category | flops | bytes accessed | tf_op | source)
XLA Modules:
  0.0 199.1 jit_solution(680499417796538980)
XLA Ops:
  1.3 1.3 copy-done.1
  2.8 2.2 %collective-permute-start = (bf16[5136,128]{1,0:T(8,128)(2,1)S(1)}, bf16[5136,128]{1,0:T(8,128)(2,1)S(1)}, u32[]{:S(2)}, u32[]{:S(2)}) collective-permute-start(bf16[5136,128]{1,0:T(8,128)(2,1)S(1)} %shard_map.64.refs_0_), channel_id=1, source_target_pairs={{0,32},{1,33},{2,34},{3,35},{4,36},{5,37},{6,38},{7,39},{8,40},{9,... | collective-permute-start | bytes 3944456 | tf_op jit(solution)/shard_map/ppermute | solution.py:27
  5.0 3.6 %collective-permute-start.2 = (bf16[96,5120]{1,0:T(8,128)(2,1)S(1)}, bf16[96,5120]{1,0:T(8,128)(2,1)S(1)}, u32[]{:S(2)}, u32[]{:S(2)}) collective-permute-start(bf16[96,5120]{1,0:T(8,128)(2,1)S(1)} %copy-done.11), channel_id=1, source_target_pairs={{0,8},{1,9},{2,10},{3,11},{4,12},{5,13},{6,14},{7,15},{8,0},{9,1},... | collective-permute-start | bytes 2949128 | tf_op jit(solution)/shard_map/ppermute | solution.py:27
  8.6 2.5 %collective-permute-start.7 = (bf16[96,5120]{1,0:T(8,128)(2,1)S(1)}, bf16[96,5120]{1,0:T(8,128)(2,1)S(1)}, u32[]{:S(2)}, u32[]{:S(2)}) collective-permute-start(bf16[96,5120]{1,0:T(8,128)(2,1)S(1)} %copy-done.11), channel_id=1, source_target_pairs={{0,6},{1,7},{2,0},{3,1},{4,2},{5,3},{6,4},{7,5},{8,14},{9,15},{10,... | collective-permute-start | bytes 2949128 | tf_op jit(solution)/shard_map/ppermute | solution.py:27
  11.1 2.7 %collective-permute-start.1 = (bf16[5136,128]{1,0:T(8,128)(2,1)S(1)}, bf16[5136,128]{1,0:T(8,128)(2,1)S(1)}, u32[]{:S(2)}, u32[]{:S(2)}) collective-permute-start(bf16[5136,128]{1,0:T(8,128)(2,1)S(1)} %shard_map.64.refs_0_), channel_id=1, source_target_pairs={{0,96},{1,97},{2,98},{3,99},{4,100},{5,101},{6,102},{7,103},{8,104... | collective-permute-start | bytes 3944456 | tf_op jit(solution)/shard_map/ppermute | solution.py:27
  13.8 16.0 %collective-permute-done.2.refs_4_ = bf16[96,5120]{1,0:T(8,128)(2,1)S(1)} collective-permute-done((bf16[96,5120]{1,0:T(8,128)(2,1)S(1)}, bf16[96,5120]{1,0:T(8,128)(2,1)S(1)}, u32[]{:S(2)}, u32[]{:S(2)}) %collective-permute-start.2) | collective-permute-done | bytes 983072 | tf_op jit(solution)/shard_map/ppermute | solution.py:27
  29.8 0.7 collective-permute-start.3
  30.5 0.4 collective-permute-done.7.refs_4_.refs_2_
  30.9 3.1 %collective-permute-done.6.refs_2_.refs_3_ = bf16[96,5120]{1,0:T(8,128)(2,1)S(1)} collective-permute-done((bf16[96,5120]{1,0:T(8,128)(2,1)S(1)}, bf16[96,5120]{1,0:T(8,128)(2,1)S(1)}, u32[]{:S(2)}, u32[]{:S(2)}) %collective-permute-start.6) | collective-permute-done | bytes 983072 | tf_op jit(solution)/shard_map/ppermute | solution.py:27
  34.1 0.3 collective-permute-start.9
  34.4 1.1 collective-permute-start.8
  35.6 1.4 collective-permute-start.4
  37.0 3.7 %collective-permute-done.1.refs_2_ = bf16[5136,128]{1,0:T(8,128)(2,1)S(1)} collective-permute-done((bf16[5136,128]{1,0:T(8,128)(2,1)S(1)}, bf16[5136,128]{1,0:T(8,128)(2,1)S(1)}, u32[]{:S(2)}, u32[]{:S(2)}) %collective-permute-start.1) | collective-permute-done | bytes 1314848 | tf_op jit(solution)/shard_map/ppermute | solution.py:27
  40.8 3.6 %collective-permute-start.5 = (bf16[2560,128]{1,0:T(8,128)(2,1)S(1)}, bf16[2560,128]{1,0:T(8,128)(2,1)S(1)}, u32[]{:S(2)}, u32[]{:S(2)}) collective-permute-start(bf16[2560,128]{1,0:T(8,128)(2,1)S(1)} %slice.66), channel_id=1, source_target_pairs={{0,96},{1,97},{2,98},{3,99},{4,100},{5,101},{6,102},{7,103},{8,104... | collective-permute-start | bytes 1966088 | tf_op jit(solution)/shard_map/ppermute | solution.py:27
  44.4 10.7 %collective-permute-done.9.refs_5_.refs_10_ = bf16[96,5120]{1,0:T(8,128)(2,1)} collective-permute-done((bf16[96,5120]{1,0:T(8,128)(2,1)S(1)}, bf16[96,5120]{1,0:T(8,128)(2,1)}, u32[]{:S(2)}, u32[]{:S(2)}) %collective-permute-start.9) | collective-permute-done | bytes 983072 | tf_op jit(solution)/shard_map/ppermute | solution.py:27
  55.0 1.6 collective-permute-done.8.refs_3_.refs_11_
  56.6 2.2 %shard_map.65 = (bf16[5136,128]{1,0:T(8,128)(2,1)S(1)}, bf16[96,5120]{1,0:T(8,128)(2,1)S(1)}, bf16[96,5120]{1,0:T(8,128)(2,1)S(1)}) custom-call(bf16[2576,128]{1,0:T(8,128)(2,1)S(1)} %collective-permute-done.4.refs_0_, bf16[2560,128]{1,0:T(8,128)(2,1)S(1)} %collective-permute-done.5.refs_1_, bf16[96,5120]{1,0:T(8,128)(2,1)S(1)} %collective-permute-done.6.refs_2_.refs_3_, ...), custom_call_target="tpu_custom_call" | custom-call | flops 1 | bytes 1 | tf_op jit(solution)/shard_map/pallas_call | solution.py:82
  58.8 3.3 %collective-permute-start.11 = (bf16[5136,128]{1,0:T(8,128)(2,1)S(1)}, bf16[5136,128]{1,0:T(8,128)(2,1)S(1)}, u32[]{:S(2)}, u32[]{:S(2)}) collective-permute-start(bf16[5136,128]{1,0:T(8,128)(2,1)S(1)} %collective-permute-done.3.refs_3_), channel_id=1, source_target_pairs={{0,96},{1,97},{2,98},{3,99},{4,100},{5,101},{6,102},{7,103},{8,104... | collective-permute-start | bytes 3944456 | tf_op jit(solution)/shard_map/ppermute | solution.py:27
  62.1 2.3 %collective-permute-start.14 = (bf16[96,5120]{1,0:T(8,128)(2,1)S(1)}, bf16[96,5120]{1,0:T(8,128)(2,1)}, u32[]{:S(2)}, u32[]{:S(2)}) collective-permute-start(bf16[96,5120]{1,0:T(8,128)(2,1)S(1)} %get-tuple-element.69), channel_id=1, source_target_pairs={{0,6},{1,7},{2,0},{3,1},{4,2},{5,3},{6,4},{7,5},{8,14},{9,15},{10,... | collective-permute-start | bytes 2949128 | tf_op jit(solution)/shard_map/ppermute | solution.py:27
  64.4 0.6 collective-permute-start.12
  65.1 17.1 %collective-permute-done.14.refs_9_.refs_1_ = bf16[96,5120]{1,0:T(8,128)(2,1)} collective-permute-done((bf16[96,5120]{1,0:T(8,128)(2,1)S(1)}, bf16[96,5120]{1,0:T(8,128)(2,1)}, u32[]{:S(2)}, u32[]{:S(2)}) %collective-permute-start.14) | collective-permute-done | bytes 983072 | tf_op jit(solution)/shard_map/ppermute | solution.py:27
  82.2 4.2 %collective-permute-start.17 = (bf16[96,5120]{1,0:T(8,128)(2,1)}, bf16[96,5120]{1,0:T(8,128)(2,1)}, u32[]{:S(2)}, u32[]{:S(2)}) collective-permute-start(bf16[96,5120]{1,0:T(8,128)(2,1)} %collective-permute-done.9.refs_5_.refs_10_), channel_id=1, source_target_pairs={{0,1},{1,0},{2,3},{3,2},{4,5},{5,4},{6,7},{7,6},{8,9},{9,8},{10,11... | collective-permute-start | bytes 2949128 | tf_op jit(solution)/shard_map/ppermute | solution.py:27
  86.4 3.5 %collective-permute-start.16 = (bf16[96,5120]{1,0:T(8,128)(2,1)}, bf16[96,5120]{1,0:T(8,128)(2,1)}, u32[]{:S(2)}, u32[]{:S(2)}) collective-permute-start(bf16[96,5120]{1,0:T(8,128)(2,1)} %collective-permute-done.14.refs_9_.refs_1_), channel_id=1, source_target_pairs={{0,1},{1,0},{2,3},{3,2},{4,5},{5,4},{6,7},{7,6},{8,9},{9,8},{10,11... | collective-permute-start | bytes 2949128 | tf_op jit(solution)/shard_map/ppermute | solution.py:27
  89.9 1.3 collective-permute-start.15
  91.2 3.4 %collective-permute-start.18 = (bf16[96,5120]{1,0:T(8,128)(2,1)}, bf16[96,5120]{1,0:T(8,128)(2,1)}, u32[]{:S(2)}, u32[]{:S(2)}) collective-permute-start(bf16[96,5120]{1,0:T(8,128)(2,1)} %collective-permute-done.8.refs_3_.refs_11_), channel_id=1, source_target_pairs={{0,1},{1,0},{2,3},{3,2},{4,5},{5,4},{6,7},{7,6},{8,9},{9,8},{10,11... | collective-permute-start | bytes 2949128 | tf_op jit(solution)/shard_map/ppermute | solution.py:27
  94.7 1.1 copy-done.17
  95.9 1.2 collective-permute-start.19
  97.2 0.4 collective-permute-start.21
  97.7 0.6 slice_bitcast_fusion.7
  98.3 17.1 %shard_map.66 = (bf16[96,5120]{1,0:T(8,128)(2,1)}, bf16[96,5120]{1,0:T(8,128)(2,1)}, bf16[96,5120]{1,0:T(8,128)(2,1)}, bf16[96,5120]{1,0:T(8,128)(2,1)}, bf16[96...) custom-call(s32[8]{0:T(128)} %get-tuple-element.109.ids, ...), custom_call_target="tpu_custom_call" | custom-call | flops 9059696640 | bytes 27525120 | tf_op jit(solution)/shard_map/pallas_call | solution.py:280
  115.5 0.5 collective-permute-start.23
  116.1 0.4 collective-permute-start.25
  116.5 1.9 collective-permute-done.23
  118.4 1.5 add_convert_fusion.6
  119.8 2.4 %collective-permute-start.28 = (bf16[96,5120]{1,0:T(8,128)(2,1)S(1)}, bf16[96,5120]{1,0:T(8,128)(2,1)}, u32[]{:S(2)}, u32[]{:S(2)}) collective-permute-start(bf16[96,5120]{1,0:T(8,128)(2,1)S(1)} %add_convert_fusion.6), channel_id=1, source_target_pairs={{0,8},{1,9},{2,10},{3,11},{4,12},{5,13},{6,14},{7,15},{8,0},{9,1},... | collective-permute-start | bytes 2949128 | tf_op jit(solution)/shard_map/ppermute | solution.py:27
  122.3 0.3 add_convert_fusion.5
  122.5 1.2 collective-permute-start.29
  123.7 0.3 add_convert_fusion.4
  123.9 1.8 collective-permute-start.30
  125.8 20.3 %shard_map.67 = (bf16[48,5120]{1,0:T(8,128)(2,1)}, bf16[48,5120]{1,0:T(8,128)(2,1)}, bf16[96,5120]{1,0:T(8,128)(2,1)}, bf16[96,5120]{1,0:T(8,128)(2,1)}, bf16[96...) custom-call(s32[8]{0:T(128)} %get-tuple-element.109.ids, ...), custom_call_target="tpu_custom_call", output_to_operand_aliasing={{10}: (13, {}), {11}: (14, {})} | custom-call | flops 12079595520 | bytes 31457280 | tf_op jit(solution)/shard_map/pallas_call | solution.py:281
  146.1 1.3 collective-permute-start.26
  147.5 1.6 collective-permute-done.26
  149.1 0.7 collective-permute-done.27
  149.8 3.0 %add_convert_fusion.7 = (bf16[48,5120]{1,0:T(8,128)(2,1)}, bf16[48,5120]{1,0:T(8,128)(2,1)}) fusion(bf16[48,5120]{1,0:T(8,128)(2,1)S(1)} %collective-permute-done.27, bf16[48,5120]{1,0:T(8,128)(2,1)} %get-tuple-element.100, bf16[96,5120]{1,0:T(8,128)(2,1)} %collective-permute-done.28, bf16[48,5120]{1,0:T(8,128)(2,1)S(1)} %collective-permute-done.26, ...), kind=kLoop, calls=%fused_computation.10 | loop fusion | flops 2949120 | bytes 3932160 | tf_op jit(solution)/shard_map/convert_element_type | solution.py:316
  152.8 0.4 collective-permute-start.33
  153.2 1.4 collective-permute-start.35
  154.6 0.7 collective-permute-start.31
  155.4 0.6 add_convert_fusion.3
  156.0 1.5 collective-permute-done.31
  157.5 0.2 convert_add_fusion.2
  157.8 1.2 collective-permute-done.32
  158.9 0.2 convert_add_fusion.1
  159.2 8.6 %shard_map.68 = (bf16[96,5120]{1,0:T(8,128)(2,1)}, bf16[96,5120]{1,0:T(8,128)(2,1)}, bf16[4,5120,256]{2,1,0:T(8,128)(2,1)S(1)}, bf16[512,5120]{1,0:T(8,128)(2,1)S(1)}) custom-call(s32[8]{0:T(128)} %get-tuple-element.109.ids, s32[8]{0:T(128)} %get-tuple-element.123.sidx, f32[64]{0:T(128)} %table.5, ...), custom_call_target="tpu_custom_call", output_to_operand_aliasing={{2}: (5, {}), {3}: (6, {})} | custom-call | flops 3019898880 | bytes 19660800 | tf_op jit(solution)/shard_map/pallas_call | solution.py:281
  167.8 0.6 collective-permute-done.34
  168.4 1.2 add_convert_fusion.2
  169.6 1.3 add_convert_fusion.1
  171.0 1.3 collective-permute-start.36
  172.3 0.7 collective-permute-start.37
  172.9 1.1 collective-permute-start.39
  174.0 0.4 collective-permute-start.38
  174.5 22.6 %collective-permute-done.37 = bf16[96,5120]{1,0:T(8,128)(2,1)S(1)} collective-permute-done((bf16[96,5120]{1,0:T(8,128)(2,1)S(1)}, bf16[96,5120]{1,0:T(8,128)(2,1)S(1)}, u32[]{:S(2)}, u32[]{:S(2)}) %collective-permute-start.37) | collective-permute-done | bytes 983072 | tf_op jit(solution)/shard_map/ppermute | solution.py:27
  197.1 0.3 convert_add_fusion
  197.5 0.4 collective-permute-done.38
  197.8 1.2 add_convert_fusion
  (93 shorter events, 1.2 us)
Async XLA Ops:
  1.3 1.3 copy-start.1
  2.6 2.3 %copy-start.11 = (bf16[96,5120]{1,0:T(8,128)(2,1)S(1)}, bf16[96,5120]{1,0:T(8,128)(2,1)}, u32[]{:S(2)}) copy-start(bf16[96,5120]{1,0:T(8,128)(2,1)} %refs_0_.1) | copy-start | bytes 2949124
  2.7 61.7 %copy-start = (bf16[5136,128]{1,0:T(8,128)(2,1)}, bf16[5136,128]{1,0:T(8,128)(2,1)S(1)}, u32[]{:S(2)}) copy-start(bf16[5136,128]{1,0:T(8,128)(2,1)S(1)} %shard_map.64.refs_0_) | copy-start | bytes 3944452
  2.8 32.8 %collective-permute-start = (bf16[5136,128]{1,0:T(8,128)(2,1)S(1)}, bf16[5136,128]{1,0:T(8,128)(2,1)S(1)}, u32[]{:S(2)}, u32[]{:S(2)}) collective-permute-start(bf16[5136,128]{1,0:T(8,128)(2,1)S(1)} %shard_map.64.refs_0_), channel_id=1, source_target_pairs={{0,32},{1,33},{2,34},{3,35},{4,36},{5,37},{6,38},{7,39},{8,40},{9,... | collective-permute-start | bytes 3944456 | tf_op jit(solution)/shard_map/ppermute | solution.py:27
  5.0 24.9 %collective-permute-start.2 = (bf16[96,5120]{1,0:T(8,128)(2,1)S(1)}, bf16[96,5120]{1,0:T(8,128)(2,1)S(1)}, u32[]{:S(2)}, u32[]{:S(2)}) collective-permute-start(bf16[96,5120]{1,0:T(8,128)(2,1)S(1)} %copy-done.11), channel_id=1, source_target_pairs={{0,8},{1,9},{2,10},{3,11},{4,12},{5,13},{6,14},{7,15},{8,0},{9,1},... | collective-permute-start | bytes 2949128 | tf_op jit(solution)/shard_map/ppermute | solution.py:27
  8.6 22.3 %collective-permute-start.7 = (bf16[96,5120]{1,0:T(8,128)(2,1)S(1)}, bf16[96,5120]{1,0:T(8,128)(2,1)S(1)}, u32[]{:S(2)}, u32[]{:S(2)}) collective-permute-start(bf16[96,5120]{1,0:T(8,128)(2,1)S(1)} %copy-done.11), channel_id=1, source_target_pairs={{0,6},{1,7},{2,0},{3,1},{4,2},{5,3},{6,4},{7,5},{8,14},{9,15},{10,... | collective-permute-start | bytes 2949128 | tf_op jit(solution)/shard_map/ppermute | solution.py:27
  11.1 23.0 %collective-permute-start.6 = (bf16[96,5120]{1,0:T(8,128)(2,1)S(1)}, bf16[96,5120]{1,0:T(8,128)(2,1)S(1)}, u32[]{:S(2)}, u32[]{:S(2)}) collective-permute-start(bf16[96,5120]{1,0:T(8,128)(2,1)S(1)} %copy-done.11), channel_id=1, source_target_pairs={{0,2},{1,3},{2,4},{3,5},{4,6},{5,7},{6,0},{7,1},{8,10},{9,11},{10,... | collective-permute-start | bytes 2949128 | tf_op jit(solution)/shard_map/ppermute | solution.py:27
  11.1 29.7 %collective-permute-start.1 = (bf16[5136,128]{1,0:T(8,128)(2,1)S(1)}, bf16[5136,128]{1,0:T(8,128)(2,1)S(1)}, u32[]{:S(2)}, u32[]{:S(2)}) collective-permute-start(bf16[5136,128]{1,0:T(8,128)(2,1)S(1)} %shard_map.64.refs_0_), channel_id=1, source_target_pairs={{0,96},{1,97},{2,98},{3,99},{4,100},{5,101},{6,102},{7,103},{8,104... | collective-permute-start | bytes 3944456 | tf_op jit(solution)/shard_map/ppermute | solution.py:27
  29.8 11.0 %copy-start.18 = (bf16[96,5120]{1,0:T(8,128)(2,1)}, bf16[96,5120]{1,0:T(8,128)(2,1)S(1)}, u32[]{:S(2)}) copy-start(bf16[96,5120]{1,0:T(8,128)(2,1)S(1)} %collective-permute-done.2.refs_4_) | copy-start | bytes 2949124
  29.8 29.0 %collective-permute-start.3 = (bf16[5136,128]{1,0:T(8,128)(2,1)S(1)}, bf16[5136,128]{1,0:T(8,128)(2,1)S(1)}, u32[]{:S(2)}, u32[]{:S(2)}) collective-permute-start(bf16[5136,128]{1,0:T(8,128)(2,1)S(1)} %shard_map.64.refs_0_), channel_id=1, source_target_pairs={{0,16},{1,17},{2,18},{3,19},{4,20},{5,21},{6,22},{7,23},{8,24},{9,... | collective-permute-start | bytes 3944456 | tf_op jit(solution)/shard_map/ppermute | solution.py:27
  30.9 64.9 %copy-start.2 = (bf16[96,5120]{1,0:T(8,128)(2,1)}, bf16[96,5120]{1,0:T(8,128)(2,1)S(1)}, u32[]{:S(2)}) copy-start(bf16[96,5120]{1,0:T(8,128)(2,1)S(1)} %collective-permute-done.7.refs_4_.refs_2_) | copy-start | bytes 2949124
  34.1 63.0 %copy-start.3 = (bf16[96,5120]{1,0:T(8,128)(2,1)}, bf16[96,5120]{1,0:T(8,128)(2,1)S(1)}, u32[]{:S(2)}) copy-start(bf16[96,5120]{1,0:T(8,128)(2,1)S(1)} %collective-permute-done.6.refs_2_.refs_3_) | copy-start | bytes 2949124
  34.1 21.0 %collective-permute-start.9 = (bf16[96,5120]{1,0:T(8,128)(2,1)S(1)}, bf16[96,5120]{1,0:T(8,128)(2,1)}, u32[]{:S(2)}, u32[]{:S(2)}) collective-permute-start(bf16[96,5120]{1,0:T(8,128)(2,1)S(1)} %collective-permute-done.2.refs_4_), channel_id=1, source_target_pairs={{0,6},{1,7},{2,0},{3,1},{4,2},{5,3},{6,4},{7,5},{8,14},{9,15},{10,... | collective-permute-start | bytes 2949128 | tf_op jit(solution)/shard_map/ppermute | solution.py:27
  34.4 22.2 %collective-permute-start.8 = (bf16[96,5120]{1,0:T(8,128)(2,1)S(1)}, bf16[96,5120]{1,0:T(8,128)(2,1)}, u32[]{:S(2)}, u32[]{:S(2)}) collective-permute-start(bf16[96,5120]{1,0:T(8,128)(2,1)S(1)} %collective-permute-done.2.refs_4_), channel_id=1, source_target_pairs={{0,2},{1,3},{2,4},{3,5},{4,6},{5,7},{6,0},{7,1},{8,10},{9,11},{10,... | collective-permute-start | bytes 2949128 | tf_op jit(solution)/shard_map/ppermute | solution.py:27
  35.5 29.5 %copy-start.12 = (bf16[5136,128]{1,0:T(8,128)(2,1)}, bf16[5136,128]{1,0:T(8,128)(2,1)S(1)}, u32[]{:S(2)}) copy-start(bf16[5136,128]{1,0:T(8,128)(2,1)S(1)} %collective-permute-done.refs_1_) | copy-start | bytes 3944452
  35.6 21.0 %collective-permute-start.4 = (bf16[2576,128]{1,0:T(8,128)(2,1)S(1)}, bf16[2576,128]{1,0:T(8,128)(2,1)S(1)}, u32[]{:S(2)}, u32[]{:S(2)}) collective-permute-start(bf16[2576,128]{1,0:T(8,128)(2,1)S(1)} %pad_maximum_fusion), channel_id=1, source_target_pairs={{0,32},{1,33},{2,34},{3,35},{4,36},{5,37},{6,38},{7,39},{8,40},{9,... | collective-permute-start | bytes 1978376 | tf_op jit(solution)/shard_map/ppermute | solution.py:27
  40.7 24.3 %copy-start.13 = (bf16[5136,128]{1,0:T(8,128)(2,1)}, bf16[5136,128]{1,0:T(8,128)(2,1)S(1)}, u32[]{:S(2)}) copy-start(bf16[5136,128]{1,0:T(8,128)(2,1)S(1)} %collective-permute-done.1.refs_2_) | copy-start | bytes 3944452
  40.8 15.8 %collective-permute-start.5 = (bf16[2560,128]{1,0:T(8,128)(2,1)S(1)}, bf16[2560,128]{1,0:T(8,128)(2,1)S(1)}, u32[]{:S(2)}, u32[]{:S(2)}) collective-permute-start(bf16[2560,128]{1,0:T(8,128)(2,1)S(1)} %slice.66), channel_id=1, source_target_pairs={{0,96},{1,97},{2,98},{3,99},{4,100},{5,101},{6,102},{7,103},{8,104... | collective-permute-start | bytes 1966088 | tf_op jit(solution)/shard_map/ppermute | solution.py:27
  58.8 32.5 %copy-start.4 = (bf16[5136,128]{1,0:T(8,128)(2,1)}, bf16[5136,128]{1,0:T(8,128)(2,1)S(1)}, u32[]{:S(2)}) copy-start(bf16[5136,128]{1,0:T(8,128)(2,1)S(1)} %get-tuple-element.67.refs_4_) | copy-start | bytes 3944452
  58.8 35.9 %copy-start.14 = (bf16[5136,128]{1,0:T(8,128)(2,1)}, bf16[5136,128]{1,0:T(8,128)(2,1)S(1)}, u32[]{:S(2)}) copy-start(bf16[5136,128]{1,0:T(8,128)(2,1)S(1)} %collective-permute-done.3.refs_3_) | copy-start | bytes 3944452
  58.8 31.1 %collective-permute-start.11 = (bf16[5136,128]{1,0:T(8,128)(2,1)S(1)}, bf16[5136,128]{1,0:T(8,128)(2,1)S(1)}, u32[]{:S(2)}, u32[]{:S(2)}) collective-permute-start(bf16[5136,128]{1,0:T(8,128)(2,1)S(1)} %collective-permute-done.3.refs_3_), channel_id=1, source_target_pairs={{0,96},{1,97},{2,98},{3,99},{4,100},{5,101},{6,102},{7,103},{8,104... | collective-permute-start | bytes 3944456 | tf_op jit(solution)/shard_map/ppermute | solution.py:27
  62.1 29.1 %collective-permute-start.10 = (bf16[5136,128]{1,0:T(8,128)(2,1)S(1)}, bf16[5136,128]{1,0:T(8,128)(2,1)S(1)}, u32[]{:S(2)}, u32[]{:S(2)}) collective-permute-start(bf16[5136,128]{1,0:T(8,128)(2,1)S(1)} %collective-permute-done.3.refs_3_), channel_id=1, source_target_pairs={{0,32},{1,33},{2,34},{3,35},{4,36},{5,37},{6,38},{7,39},{8,40},{9,... | collective-permute-start | bytes 3944456 | tf_op jit(solution)/shard_map/ppermute | solution.py:27
  62.1 20.1 %collective-permute-start.14 = (bf16[96,5120]{1,0:T(8,128)(2,1)S(1)}, bf16[96,5120]{1,0:T(8,128)(2,1)}, u32[]{:S(2)}, u32[]{:S(2)}) collective-permute-start(bf16[96,5120]{1,0:T(8,128)(2,1)S(1)} %get-tuple-element.69), channel_id=1, source_target_pairs={{0,6},{1,7},{2,0},{3,1},{4,2},{5,3},{6,4},{7,5},{8,14},{9,15},{10,... | collective-permute-start | bytes 2949128 | tf_op jit(solution)/shard_map/ppermute | solution.py:27
  64.4 22.0 %collective-permute-start.13 = (bf16[96,5120]{1,0:T(8,128)(2,1)S(1)}, bf16[96,5120]{1,0:T(8,128)(2,1)}, u32[]{:S(2)}, u32[]{:S(2)}) collective-permute-start(bf16[96,5120]{1,0:T(8,128)(2,1)S(1)} %get-tuple-element.66), channel_id=1, source_target_pairs={{0,2},{1,3},{2,4},{3,5},{4,6},{5,7},{6,0},{7,1},{8,10},{9,11},{10,... | collective-permute-start | bytes 2949128 | tf_op jit(solution)/shard_map/ppermute | solution.py:27
  64.4 30.2 %collective-permute-start.12 = (bf16[5136,128]{1,0:T(8,128)(2,1)S(1)}, bf16[5136,128]{1,0:T(8,128)(2,1)S(1)}, u32[]{:S(2)}, u32[]{:S(2)}) collective-permute-start(bf16[5136,128]{1,0:T(8,128)(2,1)S(1)} %get-tuple-element.67.refs_4_), channel_id=1, source_target_pairs={{0,16},{1,17},{2,18},{3,19},{4,20},{5,21},{6,22},{7,23},{8,24},{9,... | collective-permute-start | bytes 3944456 | tf_op jit(solution)/shard_map/ppermute | solution.py:27
  82.2 15.4 %collective-permute-start.17 = (bf16[96,5120]{1,0:T(8,128)(2,1)}, bf16[96,5120]{1,0:T(8,128)(2,1)}, u32[]{:S(2)}, u32[]{:S(2)}) collective-permute-start(bf16[96,5120]{1,0:T(8,128)(2,1)} %collective-permute-done.9.refs_5_.refs_10_), channel_id=1, source_target_pairs={{0,1},{1,0},{2,3},{3,2},{4,5},{5,4},{6,7},{7,6},{8,9},{9,8},{10,11... | collective-permute-start | bytes 2949128 | tf_op jit(solution)/shard_map/ppermute | solution.py:27
  86.4 9.4 %collective-permute-start.16 = (bf16[96,5120]{1,0:T(8,128)(2,1)}, bf16[96,5120]{1,0:T(8,128)(2,1)}, u32[]{:S(2)}, u32[]{:S(2)}) collective-permute-start(bf16[96,5120]{1,0:T(8,128)(2,1)} %collective-permute-done.14.refs_9_.refs_1_), channel_id=1, source_target_pairs={{0,1},{1,0},{2,3},{3,2},{4,5},{5,4},{6,7},{7,6},{8,9},{9,8},{10,11... | collective-permute-start | bytes 2949128 | tf_op jit(solution)/shard_map/ppermute | solution.py:27
  89.9 4.7 %copy-start.15 = (bf16[5136,128]{1,0:T(8,128)(2,1)}, bf16[5136,128]{1,0:T(8,128)(2,1)S(1)}, u32[]{:S(2)}) copy-start(bf16[5136,128]{1,0:T(8,128)(2,1)S(1)} %collective-permute-done.11.refs_6_) | copy-start | bytes 3944452
  89.9 5.9 %collective-permute-start.15 = (bf16[96,5120]{1,0:T(8,128)(2,1)}, bf16[96,5120]{1,0:T(8,128)(2,1)}, u32[]{:S(2)}, u32[]{:S(2)}) collective-permute-start(bf16[96,5120]{1,0:T(8,128)(2,1)} %collective-permute-done.13.refs_8_.refs_0_), channel_id=1, source_target_pairs={{0,1},{1,0},{2,3},{3,2},{4,5},{5,4},{6,7},{7,6},{8,9},{9,8},{10,11... | collective-permute-start | bytes 2949128 | tf_op jit(solution)/shard_map/ppermute | solution.py:27
  91.2 3.4 %copy-start.16 = (bf16[5136,128]{1,0:T(8,128)(2,1)}, bf16[5136,128]{1,0:T(8,128)(2,1)S(1)}, u32[]{:S(2)}) copy-start(bf16[5136,128]{1,0:T(8,128)(2,1)S(1)} %collective-permute-done.10.refs_5_) | copy-start | bytes 3944452
  91.2 7.0 %collective-permute-start.18 = (bf16[96,5120]{1,0:T(8,128)(2,1)}, bf16[96,5120]{1,0:T(8,128)(2,1)}, u32[]{:S(2)}, u32[]{:S(2)}) collective-permute-start(bf16[96,5120]{1,0:T(8,128)(2,1)} %collective-permute-done.8.refs_3_.refs_11_), channel_id=1, source_target_pairs={{0,1},{1,0},{2,3},{3,2},{4,5},{5,4},{6,7},{7,6},{8,9},{9,8},{10,11... | collective-permute-start | bytes 2949128 | tf_op jit(solution)/shard_map/ppermute | solution.py:27
  94.7 1.1 copy-start.17
  95.9 19.6 %collective-permute-start.19 = (bf16[96,5120]{1,0:T(8,128)(2,1)S(1)}, bf16[96,5120]{1,0:T(8,128)(2,1)}, u32[]{:S(2)}, u32[]{:S(2)}) collective-permute-start(bf16[96,5120]{1,0:T(8,128)(2,1)S(1)} %collective-permute-done.7.refs_4_.refs_2_), channel_id=1, source_target_pairs={{0,1},{1,0},{2,3},{3,2},{4,5},{5,4},{6,7},{7,6},{8,9},{9,8},{10,11... | collective-permute-start | bytes 2949128 | tf_op jit(solution)/shard_map/ppermute | solution.py:27
  97.1 18.4 %collective-permute-start.20 = (bf16[96,5120]{1,0:T(8,128)(2,1)S(1)}, bf16[96,5120]{1,0:T(8,128)(2,1)}, u32[]{:S(2)}, u32[]{:S(2)}) collective-permute-start(bf16[96,5120]{1,0:T(8,128)(2,1)S(1)} %collective-permute-done.6.refs_2_.refs_3_), channel_id=1, source_target_pairs={{0,1},{1,0},{2,3},{3,2},{4,5},{5,4},{6,7},{7,6},{8,9},{9,8},{10,11... | collective-permute-start | bytes 2949128 | tf_op jit(solution)/shard_map/ppermute | solution.py:27
  97.2 18.3 %collective-permute-start.21 = (bf16[96,5120]{1,0:T(8,128)(2,1)}, bf16[96,5120]{1,0:T(8,128)(2,1)}, u32[]{:S(2)}, u32[]{:S(2)}) collective-permute-start(bf16[96,5120]{1,0:T(8,128)(2,1)} %copy-done.18), channel_id=1, source_target_pairs={{0,1},{1,0},{2,3},{3,2},{4,5},{5,4},{6,7},{7,6},{8,9},{9,8},{10,11... | collective-permute-start | bytes 2949128 | tf_op jit(solution)/shard_map/ppermute | solution.py:27
  97.6 17.9 %collective-permute-start.22 = (bf16[96,5120]{1,0:T(8,128)(2,1)S(1)}, bf16[96,5120]{1,0:T(8,128)(2,1)}, u32[]{:S(2)}, u32[]{:S(2)}) collective-permute-start(bf16[96,5120]{1,0:T(8,128)(2,1)S(1)} %copy-done.11), channel_id=1, source_target_pairs={{0,1},{1,0},{2,3},{3,2},{4,5},{5,4},{6,7},{7,6},{8,9},{9,8},{10,11... | collective-permute-start | bytes 2949128 | tf_op jit(solution)/shard_map/ppermute | solution.py:27
  115.4 6.8 %copy-start.8 = (bf16[96,5120]{1,0:T(8,128)(2,1)S(1)}, bf16[96,5120]{1,0:T(8,128)(2,1)}, u32[]{:S(2)}) copy-start(bf16[96,5120]{1,0:T(8,128)(2,1)} %get-tuple-element.82) | copy-start | bytes 2949124
  115.5 2.9 %collective-permute-start.23 = (bf16[96,5120]{1,0:T(8,128)(2,1)}, bf16[96,5120]{1,0:T(8,128)(2,1)S(1)}, u32[]{:S(2)}, u32[]{:S(2)}) collective-permute-start(bf16[96,5120]{1,0:T(8,128)(2,1)} %get-tuple-element.81), channel_id=1, source_target_pairs={{0,1},{1,0},{2,3},{3,2},{4,5},{5,4},{6,7},{7,6},{8,9},{9,8},{10,11... | collective-permute-start | bytes 2949128 | tf_op jit(solution)/shard_map/ppermute | solution.py:27
  116.0 6.3 %collective-permute-start.24 = (bf16[96,5120]{1,0:T(8,128)(2,1)}, bf16[96,5120]{1,0:T(8,128)(2,1)S(1)}, u32[]{:S(2)}, u32[]{:S(2)}) collective-permute-start(bf16[96,5120]{1,0:T(8,128)(2,1)} %get-tuple-element.83), channel_id=1, source_target_pairs={{0,1},{1,0},{2,3},{3,2},{4,5},{5,4},{6,7},{7,6},{8,9},{9,8},{10,11... | collective-permute-start | bytes 2949128 | tf_op jit(solution)/shard_map/ppermute | solution.py:27
  116.1 7.6 %collective-permute-start.25 = (bf16[96,5120]{1,0:T(8,128)(2,1)}, bf16[96,5120]{1,0:T(8,128)(2,1)S(1)}, u32[]{:S(2)}, u32[]{:S(2)}) collective-permute-start(bf16[96,5120]{1,0:T(8,128)(2,1)} %get-tuple-element.85), channel_id=1, source_target_pairs={{0,1},{1,0},{2,3},{3,2},{4,5},{5,4},{6,7},{7,6},{8,9},{9,8},{10,11... | collective-permute-start | bytes 2949128 | tf_op jit(solution)/shard_map/ppermute | solution.py:27
  119.8 3.9 %copy-start.7 = (bf16[96,5120]{1,0:T(8,128)(2,1)S(1)}, bf16[96,5120]{1,0:T(8,128)(2,1)}, u32[]{:S(2)}) copy-start(bf16[96,5120]{1,0:T(8,128)(2,1)} %get-tuple-element.84) | copy-start | bytes 2949124
  119.8 29.9 %collective-permute-start.28 = (bf16[96,5120]{1,0:T(8,128)(2,1)S(1)}, bf16[96,5120]{1,0:T(8,128)(2,1)}, u32[]{:S(2)}, u32[]{:S(2)}) collective-permute-start(bf16[96,5120]{1,0:T(8,128)(2,1)S(1)} %add_convert_fusion.6), channel_id=1, source_target_pairs={{0,8},{1,9},{2,10},{3,11},{4,12},{5,13},{6,14},{7,15},{8,0},{9,1},... | collective-permute-start | bytes 2949128 | tf_op jit(solution)/shard_map/ppermute | solution.py:27
  122.5 27.3 %collective-permute-start.29 = (bf16[96,5120]{1,0:T(8,128)(2,1)S(1)}, bf16[96,5120]{1,0:T(8,128)(2,1)S(1)}, u32[]{:S(2)}, u32[]{:S(2)}) collective-permute-start(bf16[96,5120]{1,0:T(8,128)(2,1)S(1)} %add_convert_fusion.5), channel_id=1, source_target_pairs={{0,2},{1,3},{2,4},{3,5},{4,6},{5,7},{6,0},{7,1},{8,10},{9,11},{10,... | collective-permute-start | bytes 2949128 | tf_op jit(solution)/shard_map/ppermute | solution.py:27
  123.9 25.8 %collective-permute-start.30 = (bf16[96,5120]{1,0:T(8,128)(2,1)S(1)}, bf16[96,5120]{1,0:T(8,128)(2,1)S(1)}, u32[]{:S(2)}, u32[]{:S(2)}) collective-permute-start(bf16[96,5120]{1,0:T(8,128)(2,1)S(1)} %add_convert_fusion.4), channel_id=1, source_target_pairs={{0,6},{1,7},{2,0},{3,1},{4,2},{5,3},{6,4},{7,5},{8,14},{9,15},{10,... | collective-permute-start | bytes 2949128 | tf_op jit(solution)/shard_map/ppermute | solution.py:27
  146.1 3.0 %collective-permute-start.26 = (bf16[48,5120]{1,0:T(8,128)(2,1)}, bf16[48,5120]{1,0:T(8,128)(2,1)S(1)}, u32[]{:S(2)}, u32[]{:S(2)}) collective-permute-start(bf16[48,5120]{1,0:T(8,128)(2,1)} %get-tuple-element.95), channel_id=1, source_target_pairs={{0,1},{1,0},{2,3},{3,2},{4,5},{5,4},{6,7},{7,6},{8,9},{9,8},{10,11... | collective-permute-start | bytes 1474568 | tf_op jit(solution)/shard_map/ppermute | solution.py:27
  147.4 2.4 %collective-permute-start.27 = (bf16[48,5120]{1,0:T(8,128)(2,1)}, bf16[48,5120]{1,0:T(8,128)(2,1)S(1)}, u32[]{:S(2)}, u32[]{:S(2)}) collective-permute-start(bf16[48,5120]{1,0:T(8,128)(2,1)} %get-tuple-element.96), channel_id=1, source_target_pairs={{0,1},{1,0},{2,3},{3,2},{4,5},{5,4},{6,7},{7,6},{8,9},{9,8},{10,11... | collective-permute-start | bytes 1474568 | tf_op jit(solution)/shard_map/ppermute | solution.py:27
  149.8 3.0 %copy-start.21 = (bf16[96,5120]{1,0:T(8,128)(2,1)S(1)}, bf16[96,5120]{1,0:T(8,128)(2,1)}, u32[]{:S(2)}) copy-start(bf16[96,5120]{1,0:T(8,128)(2,1)} %get-tuple-element.106) | copy-start | bytes 2949124
  149.8 4.8 %copy-start.20 = (bf16[96,5120]{1,0:T(8,128)(2,1)S(1)}, bf16[96,5120]{1,0:T(8,128)(2,1)}, u32[]{:S(2)}) copy-start(bf16[96,5120]{1,0:T(8,128)(2,1)} %get-tuple-element.102) | copy-start | bytes 2949124
  149.8 5.5 %copy-start.19 = (bf16[96,5120]{1,0:T(8,128)(2,1)S(1)}, bf16[96,5120]{1,0:T(8,128)(2,1)}, u32[]{:S(2)}) copy-start(bf16[96,5120]{1,0:T(8,128)(2,1)} %get-tuple-element.104) | copy-start | bytes 2949124
  149.8 5.6 %copy-start.5 = (bf16[96,5120]{1,0:T(8,128)(2,1)S(1)}, bf16[96,5120]{1,0:T(8,128)(2,1)}, u32[]{:S(2)}) copy-start(bf16[96,5120]{1,0:T(8,128)(2,1)} %get-tuple-element.105) | copy-start | bytes 2949124
  152.8 2.6 %collective-permute-start.33 = (bf16[96,5120]{1,0:T(8,128)(2,1)S(1)}, bf16[96,5120]{1,0:T(8,128)(2,1)S(1)}, u32[]{:S(2)}, u32[]{:S(2)}) collective-permute-start(bf16[96,5120]{1,0:T(8,128)(2,1)S(1)} %copy-done.21), channel_id=1, source_target_pairs={{0,1},{1,0},{2,3},{3,2},{4,5},{5,4},{6,7},{7,6},{8,9},{9,8},{10,11... | collective-permute-start | bytes 2949128 | tf_op jit(solution)/shard_map/ppermute | solution.py:27
  153.2 14.7 %collective-permute-start.35 = (bf16[48,5120]{1,0:T(8,128)(2,1)}, bf16[48,5120]{1,0:T(8,128)(2,1)}, u32[]{:S(2)}, u32[]{:S(2)}) collective-permute-start(bf16[48,5120]{1,0:T(8,128)(2,1)} %get-tuple-element.121), channel_id=1, source_target_pairs={{0,6},{1,7},{2,0},{3,1},{4,2},{5,3},{6,4},{7,5},{8,14},{9,15},{10,... | collective-permute-start | bytes 1474568 | tf_op jit(solution)/shard_map/ppermute | solution.py:27
  154.5 13.9 %collective-permute-start.34 = (bf16[48,5120]{1,0:T(8,128)(2,1)}, bf16[48,5120]{1,0:T(8,128)(2,1)}, u32[]{:S(2)}, u32[]{:S(2)}) collective-permute-start(bf16[48,5120]{1,0:T(8,128)(2,1)} %get-tuple-element.122), channel_id=1, source_target_pairs={{0,2},{1,3},{2,4},{3,5},{4,6},{5,7},{6,0},{7,1},{8,10},{9,11},{10,... | collective-permute-start | bytes 1474568 | tf_op jit(solution)/shard_map/ppermute | solution.py:27
  154.6 2.9 %collective-permute-start.31 = (bf16[96,5120]{1,0:T(8,128)(2,1)S(1)}, bf16[96,5120]{1,0:T(8,128)(2,1)S(1)}, u32[]{:S(2)}, u32[]{:S(2)}) collective-permute-start(bf16[96,5120]{1,0:T(8,128)(2,1)S(1)} %copy-done.20), channel_id=1, source_target_pairs={{0,1},{1,0},{2,3},{3,2},{4,5},{5,4},{6,7},{7,6},{8,9},{9,8},{10,11... | collective-permute-start | bytes 2949128 | tf_op jit(solution)/shard_map/ppermute | solution.py:27
  155.3 3.6 %collective-permute-start.32 = (bf16[96,5120]{1,0:T(8,128)(2,1)S(1)}, bf16[96,5120]{1,0:T(8,128)(2,1)S(1)}, u32[]{:S(2)}, u32[]{:S(2)}) collective-permute-start(bf16[96,5120]{1,0:T(8,128)(2,1)S(1)} %copy-done.19), channel_id=1, source_target_pairs={{0,1},{1,0},{2,3},{3,2},{4,5},{5,4},{6,7},{7,6},{8,9},{9,8},{10,11... | collective-permute-start | bytes 2949128 | tf_op jit(solution)/shard_map/ppermute | solution.py:27
  155.4 2.1 %copy-start.10 = (bf16[96,5120]{1,0:T(8,128)(2,1)S(1)}, bf16[96,5120]{1,0:T(8,128)(2,1)}, u32[]{:S(2)}) copy-start(bf16[96,5120]{1,0:T(8,128)(2,1)} %get-tuple-element.89) | copy-start | bytes 2949124
  157.5 1.4 copy-start.9
  169.6 1.4 copy-start.22
  169.6 27.5 %copy-start.6 = (bf16[96,5120]{1,0:T(8,128)(2,1)S(1)}, bf16[96,5120]{1,0:T(8,128)(2,1)}, u32[]{:S(2)}) copy-start(bf16[96,5120]{1,0:T(8,128)(2,1)} %get-tuple-element.113) | copy-start | bytes 2949124
  171.0 3.5 %collective-permute-start.36 = (bf16[96,5120]{1,0:T(8,128)(2,1)S(1)}, bf16[96,5120]{1,0:T(8,128)(2,1)S(1)}, u32[]{:S(2)}, u32[]{:S(2)}) collective-permute-start(bf16[96,5120]{1,0:T(8,128)(2,1)S(1)} %copy-done.22), channel_id=1, source_target_pairs={{0,1},{1,0},{2,3},{3,2},{4,5},{5,4},{6,7},{7,6},{8,9},{9,8},{10,11... | collective-permute-start | bytes 2949128 | tf_op jit(solution)/shard_map/ppermute | solution.py:27
  172.3 24.8 %collective-permute-start.37 = (bf16[96,5120]{1,0:T(8,128)(2,1)S(1)}, bf16[96,5120]{1,0:T(8,128)(2,1)S(1)}, u32[]{:S(2)}, u32[]{:S(2)}) collective-permute-start(bf16[96,5120]{1,0:T(8,128)(2,1)S(1)} %add_convert_fusion.3), channel_id=1, source_target_pairs={{0,8},{1,9},{2,10},{3,11},{4,12},{5,13},{6,14},{7,15},{8,0},{9,1},... | collective-permute-start | bytes 2949128 | tf_op jit(solution)/shard_map/ppermute | solution.py:27
  172.9 24.5 %collective-permute-start.39 = (bf16[96,5120]{1,0:T(8,128)(2,1)S(1)}, bf16[96,5120]{1,0:T(8,128)(2,1)S(1)}, u32[]{:S(2)}, u32[]{:S(2)}) collective-permute-start(bf16[96,5120]{1,0:T(8,128)(2,1)S(1)} %add_convert_fusion.1), channel_id=1, source_target_pairs={{0,6},{1,7},{2,0},{3,1},{4,2},{5,3},{6,4},{7,5},{8,14},{9,15},{10,... | collective-permute-start | bytes 2949128 | tf_op jit(solution)/shard_map/ppermute | solution.py:27
  174.0 23.8 %collective-permute-start.38 = (bf16[96,5120]{1,0:T(8,128)(2,1)S(1)}, bf16[96,5120]{1,0:T(8,128)(2,1)S(1)}, u32[]{:S(2)}, u32[]{:S(2)}) collective-permute-start(bf16[96,5120]{1,0:T(8,128)(2,1)S(1)} %add_convert_fusion.2), channel_id=1, source_target_pairs={{0,2},{1,3},{2,4},{3,5},{4,6},{5,7},{6,0},{7,1},{8,10},{9,11},{10,... | collective-permute-start | bytes 2949128 | tf_op jit(solution)/shard_map/ppermute | solution.py:27

commit v8 on v7

--- a/solution.py
+++ b/solution.py
@@ -9,7 +9,7 @@
 AXES = ("dp", "tensor")
 BF16, F32 = jnp.bfloat16, jnp.float32
 NOTE = 16
-STEP = 1024
+STEP = 2560
 
 
 def place(y, zl, zh, x, c):
@@ -313,7 +313,7 @@
     got = swap(*part[5:7])
     far, got, far_in, z_right, z_left = after((far, got, far_in, z_right, z_left))
     top = add(far[0], got[0], far_in[:h_rows]).astype(BF16)
-    low = add(far[1], got[1], far_in[h_rows:]).astype(BF16)
+    low = add(after(far[1], top), got[1], far_in[h_rows:]).astype(BF16)
     past_top, past_low = move(top, dx=1), move(low, dx=-1)
 
     near_sib, z_sib = after((near_sib, z_sib), top, low)

time: 200 us -> 199 us (level)
    convert_element_type x1 -> x2, other arithmetic: 2.96 us -> 4.36 us  [the longest x1 2.34 us: body(): top = add(far[0], got[0], far_in[:h_rows]).astype(BF16)]
  transfers between devices with their start and end apart: 40 -> 40, of which waited for: 16 -> 15; matrix products, arithmetic and copies ran while one was open for 2% -> 2% of each run, Pallas kernels for 24% -> 23%
where the time goes in v8:
time: 199 us
  waiting for transfers between devices  83.8 us (42%)
  starting transfers between devices  52.5 us (26%)
  Pallas kernels  46.4 us (23%)
  other arithmetic  11.4 us (6%)
  local copies, waits for them, and re-layouts  3.28 us (2%)
    ppermute x40, waiting for transfers between devices, move(): return lax.ppermute(value, AXES, pairs)  83.8 us
    ppermute x40, starting transfers between devices, move(): return lax.ppermute(value, AXES, pairs)  52.5 us
    pallas_call x2, Pallas kernels, sums(): return tuple(run(ids, sidx, scale_table, *pieces, *weights))  27.5 us
    pallas_call x1, Pallas kernels, sums(): return tuple(run(ids, sidx, scale_table, *sources, *pieces, down_weight))  16.6 us
  transfers between devices with their start and end apart: 40, of which 15 were waited for; matrix products, arithmetic and copies ran while one was open for 2% of the time, Pallas kernels for 23%

profile of v8, /device:TPU:1, one launch (start us, length us, event | category | flops | bytes accessed | tf_op | source)
XLA Modules:
  0.0 199.1 jit_solution(13051293588318165204)
XLA Ops:
  1.3 1.3 copy-done.1
  2.8 2.2 %collective-permute-start = (bf16[5136,128]{1,0:T(8,128)(2,1)S(1)}, bf16[5136,128]{1,0:T(8,128)(2,1)S(1)}, u32[]{:S(2)}, u32[]{:S(2)}) collective-permute-start(bf16[5136,128]{1,0:T(8,128)(2,1)S(1)} %shard_map.64.refs_0_), channel_id=1, source_target_pairs={{0,32},{1,33},{2,34},{3,35},{4,36},{5,37},{6,38},{7,39},{8,40},{9,... | collective-permute-start | bytes 3944456 | tf_op jit(solution)/shard_map/ppermute | solution.py:27
  5.0 3.6 %collective-permute-start.2 = (bf16[96,5120]{1,0:T(8,128)(2,1)S(1)}, bf16[96,5120]{1,0:T(8,128)(2,1)S(1)}, u32[]{:S(2)}, u32[]{:S(2)}) collective-permute-start(bf16[96,5120]{1,0:T(8,128)(2,1)S(1)} %copy-done.11), channel_id=1, source_target_pairs={{0,8},{1,9},{2,10},{3,11},{4,12},{5,13},{6,14},{7,15},{8,0},{9,1},... | collective-permute-start | bytes 2949128 | tf_op jit(solution)/shard_map/ppermute | solution.py:27
  8.6 2.5 %collective-permute-start.7 = (bf16[96,5120]{1,0:T(8,128)(2,1)S(1)}, bf16[96,5120]{1,0:T(8,128)(2,1)S(1)}, u32[]{:S(2)}, u32[]{:S(2)}) collective-permute-start(bf16[96,5120]{1,0:T(8,128)(2,1)S(1)} %copy-done.11), channel_id=1, source_target_pairs={{0,6},{1,7},{2,0},{3,1},{4,2},{5,3},{6,4},{7,5},{8,14},{9,15},{10,... | collective-permute-start | bytes 2949128 | tf_op jit(solution)/shard_map/ppermute | solution.py:27
  11.1 2.7 %collective-permute-start.1 = (bf16[5136,128]{1,0:T(8,128)(2,1)S(1)}, bf16[5136,128]{1,0:T(8,128)(2,1)S(1)}, u32[]{:S(2)}, u32[]{:S(2)}) collective-permute-start(bf16[5136,128]{1,0:T(8,128)(2,1)S(1)} %shard_map.64.refs_0_), channel_id=1, source_target_pairs={{0,96},{1,97},{2,98},{3,99},{4,100},{5,101},{6,102},{7,103},{8,104... | collective-permute-start | bytes 3944456 | tf_op jit(solution)/shard_map/ppermute | solution.py:27
  13.8 16.0 %collective-permute-done.2.refs_4_ = bf16[96,5120]{1,0:T(8,128)(2,1)S(1)} collective-permute-done((bf16[96,5120]{1,0:T(8,128)(2,1)S(1)}, bf16[96,5120]{1,0:T(8,128)(2,1)S(1)}, u32[]{:S(2)}, u32[]{:S(2)}) %collective-permute-start.2) | collective-permute-done | bytes 983072 | tf_op jit(solution)/shard_map/ppermute | solution.py:27
  29.8 0.7 collective-permute-start.3
  30.5 0.4 collective-permute-done.7.refs_4_.refs_2_
  30.9 3.1 %collective-permute-done.6.refs_2_.refs_3_ = bf16[96,5120]{1,0:T(8,128)(2,1)S(1)} collective-permute-done((bf16[96,5120]{1,0:T(8,128)(2,1)S(1)}, bf16[96,5120]{1,0:T(8,128)(2,1)S(1)}, u32[]{:S(2)}, u32[]{:S(2)}) %collective-permute-start.6) | collective-permute-done | bytes 983072 | tf_op jit(solution)/shard_map/ppermute | solution.py:27
  34.1 0.3 collective-permute-start.9
  34.4 1.1 collective-permute-start.8
  35.6 1.4 collective-permute-start.4
  37.0 3.7 %collective-permute-done.1.refs_2_ = bf16[5136,128]{1,0:T(8,128)(2,1)S(1)} collective-permute-done((bf16[5136,128]{1,0:T(8,128)(2,1)S(1)}, bf16[5136,128]{1,0:T(8,128)(2,1)S(1)}, u32[]{:S(2)}, u32[]{:S(2)}) %collective-permute-start.1) | collective-permute-done | bytes 1314848 | tf_op jit(solution)/shard_map/ppermute | solution.py:27
  40.8 3.6 %collective-permute-start.5 = (bf16[2560,128]{1,0:T(8,128)(2,1)S(1)}, bf16[2560,128]{1,0:T(8,128)(2,1)S(1)}, u32[]{:S(2)}, u32[]{:S(2)}) collective-permute-start(bf16[2560,128]{1,0:T(8,128)(2,1)S(1)} %slice.66), channel_id=1, source_target_pairs={{0,96},{1,97},{2,98},{3,99},{4,100},{5,101},{6,102},{7,103},{8,104... | collective-permute-start | bytes 1966088 | tf_op jit(solution)/shard_map/ppermute | solution.py:27
  44.4 10.7 %collective-permute-done.9.refs_5_.refs_10_ = bf16[96,5120]{1,0:T(8,128)(2,1)} collective-permute-done((bf16[96,5120]{1,0:T(8,128)(2,1)S(1)}, bf16[96,5120]{1,0:T(8,128)(2,1)}, u32[]{:S(2)}, u32[]{:S(2)}) %collective-permute-start.9) | collective-permute-done | bytes 983072 | tf_op jit(solution)/shard_map/ppermute | solution.py:27
  55.0 1.6 collective-permute-done.8.refs_3_.refs_11_
  56.6 2.2 %shard_map.65 = (bf16[5136,128]{1,0:T(8,128)(2,1)S(1)}, bf16[96,5120]{1,0:T(8,128)(2,1)S(1)}, bf16[96,5120]{1,0:T(8,128)(2,1)S(1)}) custom-call(bf16[2576,128]{1,0:T(8,128)(2,1)S(1)} %collective-permute-done.4.refs_0_, bf16[2560,128]{1,0:T(8,128)(2,1)S(1)} %collective-permute-done.5.refs_1_, bf16[96,5120]{1,0:T(8,128)(2,1)S(1)} %collective-permute-done.6.refs_2_.refs_3_, ...), custom_call_target="tpu_custom_call" | custom-call | flops 1 | bytes 1 | tf_op jit(solution)/shard_map/pallas_call | solution.py:82
  58.8 3.3 %collective-permute-start.11 = (bf16[5136,128]{1,0:T(8,128)(2,1)S(1)}, bf16[5136,128]{1,0:T(8,128)(2,1)S(1)}, u32[]{:S(2)}, u32[]{:S(2)}) collective-permute-start(bf16[5136,128]{1,0:T(8,128)(2,1)S(1)} %collective-permute-done.3.refs_3_), channel_id=1, source_target_pairs={{0,96},{1,97},{2,98},{3,99},{4,100},{5,101},{6,102},{7,103},{8,104... | collective-permute-start | bytes 3944456 | tf_op jit(solution)/shard_map/ppermute | solution.py:27
  62.1 2.3 %collective-permute-start.14 = (bf16[96,5120]{1,0:T(8,128)(2,1)S(1)}, bf16[96,5120]{1,0:T(8,128)(2,1)}, u32[]{:S(2)}, u32[]{:S(2)}) collective-permute-start(bf16[96,5120]{1,0:T(8,128)(2,1)S(1)} %get-tuple-element.70), channel_id=1, source_target_pairs={{0,6},{1,7},{2,0},{3,1},{4,2},{5,3},{6,4},{7,5},{8,14},{9,15},{10,... | collective-permute-start | bytes 2949128 | tf_op jit(solution)/shard_map/ppermute | solution.py:27
  64.4 0.6 collective-permute-start.12
  65.1 17.1 %collective-permute-done.14.refs_9_.refs_1_ = bf16[96,5120]{1,0:T(8,128)(2,1)} collective-permute-done((bf16[96,5120]{1,0:T(8,128)(2,1)S(1)}, bf16[96,5120]{1,0:T(8,128)(2,1)}, u32[]{:S(2)}, u32[]{:S(2)}) %collective-permute-start.14) | collective-permute-done | bytes 983072 | tf_op jit(solution)/shard_map/ppermute | solution.py:27
  82.2 4.2 %collective-permute-start.17 = (bf16[96,5120]{1,0:T(8,128)(2,1)}, bf16[96,5120]{1,0:T(8,128)(2,1)}, u32[]{:S(2)}, u32[]{:S(2)}) collective-permute-start(bf16[96,5120]{1,0:T(8,128)(2,1)} %collective-permute-done.9.refs_5_.refs_10_), channel_id=1, source_target_pairs={{0,1},{1,0},{2,3},{3,2},{4,5},{5,4},{6,7},{7,6},{8,9},{9,8},{10,11... | collective-permute-start | bytes 2949128 | tf_op jit(solution)/shard_map/ppermute | solution.py:27
  86.4 3.5 %collective-permute-start.16 = (bf16[96,5120]{1,0:T(8,128)(2,1)}, bf16[96,5120]{1,0:T(8,128)(2,1)}, u32[]{:S(2)}, u32[]{:S(2)}) collective-permute-start(bf16[96,5120]{1,0:T(8,128)(2,1)} %collective-permute-done.14.refs_9_.refs_1_), channel_id=1, source_target_pairs={{0,1},{1,0},{2,3},{3,2},{4,5},{5,4},{6,7},{7,6},{8,9},{9,8},{10,11... | collective-permute-start | bytes 2949128 | tf_op jit(solution)/shard_map/ppermute | solution.py:27
  89.9 1.3 collective-permute-start.15
  91.2 3.4 %collective-permute-start.18 = (bf16[96,5120]{1,0:T(8,128)(2,1)}, bf16[96,5120]{1,0:T(8,128)(2,1)}, u32[]{:S(2)}, u32[]{:S(2)}) collective-permute-start(bf16[96,5120]{1,0:T(8,128)(2,1)} %collective-permute-done.8.refs_3_.refs_11_), channel_id=1, source_target_pairs={{0,1},{1,0},{2,3},{3,2},{4,5},{5,4},{6,7},{7,6},{8,9},{9,8},{10,11... | collective-permute-start | bytes 2949128 | tf_op jit(solution)/shard_map/ppermute | solution.py:27
  94.7 1.1 copy-done.18
  95.9 1.2 collective-permute-start.19
  97.2 0.4 collective-permute-start.21
  97.7 0.6 slice_bitcast_fusion.7
  98.3 16.6 %shard_map.66 = (bf16[96,5120]{1,0:T(8,128)(2,1)}, bf16[96,5120]{1,0:T(8,128)(2,1)}, bf16[96,5120]{1,0:T(8,128)(2,1)}, bf16[96,5120]{1,0:T(8,128)(2,1)}, bf16[96...) custom-call(s32[8]{0:T(128)} %get-tuple-element.111.ids, ...), custom_call_target="tpu_custom_call" | custom-call | flops 9059696640 | bytes 27525120 | tf_op jit(solution)/shard_map/pallas_call | solution.py:280
  115.0 0.5 collective-permute-start.23
  115.6 0.4 collective-permute-start.25
  116.0 1.9 collective-permute-done.23
  117.9 1.5 add_convert_fusion.6
  119.3 2.4 %collective-permute-start.28 = (bf16[96,5120]{1,0:T(8,128)(2,1)S(1)}, bf16[96,5120]{1,0:T(8,128)(2,1)}, u32[]{:S(2)}, u32[]{:S(2)}) collective-permute-start(bf16[96,5120]{1,0:T(8,128)(2,1)S(1)} %add_convert_fusion.6), channel_id=1, source_target_pairs={{0,8},{1,9},{2,10},{3,11},{4,12},{5,13},{6,14},{7,15},{8,0},{9,1},... | collective-permute-start | bytes 2949128 | tf_op jit(solution)/shard_map/ppermute | solution.py:27
  121.7 0.3 add_convert_fusion.5
  122.0 1.0 collective-permute-start.29
  123.0 0.3 add_convert_fusion.4
  123.3 1.8 collective-permute-start.30
  125.1 19.9 %shard_map.67 = (bf16[48,5120]{1,0:T(8,128)(2,1)}, bf16[48,5120]{1,0:T(8,128)(2,1)}, bf16[96,5120]{1,0:T(8,128)(2,1)}, bf16[96,5120]{1,0:T(8,128)(2,1)}, bf16[96...) custom-call(s32[8]{0:T(128)} %get-tuple-element.111.ids, ...), custom_call_target="tpu_custom_call", output_to_operand_aliasing={{10}: (13, {}), {11}: (14, {})} | custom-call | flops 12079595520 | bytes 31457280 | tf_op jit(solution)/shard_map/pallas_call | solution.py:281
  145.0 1.3 collective-permute-start.26
  146.4 1.6 collective-permute-done.26
  148.0 0.7 collective-permute-done.27
  148.8 2.3 %add_convert_fusion.8 = bf16[48,5120]{1,0:T(8,128)(2,1)} fusion(bf16[48,5120]{1,0:T(8,128)(2,1)S(1)} %collective-permute-done.26, bf16[48,5120]{1,0:T(8,128)(2,1)} %get-tuple-element.98, bf16[96,5120]{1,0:T(8,128)(2,1)} %collective-permute-done.28), kind=kLoop, calls=%fused_computation.11 | loop fusion | flops 1474560 | bytes 1966080 | tf_op jit(solution)/shard_map/convert_element_type | solution.py:315
  151.1 2.0 %add_convert_fusion.7 = bf16[48,5120]{1,0:T(8,128)(2,1)} fusion(bf16[48,5120]{1,0:T(8,128)(2,1)S(1)} %collective-permute-done.27, bf16[48,5120]{1,0:T(8,128)(2,1)S(1)} %copy-done.12, bf16[96,5120]{1,0:T(8,128)(2,1)} %collective-permute-done.28), kind=kLoop, calls=%fused_computation.10 | loop fusion | flops 1474560 | bytes 1966080 | tf_op jit(solution)/shard_map/convert_element_type | solution.py:316
  153.1 0.4 collective-permute-start.33
  153.5 1.4 collective-permute-start.35
  155.0 0.7 collective-permute-start.31
  155.8 0.1 collective-permute-done.33
  155.9 0.6 add_convert_fusion.3
  156.5 1.4 collective-permute-done.31
  157.9 0.2 convert_add_fusion.2
  158.1 1.2 collective-permute-done.32
  159.3 0.2 convert_add_fusion.1
  159.5 7.6 %shard_map.68 = (bf16[96,5120]{1,0:T(8,128)(2,1)}, bf16[96,5120]{1,0:T(8,128)(2,1)}, bf16[4,5120,256]{2,1,0:T(8,128)(2,1)S(1)}, bf16[512,5120]{1,0:T(8,128)(2,1)S(1)}) custom-call(s32[8]{0:T(128)} %get-tuple-element.111.ids, s32[8]{0:T(128)} %get-tuple-element.123.sidx, f32[64]{0:T(128)} %table.5, ...), custom_call_target="tpu_custom_call", output_to_operand_aliasing={{2}: (5, {}), {3}: (6, {})} | custom-call | flops 3019898880 | bytes 19660800 | tf_op jit(solution)/shard_map/pallas_call | solution.py:281
  167.1 1.7 collective-permute-done.34
  168.8 1.2 add_convert_fusion.2
  170.0 1.3 add_convert_fusion.1
  171.3 1.3 collective-permute-start.36
  172.7 0.8 collective-permute-start.37
  173.5 1.5 collective-permute-start.38
  174.9 22.6 %collective-permute-done.37 = bf16[96,5120]{1,0:T(8,128)(2,1)S(1)} collective-permute-done((bf16[96,5120]{1,0:T(8,128)(2,1)S(1)}, bf16[96,5120]{1,0:T(8,128)(2,1)S(1)}, u32[]{:S(2)}, u32[]{:S(2)}) %collective-permute-start.37) | collective-permute-done | bytes 983072 | tf_op jit(solution)/shard_map/ppermute | solution.py:27
  197.5 0.3 convert_add_fusion
  197.8 1.2 add_convert_fusion
  (94 shorter events, 1.1 us)
Async XLA Ops:
  1.3 1.3 copy-start.1
  2.6 2.3 %copy-start.11 = (bf16[96,5120]{1,0:T(8,128)(2,1)S(1)}, bf16[96,5120]{1,0:T(8,128)(2,1)}, u32[]{:S(2)}) copy-start(bf16[96,5120]{1,0:T(8,128)(2,1)} %refs_0_.1) | copy-start | bytes 2949124
  2.7 61.7 %copy-start = (bf16[5136,128]{1,0:T(8,128)(2,1)}, bf16[5136,128]{1,0:T(8,128)(2,1)S(1)}, u32[]{:S(2)}) copy-start(bf16[5136,128]{1,0:T(8,128)(2,1)S(1)} %shard_map.64.refs_0_) | copy-start | bytes 3944452
  2.8 32.8 %collective-permute-start = (bf16[5136,128]{1,0:T(8,128)(2,1)S(1)}, bf16[5136,128]{1,0:T(8,128)(2,1)S(1)}, u32[]{:S(2)}, u32[]{:S(2)}) collective-permute-start(bf16[5136,128]{1,0:T(8,128)(2,1)S(1)} %shard_map.64.refs_0_), channel_id=1, source_target_pairs={{0,32},{1,33},{2,34},{3,35},{4,36},{5,37},{6,38},{7,39},{8,40},{9,... | collective-permute-start | bytes 3944456 | tf_op jit(solution)/shard_map/ppermute | solution.py:27
  5.0 24.9 %collective-permute-start.2 = (bf16[96,5120]{1,0:T(8,128)(2,1)S(1)}, bf16[96,5120]{1,0:T(8,128)(2,1)S(1)}, u32[]{:S(2)}, u32[]{:S(2)}) collective-permute-start(bf16[96,5120]{1,0:T(8,128)(2,1)S(1)} %copy-done.11), channel_id=1, source_target_pairs={{0,8},{1,9},{2,10},{3,11},{4,12},{5,13},{6,14},{7,15},{8,0},{9,1},... | collective-permute-start | bytes 2949128 | tf_op jit(solution)/shard_map/ppermute | solution.py:27
  8.6 22.3 %collective-permute-start.7 = (bf16[96,5120]{1,0:T(8,128)(2,1)S(1)}, bf16[96,5120]{1,0:T(8,128)(2,1)S(1)}, u32[]{:S(2)}, u32[]{:S(2)}) collective-permute-start(bf16[96,5120]{1,0:T(8,128)(2,1)S(1)} %copy-done.11), channel_id=1, source_target_pairs={{0,6},{1,7},{2,0},{3,1},{4,2},{5,3},{6,4},{7,5},{8,14},{9,15},{10,... | collective-permute-start | bytes 2949128 | tf_op jit(solution)/shard_map/ppermute | solution.py:27
  11.1 23.0 %collective-permute-start.6 = (bf16[96,5120]{1,0:T(8,128)(2,1)S(1)}, bf16[96,5120]{1,0:T(8,128)(2,1)S(1)}, u32[]{:S(2)}, u32[]{:S(2)}) collective-permute-start(bf16[96,5120]{1,0:T(8,128)(2,1)S(1)} %copy-done.11), channel_id=1, source_target_pairs={{0,2},{1,3},{2,4},{3,5},{4,6},{5,7},{6,0},{7,1},{8,10},{9,11},{10,... | collective-permute-start | bytes 2949128 | tf_op jit(solution)/shard_map/ppermute | solution.py:27
  11.1 29.7 %collective-permute-start.1 = (bf16[5136,128]{1,0:T(8,128)(2,1)S(1)}, bf16[5136,128]{1,0:T(8,128)(2,1)S(1)}, u32[]{:S(2)}, u32[]{:S(2)}) collective-permute-start(bf16[5136,128]{1,0:T(8,128)(2,1)S(1)} %shard_map.64.refs_0_), channel_id=1, source_target_pairs={{0,96},{1,97},{2,98},{3,99},{4,100},{5,101},{6,102},{7,103},{8,104... | collective-permute-start | bytes 3944456 | tf_op jit(solution)/shard_map/ppermute | solution.py:27
  29.8 11.0 %copy-start.19 = (bf16[96,5120]{1,0:T(8,128)(2,1)}, bf16[96,5120]{1,0:T(8,128)(2,1)S(1)}, u32[]{:S(2)}) copy-start(bf16[96,5120]{1,0:T(8,128)(2,1)S(1)} %collective-permute-done.2.refs_4_) | copy-start | bytes 2949124
  29.8 29.0 %collective-permute-start.3 = (bf16[5136,128]{1,0:T(8,128)(2,1)S(1)}, bf16[5136,128]{1,0:T(8,128)(2,1)S(1)}, u32[]{:S(2)}, u32[]{:S(2)}) collective-permute-start(bf16[5136,128]{1,0:T(8,128)(2,1)S(1)} %shard_map.64.refs_0_), channel_id=1, source_target_pairs={{0,16},{1,17},{2,18},{3,19},{4,20},{5,21},{6,22},{7,23},{8,24},{9,... | collective-permute-start | bytes 3944456 | tf_op jit(solution)/shard_map/ppermute | solution.py:27
  30.9 64.9 %copy-start.2 = (bf16[96,5120]{1,0:T(8,128)(2,1)}, bf16[96,5120]{1,0:T(8,128)(2,1)S(1)}, u32[]{:S(2)}) copy-start(bf16[96,5120]{1,0:T(8,128)(2,1)S(1)} %collective-permute-done.7.refs_4_.refs_2_) | copy-start | bytes 2949124
  34.1 63.0 %copy-start.3 = (bf16[96,5120]{1,0:T(8,128)(2,1)}, bf16[96,5120]{1,0:T(8,128)(2,1)S(1)}, u32[]{:S(2)}) copy-start(bf16[96,5120]{1,0:T(8,128)(2,1)S(1)} %collective-permute-done.6.refs_2_.refs_3_) | copy-start | bytes 2949124
  34.1 21.0 %collective-permute-start.9 = (bf16[96,5120]{1,0:T(8,128)(2,1)S(1)}, bf16[96,5120]{1,0:T(8,128)(2,1)}, u32[]{:S(2)}, u32[]{:S(2)}) collective-permute-start(bf16[96,5120]{1,0:T(8,128)(2,1)S(1)} %collective-permute-done.2.refs_4_), channel_id=1, source_target_pairs={{0,6},{1,7},{2,0},{3,1},{4,2},{5,3},{6,4},{7,5},{8,14},{9,15},{10,... | collective-permute-start | bytes 2949128 | tf_op jit(solution)/shard_map/ppermute | solution.py:27
  34.4 22.2 %collective-permute-start.8 = (bf16[96,5120]{1,0:T(8,128)(2,1)S(1)}, bf16[96,5120]{1,0:T(8,128)(2,1)}, u32[]{:S(2)}, u32[]{:S(2)}) collective-permute-start(bf16[96,5120]{1,0:T(8,128)(2,1)S(1)} %collective-permute-done.2.refs_4_), channel_id=1, source_target_pairs={{0,2},{1,3},{2,4},{3,5},{4,6},{5,7},{6,0},{7,1},{8,10},{9,11},{10,... | collective-permute-start | bytes 2949128 | tf_op jit(solution)/shard_map/ppermute | solution.py:27
  35.5 29.5 %copy-start.13 = (bf16[5136,128]{1,0:T(8,128)(2,1)}, bf16[5136,128]{1,0:T(8,128)(2,1)S(1)}, u32[]{:S(2)}) copy-start(bf16[5136,128]{1,0:T(8,128)(2,1)S(1)} %collective-permute-done.refs_1_) | copy-start | bytes 3944452
  35.6 21.0 %collective-permute-start.4 = (bf16[2576,128]{1,0:T(8,128)(2,1)S(1)}, bf16[2576,128]{1,0:T(8,128)(2,1)S(1)}, u32[]{:S(2)}, u32[]{:S(2)}) collective-permute-start(bf16[2576,128]{1,0:T(8,128)(2,1)S(1)} %pad_maximum_fusion), channel_id=1, source_target_pairs={{0,32},{1,33},{2,34},{3,35},{4,36},{5,37},{6,38},{7,39},{8,40},{9,... | collective-permute-start | bytes 1978376 | tf_op jit(solution)/shard_map/ppermute | solution.py:27
  40.7 24.3 %copy-start.14 = (bf16[5136,128]{1,0:T(8,128)(2,1)}, bf16[5136,128]{1,0:T(8,128)(2,1)S(1)}, u32[]{:S(2)}) copy-start(bf16[5136,128]{1,0:T(8,128)(2,1)S(1)} %collective-permute-done.1.refs_2_) | copy-start | bytes 3944452
  40.8 15.8 %collective-permute-start.5 = (bf16[2560,128]{1,0:T(8,128)(2,1)S(1)}, bf16[2560,128]{1,0:T(8,128)(2,1)S(1)}, u32[]{:S(2)}, u32[]{:S(2)}) collective-permute-start(bf16[2560,128]{1,0:T(8,128)(2,1)S(1)} %slice.66), channel_id=1, source_target_pairs={{0,96},{1,97},{2,98},{3,99},{4,100},{5,101},{6,102},{7,103},{8,104... | collective-permute-start | bytes 1966088 | tf_op jit(solution)/shard_map/ppermute | solution.py:27
  58.8 32.5 %copy-start.4 = (bf16[5136,128]{1,0:T(8,128)(2,1)}, bf16[5136,128]{1,0:T(8,128)(2,1)S(1)}, u32[]{:S(2)}) copy-start(bf16[5136,128]{1,0:T(8,128)(2,1)S(1)} %get-tuple-element.68.refs_4_) | copy-start | bytes 3944452
  58.8 35.9 %copy-start.15 = (bf16[5136,128]{1,0:T(8,128)(2,1)}, bf16[5136,128]{1,0:T(8,128)(2,1)S(1)}, u32[]{:S(2)}) copy-start(bf16[5136,128]{1,0:T(8,128)(2,1)S(1)} %collective-permute-done.3.refs_3_) | copy-start | bytes 3944452
  58.8 31.1 %collective-permute-start.11 = (bf16[5136,128]{1,0:T(8,128)(2,1)S(1)}, bf16[5136,128]{1,0:T(8,128)(2,1)S(1)}, u32[]{:S(2)}, u32[]{:S(2)}) collective-permute-start(bf16[5136,128]{1,0:T(8,128)(2,1)S(1)} %collective-permute-done.3.refs_3_), channel_id=1, source_target_pairs={{0,96},{1,97},{2,98},{3,99},{4,100},{5,101},{6,102},{7,103},{8,104... | collective-permute-start | bytes 3944456 | tf_op jit(solution)/shard_map/ppermute | solution.py:27
  62.1 29.1 %collective-permute-start.10 = (bf16[5136,128]{1,0:T(8,128)(2,1)S(1)}, bf16[5136,128]{1,0:T(8,128)(2,1)S(1)}, u32[]{:S(2)}, u32[]{:S(2)}) collective-permute-start(bf16[5136,128]{1,0:T(8,128)(2,1)S(1)} %collective-permute-done.3.refs_3_), channel_id=1, source_target_pairs={{0,32},{1,33},{2,34},{3,35},{4,36},{5,37},{6,38},{7,39},{8,40},{9,... | collective-permute-start | bytes 3944456 | tf_op jit(solution)/shard_map/ppermute | solution.py:27
  62.1 20.1 %collective-permute-start.14 = (bf16[96,5120]{1,0:T(8,128)(2,1)S(1)}, bf16[96,5120]{1,0:T(8,128)(2,1)}, u32[]{:S(2)}, u32[]{:S(2)}) collective-permute-start(bf16[96,5120]{1,0:T(8,128)(2,1)S(1)} %get-tuple-element.70), channel_id=1, source_target_pairs={{0,6},{1,7},{2,0},{3,1},{4,2},{5,3},{6,4},{7,5},{8,14},{9,15},{10,... | collective-permute-start | bytes 2949128 | tf_op jit(solution)/shard_map/ppermute | solution.py:27
  64.4 22.0 %collective-permute-start.13 = (bf16[96,5120]{1,0:T(8,128)(2,1)S(1)}, bf16[96,5120]{1,0:T(8,128)(2,1)}, u32[]{:S(2)}, u32[]{:S(2)}) collective-permute-start(bf16[96,5120]{1,0:T(8,128)(2,1)S(1)} %get-tuple-element.67), channel_id=1, source_target_pairs={{0,2},{1,3},{2,4},{3,5},{4,6},{5,7},{6,0},{7,1},{8,10},{9,11},{10,... | collective-permute-start | bytes 2949128 | tf_op jit(solution)/shard_map/ppermute | solution.py:27
  64.4 30.2 %collective-permute-start.12 = (bf16[5136,128]{1,0:T(8,128)(2,1)S(1)}, bf16[5136,128]{1,0:T(8,128)(2,1)S(1)}, u32[]{:S(2)}, u32[]{:S(2)}) collective-permute-start(bf16[5136,128]{1,0:T(8,128)(2,1)S(1)} %get-tuple-element.68.refs_4_), channel_id=1, source_target_pairs={{0,16},{1,17},{2,18},{3,19},{4,20},{5,21},{6,22},{7,23},{8,24},{9,... | collective-permute-start | bytes 3944456 | tf_op jit(solution)/shard_map/ppermute | solution.py:27
  82.2 15.4 %collective-permute-start.17 = (bf16[96,5120]{1,0:T(8,128)(2,1)}, bf16[96,5120]{1,0:T(8,128)(2,1)}, u32[]{:S(2)}, u32[]{:S(2)}) collective-permute-start(bf16[96,5120]{1,0:T(8,128)(2,1)} %collective-permute-done.9.refs_5_.refs_10_), channel_id=1, source_target_pairs={{0,1},{1,0},{2,3},{3,2},{4,5},{5,4},{6,7},{7,6},{8,9},{9,8},{10,11... | collective-permute-start | bytes 2949128 | tf_op jit(solution)/shard_map/ppermute | solution.py:27
  86.4 9.4 %collective-permute-start.16 = (bf16[96,5120]{1,0:T(8,128)(2,1)}, bf16[96,5120]{1,0:T(8,128)(2,1)}, u32[]{:S(2)}, u32[]{:S(2)}) collective-permute-start(bf16[96,5120]{1,0:T(8,128)(2,1)} %collective-permute-done.14.refs_9_.refs_1_), channel_id=1, source_target_pairs={{0,1},{1,0},{2,3},{3,2},{4,5},{5,4},{6,7},{7,6},{8,9},{9,8},{10,11... | collective-permute-start | bytes 2949128 | tf_op jit(solution)/shard_map/ppermute | solution.py:27
  89.9 4.7 %copy-start.16 = (bf16[5136,128]{1,0:T(8,128)(2,1)}, bf16[5136,128]{1,0:T(8,128)(2,1)S(1)}, u32[]{:S(2)}) copy-start(bf16[5136,128]{1,0:T(8,128)(2,1)S(1)} %collective-permute-done.11.refs_6_) | copy-start | bytes 3944452
  89.9 5.9 %collective-permute-start.15 = (bf16[96,5120]{1,0:T(8,128)(2,1)}, bf16[96,5120]{1,0:T(8,128)(2,1)}, u32[]{:S(2)}, u32[]{:S(2)}) collective-permute-start(bf16[96,5120]{1,0:T(8,128)(2,1)} %collective-permute-done.13.refs_8_.refs_0_), channel_id=1, source_target_pairs={{0,1},{1,0},{2,3},{3,2},{4,5},{5,4},{6,7},{7,6},{8,9},{9,8},{10,11... | collective-permute-start | bytes 2949128 | tf_op jit(solution)/shard_map/ppermute | solution.py:27
  91.2 3.4 %copy-start.17 = (bf16[5136,128]{1,0:T(8,128)(2,1)}, bf16[5136,128]{1,0:T(8,128)(2,1)S(1)}, u32[]{:S(2)}) copy-start(bf16[5136,128]{1,0:T(8,128)(2,1)S(1)} %collective-permute-done.10.refs_5_) | copy-start | bytes 3944452
  91.2 7.1 %collective-permute-start.18 = (bf16[96,5120]{1,0:T(8,128)(2,1)}, bf16[96,5120]{1,0:T(8,128)(2,1)}, u32[]{:S(2)}, u32[]{:S(2)}) collective-permute-start(bf16[96,5120]{1,0:T(8,128)(2,1)} %collective-permute-done.8.refs_3_.refs_11_), channel_id=1, source_target_pairs={{0,1},{1,0},{2,3},{3,2},{4,5},{5,4},{6,7},{7,6},{8,9},{9,8},{10,11... | collective-permute-start | bytes 2949128 | tf_op jit(solution)/shard_map/ppermute | solution.py:27
  94.7 1.1 copy-start.18
  95.9 19.1 %collective-permute-start.19 = (bf16[96,5120]{1,0:T(8,128)(2,1)S(1)}, bf16[96,5120]{1,0:T(8,128)(2,1)}, u32[]{:S(2)}, u32[]{:S(2)}) collective-permute-start(bf16[96,5120]{1,0:T(8,128)(2,1)S(1)} %collective-permute-done.7.refs_4_.refs_2_), channel_id=1, source_target_pairs={{0,1},{1,0},{2,3},{3,2},{4,5},{5,4},{6,7},{7,6},{8,9},{9,8},{10,11... | collective-permute-start | bytes 2949128 | tf_op jit(solution)/shard_map/ppermute | solution.py:27
  97.1 17.9 %collective-permute-start.20 = (bf16[96,5120]{1,0:T(8,128)(2,1)S(1)}, bf16[96,5120]{1,0:T(8,128)(2,1)}, u32[]{:S(2)}, u32[]{:S(2)}) collective-permute-start(bf16[96,5120]{1,0:T(8,128)(2,1)S(1)} %collective-permute-done.6.refs_2_.refs_3_), channel_id=1, source_target_pairs={{0,1},{1,0},{2,3},{3,2},{4,5},{5,4},{6,7},{7,6},{8,9},{9,8},{10,11... | collective-permute-start | bytes 2949128 | tf_op jit(solution)/shard_map/ppermute | solution.py:27
  97.2 17.8 %collective-permute-start.21 = (bf16[96,5120]{1,0:T(8,128)(2,1)}, bf16[96,5120]{1,0:T(8,128)(2,1)}, u32[]{:S(2)}, u32[]{:S(2)}) collective-permute-start(bf16[96,5120]{1,0:T(8,128)(2,1)} %copy-done.19), channel_id=1, source_target_pairs={{0,1},{1,0},{2,3},{3,2},{4,5},{5,4},{6,7},{7,6},{8,9},{9,8},{10,11... | collective-permute-start | bytes 2949128 | tf_op jit(solution)/shard_map/ppermute | solution.py:27
  97.6 17.4 %collective-permute-start.22 = (bf16[96,5120]{1,0:T(8,128)(2,1)S(1)}, bf16[96,5120]{1,0:T(8,128)(2,1)}, u32[]{:S(2)}, u32[]{:S(2)}) collective-permute-start(bf16[96,5120]{1,0:T(8,128)(2,1)S(1)} %copy-done.11), channel_id=1, source_target_pairs={{0,1},{1,0},{2,3},{3,2},{4,5},{5,4},{6,7},{7,6},{8,9},{9,8},{10,11... | collective-permute-start | bytes 2949128 | tf_op jit(solution)/shard_map/ppermute | solution.py:27
  114.9 6.8 %copy-start.8 = (bf16[96,5120]{1,0:T(8,128)(2,1)S(1)}, bf16[96,5120]{1,0:T(8,128)(2,1)}, u32[]{:S(2)}) copy-start(bf16[96,5120]{1,0:T(8,128)(2,1)} %get-tuple-element.83) | copy-start | bytes 2949124
  115.0 2.9 %collective-permute-start.23 = (bf16[96,5120]{1,0:T(8,128)(2,1)}, bf16[96,5120]{1,0:T(8,128)(2,1)S(1)}, u32[]{:S(2)}, u32[]{:S(2)}) collective-permute-start(bf16[96,5120]{1,0:T(8,128)(2,1)} %get-tuple-element.82), channel_id=1, source_target_pairs={{0,1},{1,0},{2,3},{3,2},{4,5},{5,4},{6,7},{7,6},{8,9},{9,8},{10,11... | collective-permute-start | bytes 2949128 | tf_op jit(solution)/shard_map/ppermute | solution.py:27
  115.5 6.3 %collective-permute-start.24 = (bf16[96,5120]{1,0:T(8,128)(2,1)}, bf16[96,5120]{1,0:T(8,128)(2,1)S(1)}, u32[]{:S(2)}, u32[]{:S(2)}) collective-permute-start(bf16[96,5120]{1,0:T(8,128)(2,1)} %get-tuple-element.84), channel_id=1, source_target_pairs={{0,1},{1,0},{2,3},{3,2},{4,5},{5,4},{6,7},{7,6},{8,9},{9,8},{10,11... | collective-permute-start | bytes 2949128 | tf_op jit(solution)/shard_map/ppermute | solution.py:27
  115.6 7.4 %collective-permute-start.25 = (bf16[96,5120]{1,0:T(8,128)(2,1)}, bf16[96,5120]{1,0:T(8,128)(2,1)S(1)}, u32[]{:S(2)}, u32[]{:S(2)}) collective-permute-start(bf16[96,5120]{1,0:T(8,128)(2,1)} %get-tuple-element.86), channel_id=1, source_target_pairs={{0,1},{1,0},{2,3},{3,2},{4,5},{5,4},{6,7},{7,6},{8,9},{9,8},{10,11... | collective-permute-start | bytes 2949128 | tf_op jit(solution)/shard_map/ppermute | solution.py:27
  119.3 3.7 %copy-start.7 = (bf16[96,5120]{1,0:T(8,128)(2,1)S(1)}, bf16[96,5120]{1,0:T(8,128)(2,1)}, u32[]{:S(2)}) copy-start(bf16[96,5120]{1,0:T(8,128)(2,1)} %get-tuple-element.85) | copy-start | bytes 2949124
  119.3 29.4 %collective-permute-start.28 = (bf16[96,5120]{1,0:T(8,128)(2,1)S(1)}, bf16[96,5120]{1,0:T(8,128)(2,1)}, u32[]{:S(2)}, u32[]{:S(2)}) collective-permute-start(bf16[96,5120]{1,0:T(8,128)(2,1)S(1)} %add_convert_fusion.6), channel_id=1, source_target_pairs={{0,8},{1,9},{2,10},{3,11},{4,12},{5,13},{6,14},{7,15},{8,0},{9,1},... | collective-permute-start | bytes 2949128 | tf_op jit(solution)/shard_map/ppermute | solution.py:27
  122.0 26.7 %collective-permute-start.29 = (bf16[96,5120]{1,0:T(8,128)(2,1)S(1)}, bf16[96,5120]{1,0:T(8,128)(2,1)S(1)}, u32[]{:S(2)}, u32[]{:S(2)}) collective-permute-start(bf16[96,5120]{1,0:T(8,128)(2,1)S(1)} %add_convert_fusion.5), channel_id=1, source_target_pairs={{0,2},{1,3},{2,4},{3,5},{4,6},{5,7},{6,0},{7,1},{8,10},{9,11},{10,... | collective-permute-start | bytes 2949128 | tf_op jit(solution)/shard_map/ppermute | solution.py:27
  123.3 25.5 %collective-permute-start.30 = (bf16[96,5120]{1,0:T(8,128)(2,1)S(1)}, bf16[96,5120]{1,0:T(8,128)(2,1)S(1)}, u32[]{:S(2)}, u32[]{:S(2)}) collective-permute-start(bf16[96,5120]{1,0:T(8,128)(2,1)S(1)} %add_convert_fusion.4), channel_id=1, source_target_pairs={{0,6},{1,7},{2,0},{3,1},{4,2},{5,3},{6,4},{7,5},{8,14},{9,15},{10,... | collective-permute-start | bytes 2949128 | tf_op jit(solution)/shard_map/ppermute | solution.py:27
  145.0 6.1 %copy-start.12 = (bf16[48,5120]{1,0:T(8,128)(2,1)S(1)}, bf16[48,5120]{1,0:T(8,128)(2,1)}, u32[]{:S(2)}) copy-start(bf16[48,5120]{1,0:T(8,128)(2,1)} %get-tuple-element.102) | copy-start | bytes 1474564
  145.0 3.0 %collective-permute-start.26 = (bf16[48,5120]{1,0:T(8,128)(2,1)}, bf16[48,5120]{1,0:T(8,128)(2,1)S(1)}, u32[]{:S(2)}, u32[]{:S(2)}) collective-permute-start(bf16[48,5120]{1,0:T(8,128)(2,1)} %get-tuple-element.96), channel_id=1, source_target_pairs={{0,1},{1,0},{2,3},{3,2},{4,5},{5,4},{6,7},{7,6},{8,9},{9,8},{10,11... | collective-permute-start | bytes 1474568 | tf_op jit(solution)/shard_map/ppermute | solution.py:27
  146.3 2.4 %collective-permute-start.27 = (bf16[48,5120]{1,0:T(8,128)(2,1)}, bf16[48,5120]{1,0:T(8,128)(2,1)S(1)}, u32[]{:S(2)}, u32[]{:S(2)}) collective-permute-start(bf16[48,5120]{1,0:T(8,128)(2,1)} %get-tuple-element.97), channel_id=1, source_target_pairs={{0,1},{1,0},{2,3},{3,2},{4,5},{5,4},{6,7},{7,6},{8,9},{9,8},{10,11... | collective-permute-start | bytes 1474568 | tf_op jit(solution)/shard_map/ppermute | solution.py:27
  148.8 6.2 %copy-start.21 = (bf16[96,5120]{1,0:T(8,128)(2,1)S(1)}, bf16[96,5120]{1,0:T(8,128)(2,1)}, u32[]{:S(2)}) copy-start(bf16[96,5120]{1,0:T(8,128)(2,1)} %get-tuple-element.104) | copy-start | bytes 2949124
  148.8 6.9 %copy-start.20 = (bf16[96,5120]{1,0:T(8,128)(2,1)S(1)}, bf16[96,5120]{1,0:T(8,128)(2,1)}, u32[]{:S(2)}) copy-start(bf16[96,5120]{1,0:T(8,128)(2,1)} %get-tuple-element.106) | copy-start | bytes 2949124
  148.8 7.2 %copy-start.5 = (bf16[96,5120]{1,0:T(8,128)(2,1)S(1)}, bf16[96,5120]{1,0:T(8,128)(2,1)}, u32[]{:S(2)}) copy-start(bf16[96,5120]{1,0:T(8,128)(2,1)} %get-tuple-element.107) | copy-start | bytes 2949124
  153.1 2.8 %collective-permute-start.33 = (bf16[96,5120]{1,0:T(8,128)(2,1)}, bf16[96,5120]{1,0:T(8,128)(2,1)S(1)}, u32[]{:S(2)}, u32[]{:S(2)}) collective-permute-start(bf16[96,5120]{1,0:T(8,128)(2,1)} %get-tuple-element.108), channel_id=1, source_target_pairs={{0,1},{1,0},{2,3},{3,2},{4,5},{5,4},{6,7},{7,6},{8,9},{9,8},{10,11... | collective-permute-start | bytes 2949128 | tf_op jit(solution)/shard_map/ppermute | solution.py:27
  153.5 13.6 %collective-permute-start.35 = (bf16[48,5120]{1,0:T(8,128)(2,1)}, bf16[48,5120]{1,0:T(8,128)(2,1)}, u32[]{:S(2)}, u32[]{:S(2)}) collective-permute-start(bf16[48,5120]{1,0:T(8,128)(2,1)} %add_convert_fusion.7), channel_id=1, source_target_pairs={{0,6},{1,7},{2,0},{3,1},{4,2},{5,3},{6,4},{7,5},{8,14},{9,15},{10,... | collective-permute-start | bytes 1474568 | tf_op jit(solution)/shard_map/ppermute | solution.py:27
  154.9 13.9 %collective-permute-start.34 = (bf16[48,5120]{1,0:T(8,128)(2,1)}, bf16[48,5120]{1,0:T(8,128)(2,1)}, u32[]{:S(2)}, u32[]{:S(2)}) collective-permute-start(bf16[48,5120]{1,0:T(8,128)(2,1)} %add_convert_fusion.8), channel_id=1, source_target_pairs={{0,2},{1,3},{2,4},{3,5},{4,6},{5,7},{6,0},{7,1},{8,10},{9,11},{10,... | collective-permute-start | bytes 1474568 | tf_op jit(solution)/shard_map/ppermute | solution.py:27
  155.0 2.9 %collective-permute-start.31 = (bf16[96,5120]{1,0:T(8,128)(2,1)S(1)}, bf16[96,5120]{1,0:T(8,128)(2,1)S(1)}, u32[]{:S(2)}, u32[]{:S(2)}) collective-permute-start(bf16[96,5120]{1,0:T(8,128)(2,1)S(1)} %copy-done.21), channel_id=1, source_target_pairs={{0,1},{1,0},{2,3},{3,2},{4,5},{5,4},{6,7},{7,6},{8,9},{9,8},{10,11... | collective-permute-start | bytes 2949128 | tf_op jit(solution)/shard_map/ppermute | solution.py:27
  155.7 3.6 %collective-permute-start.32 = (bf16[96,5120]{1,0:T(8,128)(2,1)S(1)}, bf16[96,5120]{1,0:T(8,128)(2,1)S(1)}, u32[]{:S(2)}, u32[]{:S(2)}) collective-permute-start(bf16[96,5120]{1,0:T(8,128)(2,1)S(1)} %copy-done.20), channel_id=1, source_target_pairs={{0,1},{1,0},{2,3},{3,2},{4,5},{5,4},{6,7},{7,6},{8,9},{9,8},{10,11... | collective-permute-start | bytes 2949128 | tf_op jit(solution)/shard_map/ppermute | solution.py:27
  155.9 2.0 copy-start.10
  157.9 1.4 copy-start.9
  170.0 1.4 copy-start.22
  170.0 27.5 %copy-start.6 = (bf16[96,5120]{1,0:T(8,128)(2,1)S(1)}, bf16[96,5120]{1,0:T(8,128)(2,1)}, u32[]{:S(2)}) copy-start(bf16[96,5120]{1,0:T(8,128)(2,1)} %get-tuple-element.115) | copy-start | bytes 2949124
  171.3 3.6 %collective-permute-start.36 = (bf16[96,5120]{1,0:T(8,128)(2,1)S(1)}, bf16[96,5120]{1,0:T(8,128)(2,1)S(1)}, u32[]{:S(2)}, u32[]{:S(2)}) collective-permute-start(bf16[96,5120]{1,0:T(8,128)(2,1)S(1)} %copy-done.22), channel_id=1, source_target_pairs={{0,1},{1,0},{2,3},{3,2},{4,5},{5,4},{6,7},{7,6},{8,9},{9,8},{10,11... | collective-permute-start | bytes 2949128 | tf_op jit(solution)/shard_map/ppermute | solution.py:27
  172.7 24.8 %collective-permute-start.37 = (bf16[96,5120]{1,0:T(8,128)(2,1)S(1)}, bf16[96,5120]{1,0:T(8,128)(2,1)S(1)}, u32[]{:S(2)}, u32[]{:S(2)}) collective-permute-start(bf16[96,5120]{1,0:T(8,128)(2,1)S(1)} %add_convert_fusion.3), channel_id=1, source_target_pairs={{0,8},{1,9},{2,10},{3,11},{4,12},{5,13},{6,14},{7,15},{8,0},{9,1},... | collective-permute-start | bytes 2949128 | tf_op jit(solution)/shard_map/ppermute | solution.py:27
  173.5 24.4 %collective-permute-start.39 = (bf16[96,5120]{1,0:T(8,128)(2,1)S(1)}, bf16[96,5120]{1,0:T(8,128)(2,1)S(1)}, u32[]{:S(2)}, u32[]{:S(2)}) collective-permute-start(bf16[96,5120]{1,0:T(8,128)(2,1)S(1)} %add_convert_fusion.1), channel_id=1, source_target_pairs={{0,6},{1,7},{2,0},{3,1},{4,2},{5,3},{6,4},{7,5},{8,14},{9,15},{10,... | collective-permute-start | bytes 2949128 | tf_op jit(solution)/shard_map/ppermute | solution.py:27
  173.5 24.4 %collective-permute-start.38 = (bf16[96,5120]{1,0:T(8,128)(2,1)S(1)}, bf16[96,5120]{1,0:T(8,128)(2,1)S(1)}, u32[]{:S(2)}, u32[]{:S(2)}) collective-permute-start(bf16[96,5120]{1,0:T(8,128)(2,1)S(1)} %add_convert_fusion.2), channel_id=1, source_target_pairs={{0,2},{1,3},{2,4},{3,5},{4,6},{5,7},{6,0},{7,1},{8,10},{9,11},{10,... | collective-permute-start | bytes 2949128 | tf_op jit(solution)/shard_map/ppermute | solution.py:27

commit v9 on v8

--- a/solution.py
+++ b/solution.py
@@ -313,7 +313,7 @@
     got = swap(*part[5:7])
     far, got, far_in, z_right, z_left = after((far, got, far_in, z_right, z_left))
     top = add(far[0], got[0], far_in[:h_rows]).astype(BF16)
-    low = add(after(far[1], top), got[1], far_in[h_rows:]).astype(BF16)
+    low = add(far[1], got[1], far_in[h_rows:]).astype(BF16)
     past_top, past_low = move(top, dx=1), move(low, dx=-1)
 
     near_sib, z_sib = after((near_sib, z_sib), top, low)

time: 199 us -> 198 us (level)
    convert_element_type x2 -> x1, other arithmetic: 4.36 us -> 2.96 us  [body(): low = add(far[1], got[1], far_in[h_rows:]).astype(BF16)]
  transfers between devices with their start and end apart: 40 -> 40, of which waited for: 15 -> 14; matrix products, arithmetic and copies ran while one was open for 2% -> 2% of each run, Pallas kernels for 23% -> 23%
where the time goes in v9:
time: 198 us
  waiting for transfers between devices  83.8 us (42%)
  starting transfers between devices  52.5 us (27%)
  Pallas kernels  46.4 us (23%)
  other arithmetic  10 us (5%)
  local copies, waits for them, and re-layouts  3.26 us (2%)
    ppermute x40, waiting for transfers between devices, move(): return lax.ppermute(value, AXES, pairs)  83.8 us
    ppermute x40, starting transfers between devices, move(): return lax.ppermute(value, AXES, pairs)  52.5 us
    pallas_call x2, Pallas kernels, sums(): return tuple(run(ids, sidx, scale_table, *pieces, *weights))  27.5 us
    pallas_call x1, Pallas kernels, sums(): return tuple(run(ids, sidx, scale_table, *sources, *pieces, down_weight))  16.6 us
  transfers between devices with their start and end apart: 40, of which 14 were waited for; matrix products, arithmetic and copies ran while one was open for 2% of the time, Pallas kernels for 23%

profile of v9, /device:TPU:1, one launch (start us, length us, event | category | flops | bytes accessed | tf_op | source)
XLA Modules:
  0.0 197.6 jit_solution(6588394645921647251)
XLA Ops:
  1.3 1.3 copy-done.1
  2.6 0.1 shard_map.64.refs_0_
  2.8 2.2 %collective-permute-start = (bf16[5136,128]{1,0:T(8,128)(2,1)S(1)}, bf16[5136,128]{1,0:T(8,128)(2,1)S(1)}, u32[]{:S(2)}, u32[]{:S(2)}) collective-permute-start(bf16[5136,128]{1,0:T(8,128)(2,1)S(1)} %shard_map.64.refs_0_), channel_id=1, source_target_pairs={{0,32},{1,33},{2,34},{3,35},{4,36},{5,37},{6,38},{7,39},{8,40},{9,... | collective-permute-start | bytes 3944456 | tf_op jit(solution)/shard_map/ppermute | solution.py:27
  5.0 3.6 %collective-permute-start.2 = (bf16[96,5120]{1,0:T(8,128)(2,1)S(1)}, bf16[96,5120]{1,0:T(8,128)(2,1)S(1)}, u32[]{:S(2)}, u32[]{:S(2)}) collective-permute-start(bf16[96,5120]{1,0:T(8,128)(2,1)S(1)} %copy-done.11), channel_id=1, source_target_pairs={{0,8},{1,9},{2,10},{3,11},{4,12},{5,13},{6,14},{7,15},{8,0},{9,1},... | collective-permute-start | bytes 2949128 | tf_op jit(solution)/shard_map/ppermute | solution.py:27
  8.6 2.5 %collective-permute-start.7 = (bf16[96,5120]{1,0:T(8,128)(2,1)S(1)}, bf16[96,5120]{1,0:T(8,128)(2,1)S(1)}, u32[]{:S(2)}, u32[]{:S(2)}) collective-permute-start(bf16[96,5120]{1,0:T(8,128)(2,1)S(1)} %copy-done.11), channel_id=1, source_target_pairs={{0,6},{1,7},{2,0},{3,1},{4,2},{5,3},{6,4},{7,5},{8,14},{9,15},{10,... | collective-permute-start | bytes 2949128 | tf_op jit(solution)/shard_map/ppermute | solution.py:27
  11.1 2.7 %collective-permute-start.1 = (bf16[5136,128]{1,0:T(8,128)(2,1)S(1)}, bf16[5136,128]{1,0:T(8,128)(2,1)S(1)}, u32[]{:S(2)}, u32[]{:S(2)}) collective-permute-start(bf16[5136,128]{1,0:T(8,128)(2,1)S(1)} %shard_map.64.refs_0_), channel_id=1, source_target_pairs={{0,96},{1,97},{2,98},{3,99},{4,100},{5,101},{6,102},{7,103},{8,104... | collective-permute-start | bytes 3944456 | tf_op jit(solution)/shard_map/ppermute | solution.py:27
  13.8 16.0 %collective-permute-done.2.refs_4_ = bf16[96,5120]{1,0:T(8,128)(2,1)S(1)} collective-permute-done((bf16[96,5120]{1,0:T(8,128)(2,1)S(1)}, bf16[96,5120]{1,0:T(8,128)(2,1)S(1)}, u32[]{:S(2)}, u32[]{:S(2)}) %collective-permute-start.2) | collective-permute-done | bytes 983072 | tf_op jit(solution)/shard_map/ppermute | solution.py:27
  29.8 0.7 collective-permute-start.3
  30.5 0.4 collective-permute-done.7.refs_4_.refs_2_
  30.9 3.1 %collective-permute-done.6.refs_2_.refs_3_ = bf16[96,5120]{1,0:T(8,128)(2,1)S(1)} collective-permute-done((bf16[96,5120]{1,0:T(8,128)(2,1)S(1)}, bf16[96,5120]{1,0:T(8,128)(2,1)S(1)}, u32[]{:S(2)}, u32[]{:S(2)}) %collective-permute-start.6) | collective-permute-done | bytes 983072 | tf_op jit(solution)/shard_map/ppermute | solution.py:27
  34.1 0.3 collective-permute-start.9
  34.4 1.1 collective-permute-start.8
  35.6 1.4 collective-permute-start.4
  37.0 3.7 %collective-permute-done.1.refs_2_ = bf16[5136,128]{1,0:T(8,128)(2,1)S(1)} collective-permute-done((bf16[5136,128]{1,0:T(8,128)(2,1)S(1)}, bf16[5136,128]{1,0:T(8,128)(2,1)S(1)}, u32[]{:S(2)}, u32[]{:S(2)}) %collective-permute-start.1) | collective-permute-done | bytes 1314848 | tf_op jit(solution)/shard_map/ppermute | solution.py:27
  40.8 3.6 %collective-permute-start.5 = (bf16[2560,128]{1,0:T(8,128)(2,1)S(1)}, bf16[2560,128]{1,0:T(8,128)(2,1)S(1)}, u32[]{:S(2)}, u32[]{:S(2)}) collective-permute-start(bf16[2560,128]{1,0:T(8,128)(2,1)S(1)} %slice.66), channel_id=1, source_target_pairs={{0,96},{1,97},{2,98},{3,99},{4,100},{5,101},{6,102},{7,103},{8,104... | collective-permute-start | bytes 1966088 | tf_op jit(solution)/shard_map/ppermute | solution.py:27
  44.4 10.7 %collective-permute-done.9.refs_5_.refs_10_ = bf16[96,5120]{1,0:T(8,128)(2,1)} collective-permute-done((bf16[96,5120]{1,0:T(8,128)(2,1)S(1)}, bf16[96,5120]{1,0:T(8,128)(2,1)}, u32[]{:S(2)}, u32[]{:S(2)}) %collective-permute-start.9) | collective-permute-done | bytes 983072 | tf_op jit(solution)/shard_map/ppermute | solution.py:27
  55.0 1.6 collective-permute-done.8.refs_3_.refs_11_
  56.6 2.2 %shard_map.65 = (bf16[5136,128]{1,0:T(8,128)(2,1)S(1)}, bf16[96,5120]{1,0:T(8,128)(2,1)S(1)}, bf16[96,5120]{1,0:T(8,128)(2,1)S(1)}) custom-call(bf16[2576,128]{1,0:T(8,128)(2,1)S(1)} %collective-permute-done.4.refs_0_, bf16[2560,128]{1,0:T(8,128)(2,1)S(1)} %collective-permute-done.5.refs_1_, bf16[96,5120]{1,0:T(8,128)(2,1)S(1)} %collective-permute-done.6.refs_2_.refs_3_, ...), custom_call_target="tpu_custom_call" | custom-call | flops 1 | bytes 1 | tf_op jit(solution)/shard_map/pallas_call | solution.py:82
  58.8 3.3 %collective-permute-start.11 = (bf16[5136,128]{1,0:T(8,128)(2,1)S(1)}, bf16[5136,128]{1,0:T(8,128)(2,1)S(1)}, u32[]{:S(2)}, u32[]{:S(2)}) collective-permute-start(bf16[5136,128]{1,0:T(8,128)(2,1)S(1)} %collective-permute-done.3.refs_3_), channel_id=1, source_target_pairs={{0,96},{1,97},{2,98},{3,99},{4,100},{5,101},{6,102},{7,103},{8,104... | collective-permute-start | bytes 3944456 | tf_op jit(solution)/shard_map/ppermute | solution.py:27
  62.1 2.3 %collective-permute-start.14 = (bf16[96,5120]{1,0:T(8,128)(2,1)S(1)}, bf16[96,5120]{1,0:T(8,128)(2,1)}, u32[]{:S(2)}, u32[]{:S(2)}) collective-permute-start(bf16[96,5120]{1,0:T(8,128)(2,1)S(1)} %get-tuple-element.69), channel_id=1, source_target_pairs={{0,6},{1,7},{2,0},{3,1},{4,2},{5,3},{6,4},{7,5},{8,14},{9,15},{10,... | collective-permute-start | bytes 2949128 | tf_op jit(solution)/shard_map/ppermute | solution.py:27
  64.4 0.6 collective-permute-start.12
  65.1 17.1 %collective-permute-done.14.refs_9_.refs_1_ = bf16[96,5120]{1,0:T(8,128)(2,1)} collective-permute-done((bf16[96,5120]{1,0:T(8,128)(2,1)S(1)}, bf16[96,5120]{1,0:T(8,128)(2,1)}, u32[]{:S(2)}, u32[]{:S(2)}) %collective-permute-start.14) | collective-permute-done | bytes 983072 | tf_op jit(solution)/shard_map/ppermute | solution.py:27
  82.2 4.2 %collective-permute-start.17 = (bf16[96,5120]{1,0:T(8,128)(2,1)}, bf16[96,5120]{1,0:T(8,128)(2,1)}, u32[]{:S(2)}, u32[]{:S(2)}) collective-permute-start(bf16[96,5120]{1,0:T(8,128)(2,1)} %collective-permute-done.9.refs_5_.refs_10_), channel_id=1, source_target_pairs={{0,1},{1,0},{2,3},{3,2},{4,5},{5,4},{6,7},{7,6},{8,9},{9,8},{10,11... | collective-permute-start | bytes 2949128 | tf_op jit(solution)/shard_map/ppermute | solution.py:27
  86.4 3.5 %collective-permute-start.16 = (bf16[96,5120]{1,0:T(8,128)(2,1)}, bf16[96,5120]{1,0:T(8,128)(2,1)}, u32[]{:S(2)}, u32[]{:S(2)}) collective-permute-start(bf16[96,5120]{1,0:T(8,128)(2,1)} %collective-permute-done.14.refs_9_.refs_1_), channel_id=1, source_target_pairs={{0,1},{1,0},{2,3},{3,2},{4,5},{5,4},{6,7},{7,6},{8,9},{9,8},{10,11... | collective-permute-start | bytes 2949128 | tf_op jit(solution)/shard_map/ppermute | solution.py:27
  89.9 1.3 collective-permute-start.15
  91.2 3.4 %collective-permute-start.18 = (bf16[96,5120]{1,0:T(8,128)(2,1)}, bf16[96,5120]{1,0:T(8,128)(2,1)}, u32[]{:S(2)}, u32[]{:S(2)}) collective-permute-start(bf16[96,5120]{1,0:T(8,128)(2,1)} %collective-permute-done.8.refs_3_.refs_11_), channel_id=1, source_target_pairs={{0,1},{1,0},{2,3},{3,2},{4,5},{5,4},{6,7},{7,6},{8,9},{9,8},{10,11... | collective-permute-start | bytes 2949128 | tf_op jit(solution)/shard_map/ppermute | solution.py:27
  94.7 1.1 copy-done.17
  95.7 0.1 stack.3
  95.9 1.2 collective-permute-start.19
  97.2 0.4 collective-permute-start.21
  97.7 0.6 slice_bitcast_fusion.7
  98.3 16.6 %shard_map.66 = (bf16[96,5120]{1,0:T(8,128)(2,1)}, bf16[96,5120]{1,0:T(8,128)(2,1)}, bf16[96,5120]{1,0:T(8,128)(2,1)}, bf16[96,5120]{1,0:T(8,128)(2,1)}, bf16[96...) custom-call(s32[8]{0:T(128)} %get-tuple-element.109.ids, ...), custom_call_target="tpu_custom_call" | custom-call | flops 9059696640 | bytes 27525120 | tf_op jit(solution)/shard_map/pallas_call | solution.py:280
  115.0 0.5 collective-permute-start.23
  115.5 0.4 collective-permute-start.25
  116.0 1.9 collective-permute-done.23
  117.9 1.5 add_convert_fusion.6
  119.3 2.4 %collective-permute-start.28 = (bf16[96,5120]{1,0:T(8,128)(2,1)S(1)}, bf16[96,5120]{1,0:T(8,128)(2,1)}, u32[]{:S(2)}, u32[]{:S(2)}) collective-permute-start(bf16[96,5120]{1,0:T(8,128)(2,1)S(1)} %add_convert_fusion.6), channel_id=1, source_target_pairs={{0,8},{1,9},{2,10},{3,11},{4,12},{5,13},{6,14},{7,15},{8,0},{9,1},... | collective-permute-start | bytes 2949128 | tf_op jit(solution)/shard_map/ppermute | solution.py:27
  121.7 0.3 add_convert_fusion.5
  122.0 1.0 collective-permute-start.29
  123.0 0.3 add_convert_fusion.4
  123.3 1.8 collective-permute-start.30
  125.1 19.9 %shard_map.67 = (bf16[48,5120]{1,0:T(8,128)(2,1)}, bf16[48,5120]{1,0:T(8,128)(2,1)}, bf16[96,5120]{1,0:T(8,128)(2,1)}, bf16[96,5120]{1,0:T(8,128)(2,1)}, bf16[96...) custom-call(s32[8]{0:T(128)} %get-tuple-element.109.ids, ...), custom_call_target="tpu_custom_call", output_to_operand_aliasing={{10}: (13, {}), {11}: (14, {})} | custom-call | flops 12079595520 | bytes 31457280 | tf_op jit(solution)/shard_map/pallas_call | solution.py:281
  145.0 1.3 collective-permute-start.26
  146.4 1.6 collective-permute-done.26
  148.0 0.7 collective-permute-done.27
  148.8 3.0 %add_convert_fusion.7 = (bf16[48,5120]{1,0:T(8,128)(2,1)}, bf16[48,5120]{1,0:T(8,128)(2,1)}) fusion(bf16[48,5120]{1,0:T(8,128)(2,1)S(1)} %collective-permute-done.27, bf16[48,5120]{1,0:T(8,128)(2,1)} %get-tuple-element.100, bf16[96,5120]{1,0:T(8,128)(2,1)} %collective-permute-done.28, bf16[48,5120]{1,0:T(8,128)(2,1)S(1)} %collective-permute-done.26, ...), kind=kLoop, calls=%fused_computation.10 | loop fusion | flops 2949120 | bytes 3932160 | tf_op jit(solution)/shard_map/convert_element_type | solution.py:316
  151.7 0.4 collective-permute-start.33
  152.1 1.4 collective-permute-start.35
  153.6 0.7 collective-permute-start.31
  154.4 0.6 add_convert_fusion.3
  155.0 1.5 collective-permute-done.31
  156.5 0.2 convert_add_fusion.2
  156.7 1.2 collective-permute-done.32
  157.9 0.2 convert_add_fusion.1
  158.1 7.5 %shard_map.68 = (bf16[96,5120]{1,0:T(8,128)(2,1)}, bf16[96,5120]{1,0:T(8,128)(2,1)}, bf16[4,5120,256]{2,1,0:T(8,128)(2,1)S(1)}, bf16[512,5120]{1,0:T(8,128)(2,1)S(1)}) custom-call(s32[8]{0:T(128)} %get-tuple-element.109.ids, s32[8]{0:T(128)} %get-tuple-element.123.sidx, f32[64]{0:T(128)} %table.5, ...), custom_call_target="tpu_custom_call", output_to_operand_aliasing={{2}: (5, {}), {3}: (6, {})} | custom-call | flops 3019898880 | bytes 19660800 | tf_op jit(solution)/shard_map/pallas_call | solution.py:281
  165.7 1.7 collective-permute-done.34
  167.4 1.2 add_convert_fusion.2
  168.6 1.3 add_convert_fusion.1
  169.9 1.3 collective-permute-start.36
  171.2 0.8 collective-permute-start.37
  172.1 1.5 collective-permute-start.38
  173.5 22.5 %collective-permute-done.37 = bf16[96,5120]{1,0:T(8,128)(2,1)S(1)} collective-permute-done((bf16[96,5120]{1,0:T(8,128)(2,1)S(1)}, bf16[96,5120]{1,0:T(8,128)(2,1)S(1)}, u32[]{:S(2)}, u32[]{:S(2)}) %collective-permute-start.37) | collective-permute-done | bytes 983072 | tf_op jit(solution)/shard_map/ppermute | solution.py:27
  196.1 0.3 convert_add_fusion
  196.4 1.2 add_convert_fusion
  (93 shorter events, 0.9 us)
Async XLA Ops:
  1.3 1.3 copy-start.1
  2.6 2.3 %copy-start.11 = (bf16[96,5120]{1,0:T(8,128)(2,1)S(1)}, bf16[96,5120]{1,0:T(8,128)(2,1)}, u32[]{:S(2)}) copy-start(bf16[96,5120]{1,0:T(8,128)(2,1)} %refs_0_.1) | copy-start | bytes 2949124
  2.7 61.7 %copy-start = (bf16[5136,128]{1,0:T(8,128)(2,1)}, bf16[5136,128]{1,0:T(8,128)(2,1)S(1)}, u32[]{:S(2)}) copy-start(bf16[5136,128]{1,0:T(8,128)(2,1)S(1)} %shard_map.64.refs_0_) | copy-start | bytes 3944452
  2.8 32.8 %collective-permute-start = (bf16[5136,128]{1,0:T(8,128)(2,1)S(1)}, bf16[5136,128]{1,0:T(8,128)(2,1)S(1)}, u32[]{:S(2)}, u32[]{:S(2)}) collective-permute-start(bf16[5136,128]{1,0:T(8,128)(2,1)S(1)} %shard_map.64.refs_0_), channel_id=1, source_target_pairs={{0,32},{1,33},{2,34},{3,35},{4,36},{5,37},{6,38},{7,39},{8,40},{9,... | collective-permute-start | bytes 3944456 | tf_op jit(solution)/shard_map/ppermute | solution.py:27
  5.0 24.9 %collective-permute-start.2 = (bf16[96,5120]{1,0:T(8,128)(2,1)S(1)}, bf16[96,5120]{1,0:T(8,128)(2,1)S(1)}, u32[]{:S(2)}, u32[]{:S(2)}) collective-permute-start(bf16[96,5120]{1,0:T(8,128)(2,1)S(1)} %copy-done.11), channel_id=1, source_target_pairs={{0,8},{1,9},{2,10},{3,11},{4,12},{5,13},{6,14},{7,15},{8,0},{9,1},... | collective-permute-start | bytes 2949128 | tf_op jit(solution)/shard_map/ppermute | solution.py:27
  8.6 22.3 %collective-permute-start.7 = (bf16[96,5120]{1,0:T(8,128)(2,1)S(1)}, bf16[96,5120]{1,0:T(8,128)(2,1)S(1)}, u32[]{:S(2)}, u32[]{:S(2)}) collective-permute-start(bf16[96,5120]{1,0:T(8,128)(2,1)S(1)} %copy-done.11), channel_id=1, source_target_pairs={{0,6},{1,7},{2,0},{3,1},{4,2},{5,3},{6,4},{7,5},{8,14},{9,15},{10,... | collective-permute-start | bytes 2949128 | tf_op jit(solution)/shard_map/ppermute | solution.py:27
  11.1 23.0 %collective-permute-start.6 = (bf16[96,5120]{1,0:T(8,128)(2,1)S(1)}, bf16[96,5120]{1,0:T(8,128)(2,1)S(1)}, u32[]{:S(2)}, u32[]{:S(2)}) collective-permute-start(bf16[96,5120]{1,0:T(8,128)(2,1)S(1)} %copy-done.11), channel_id=1, source_target_pairs={{0,2},{1,3},{2,4},{3,5},{4,6},{5,7},{6,0},{7,1},{8,10},{9,11},{10,... | collective-permute-start | bytes 2949128 | tf_op jit(solution)/shard_map/ppermute | solution.py:27
  11.1 29.7 %collective-permute-start.1 = (bf16[5136,128]{1,0:T(8,128)(2,1)S(1)}, bf16[5136,128]{1,0:T(8,128)(2,1)S(1)}, u32[]{:S(2)}, u32[]{:S(2)}) collective-permute-start(bf16[5136,128]{1,0:T(8,128)(2,1)S(1)} %shard_map.64.refs_0_), channel_id=1, source_target_pairs={{0,96},{1,97},{2,98},{3,99},{4,100},{5,101},{6,102},{7,103},{8,104... | collective-permute-start | bytes 3944456 | tf_op jit(solution)/shard_map/ppermute | solution.py:27
  29.8 11.0 %copy-start.18 = (bf16[96,5120]{1,0:T(8,128)(2,1)}, bf16[96,5120]{1,0:T(8,128)(2,1)S(1)}, u32[]{:S(2)}) copy-start(bf16[96,5120]{1,0:T(8,128)(2,1)S(1)} %collective-permute-done.2.refs_4_) | copy-start | bytes 2949124
  29.8 29.0 %collective-permute-start.3 = (bf16[5136,128]{1,0:T(8,128)(2,1)S(1)}, bf16[5136,128]{1,0:T(8,128)(2,1)S(1)}, u32[]{:S(2)}, u32[]{:S(2)}) collective-permute-start(bf16[5136,128]{1,0:T(8,128)(2,1)S(1)} %shard_map.64.refs_0_), channel_id=1, source_target_pairs={{0,16},{1,17},{2,18},{3,19},{4,20},{5,21},{6,22},{7,23},{8,24},{9,... | collective-permute-start | bytes 3944456 | tf_op jit(solution)/shard_map/ppermute | solution.py:27
  30.9 64.9 %copy-start.2 = (bf16[96,5120]{1,0:T(8,128)(2,1)}, bf16[96,5120]{1,0:T(8,128)(2,1)S(1)}, u32[]{:S(2)}) copy-start(bf16[96,5120]{1,0:T(8,128)(2,1)S(1)} %collective-permute-done.7.refs_4_.refs_2_) | copy-start | bytes 2949124
  34.1 63.0 %copy-start.3 = (bf16[96,5120]{1,0:T(8,128)(2,1)}, bf16[96,5120]{1,0:T(8,128)(2,1)S(1)}, u32[]{:S(2)}) copy-start(bf16[96,5120]{1,0:T(8,128)(2,1)S(1)} %collective-permute-done.6.refs_2_.refs_3_) | copy-start | bytes 2949124
  34.1 21.0 %collective-permute-start.9 = (bf16[96,5120]{1,0:T(8,128)(2,1)S(1)}, bf16[96,5120]{1,0:T(8,128)(2,1)}, u32[]{:S(2)}, u32[]{:S(2)}) collective-permute-start(bf16[96,5120]{1,0:T(8,128)(2,1)S(1)} %collective-permute-done.2.refs_4_), channel_id=1, source_target_pairs={{0,6},{1,7},{2,0},{3,1},{4,2},{5,3},{6,4},{7,5},{8,14},{9,15},{10,... | collective-permute-start | bytes 2949128 | tf_op jit(solution)/shard_map/ppermute | solution.py:27
  34.4 22.2 %collective-permute-start.8 = (bf16[96,5120]{1,0:T(8,128)(2,1)S(1)}, bf16[96,5120]{1,0:T(8,128)(2,1)}, u32[]{:S(2)}, u32[]{:S(2)}) collective-permute-start(bf16[96,5120]{1,0:T(8,128)(2,1)S(1)} %collective-permute-done.2.refs_4_), channel_id=1, source_target_pairs={{0,2},{1,3},{2,4},{3,5},{4,6},{5,7},{6,0},{7,1},{8,10},{9,11},{10,... | collective-permute-start | bytes 2949128 | tf_op jit(solution)/shard_map/ppermute | solution.py:27
  35.5 29.5 %copy-start.12 = (bf16[5136,128]{1,0:T(8,128)(2,1)}, bf16[5136,128]{1,0:T(8,128)(2,1)S(1)}, u32[]{:S(2)}) copy-start(bf16[5136,128]{1,0:T(8,128)(2,1)S(1)} %collective-permute-done.refs_1_) | copy-start | bytes 3944452
  35.6 21.0 %collective-permute-start.4 = (bf16[2576,128]{1,0:T(8,128)(2,1)S(1)}, bf16[2576,128]{1,0:T(8,128)(2,1)S(1)}, u32[]{:S(2)}, u32[]{:S(2)}) collective-permute-start(bf16[2576,128]{1,0:T(8,128)(2,1)S(1)} %pad_maximum_fusion), channel_id=1, source_target_pairs={{0,32},{1,33},{2,34},{3,35},{4,36},{5,37},{6,38},{7,39},{8,40},{9,... | collective-permute-start | bytes 1978376 | tf_op jit(solution)/shard_map/ppermute | solution.py:27
  40.7 24.3 %copy-start.13 = (bf16[5136,128]{1,0:T(8,128)(2,1)}, bf16[5136,128]{1,0:T(8,128)(2,1)S(1)}, u32[]{:S(2)}) copy-start(bf16[5136,128]{1,0:T(8,128)(2,1)S(1)} %collective-permute-done.1.refs_2_) | copy-start | bytes 3944452
  40.8 15.8 %collective-permute-start.5 = (bf16[2560,128]{1,0:T(8,128)(2,1)S(1)}, bf16[2560,128]{1,0:T(8,128)(2,1)S(1)}, u32[]{:S(2)}, u32[]{:S(2)}) collective-permute-start(bf16[2560,128]{1,0:T(8,128)(2,1)S(1)} %slice.66), channel_id=1, source_target_pairs={{0,96},{1,97},{2,98},{3,99},{4,100},{5,101},{6,102},{7,103},{8,104... | collective-permute-start | bytes 1966088 | tf_op jit(solution)/shard_map/ppermute | solution.py:27
  58.8 32.5 %copy-start.4 = (bf16[5136,128]{1,0:T(8,128)(2,1)}, bf16[5136,128]{1,0:T(8,128)(2,1)S(1)}, u32[]{:S(2)}) copy-start(bf16[5136,128]{1,0:T(8,128)(2,1)S(1)} %get-tuple-element.67.refs_4_) | copy-start | bytes 3944452
  58.8 35.9 %copy-start.14 = (bf16[5136,128]{1,0:T(8,128)(2,1)}, bf16[5136,128]{1,0:T(8,128)(2,1)S(1)}, u32[]{:S(2)}) copy-start(bf16[5136,128]{1,0:T(8,128)(2,1)S(1)} %collective-permute-done.3.refs_3_) | copy-start | bytes 3944452
  58.8 31.1 %collective-permute-start.11 = (bf16[5136,128]{1,0:T(8,128)(2,1)S(1)}, bf16[5136,128]{1,0:T(8,128)(2,1)S(1)}, u32[]{:S(2)}, u32[]{:S(2)}) collective-permute-start(bf16[5136,128]{1,0:T(8,128)(2,1)S(1)} %collective-permute-done.3.refs_3_), channel_id=1, source_target_pairs={{0,96},{1,97},{2,98},{3,99},{4,100},{5,101},{6,102},{7,103},{8,104... | collective-permute-start | bytes 3944456 | tf_op jit(solution)/shard_map/ppermute | solution.py:27
  62.1 29.1 %collective-permute-start.10 = (bf16[5136,128]{1,0:T(8,128)(2,1)S(1)}, bf16[5136,128]{1,0:T(8,128)(2,1)S(1)}, u32[]{:S(2)}, u32[]{:S(2)}) collective-permute-start(bf16[5136,128]{1,0:T(8,128)(2,1)S(1)} %collective-permute-done.3.refs_3_), channel_id=1, source_target_pairs={{0,32},{1,33},{2,34},{3,35},{4,36},{5,37},{6,38},{7,39},{8,40},{9,... | collective-permute-start | bytes 3944456 | tf_op jit(solution)/shard_map/ppermute | solution.py:27
  62.1 20.1 %collective-permute-start.14 = (bf16[96,5120]{1,0:T(8,128)(2,1)S(1)}, bf16[96,5120]{1,0:T(8,128)(2,1)}, u32[]{:S(2)}, u32[]{:S(2)}) collective-permute-start(bf16[96,5120]{1,0:T(8,128)(2,1)S(1)} %get-tuple-element.69), channel_id=1, source_target_pairs={{0,6},{1,7},{2,0},{3,1},{4,2},{5,3},{6,4},{7,5},{8,14},{9,15},{10,... | collective-permute-start | bytes 2949128 | tf_op jit(solution)/shard_map/ppermute | solution.py:27
  64.4 22.0 %collective-permute-start.13 = (bf16[96,5120]{1,0:T(8,128)(2,1)S(1)}, bf16[96,5120]{1,0:T(8,128)(2,1)}, u32[]{:S(2)}, u32[]{:S(2)}) collective-permute-start(bf16[96,5120]{1,0:T(8,128)(2,1)S(1)} %get-tuple-element.66), channel_id=1, source_target_pairs={{0,2},{1,3},{2,4},{3,5},{4,6},{5,7},{6,0},{7,1},{8,10},{9,11},{10,... | collective-permute-start | bytes 2949128 | tf_op jit(solution)/shard_map/ppermute | solution.py:27
  64.4 30.2 %collective-permute-start.12 = (bf16[5136,128]{1,0:T(8,128)(2,1)S(1)}, bf16[5136,128]{1,0:T(8,128)(2,1)S(1)}, u32[]{:S(2)}, u32[]{:S(2)}) collective-permute-start(bf16[5136,128]{1,0:T(8,128)(2,1)S(1)} %get-tuple-element.67.refs_4_), channel_id=1, source_target_pairs={{0,16},{1,17},{2,18},{3,19},{4,20},{5,21},{6,22},{7,23},{8,24},{9,... | collective-permute-start | bytes 3944456 | tf_op jit(solution)/shard_map/ppermute | solution.py:27
  82.2 15.4 %collective-permute-start.17 = (bf16[96,5120]{1,0:T(8,128)(2,1)}, bf16[96,5120]{1,0:T(8,128)(2,1)}, u32[]{:S(2)}, u32[]{:S(2)}) collective-permute-start(bf16[96,5120]{1,0:T(8,128)(2,1)} %collective-permute-done.9.refs_5_.refs_10_), channel_id=1, source_target_pairs={{0,1},{1,0},{2,3},{3,2},{4,5},{5,4},{6,7},{7,6},{8,9},{9,8},{10,11... | collective-permute-start | bytes 2949128 | tf_op jit(solution)/shard_map/ppermute | solution.py:27
  86.4 9.4 %collective-permute-start.16 = (bf16[96,5120]{1,0:T(8,128)(2,1)}, bf16[96,5120]{1,0:T(8,128)(2,1)}, u32[]{:S(2)}, u32[]{:S(2)}) collective-permute-start(bf16[96,5120]{1,0:T(8,128)(2,1)} %collective-permute-done.14.refs_9_.refs_1_), channel_id=1, source_target_pairs={{0,1},{1,0},{2,3},{3,2},{4,5},{5,4},{6,7},{7,6},{8,9},{9,8},{10,11... | collective-permute-start | bytes 2949128 | tf_op jit(solution)/shard_map/ppermute | solution.py:27
  89.9 4.7 %copy-start.15 = (bf16[5136,128]{1,0:T(8,128)(2,1)}, bf16[5136,128]{1,0:T(8,128)(2,1)S(1)}, u32[]{:S(2)}) copy-start(bf16[5136,128]{1,0:T(8,128)(2,1)S(1)} %collective-permute-done.11.refs_6_) | copy-start | bytes 3944452
  89.9 5.9 %collective-permute-start.15 = (bf16[96,5120]{1,0:T(8,128)(2,1)}, bf16[96,5120]{1,0:T(8,128)(2,1)}, u32[]{:S(2)}, u32[]{:S(2)}) collective-permute-start(bf16[96,5120]{1,0:T(8,128)(2,1)} %collective-permute-done.13.refs_8_.refs_0_), channel_id=1, source_target_pairs={{0,1},{1,0},{2,3},{3,2},{4,5},{5,4},{6,7},{7,6},{8,9},{9,8},{10,11... | collective-permute-start | bytes 2949128 | tf_op jit(solution)/shard_map/ppermute | solution.py:27
  91.2 3.4 %copy-start.16 = (bf16[5136,128]{1,0:T(8,128)(2,1)}, bf16[5136,128]{1,0:T(8,128)(2,1)S(1)}, u32[]{:S(2)}) copy-start(bf16[5136,128]{1,0:T(8,128)(2,1)S(1)} %collective-permute-done.10.refs_5_) | copy-start | bytes 3944452
  91.2 7.0 %collective-permute-start.18 = (bf16[96,5120]{1,0:T(8,128)(2,1)}, bf16[96,5120]{1,0:T(8,128)(2,1)}, u32[]{:S(2)}, u32[]{:S(2)}) collective-permute-start(bf16[96,5120]{1,0:T(8,128)(2,1)} %collective-permute-done.8.refs_3_.refs_11_), channel_id=1, source_target_pairs={{0,1},{1,0},{2,3},{3,2},{4,5},{5,4},{6,7},{7,6},{8,9},{9,8},{10,11... | collective-permute-start | bytes 2949128 | tf_op jit(solution)/shard_map/ppermute | solution.py:27
  94.7 1.1 copy-start.17
  95.9 19.1 %collective-permute-start.19 = (bf16[96,5120]{1,0:T(8,128)(2,1)S(1)}, bf16[96,5120]{1,0:T(8,128)(2,1)}, u32[]{:S(2)}, u32[]{:S(2)}) collective-permute-start(bf16[96,5120]{1,0:T(8,128)(2,1)S(1)} %collective-permute-done.7.refs_4_.refs_2_), channel_id=1, source_target_pairs={{0,1},{1,0},{2,3},{3,2},{4,5},{5,4},{6,7},{7,6},{8,9},{9,8},{10,11... | collective-permute-start | bytes 2949128 | tf_op jit(solution)/shard_map/ppermute | solution.py:27
  97.1 17.9 %collective-permute-start.20 = (bf16[96,5120]{1,0:T(8,128)(2,1)S(1)}, bf16[96,5120]{1,0:T(8,128)(2,1)}, u32[]{:S(2)}, u32[]{:S(2)}) collective-permute-start(bf16[96,5120]{1,0:T(8,128)(2,1)S(1)} %collective-permute-done.6.refs_2_.refs_3_), channel_id=1, source_target_pairs={{0,1},{1,0},{2,3},{3,2},{4,5},{5,4},{6,7},{7,6},{8,9},{9,8},{10,11... | collective-permute-start | bytes 2949128 | tf_op jit(solution)/shard_map/ppermute | solution.py:27
  97.2 17.8 %collective-permute-start.21 = (bf16[96,5120]{1,0:T(8,128)(2,1)}, bf16[96,5120]{1,0:T(8,128)(2,1)}, u32[]{:S(2)}, u32[]{:S(2)}) collective-permute-start(bf16[96,5120]{1,0:T(8,128)(2,1)} %copy-done.18), channel_id=1, source_target_pairs={{0,1},{1,0},{2,3},{3,2},{4,5},{5,4},{6,7},{7,6},{8,9},{9,8},{10,11... | collective-permute-start | bytes 2949128 | tf_op jit(solution)/shard_map/ppermute | solution.py:27
  97.6 17.4 %collective-permute-start.22 = (bf16[96,5120]{1,0:T(8,128)(2,1)S(1)}, bf16[96,5120]{1,0:T(8,128)(2,1)}, u32[]{:S(2)}, u32[]{:S(2)}) collective-permute-start(bf16[96,5120]{1,0:T(8,128)(2,1)S(1)} %copy-done.11), channel_id=1, source_target_pairs={{0,1},{1,0},{2,3},{3,2},{4,5},{5,4},{6,7},{7,6},{8,9},{9,8},{10,11... | collective-permute-start | bytes 2949128 | tf_op jit(solution)/shard_map/ppermute | solution.py:27
  114.9 6.8 %copy-start.8 = (bf16[96,5120]{1,0:T(8,128)(2,1)S(1)}, bf16[96,5120]{1,0:T(8,128)(2,1)}, u32[]{:S(2)}) copy-start(bf16[96,5120]{1,0:T(8,128)(2,1)} %get-tuple-element.82) | copy-start | bytes 2949124
  115.0 2.9 %collective-permute-start.23 = (bf16[96,5120]{1,0:T(8,128)(2,1)}, bf16[96,5120]{1,0:T(8,128)(2,1)S(1)}, u32[]{:S(2)}, u32[]{:S(2)}) collective-permute-start(bf16[96,5120]{1,0:T(8,128)(2,1)} %get-tuple-element.81), channel_id=1, source_target_pairs={{0,1},{1,0},{2,3},{3,2},{4,5},{5,4},{6,7},{7,6},{8,9},{9,8},{10,11... | collective-permute-start | bytes 2949128 | tf_op jit(solution)/shard_map/ppermute | solution.py:27
  115.5 6.3 %collective-permute-start.24 = (bf16[96,5120]{1,0:T(8,128)(2,1)}, bf16[96,5120]{1,0:T(8,128)(2,1)S(1)}, u32[]{:S(2)}, u32[]{:S(2)}) collective-permute-start(bf16[96,5120]{1,0:T(8,128)(2,1)} %get-tuple-element.83), channel_id=1, source_target_pairs={{0,1},{1,0},{2,3},{3,2},{4,5},{5,4},{6,7},{7,6},{8,9},{9,8},{10,11... | collective-permute-start | bytes 2949128 | tf_op jit(solution)/shard_map/ppermute | solution.py:27
  115.5 7.4 %collective-permute-start.25 = (bf16[96,5120]{1,0:T(8,128)(2,1)}, bf16[96,5120]{1,0:T(8,128)(2,1)S(1)}, u32[]{:S(2)}, u32[]{:S(2)}) collective-permute-start(bf16[96,5120]{1,0:T(8,128)(2,1)} %get-tuple-element.85), channel_id=1, source_target_pairs={{0,1},{1,0},{2,3},{3,2},{4,5},{5,4},{6,7},{7,6},{8,9},{9,8},{10,11... | collective-permute-start | bytes 2949128 | tf_op jit(solution)/shard_map/ppermute | solution.py:27
  119.3 3.7 %copy-start.7 = (bf16[96,5120]{1,0:T(8,128)(2,1)S(1)}, bf16[96,5120]{1,0:T(8,128)(2,1)}, u32[]{:S(2)}) copy-start(bf16[96,5120]{1,0:T(8,128)(2,1)} %get-tuple-element.84) | copy-start | bytes 2949124
  119.3 29.4 %collective-permute-start.28 = (bf16[96,5120]{1,0:T(8,128)(2,1)S(1)}, bf16[96,5120]{1,0:T(8,128)(2,1)}, u32[]{:S(2)}, u32[]{:S(2)}) collective-permute-start(bf16[96,5120]{1,0:T(8,128)(2,1)S(1)} %add_convert_fusion.6), channel_id=1, source_target_pairs={{0,8},{1,9},{2,10},{3,11},{4,12},{5,13},{6,14},{7,15},{8,0},{9,1},... | collective-permute-start | bytes 2949128 | tf_op jit(solution)/shard_map/ppermute | solution.py:27
  122.0 26.7 %collective-permute-start.29 = (bf16[96,5120]{1,0:T(8,128)(2,1)S(1)}, bf16[96,5120]{1,0:T(8,128)(2,1)S(1)}, u32[]{:S(2)}, u32[]{:S(2)}) collective-permute-start(bf16[96,5120]{1,0:T(8,128)(2,1)S(1)} %add_convert_fusion.5), channel_id=1, source_target_pairs={{0,2},{1,3},{2,4},{3,5},{4,6},{5,7},{6,0},{7,1},{8,10},{9,11},{10,... | collective-permute-start | bytes 2949128 | tf_op jit(solution)/shard_map/ppermute | solution.py:27
  123.3 25.5 %collective-permute-start.30 = (bf16[96,5120]{1,0:T(8,128)(2,1)S(1)}, bf16[96,5120]{1,0:T(8,128)(2,1)S(1)}, u32[]{:S(2)}, u32[]{:S(2)}) collective-permute-start(bf16[96,5120]{1,0:T(8,128)(2,1)S(1)} %add_convert_fusion.4), channel_id=1, source_target_pairs={{0,6},{1,7},{2,0},{3,1},{4,2},{5,3},{6,4},{7,5},{8,14},{9,15},{10,... | collective-permute-start | bytes 2949128 | tf_op jit(solution)/shard_map/ppermute | solution.py:27
  145.0 3.0 %collective-permute-start.26 = (bf16[48,5120]{1,0:T(8,128)(2,1)}, bf16[48,5120]{1,0:T(8,128)(2,1)S(1)}, u32[]{:S(2)}, u32[]{:S(2)}) collective-permute-start(bf16[48,5120]{1,0:T(8,128)(2,1)} %get-tuple-element.95), channel_id=1, source_target_pairs={{0,1},{1,0},{2,3},{3,2},{4,5},{5,4},{6,7},{7,6},{8,9},{9,8},{10,11... | collective-permute-start | bytes 1474568 | tf_op jit(solution)/shard_map/ppermute | solution.py:27
  146.3 2.4 %collective-permute-start.27 = (bf16[48,5120]{1,0:T(8,128)(2,1)}, bf16[48,5120]{1,0:T(8,128)(2,1)S(1)}, u32[]{:S(2)}, u32[]{:S(2)}) collective-permute-start(bf16[48,5120]{1,0:T(8,128)(2,1)} %get-tuple-element.96), channel_id=1, source_target_pairs={{0,1},{1,0},{2,3},{3,2},{4,5},{5,4},{6,7},{7,6},{8,9},{9,8},{10,11... | collective-permute-start | bytes 1474568 | tf_op jit(solution)/shard_map/ppermute | solution.py:27
  148.7 3.0 %copy-start.21 = (bf16[96,5120]{1,0:T(8,128)(2,1)S(1)}, bf16[96,5120]{1,0:T(8,128)(2,1)}, u32[]{:S(2)}) copy-start(bf16[96,5120]{1,0:T(8,128)(2,1)} %get-tuple-element.106) | copy-start | bytes 2949124
  148.7 4.8 %copy-start.20 = (bf16[96,5120]{1,0:T(8,128)(2,1)S(1)}, bf16[96,5120]{1,0:T(8,128)(2,1)}, u32[]{:S(2)}) copy-start(bf16[96,5120]{1,0:T(8,128)(2,1)} %get-tuple-element.102) | copy-start | bytes 2949124
  148.7 5.5 %copy-start.19 = (bf16[96,5120]{1,0:T(8,128)(2,1)S(1)}, bf16[96,5120]{1,0:T(8,128)(2,1)}, u32[]{:S(2)}) copy-start(bf16[96,5120]{1,0:T(8,128)(2,1)} %get-tuple-element.104) | copy-start | bytes 2949124
  148.8 5.6 %copy-start.5 = (bf16[96,5120]{1,0:T(8,128)(2,1)S(1)}, bf16[96,5120]{1,0:T(8,128)(2,1)}, u32[]{:S(2)}) copy-start(bf16[96,5120]{1,0:T(8,128)(2,1)} %get-tuple-element.105) | copy-start | bytes 2949124
  151.7 2.6 %collective-permute-start.33 = (bf16[96,5120]{1,0:T(8,128)(2,1)S(1)}, bf16[96,5120]{1,0:T(8,128)(2,1)S(1)}, u32[]{:S(2)}, u32[]{:S(2)}) collective-permute-start(bf16[96,5120]{1,0:T(8,128)(2,1)S(1)} %copy-done.21), channel_id=1, source_target_pairs={{0,1},{1,0},{2,3},{3,2},{4,5},{5,4},{6,7},{7,6},{8,9},{9,8},{10,11... | collective-permute-start | bytes 2949128 | tf_op jit(solution)/shard_map/ppermute | solution.py:27
  152.1 13.6 %collective-permute-start.35 = (bf16[48,5120]{1,0:T(8,128)(2,1)}, bf16[48,5120]{1,0:T(8,128)(2,1)}, u32[]{:S(2)}, u32[]{:S(2)}) collective-permute-start(bf16[48,5120]{1,0:T(8,128)(2,1)} %get-tuple-element.121), channel_id=1, source_target_pairs={{0,6},{1,7},{2,0},{3,1},{4,2},{5,3},{6,4},{7,5},{8,14},{9,15},{10,... | collective-permute-start | bytes 1474568 | tf_op jit(solution)/shard_map/ppermute | solution.py:27
  153.5 13.9 %collective-permute-start.34 = (bf16[48,5120]{1,0:T(8,128)(2,1)}, bf16[48,5120]{1,0:T(8,128)(2,1)}, u32[]{:S(2)}, u32[]{:S(2)}) collective-permute-start(bf16[48,5120]{1,0:T(8,128)(2,1)} %get-tuple-element.122), channel_id=1, source_target_pairs={{0,2},{1,3},{2,4},{3,5},{4,6},{5,7},{6,0},{7,1},{8,10},{9,11},{10,... | collective-permute-start | bytes 1474568 | tf_op jit(solution)/shard_map/ppermute | solution.py:27
  153.6 2.9 %collective-permute-start.31 = (bf16[96,5120]{1,0:T(8,128)(2,1)S(1)}, bf16[96,5120]{1,0:T(8,128)(2,1)S(1)}, u32[]{:S(2)}, u32[]{:S(2)}) collective-permute-start(bf16[96,5120]{1,0:T(8,128)(2,1)S(1)} %copy-done.20), channel_id=1, source_target_pairs={{0,1},{1,0},{2,3},{3,2},{4,5},{5,4},{6,7},{7,6},{8,9},{9,8},{10,11... | collective-permute-start | bytes 2949128 | tf_op jit(solution)/shard_map/ppermute | solution.py:27
  154.3 3.6 %collective-permute-start.32 = (bf16[96,5120]{1,0:T(8,128)(2,1)S(1)}, bf16[96,5120]{1,0:T(8,128)(2,1)S(1)}, u32[]{:S(2)}, u32[]{:S(2)}) collective-permute-start(bf16[96,5120]{1,0:T(8,128)(2,1)S(1)} %copy-done.19), channel_id=1, source_target_pairs={{0,1},{1,0},{2,3},{3,2},{4,5},{5,4},{6,7},{7,6},{8,9},{9,8},{10,11... | collective-permute-start | bytes 2949128 | tf_op jit(solution)/shard_map/ppermute | solution.py:27
  154.4 2.1 %copy-start.10 = (bf16[96,5120]{1,0:T(8,128)(2,1)S(1)}, bf16[96,5120]{1,0:T(8,128)(2,1)}, u32[]{:S(2)}) copy-start(bf16[96,5120]{1,0:T(8,128)(2,1)} %get-tuple-element.89) | copy-start | bytes 2949124
  156.5 1.4 copy-start.9
  168.6 1.4 copy-start.22
  168.6 27.5 %copy-start.6 = (bf16[96,5120]{1,0:T(8,128)(2,1)S(1)}, bf16[96,5120]{1,0:T(8,128)(2,1)}, u32[]{:S(2)}) copy-start(bf16[96,5120]{1,0:T(8,128)(2,1)} %get-tuple-element.113) | copy-start | bytes 2949124
  169.9 3.6 %collective-permute-start.36 = (bf16[96,5120]{1,0:T(8,128)(2,1)S(1)}, bf16[96,5120]{1,0:T(8,128)(2,1)S(1)}, u32[]{:S(2)}, u32[]{:S(2)}) collective-permute-start(bf16[96,5120]{1,0:T(8,128)(2,1)S(1)} %copy-done.22), channel_id=1, source_target_pairs={{0,1},{1,0},{2,3},{3,2},{4,5},{5,4},{6,7},{7,6},{8,9},{9,8},{10,11... | collective-permute-start | bytes 2949128 | tf_op jit(solution)/shard_map/ppermute | solution.py:27
  171.2 24.8 %collective-permute-start.37 = (bf16[96,5120]{1,0:T(8,128)(2,1)S(1)}, bf16[96,5120]{1,0:T(8,128)(2,1)S(1)}, u32[]{:S(2)}, u32[]{:S(2)}) collective-permute-start(bf16[96,5120]{1,0:T(8,128)(2,1)S(1)} %add_convert_fusion.3), channel_id=1, source_target_pairs={{0,8},{1,9},{2,10},{3,11},{4,12},{5,13},{6,14},{7,15},{8,0},{9,1},... | collective-permute-start | bytes 2949128 | tf_op jit(solution)/shard_map/ppermute | solution.py:27
  172.1 24.3 %collective-permute-start.39 = (bf16[96,5120]{1,0:T(8,128)(2,1)S(1)}, bf16[96,5120]{1,0:T(8,128)(2,1)S(1)}, u32[]{:S(2)}, u32[]{:S(2)}) collective-permute-start(bf16[96,5120]{1,0:T(8,128)(2,1)S(1)} %add_convert_fusion.1), channel_id=1, source_target_pairs={{0,6},{1,7},{2,0},{3,1},{4,2},{5,3},{6,4},{7,5},{8,14},{9,15},{10,... | collective-permute-start | bytes 2949128 | tf_op jit(solution)/shard_map/ppermute | solution.py:27
  172.1 24.3 %collective-permute-start.38 = (bf16[96,5120]{1,0:T(8,128)(2,1)S(1)}, bf16[96,5120]{1,0:T(8,128)(2,1)S(1)}, u32[]{:S(2)}, u32[]{:S(2)}) collective-permute-start(bf16[96,5120]{1,0:T(8,128)(2,1)S(1)} %add_convert_fusion.2), channel_id=1, source_target_pairs={{0,2},{1,3},{2,4},{3,5},{4,6},{5,7},{6,0},{7,1},{8,10},{9,11},{10,... | collective-permute-start | bytes 2949128 | tf_op jit(solution)/shard_map/ppermute | solution.py:27

commit v10 on v9

--- a/solution.py
+++ b/solution.py
@@ -223,7 +223,7 @@
             pltpu.VMEM((2, rows, STEP), BF16),
             pltpu.SemaphoreType.DMA((n_copies,)),
         ],
-        compiler_params=pltpu.CompilerParams(vmem_limit_bytes=44 * 2**20),
+        compiler_params=pltpu.CompilerParams(vmem_limit_bytes=36 * 2**20),
         cost_estimate=pl.CostEstimate(
             flops=2 * rows * depth * local_ff * 3,
             bytes_accessed=2 * (depth * slots * width + local_ff * depth + 2 * rows * depth),

time: 198 us -> 192 us (0.970)
  other arithmetic: 10 us -> 4.01 us
  waiting for transfers between devices: 83.8 us -> 86.6 us
  starting transfers between devices: 52.5 us -> 50.3 us
    ppermute x40, waiting for transfers between devices: 83.8 us -> 86.6 us  [move(): return lax.ppermute(value, AXES, pairs)]
    convert_element_type x1, other arithmetic: 2.96 us -> 0.37 us  [body(): low = add(far[1], got[1], far_in[h_rows:]).astype(BF16)]
    ppermute x40, starting transfers between devices: 52.5 us -> 50.3 us  [move(): return lax.ppermute(value, AXES, pairs)]
    unnamed x46 -> x44, local copies, waits for them, and re-layouts: 2.48 us -> 4.21 us
  transfers between devices with their start and end apart: 40 -> 40, of which waited for: 14 -> 16; matrix products, arithmetic and copies ran while one was open for 2% -> 1% of each run, Pallas kernels for 23% -> 23%
where the time goes in v10:
time: 192 us
  waiting for transfers between devices  86.6 us (45%)
  starting transfers between devices  50.3 us (26%)
  Pallas kernels  44.7 us (23%)
  local copies, waits for them, and re-layouts  4.42 us (2%)
  other arithmetic  4.01 us (2%)
    ppermute x40, waiting for transfers between devices, move(): return lax.ppermute(value, AXES, pairs)  86.6 us
    ppermute x40, starting transfers between devices, move(): return lax.ppermute(value, AXES, pairs)  50.3 us
    pallas_call x2, Pallas kernels, sums(): return tuple(run(ids, sidx, scale_table, *pieces, *weights))  26.5 us
    pallas_call x1, Pallas kernels, sums(): return tuple(run(ids, sidx, scale_table, *sources, *pieces, down_weight))  16.3 us
    unnamed x44, local copies, waits for them, and re-layouts  4.21 us
  transfers between devices with their start and end apart: 40, of which 16 were waited for; matrix products, arithmetic and copies ran while one was open for 1% of the time, Pallas kernels for 23%

profile of v10, /device:TPU:1, one launch (start us, length us, event | category | flops | bytes accessed | tf_op | source)
XLA Modules:
  0.0 191.8 jit_solution(10218152952104701788)
XLA Ops:
  1.3 1.3 copy-done.1
  2.8 2.2 %collective-permute-start = (bf16[5136,128]{1,0:T(8,128)(2,1)S(1)}, bf16[5136,128]{1,0:T(8,128)(2,1)S(1)}, u32[]{:S(2)}, u32[]{:S(2)}) collective-permute-start(bf16[5136,128]{1,0:T(8,128)(2,1)S(1)} %shard_map.64.refs_0_), channel_id=1, source_target_pairs={{0,32},{1,33},{2,34},{3,35},{4,36},{5,37},{6,38},{7,39},{8,40},{9,... | collective-permute-start | bytes 3944456 | tf_op jit(solution)/shard_map/ppermute | solution.py:27
  5.0 3.6 %collective-permute-start.2 = (bf16[96,5120]{1,0:T(8,128)(2,1)}, bf16[96,5120]{1,0:T(8,128)(2,1)S(1)}, u32[]{:S(2)}, u32[]{:S(2)}) collective-permute-start(bf16[96,5120]{1,0:T(8,128)(2,1)} %refs_0_.1), channel_id=1, source_target_pairs={{0,8},{1,9},{2,10},{3,11},{4,12},{5,13},{6,14},{7,15},{8,0},{9,1},... | collective-permute-start | bytes 2949128 | tf_op jit(solution)/shard_map/ppermute | solution.py:27
  8.5 2.5 %collective-permute-start.7 = (bf16[96,5120]{1,0:T(8,128)(2,1)}, bf16[96,5120]{1,0:T(8,128)(2,1)}, u32[]{:S(2)}, u32[]{:S(2)}) collective-permute-start(bf16[96,5120]{1,0:T(8,128)(2,1)} %refs_0_.1), channel_id=1, source_target_pairs={{0,6},{1,7},{2,0},{3,1},{4,2},{5,3},{6,4},{7,5},{8,14},{9,15},{10,... | collective-permute-start | bytes 2949128 | tf_op jit(solution)/shard_map/ppermute | solution.py:27
  11.0 1.5 collective-permute-start.1
  12.6 17.4 %collective-permute-done.2.refs_4_ = bf16[96,5120]{1,0:T(8,128)(2,1)S(1)} collective-permute-done((bf16[96,5120]{1,0:T(8,128)(2,1)}, bf16[96,5120]{1,0:T(8,128)(2,1)S(1)}, u32[]{:S(2)}, u32[]{:S(2)}) %collective-permute-start.2) | collective-permute-done | bytes 983072 | tf_op jit(solution)/shard_map/ppermute | solution.py:27
  29.9 0.8 collective-permute-start.3
  30.7 0.4 collective-permute-done.7.refs_4_.refs_2_
  31.2 3.1 %collective-permute-done.6.refs_2_.refs_3_ = bf16[96,5120]{1,0:T(8,128)(2,1)} collective-permute-done((bf16[96,5120]{1,0:T(8,128)(2,1)}, bf16[96,5120]{1,0:T(8,128)(2,1)}, u32[]{:S(2)}, u32[]{:S(2)}) %collective-permute-start.6) | collective-permute-done | bytes 983072 | tf_op jit(solution)/shard_map/ppermute | solution.py:27
  34.3 0.3 collective-permute-start.9
  34.6 1.2 collective-permute-start.8
  35.9 1.4 collective-permute-start.4
  37.2 2.6 %collective-permute-done.1.refs_2_ = bf16[5136,128]{1,0:T(8,128)(2,1)S(1)} collective-permute-done((bf16[5136,128]{1,0:T(8,128)(2,1)S(1)}, bf16[5136,128]{1,0:T(8,128)(2,1)S(1)}, u32[]{:S(2)}, u32[]{:S(2)}) %collective-permute-start.1) | collective-permute-done | bytes 1314848 | tf_op jit(solution)/shard_map/ppermute | solution.py:27
  39.9 3.0 %collective-permute-start.5 = (bf16[2560,128]{1,0:T(8,128)(2,1)S(1)}, bf16[2560,128]{1,0:T(8,128)(2,1)S(1)}, u32[]{:S(2)}, u32[]{:S(2)}) collective-permute-start(bf16[2560,128]{1,0:T(8,128)(2,1)S(1)} %slice.66), channel_id=1, source_target_pairs={{0,96},{1,97},{2,98},{3,99},{4,100},{5,101},{6,102},{7,103},{8,104... | collective-permute-start | bytes 1966088 | tf_op jit(solution)/shard_map/ppermute | solution.py:27
  42.9 12.2 %collective-permute-done.9.refs_5_.refs_10_ = bf16[96,5120]{1,0:T(8,128)(2,1)S(1)} collective-permute-done((bf16[96,5120]{1,0:T(8,128)(2,1)S(1)}, bf16[96,5120]{1,0:T(8,128)(2,1)S(1)}, u32[]{:S(2)}, u32[]{:S(2)}) %collective-permute-start.9) | collective-permute-done | bytes 983072 | tf_op jit(solution)/shard_map/ppermute | solution.py:27
  55.1 1.5 collective-permute-done.8.refs_3_.refs_11_
  56.6 1.9 shard_map.65
  58.5 0.3 collective-permute-done.3.refs_3_
  58.7 1.9 collective-permute-start.11
  60.6 2.5 %collective-permute-start.14 = (bf16[96,5120]{1,0:T(8,128)(2,1)S(1)}, bf16[96,5120]{1,0:T(8,128)(2,1)}, u32[]{:S(2)}, u32[]{:S(2)}) collective-permute-start(bf16[96,5120]{1,0:T(8,128)(2,1)S(1)} %get-tuple-element.69), channel_id=1, source_target_pairs={{0,6},{1,7},{2,0},{3,1},{4,2},{5,3},{6,4},{7,5},{8,14},{9,15},{10,... | collective-permute-start | bytes 2949128 | tf_op jit(solution)/shard_map/ppermute | solution.py:27
  63.1 0.6 collective-permute-start.12
  63.8 17.6 %collective-permute-done.14.refs_9_.refs_1_ = bf16[96,5120]{1,0:T(8,128)(2,1)} collective-permute-done((bf16[96,5120]{1,0:T(8,128)(2,1)S(1)}, bf16[96,5120]{1,0:T(8,128)(2,1)}, u32[]{:S(2)}, u32[]{:S(2)}) %collective-permute-start.14) | collective-permute-done | bytes 983072 | tf_op jit(solution)/shard_map/ppermute | solution.py:27
  81.4 3.7 %collective-permute-start.17 = (bf16[96,5120]{1,0:T(8,128)(2,1)S(1)}, bf16[96,5120]{1,0:T(8,128)(2,1)}, u32[]{:S(2)}, u32[]{:S(2)}) collective-permute-start(bf16[96,5120]{1,0:T(8,128)(2,1)S(1)} %collective-permute-done.9.refs_5_.refs_10_), channel_id=1, source_target_pairs={{0,1},{1,0},{2,3},{3,2},{4,5},{5,4},{6,7},{7,6},{8,9},{9,8},{10,11... | collective-permute-start | bytes 2949128 | tf_op jit(solution)/shard_map/ppermute | solution.py:27
  85.1 3.5 %collective-permute-start.16 = (bf16[96,5120]{1,0:T(8,128)(2,1)}, bf16[96,5120]{1,0:T(8,128)(2,1)}, u32[]{:S(2)}, u32[]{:S(2)}) collective-permute-start(bf16[96,5120]{1,0:T(8,128)(2,1)} %collective-permute-done.14.refs_9_.refs_1_), channel_id=1, source_target_pairs={{0,1},{1,0},{2,3},{3,2},{4,5},{5,4},{6,7},{7,6},{8,9},{9,8},{10,11... | collective-permute-start | bytes 2949128 | tf_op jit(solution)/shard_map/ppermute | solution.py:27
  88.6 1.4 collective-permute-start.15
  90.0 3.1 %collective-permute-start.18 = (bf16[96,5120]{1,0:T(8,128)(2,1)S(1)}, bf16[96,5120]{1,0:T(8,128)(2,1)}, u32[]{:S(2)}, u32[]{:S(2)}) collective-permute-start(bf16[96,5120]{1,0:T(8,128)(2,1)S(1)} %collective-permute-done.8.refs_3_.refs_11_), channel_id=1, source_target_pairs={{0,1},{1,0},{2,3},{3,2},{4,5},{5,4},{6,7},{7,6},{8,9},{9,8},{10,11... | collective-permute-start | bytes 2949128 | tf_op jit(solution)/shard_map/ppermute | solution.py:27
  93.2 1.1 copy-done.14
  94.3 1.4 collective-permute-start.19
  95.8 0.4 collective-permute-start.21
  96.4 16.3 %shard_map.66 = (bf16[96,5120]{1,0:T(8,128)(2,1)S(1)}, bf16[96,5120]{1,0:T(8,128)(2,1)S(1)}, bf16[96,5120]{1,0:T(8,128)(2,1)S(1)}, bf16[96,5120]{1,0:T(8,128)(2,...) custom-call(s32[8]{0:T(128)S(1)} %get-tuple-element.109.ids, ...), custom_call_target="tpu_custom_call" | custom-call | flops 9059696640 | bytes 27525120 | tf_op jit(solution)/shard_map/pallas_call | solution.py:280
  112.8 1.0 copy-done.18
  113.8 0.4 collective-permute-start.23
  114.3 0.4 collective-permute-start.25
  114.7 1.9 collective-permute-done.23
  116.6 0.2 add_convert_fusion.6
  116.8 2.6 %collective-permute-start.28 = (bf16[96,5120]{1,0:T(8,128)(2,1)S(1)}, bf16[96,5120]{1,0:T(8,128)(2,1)S(1)}, u32[]{:S(2)}, u32[]{:S(2)}) collective-permute-start(bf16[96,5120]{1,0:T(8,128)(2,1)S(1)} %add_convert_fusion.6), channel_id=1, source_target_pairs={{0,8},{1,9},{2,10},{3,11},{4,12},{5,13},{6,14},{7,15},{8,0},{9,1},... | collective-permute-start | bytes 2949128 | tf_op jit(solution)/shard_map/ppermute | solution.py:27
  119.4 0.2 add_convert_fusion.5
  119.7 0.8 collective-permute-start.29
  120.5 0.2 add_convert_fusion.4
  120.7 2.0 %collective-permute-start.30 = (bf16[96,5120]{1,0:T(8,128)(2,1)S(1)}, bf16[96,5120]{1,0:T(8,128)(2,1)S(1)}, u32[]{:S(2)}, u32[]{:S(2)}) collective-permute-start(bf16[96,5120]{1,0:T(8,128)(2,1)S(1)} %add_convert_fusion.4), channel_id=1, source_target_pairs={{0,6},{1,7},{2,0},{3,1},{4,2},{5,3},{6,4},{7,5},{8,14},{9,15},{10,... | collective-permute-start | bytes 2949128 | tf_op jit(solution)/shard_map/ppermute | solution.py:27
  122.8 19.7 %shard_map.67 = (bf16[48,5120]{1,0:T(8,128)(2,1)S(1)}, bf16[48,5120]{1,0:T(8,128)(2,1)S(1)}, bf16[96,5120]{1,0:T(8,128)(2,1)S(1)}, bf16[96,5120]{1,0:T(8,128)(2,...) custom-call(s32[8]{0:T(128)S(1)} %get-tuple-element.109.ids, ...), custom_call_target="tpu_custom_call", output_to_operand_aliasing={{10}: (13, {}), {11}: (14, {})} | custom-call | flops 12079595520 | bytes 31457280 | tf_op jit(solution)/shard_map/pallas_call | solution.py:281
  142.5 1.3 collective-permute-start.26
  143.9 1.4 collective-permute-done.26
  145.3 0.7 collective-permute-done.27
  146.0 0.4 add_convert_fusion.7
  146.4 0.8 copy-done.21
  147.2 0.4 collective-permute-start.33
  147.6 1.8 collective-permute-start.35
  149.4 0.4 collective-permute-start.31
  149.9 0.6 add_convert_fusion.3
  150.5 1.5 collective-permute-done.31
  152.0 0.2 convert_add_fusion.2
  152.2 1.2 collective-permute-done.32
  153.4 0.2 convert_add_fusion.1
  153.6 6.7 %shard_map.68 = (bf16[96,5120]{1,0:T(8,128)(2,1)S(1)}, bf16[96,5120]{1,0:T(8,128)(2,1)S(1)}, bf16[4,5120,256]{2,1,0:T(8,128)(2,1)S(1)}, bf16[512,5120]{1,0:T(8,128)(2,1)S(1)}) custom-call(s32[8]{0:T(128)S(1)} %get-tuple-element.109.ids, s32[8]{0:T(128)S(1)} %get-tuple-element.123.sidx, ...), custom_call_target="tpu_custom_call", output_to_operand_aliasing={{2}: (5, {}), {3}: (6, {})} | custom-call | flops 3019898880 | bytes 19660800 | tf_op jit(solution)/shard_map/pallas_call | solution.py:281
  160.3 2.8 %collective-permute-done.34 = bf16[48,5120]{1,0:T(8,128)(2,1)S(1)} collective-permute-done((bf16[48,5120]{1,0:T(8,128)(2,1)S(1)}, bf16[48,5120]{1,0:T(8,128)(2,1)S(1)}, u32[]{:S(2)}, u32[]{:S(2)}) %collective-permute-start.34) | collective-permute-done | bytes 491552 | tf_op jit(solution)/shard_map/ppermute | solution.py:27
  163.1 0.1 add_convert_fusion.2
  163.4 1.2 collective-permute-start.36
  164.6 2.1 %collective-permute-start.37 = (bf16[96,5120]{1,0:T(8,128)(2,1)S(1)}, bf16[96,5120]{1,0:T(8,128)(2,1)S(1)}, u32[]{:S(2)}, u32[]{:S(2)}) collective-permute-start(bf16[96,5120]{1,0:T(8,128)(2,1)S(1)} %add_convert_fusion.3), channel_id=1, source_target_pairs={{0,8},{1,9},{2,10},{3,11},{4,12},{5,13},{6,14},{7,15},{8,0},{9,1},... | collective-permute-start | bytes 2949128 | tf_op jit(solution)/shard_map/ppermute | solution.py:27
  166.6 1.5 collective-permute-start.38
  168.1 21.3 %collective-permute-done.37 = bf16[96,5120]{1,0:T(8,128)(2,1)S(1)} collective-permute-done((bf16[96,5120]{1,0:T(8,128)(2,1)S(1)}, bf16[96,5120]{1,0:T(8,128)(2,1)S(1)}, u32[]{:S(2)}, u32[]{:S(2)}) %collective-permute-start.37) | collective-permute-done | bytes 983072 | tf_op jit(solution)/shard_map/ppermute | solution.py:27
  189.4 0.3 convert_add_fusion
  189.7 0.8 collective-permute-done.38
  190.5 1.2 add_convert_fusion
  (91 shorter events, 1.1 us)
Async XLA Ops:
  1.3 1.3 copy-start.1
  2.7 60.4 %copy-start = (bf16[5136,128]{1,0:T(8,128)(2,1)}, bf16[5136,128]{1,0:T(8,128)(2,1)S(1)}, u32[]{:S(2)}) copy-start(bf16[5136,128]{1,0:T(8,128)(2,1)S(1)} %shard_map.64.refs_0_) | copy-start | bytes 3944452
  2.8 33.0 %collective-permute-start = (bf16[5136,128]{1,0:T(8,128)(2,1)S(1)}, bf16[5136,128]{1,0:T(8,128)(2,1)S(1)}, u32[]{:S(2)}, u32[]{:S(2)}) collective-permute-start(bf16[5136,128]{1,0:T(8,128)(2,1)S(1)} %shard_map.64.refs_0_), channel_id=1, source_target_pairs={{0,32},{1,33},{2,34},{3,35},{4,36},{5,37},{6,38},{7,39},{8,40},{9,... | collective-permute-start | bytes 3944456 | tf_op jit(solution)/shard_map/ppermute | solution.py:27
  5.0 25.0 %collective-permute-start.2 = (bf16[96,5120]{1,0:T(8,128)(2,1)}, bf16[96,5120]{1,0:T(8,128)(2,1)S(1)}, u32[]{:S(2)}, u32[]{:S(2)}) collective-permute-start(bf16[96,5120]{1,0:T(8,128)(2,1)} %refs_0_.1), channel_id=1, source_target_pairs={{0,8},{1,9},{2,10},{3,11},{4,12},{5,13},{6,14},{7,15},{8,0},{9,1},... | collective-permute-start | bytes 2949128 | tf_op jit(solution)/shard_map/ppermute | solution.py:27
  8.5 22.6 %collective-permute-start.7 = (bf16[96,5120]{1,0:T(8,128)(2,1)}, bf16[96,5120]{1,0:T(8,128)(2,1)}, u32[]{:S(2)}, u32[]{:S(2)}) collective-permute-start(bf16[96,5120]{1,0:T(8,128)(2,1)} %refs_0_.1), channel_id=1, source_target_pairs={{0,6},{1,7},{2,0},{3,1},{4,2},{5,3},{6,4},{7,5},{8,14},{9,15},{10,... | collective-permute-start | bytes 2949128 | tf_op jit(solution)/shard_map/ppermute | solution.py:27
  11.0 23.3 %collective-permute-start.6 = (bf16[96,5120]{1,0:T(8,128)(2,1)}, bf16[96,5120]{1,0:T(8,128)(2,1)}, u32[]{:S(2)}, u32[]{:S(2)}) collective-permute-start(bf16[96,5120]{1,0:T(8,128)(2,1)} %refs_0_.1), channel_id=1, source_target_pairs={{0,2},{1,3},{2,4},{3,5},{4,6},{5,7},{6,0},{7,1},{8,10},{9,11},{10,... | collective-permute-start | bytes 2949128 | tf_op jit(solution)/shard_map/ppermute | solution.py:27
  11.0 28.8 %collective-permute-start.1 = (bf16[5136,128]{1,0:T(8,128)(2,1)S(1)}, bf16[5136,128]{1,0:T(8,128)(2,1)S(1)}, u32[]{:S(2)}, u32[]{:S(2)}) collective-permute-start(bf16[5136,128]{1,0:T(8,128)(2,1)S(1)} %shard_map.64.refs_0_), channel_id=1, source_target_pairs={{0,96},{1,97},{2,98},{3,99},{4,100},{5,101},{6,102},{7,103},{8,104... | collective-permute-start | bytes 3944456 | tf_op jit(solution)/shard_map/ppermute | solution.py:27
  29.9 10.0 %copy-start.15 = (bf16[96,5120]{1,0:T(8,128)(2,1)}, bf16[96,5120]{1,0:T(8,128)(2,1)S(1)}, u32[]{:S(2)}) copy-start(bf16[96,5120]{1,0:T(8,128)(2,1)S(1)} %collective-permute-done.2.refs_4_) | copy-start | bytes 2949124
  29.9 28.8 %collective-permute-start.3 = (bf16[5136,128]{1,0:T(8,128)(2,1)S(1)}, bf16[5136,128]{1,0:T(8,128)(2,1)S(1)}, u32[]{:S(2)}, u32[]{:S(2)}) collective-permute-start(bf16[5136,128]{1,0:T(8,128)(2,1)S(1)} %shard_map.64.refs_0_), channel_id=1, source_target_pairs={{0,16},{1,17},{2,18},{3,19},{4,20},{5,21},{6,22},{7,23},{8,24},{9,... | collective-permute-start | bytes 3944456 | tf_op jit(solution)/shard_map/ppermute | solution.py:27
  34.3 20.8 %collective-permute-start.9 = (bf16[96,5120]{1,0:T(8,128)(2,1)S(1)}, bf16[96,5120]{1,0:T(8,128)(2,1)S(1)}, u32[]{:S(2)}, u32[]{:S(2)}) collective-permute-start(bf16[96,5120]{1,0:T(8,128)(2,1)S(1)} %collective-permute-done.2.refs_4_), channel_id=1, source_target_pairs={{0,6},{1,7},{2,0},{3,1},{4,2},{5,3},{6,4},{7,5},{8,14},{9,15},{10,... | collective-permute-start | bytes 2949128 | tf_op jit(solution)/shard_map/ppermute | solution.py:27
  34.6 22.0 %collective-permute-start.8 = (bf16[96,5120]{1,0:T(8,128)(2,1)S(1)}, bf16[96,5120]{1,0:T(8,128)(2,1)S(1)}, u32[]{:S(2)}, u32[]{:S(2)}) collective-permute-start(bf16[96,5120]{1,0:T(8,128)(2,1)S(1)} %collective-permute-done.2.refs_4_), channel_id=1, source_target_pairs={{0,2},{1,3},{2,4},{3,5},{4,6},{5,7},{6,0},{7,1},{8,10},{9,11},{10,... | collective-permute-start | bytes 2949128 | tf_op jit(solution)/shard_map/ppermute | solution.py:27
  35.8 28.0 %copy-start.9 = (bf16[5136,128]{1,0:T(8,128)(2,1)}, bf16[5136,128]{1,0:T(8,128)(2,1)S(1)}, u32[]{:S(2)}) copy-start(bf16[5136,128]{1,0:T(8,128)(2,1)S(1)} %collective-permute-done.refs_1_) | copy-start | bytes 3944452
  35.9 20.7 %collective-permute-start.4 = (bf16[2576,128]{1,0:T(8,128)(2,1)S(1)}, bf16[2576,128]{1,0:T(8,128)(2,1)S(1)}, u32[]{:S(2)}, u32[]{:S(2)}) collective-permute-start(bf16[2576,128]{1,0:T(8,128)(2,1)S(1)} %pad_maximum_fusion), channel_id=1, source_target_pairs={{0,32},{1,33},{2,34},{3,35},{4,36},{5,37},{6,38},{7,39},{8,40},{9,... | collective-permute-start | bytes 1978376 | tf_op jit(solution)/shard_map/ppermute | solution.py:27
  39.9 23.9 %copy-start.10 = (bf16[5136,128]{1,0:T(8,128)(2,1)}, bf16[5136,128]{1,0:T(8,128)(2,1)S(1)}, u32[]{:S(2)}) copy-start(bf16[5136,128]{1,0:T(8,128)(2,1)S(1)} %collective-permute-done.1.refs_2_) | copy-start | bytes 3944452
  39.9 56.4 %copy-start.4 = (f32[64]{0:T(128)S(1)}, f32[64]{0:T(128)}, u32[]{:S(2)}) copy-start(f32[64]{0:T(128)} %table.5) | copy-start | bytes 772
  39.9 16.6 %collective-permute-start.5 = (bf16[2560,128]{1,0:T(8,128)(2,1)S(1)}, bf16[2560,128]{1,0:T(8,128)(2,1)S(1)}, u32[]{:S(2)}, u32[]{:S(2)}) collective-permute-start(bf16[2560,128]{1,0:T(8,128)(2,1)S(1)} %slice.66), channel_id=1, source_target_pairs={{0,96},{1,97},{2,98},{3,99},{4,100},{5,101},{6,102},{7,103},{8,104... | collective-permute-start | bytes 1966088 | tf_op jit(solution)/shard_map/ppermute | solution.py:27
  55.1 26.3 %copy-start.2 = (bf16[96,5120]{1,0:T(8,128)(2,1)}, bf16[96,5120]{1,0:T(8,128)(2,1)S(1)}, u32[]{:S(2)}) copy-start(bf16[96,5120]{1,0:T(8,128)(2,1)S(1)} %collective-permute-done.9.refs_5_.refs_10_) | copy-start | bytes 2949124
  56.6 33.4 %copy-start.3 = (bf16[96,5120]{1,0:T(8,128)(2,1)}, bf16[96,5120]{1,0:T(8,128)(2,1)S(1)}, u32[]{:S(2)}) copy-start(bf16[96,5120]{1,0:T(8,128)(2,1)S(1)} %collective-permute-done.8.refs_3_.refs_11_) | copy-start | bytes 2949124
  58.5 37.9 %copy-start.5 = (bf16[5136,128]{1,0:T(8,128)(2,1)}, bf16[5136,128]{1,0:T(8,128)(2,1)S(1)}, u32[]{:S(2)}) copy-start(bf16[5136,128]{1,0:T(8,128)(2,1)S(1)} %get-tuple-element.67.refs_4_) | copy-start | bytes 3944452
  58.7 34.4 %copy-start.11 = (bf16[5136,128]{1,0:T(8,128)(2,1)}, bf16[5136,128]{1,0:T(8,128)(2,1)S(1)}, u32[]{:S(2)}) copy-start(bf16[5136,128]{1,0:T(8,128)(2,1)S(1)} %collective-permute-done.3.refs_3_) | copy-start | bytes 3944452
  58.7 29.9 %collective-permute-start.11 = (bf16[5136,128]{1,0:T(8,128)(2,1)S(1)}, bf16[5136,128]{1,0:T(8,128)(2,1)S(1)}, u32[]{:S(2)}, u32[]{:S(2)}) collective-permute-start(bf16[5136,128]{1,0:T(8,128)(2,1)S(1)} %collective-permute-done.3.refs_3_), channel_id=1, source_target_pairs={{0,96},{1,97},{2,98},{3,99},{4,100},{5,101},{6,102},{7,103},{8,104... | collective-permute-start | bytes 3944456 | tf_op jit(solution)/shard_map/ppermute | solution.py:27
  60.6 29.4 %collective-permute-start.10 = (bf16[5136,128]{1,0:T(8,128)(2,1)S(1)}, bf16[5136,128]{1,0:T(8,128)(2,1)S(1)}, u32[]{:S(2)}, u32[]{:S(2)}) collective-permute-start(bf16[5136,128]{1,0:T(8,128)(2,1)S(1)} %collective-permute-done.3.refs_3_), channel_id=1, source_target_pairs={{0,32},{1,33},{2,34},{3,35},{4,36},{5,37},{6,38},{7,39},{8,40},{9,... | collective-permute-start | bytes 3944456 | tf_op jit(solution)/shard_map/ppermute | solution.py:27
  60.6 20.7 %collective-permute-start.14 = (bf16[96,5120]{1,0:T(8,128)(2,1)S(1)}, bf16[96,5120]{1,0:T(8,128)(2,1)}, u32[]{:S(2)}, u32[]{:S(2)}) collective-permute-start(bf16[96,5120]{1,0:T(8,128)(2,1)S(1)} %get-tuple-element.69), channel_id=1, source_target_pairs={{0,6},{1,7},{2,0},{3,1},{4,2},{5,3},{6,4},{7,5},{8,14},{9,15},{10,... | collective-permute-start | bytes 2949128 | tf_op jit(solution)/shard_map/ppermute | solution.py:27
  63.1 22.0 %collective-permute-start.13 = (bf16[96,5120]{1,0:T(8,128)(2,1)S(1)}, bf16[96,5120]{1,0:T(8,128)(2,1)}, u32[]{:S(2)}, u32[]{:S(2)}) collective-permute-start(bf16[96,5120]{1,0:T(8,128)(2,1)S(1)} %get-tuple-element.66), channel_id=1, source_target_pairs={{0,2},{1,3},{2,4},{3,5},{4,6},{5,7},{6,0},{7,1},{8,10},{9,11},{10,... | collective-permute-start | bytes 2949128 | tf_op jit(solution)/shard_map/ppermute | solution.py:27
  63.1 30.0 %collective-permute-start.12 = (bf16[5136,128]{1,0:T(8,128)(2,1)S(1)}, bf16[5136,128]{1,0:T(8,128)(2,1)S(1)}, u32[]{:S(2)}, u32[]{:S(2)}) collective-permute-start(bf16[5136,128]{1,0:T(8,128)(2,1)S(1)} %get-tuple-element.67.refs_4_), channel_id=1, source_target_pairs={{0,16},{1,17},{2,18},{3,19},{4,20},{5,21},{6,22},{7,23},{8,24},{9,... | collective-permute-start | bytes 3944456 | tf_op jit(solution)/shard_map/ppermute | solution.py:27
  81.4 14.9 %collective-permute-start.17 = (bf16[96,5120]{1,0:T(8,128)(2,1)S(1)}, bf16[96,5120]{1,0:T(8,128)(2,1)}, u32[]{:S(2)}, u32[]{:S(2)}) collective-permute-start(bf16[96,5120]{1,0:T(8,128)(2,1)S(1)} %collective-permute-done.9.refs_5_.refs_10_), channel_id=1, source_target_pairs={{0,1},{1,0},{2,3},{3,2},{4,5},{5,4},{6,7},{7,6},{8,9},{9,8},{10,11... | collective-permute-start | bytes 2949128 | tf_op jit(solution)/shard_map/ppermute | solution.py:27
  85.1 9.3 %collective-permute-start.16 = (bf16[96,5120]{1,0:T(8,128)(2,1)}, bf16[96,5120]{1,0:T(8,128)(2,1)}, u32[]{:S(2)}, u32[]{:S(2)}) collective-permute-start(bf16[96,5120]{1,0:T(8,128)(2,1)} %collective-permute-done.14.refs_9_.refs_1_), channel_id=1, source_target_pairs={{0,1},{1,0},{2,3},{3,2},{4,5},{5,4},{6,7},{7,6},{8,9},{9,8},{10,11... | collective-permute-start | bytes 2949128 | tf_op jit(solution)/shard_map/ppermute | solution.py:27
  88.6 4.5 %copy-start.12 = (bf16[5136,128]{1,0:T(8,128)(2,1)}, bf16[5136,128]{1,0:T(8,128)(2,1)S(1)}, u32[]{:S(2)}) copy-start(bf16[5136,128]{1,0:T(8,128)(2,1)S(1)} %collective-permute-done.11.refs_6_) | copy-start | bytes 3944452
  88.6 5.7 %collective-permute-start.15 = (bf16[96,5120]{1,0:T(8,128)(2,1)}, bf16[96,5120]{1,0:T(8,128)(2,1)}, u32[]{:S(2)}, u32[]{:S(2)}) collective-permute-start(bf16[96,5120]{1,0:T(8,128)(2,1)} %collective-permute-done.13.refs_8_.refs_0_), channel_id=1, source_target_pairs={{0,1},{1,0},{2,3},{3,2},{4,5},{5,4},{6,7},{7,6},{8,9},{9,8},{10,11... | collective-permute-start | bytes 2949128 | tf_op jit(solution)/shard_map/ppermute | solution.py:27
  90.0 3.1 %copy-start.13 = (bf16[5136,128]{1,0:T(8,128)(2,1)}, bf16[5136,128]{1,0:T(8,128)(2,1)S(1)}, u32[]{:S(2)}) copy-start(bf16[5136,128]{1,0:T(8,128)(2,1)S(1)} %collective-permute-done.10.refs_5_) | copy-start | bytes 3944452
  90.0 6.3 %collective-permute-start.18 = (bf16[96,5120]{1,0:T(8,128)(2,1)S(1)}, bf16[96,5120]{1,0:T(8,128)(2,1)}, u32[]{:S(2)}, u32[]{:S(2)}) collective-permute-start(bf16[96,5120]{1,0:T(8,128)(2,1)S(1)} %collective-permute-done.8.refs_3_.refs_11_), channel_id=1, source_target_pairs={{0,1},{1,0},{2,3},{3,2},{4,5},{5,4},{6,7},{7,6},{8,9},{9,8},{10,11... | collective-permute-start | bytes 2949128 | tf_op jit(solution)/shard_map/ppermute | solution.py:27
  93.2 1.1 copy-start.14
  94.3 18.3 %collective-permute-start.19 = (bf16[96,5120]{1,0:T(8,128)(2,1)}, bf16[96,5120]{1,0:T(8,128)(2,1)S(1)}, u32[]{:S(2)}, u32[]{:S(2)}) collective-permute-start(bf16[96,5120]{1,0:T(8,128)(2,1)} %collective-permute-done.7.refs_4_.refs_2_), channel_id=1, source_target_pairs={{0,1},{1,0},{2,3},{3,2},{4,5},{5,4},{6,7},{7,6},{8,9},{9,8},{10,11... | collective-permute-start | bytes 2949128 | tf_op jit(solution)/shard_map/ppermute | solution.py:27
  95.7 17.0 %collective-permute-start.20 = (bf16[96,5120]{1,0:T(8,128)(2,1)}, bf16[96,5120]{1,0:T(8,128)(2,1)S(1)}, u32[]{:S(2)}, u32[]{:S(2)}) collective-permute-start(bf16[96,5120]{1,0:T(8,128)(2,1)} %collective-permute-done.6.refs_2_.refs_3_), channel_id=1, source_target_pairs={{0,1},{1,0},{2,3},{3,2},{4,5},{5,4},{6,7},{7,6},{8,9},{9,8},{10,11... | collective-permute-start | bytes 2949128 | tf_op jit(solution)/shard_map/ppermute | solution.py:27
  95.8 16.9 %collective-permute-start.21 = (bf16[96,5120]{1,0:T(8,128)(2,1)}, bf16[96,5120]{1,0:T(8,128)(2,1)S(1)}, u32[]{:S(2)}, u32[]{:S(2)}) collective-permute-start(bf16[96,5120]{1,0:T(8,128)(2,1)} %copy-done.15), channel_id=1, source_target_pairs={{0,1},{1,0},{2,3},{3,2},{4,5},{5,4},{6,7},{7,6},{8,9},{9,8},{10,11... | collective-permute-start | bytes 2949128 | tf_op jit(solution)/shard_map/ppermute | solution.py:27
  96.3 16.5 %collective-permute-start.22 = (bf16[96,5120]{1,0:T(8,128)(2,1)}, bf16[96,5120]{1,0:T(8,128)(2,1)S(1)}, u32[]{:S(2)}, u32[]{:S(2)}) collective-permute-start(bf16[96,5120]{1,0:T(8,128)(2,1)} %refs_0_.1), channel_id=1, source_target_pairs={{0,1},{1,0},{2,3},{3,2},{4,5},{5,4},{6,7},{7,6},{8,9},{9,8},{10,11... | collective-permute-start | bytes 2949128 | tf_op jit(solution)/shard_map/ppermute | solution.py:27
  112.7 7.0 %copy-start.16 = (bf16[96,5120]{1,0:T(8,128)(2,1)}, bf16[96,5120]{1,0:T(8,128)(2,1)S(1)}, u32[]{:S(2)}) copy-start(bf16[96,5120]{1,0:T(8,128)(2,1)S(1)} %collective-permute-done.19.refs_7_) | copy-start | bytes 2949124
  112.7 2.0 %copy-start.17 = (bf16[96,5120]{1,0:T(8,128)(2,1)}, bf16[96,5120]{1,0:T(8,128)(2,1)S(1)}, u32[]{:S(2)}) copy-start(bf16[96,5120]{1,0:T(8,128)(2,1)S(1)} %collective-permute-done.20.refs_8_) | copy-start | bytes 2949124
  112.7 1.0 copy-start.18
  112.8 6.9 %copy-start.8 = (bf16[96,5120]{1,0:T(8,128)(2,1)}, bf16[96,5120]{1,0:T(8,128)(2,1)S(1)}, u32[]{:S(2)}) copy-start(bf16[96,5120]{1,0:T(8,128)(2,1)S(1)} %collective-permute-done.22.refs_1_) | copy-start | bytes 2949124
  113.8 2.8 %collective-permute-start.23 = (bf16[96,5120]{1,0:T(8,128)(2,1)}, bf16[96,5120]{1,0:T(8,128)(2,1)S(1)}, u32[]{:S(2)}, u32[]{:S(2)}) collective-permute-start(bf16[96,5120]{1,0:T(8,128)(2,1)} %get-tuple-element.81), channel_id=1, source_target_pairs={{0,1},{1,0},{2,3},{3,2},{4,5},{5,4},{6,7},{7,6},{8,9},{9,8},{10,11... | collective-permute-start | bytes 2949128 | tf_op jit(solution)/shard_map/ppermute | solution.py:27
  114.2 5.3 %collective-permute-start.24 = (bf16[96,5120]{1,0:T(8,128)(2,1)}, bf16[96,5120]{1,0:T(8,128)(2,1)S(1)}, u32[]{:S(2)}, u32[]{:S(2)}) collective-permute-start(bf16[96,5120]{1,0:T(8,128)(2,1)} %get-tuple-element.83), channel_id=1, source_target_pairs={{0,1},{1,0},{2,3},{3,2},{4,5},{5,4},{6,7},{7,6},{8,9},{9,8},{10,11... | collective-permute-start | bytes 2949128 | tf_op jit(solution)/shard_map/ppermute | solution.py:27
  114.3 6.2 %collective-permute-start.25 = (bf16[96,5120]{1,0:T(8,128)(2,1)}, bf16[96,5120]{1,0:T(8,128)(2,1)S(1)}, u32[]{:S(2)}, u32[]{:S(2)}) collective-permute-start(bf16[96,5120]{1,0:T(8,128)(2,1)} %get-tuple-element.85), channel_id=1, source_target_pairs={{0,1},{1,0},{2,3},{3,2},{4,5},{5,4},{6,7},{7,6},{8,9},{9,8},{10,11... | collective-permute-start | bytes 2949128 | tf_op jit(solution)/shard_map/ppermute | solution.py:27
  116.8 29.2 %collective-permute-start.28 = (bf16[96,5120]{1,0:T(8,128)(2,1)S(1)}, bf16[96,5120]{1,0:T(8,128)(2,1)S(1)}, u32[]{:S(2)}, u32[]{:S(2)}) collective-permute-start(bf16[96,5120]{1,0:T(8,128)(2,1)S(1)} %add_convert_fusion.6), channel_id=1, source_target_pairs={{0,8},{1,9},{2,10},{3,11},{4,12},{5,13},{6,14},{7,15},{8,0},{9,1},... | collective-permute-start | bytes 2949128 | tf_op jit(solution)/shard_map/ppermute | solution.py:27
  119.7 26.3 %collective-permute-start.29 = (bf16[96,5120]{1,0:T(8,128)(2,1)S(1)}, bf16[96,5120]{1,0:T(8,128)(2,1)S(1)}, u32[]{:S(2)}, u32[]{:S(2)}) collective-permute-start(bf16[96,5120]{1,0:T(8,128)(2,1)S(1)} %add_convert_fusion.5), channel_id=1, source_target_pairs={{0,2},{1,3},{2,4},{3,5},{4,6},{5,7},{6,0},{7,1},{8,10},{9,11},{10,... | collective-permute-start | bytes 2949128 | tf_op jit(solution)/shard_map/ppermute | solution.py:27
  120.7 25.3 %collective-permute-start.30 = (bf16[96,5120]{1,0:T(8,128)(2,1)S(1)}, bf16[96,5120]{1,0:T(8,128)(2,1)S(1)}, u32[]{:S(2)}, u32[]{:S(2)}) collective-permute-start(bf16[96,5120]{1,0:T(8,128)(2,1)S(1)} %add_convert_fusion.4), channel_id=1, source_target_pairs={{0,6},{1,7},{2,0},{3,1},{4,2},{5,3},{6,4},{7,5},{8,14},{9,15},{10,... | collective-permute-start | bytes 2949128 | tf_op jit(solution)/shard_map/ppermute | solution.py:27
  142.5 2.8 %collective-permute-start.26 = (bf16[48,5120]{1,0:T(8,128)(2,1)S(1)}, bf16[48,5120]{1,0:T(8,128)(2,1)S(1)}, u32[]{:S(2)}, u32[]{:S(2)}) collective-permute-start(bf16[48,5120]{1,0:T(8,128)(2,1)S(1)} %get-tuple-element.95), channel_id=1, source_target_pairs={{0,1},{1,0},{2,3},{3,2},{4,5},{5,4},{6,7},{7,6},{8,9},{9,8},{10,11... | collective-permute-start | bytes 1474568 | tf_op jit(solution)/shard_map/ppermute | solution.py:27
  143.8 2.2 %collective-permute-start.27 = (bf16[48,5120]{1,0:T(8,128)(2,1)S(1)}, bf16[48,5120]{1,0:T(8,128)(2,1)S(1)}, u32[]{:S(2)}, u32[]{:S(2)}) collective-permute-start(bf16[48,5120]{1,0:T(8,128)(2,1)S(1)} %get-tuple-element.96), channel_id=1, source_target_pairs={{0,1},{1,0},{2,3},{3,2},{4,5},{5,4},{6,7},{7,6},{8,9},{9,8},{10,11... | collective-permute-start | bytes 1474568 | tf_op jit(solution)/shard_map/ppermute | solution.py:27
  146.0 1.2 copy-start.21
  146.0 3.3 %copy-start.20 = (bf16[96,5120]{1,0:T(8,128)(2,1)S(1)}, bf16[96,5120]{1,0:T(8,128)(2,1)}, u32[]{:S(2)}) copy-start(bf16[96,5120]{1,0:T(8,128)(2,1)} %get-tuple-element.102) | copy-start | bytes 2949124
  146.0 3.7 %copy-start.19 = (bf16[96,5120]{1,0:T(8,128)(2,1)S(1)}, bf16[96,5120]{1,0:T(8,128)(2,1)}, u32[]{:S(2)}) copy-start(bf16[96,5120]{1,0:T(8,128)(2,1)} %get-tuple-element.104) | copy-start | bytes 2949124
  146.0 3.8 %copy-start.6 = (bf16[96,5120]{1,0:T(8,128)(2,1)S(1)}, bf16[96,5120]{1,0:T(8,128)(2,1)}, u32[]{:S(2)}) copy-start(bf16[96,5120]{1,0:T(8,128)(2,1)} %get-tuple-element.105) | copy-start | bytes 2949124
  147.2 2.7 %collective-permute-start.33 = (bf16[96,5120]{1,0:T(8,128)(2,1)S(1)}, bf16[96,5120]{1,0:T(8,128)(2,1)S(1)}, u32[]{:S(2)}, u32[]{:S(2)}) collective-permute-start(bf16[96,5120]{1,0:T(8,128)(2,1)S(1)} %copy-done.21), channel_id=1, source_target_pairs={{0,1},{1,0},{2,3},{3,2},{4,5},{5,4},{6,7},{7,6},{8,9},{9,8},{10,11... | collective-permute-start | bytes 2949128 | tf_op jit(solution)/shard_map/ppermute | solution.py:27
  147.6 12.7 %collective-permute-start.35 = (bf16[48,5120]{1,0:T(8,128)(2,1)S(1)}, bf16[48,5120]{1,0:T(8,128)(2,1)S(1)}, u32[]{:S(2)}, u32[]{:S(2)}) collective-permute-start(bf16[48,5120]{1,0:T(8,128)(2,1)S(1)} %get-tuple-element.121), channel_id=1, source_target_pairs={{0,6},{1,7},{2,0},{3,1},{4,2},{5,3},{6,4},{7,5},{8,14},{9,15},{10,... | collective-permute-start | bytes 1474568 | tf_op jit(solution)/shard_map/ppermute | solution.py:27
  149.3 13.7 %collective-permute-start.34 = (bf16[48,5120]{1,0:T(8,128)(2,1)S(1)}, bf16[48,5120]{1,0:T(8,128)(2,1)S(1)}, u32[]{:S(2)}, u32[]{:S(2)}) collective-permute-start(bf16[48,5120]{1,0:T(8,128)(2,1)S(1)} %get-tuple-element.122), channel_id=1, source_target_pairs={{0,2},{1,3},{2,4},{3,5},{4,6},{5,7},{6,0},{7,1},{8,10},{9,11},{10,... | collective-permute-start | bytes 1474568 | tf_op jit(solution)/shard_map/ppermute | solution.py:27
  149.4 2.6 %collective-permute-start.31 = (bf16[96,5120]{1,0:T(8,128)(2,1)S(1)}, bf16[96,5120]{1,0:T(8,128)(2,1)S(1)}, u32[]{:S(2)}, u32[]{:S(2)}) collective-permute-start(bf16[96,5120]{1,0:T(8,128)(2,1)S(1)} %copy-done.20), channel_id=1, source_target_pairs={{0,1},{1,0},{2,3},{3,2},{4,5},{5,4},{6,7},{7,6},{8,9},{9,8},{10,11... | collective-permute-start | bytes 2949128 | tf_op jit(solution)/shard_map/ppermute | solution.py:27
  149.8 3.6 %collective-permute-start.32 = (bf16[96,5120]{1,0:T(8,128)(2,1)S(1)}, bf16[96,5120]{1,0:T(8,128)(2,1)S(1)}, u32[]{:S(2)}, u32[]{:S(2)}) collective-permute-start(bf16[96,5120]{1,0:T(8,128)(2,1)S(1)} %copy-done.19), channel_id=1, source_target_pairs={{0,1},{1,0},{2,3},{3,2},{4,5},{5,4},{6,7},{7,6},{8,9},{9,8},{10,11... | collective-permute-start | bytes 2949128 | tf_op jit(solution)/shard_map/ppermute | solution.py:27
  152.0 1.4 copy-start.7
  163.4 4.7 %collective-permute-start.36 = (bf16[96,5120]{1,0:T(8,128)(2,1)S(1)}, bf16[96,5120]{1,0:T(8,128)(2,1)S(1)}, u32[]{:S(2)}, u32[]{:S(2)}) collective-permute-start(bf16[96,5120]{1,0:T(8,128)(2,1)S(1)} %get-tuple-element.120), channel_id=1, source_target_pairs={{0,1},{1,0},{2,3},{3,2},{4,5},{5,4},{6,7},{7,6},{8,9},{9,8},{10,11... | collective-permute-start | bytes 2949128 | tf_op jit(solution)/shard_map/ppermute | solution.py:27
  164.6 24.8 %collective-permute-start.37 = (bf16[96,5120]{1,0:T(8,128)(2,1)S(1)}, bf16[96,5120]{1,0:T(8,128)(2,1)S(1)}, u32[]{:S(2)}, u32[]{:S(2)}) collective-permute-start(bf16[96,5120]{1,0:T(8,128)(2,1)S(1)} %add_convert_fusion.3), channel_id=1, source_target_pairs={{0,8},{1,9},{2,10},{3,11},{4,12},{5,13},{6,14},{7,15},{8,0},{9,1},... | collective-permute-start | bytes 2949128 | tf_op jit(solution)/shard_map/ppermute | solution.py:27
  166.6 23.1 %collective-permute-start.39 = (bf16[96,5120]{1,0:T(8,128)(2,1)S(1)}, bf16[96,5120]{1,0:T(8,128)(2,1)S(1)}, u32[]{:S(2)}, u32[]{:S(2)}) collective-permute-start(bf16[96,5120]{1,0:T(8,128)(2,1)S(1)} %add_convert_fusion.1), channel_id=1, source_target_pairs={{0,6},{1,7},{2,0},{3,1},{4,2},{5,3},{6,4},{7,5},{8,14},{9,15},{10,... | collective-permute-start | bytes 2949128 | tf_op jit(solution)/shard_map/ppermute | solution.py:27
  166.6 23.9 %collective-permute-start.38 = (bf16[96,5120]{1,0:T(8,128)(2,1)S(1)}, bf16[96,5120]{1,0:T(8,128)(2,1)S(1)}, u32[]{:S(2)}, u32[]{:S(2)}) collective-permute-start(bf16[96,5120]{1,0:T(8,128)(2,1)S(1)} %add_convert_fusion.2), channel_id=1, source_target_pairs={{0,2},{1,3},{2,4},{3,5},{4,6},{5,7},{6,0},{7,1},{8,10},{9,11},{10,... | collective-permute-start | bytes 2949128 | tf_op jit(solution)/shard_map/ppermute | solution.py:27

commit v11 on v10

--- a/solution.py
+++ b/solution.py
@@ -223,7 +223,7 @@
             pltpu.VMEM((2, rows, STEP), BF16),
             pltpu.SemaphoreType.DMA((n_copies,)),
         ],
-        compiler_params=pltpu.CompilerParams(vmem_limit_bytes=36 * 2**20),
+        compiler_params=pltpu.CompilerParams(vmem_limit_bytes=32 * 2**20),
         cost_estimate=pl.CostEstimate(
             flops=2 * rows * depth * local_ff * 3,
             bytes_accessed=2 * (depth * slots * width + local_ff * depth + 2 * rows * depth),

time: 192 us -> 192 us (level)
    unnamed x44 -> x38, local copies, waits for them, and re-layouts: 4.21 us -> 5.38 us
where the time goes in v11:
time: 192 us; the launch traced here: 191 us
  waiting for transfers between devices  86.7 us (45%)
  starting transfers between devices  49.6 us (26%)
  Pallas kernels  43.5 us (23%)
  local copies, waits for them, and re-layouts  5.59 us (3%)
  other arithmetic  4.03 us (2%)
    ppermute x40, waiting for transfers between devices, move(): return lax.ppermute(value, AXES, pairs)  86.7 us
    ppermute x40, starting transfers between devices, move(): return lax.ppermute(value, AXES, pairs)  49.6 us
    pallas_call x2, Pallas kernels, sums(): return tuple(run(ids, sidx, scale_table, *pieces, *weights))  25.9 us
    pallas_call x1, Pallas kernels, sums(): return tuple(run(ids, sidx, scale_table, *sources, *pieces, down_weight))  15.6 us
    unnamed x38, local copies, waits for them, and re-layouts  5.38 us
  transfers between devices with their start and end apart: 40, of which 16 were waited for; matrix products, arithmetic and copies ran while one was open for 1% of the time, Pallas kernels for 23%

profile of v11, /device:TPU:1, one launch (start us, length us, event | category | flops | bytes accessed | tf_op | source)
XLA Modules:
  0.0 191.1 jit_solution(11016938292867364990)
XLA Ops:
  1.3 1.3 copy-done.1
  2.8 2.2 %collective-permute-start = (bf16[5136,128]{1,0:T(8,128)(2,1)S(1)}, bf16[5136,128]{1,0:T(8,128)(2,1)S(1)}, u32[]{:S(2)}, u32[]{:S(2)}) collective-permute-start(bf16[5136,128]{1,0:T(8,128)(2,1)S(1)} %shard_map.64.refs_0_), channel_id=1, source_target_pairs={{0,32},{1,33},{2,34},{3,35},{4,36},{5,37},{6,38},{7,39},{8,40},{9,... | collective-permute-start | bytes 3944456 | tf_op jit(solution)/shard_map/ppermute | solution.py:27
  5.0 3.6 %collective-permute-start.2 = (bf16[96,5120]{1,0:T(8,128)(2,1)}, bf16[96,5120]{1,0:T(8,128)(2,1)S(1)}, u32[]{:S(2)}, u32[]{:S(2)}) collective-permute-start(bf16[96,5120]{1,0:T(8,128)(2,1)} %refs_0_.1), channel_id=1, source_target_pairs={{0,8},{1,9},{2,10},{3,11},{4,12},{5,13},{6,14},{7,15},{8,0},{9,1},... | collective-permute-start | bytes 2949128 | tf_op jit(solution)/shard_map/ppermute | solution.py:27
  8.5 2.5 %collective-permute-start.7 = (bf16[96,5120]{1,0:T(8,128)(2,1)}, bf16[96,5120]{1,0:T(8,128)(2,1)}, u32[]{:S(2)}, u32[]{:S(2)}) collective-permute-start(bf16[96,5120]{1,0:T(8,128)(2,1)} %refs_0_.1), channel_id=1, source_target_pairs={{0,6},{1,7},{2,0},{3,1},{4,2},{5,3},{6,4},{7,5},{8,14},{9,15},{10,... | collective-permute-start | bytes 2949128 | tf_op jit(solution)/shard_map/ppermute | solution.py:27
  11.0 1.5 collective-permute-start.1
  12.6 17.4 %collective-permute-done.2.refs_4_ = bf16[96,5120]{1,0:T(8,128)(2,1)S(1)} collective-permute-done((bf16[96,5120]{1,0:T(8,128)(2,1)}, bf16[96,5120]{1,0:T(8,128)(2,1)S(1)}, u32[]{:S(2)}, u32[]{:S(2)}) %collective-permute-start.2) | collective-permute-done | bytes 983072 | tf_op jit(solution)/shard_map/ppermute | solution.py:27
  29.9 0.8 collective-permute-start.3
  30.7 0.4 collective-permute-done.7.refs_4_.refs_2_
  31.2 3.1 %collective-permute-done.6.refs_2_.refs_3_ = bf16[96,5120]{1,0:T(8,128)(2,1)} collective-permute-done((bf16[96,5120]{1,0:T(8,128)(2,1)}, bf16[96,5120]{1,0:T(8,128)(2,1)}, u32[]{:S(2)}, u32[]{:S(2)}) %collective-permute-start.6) | collective-permute-done | bytes 983072 | tf_op jit(solution)/shard_map/ppermute | solution.py:27
  34.3 0.3 collective-permute-start.9
  34.6 1.2 collective-permute-start.8
  35.9 1.4 collective-permute-start.4
  37.2 2.6 %collective-permute-done.1.refs_2_ = bf16[5136,128]{1,0:T(8,128)(2,1)S(1)} collective-permute-done((bf16[5136,128]{1,0:T(8,128)(2,1)S(1)}, bf16[5136,128]{1,0:T(8,128)(2,1)S(1)}, u32[]{:S(2)}, u32[]{:S(2)}) %collective-permute-start.1) | collective-permute-done | bytes 1314848 | tf_op jit(solution)/shard_map/ppermute | solution.py:27
  39.9 3.0 %collective-permute-start.5 = (bf16[2560,128]{1,0:T(8,128)(2,1)S(1)}, bf16[2560,128]{1,0:T(8,128)(2,1)S(1)}, u32[]{:S(2)}, u32[]{:S(2)}) collective-permute-start(bf16[2560,128]{1,0:T(8,128)(2,1)S(1)} %slice.66), channel_id=1, source_target_pairs={{0,96},{1,97},{2,98},{3,99},{4,100},{5,101},{6,102},{7,103},{8,104... | collective-permute-start | bytes 1966088 | tf_op jit(solution)/shard_map/ppermute | solution.py:27
  42.9 12.2 %collective-permute-done.9.refs_5_.refs_10_ = bf16[96,5120]{1,0:T(8,128)(2,1)S(1)} collective-permute-done((bf16[96,5120]{1,0:T(8,128)(2,1)S(1)}, bf16[96,5120]{1,0:T(8,128)(2,1)S(1)}, u32[]{:S(2)}, u32[]{:S(2)}) %collective-permute-start.9) | collective-permute-done | bytes 983072 | tf_op jit(solution)/shard_map/ppermute | solution.py:27
  55.1 1.5 collective-permute-done.8.refs_3_.refs_11_
  56.6 1.9 shard_map.65
  58.5 0.3 collective-permute-done.3.refs_3_
  58.7 1.9 collective-permute-start.11
  60.6 2.5 %collective-permute-start.14 = (bf16[96,5120]{1,0:T(8,128)(2,1)S(1)}, bf16[96,5120]{1,0:T(8,128)(2,1)}, u32[]{:S(2)}, u32[]{:S(2)}) collective-permute-start(bf16[96,5120]{1,0:T(8,128)(2,1)S(1)} %get-tuple-element.69), channel_id=1, source_target_pairs={{0,6},{1,7},{2,0},{3,1},{4,2},{5,3},{6,4},{7,5},{8,14},{9,15},{10,... | collective-permute-start | bytes 2949128 | tf_op jit(solution)/shard_map/ppermute | solution.py:27
  63.1 0.6 collective-permute-start.12
  63.8 17.6 %collective-permute-done.14.refs_9_.refs_1_ = bf16[96,5120]{1,0:T(8,128)(2,1)} collective-permute-done((bf16[96,5120]{1,0:T(8,128)(2,1)S(1)}, bf16[96,5120]{1,0:T(8,128)(2,1)}, u32[]{:S(2)}, u32[]{:S(2)}) %collective-permute-start.14) | collective-permute-done | bytes 983072 | tf_op jit(solution)/shard_map/ppermute | solution.py:27
  81.4 3.7 %collective-permute-start.17 = (bf16[96,5120]{1,0:T(8,128)(2,1)S(1)}, bf16[96,5120]{1,0:T(8,128)(2,1)}, u32[]{:S(2)}, u32[]{:S(2)}) collective-permute-start(bf16[96,5120]{1,0:T(8,128)(2,1)S(1)} %collective-permute-done.9.refs_5_.refs_10_), channel_id=1, source_target_pairs={{0,1},{1,0},{2,3},{3,2},{4,5},{5,4},{6,7},{7,6},{8,9},{9,8},{10,11... | collective-permute-start | bytes 2949128 | tf_op jit(solution)/shard_map/ppermute | solution.py:27
  85.1 3.4 %collective-permute-start.16 = (bf16[96,5120]{1,0:T(8,128)(2,1)}, bf16[96,5120]{1,0:T(8,128)(2,1)}, u32[]{:S(2)}, u32[]{:S(2)}) collective-permute-start(bf16[96,5120]{1,0:T(8,128)(2,1)} %collective-permute-done.14.refs_9_.refs_1_), channel_id=1, source_target_pairs={{0,1},{1,0},{2,3},{3,2},{4,5},{5,4},{6,7},{7,6},{8,9},{9,8},{10,11... | collective-permute-start | bytes 2949128 | tf_op jit(solution)/shard_map/ppermute | solution.py:27
  88.5 1.5 collective-permute-start.15
  90.0 0.9 copy-done.6
  91.0 2.1 %collective-permute-start.18 = (bf16[96,5120]{1,0:T(8,128)(2,1)S(1)}, bf16[96,5120]{1,0:T(8,128)(2,1)}, u32[]{:S(2)}, u32[]{:S(2)}) collective-permute-start(bf16[96,5120]{1,0:T(8,128)(2,1)S(1)} %collective-permute-done.8.refs_3_.refs_11_), channel_id=1, source_target_pairs={{0,1},{1,0},{2,3},{3,2},{4,5},{5,4},{6,7},{7,6},{8,9},{9,8},{10,11... | collective-permute-start | bytes 2949128 | tf_op jit(solution)/shard_map/ppermute | solution.py:27
  93.2 1.1 copy-done.13
  94.4 1.4 collective-permute-start.19
  95.8 0.4 collective-permute-start.21
  96.4 1.2 copy-done.7
  97.6 15.6 %shard_map.66 = (bf16[96,5120]{1,0:T(8,128)(2,1)S(1)}, bf16[96,5120]{1,0:T(8,128)(2,1)S(1)}, bf16[96,5120]{1,0:T(8,128)(2,1)S(1)}, bf16[96,5120]{1,0:T(8,128)(2,...) custom-call(s32[8]{0:T(128)S(1)} %get-tuple-element.109.ids, ...), custom_call_target="tpu_custom_call" | custom-call | flops 9059696640 | bytes 27525120 | tf_op jit(solution)/shard_map/pallas_call | solution.py:280
  113.3 0.5 collective-permute-start.23
  113.9 0.4 collective-permute-start.25
  114.3 1.7 collective-permute-done.23
  116.0 0.3 add_convert_fusion.6
  116.2 2.6 %collective-permute-start.28 = (bf16[96,5120]{1,0:T(8,128)(2,1)S(1)}, bf16[96,5120]{1,0:T(8,128)(2,1)S(1)}, u32[]{:S(2)}, u32[]{:S(2)}) collective-permute-start(bf16[96,5120]{1,0:T(8,128)(2,1)S(1)} %add_convert_fusion.6), channel_id=1, source_target_pairs={{0,8},{1,9},{2,10},{3,11},{4,12},{5,13},{6,14},{7,15},{8,0},{9,1},... | collective-permute-start | bytes 2949128 | tf_op jit(solution)/shard_map/ppermute | solution.py:27
  118.8 0.3 add_convert_fusion.5
  119.1 0.8 collective-permute-start.29
  119.9 0.2 add_convert_fusion.4
  120.2 2.0 %collective-permute-start.30 = (bf16[96,5120]{1,0:T(8,128)(2,1)S(1)}, bf16[96,5120]{1,0:T(8,128)(2,1)S(1)}, u32[]{:S(2)}, u32[]{:S(2)}) collective-permute-start(bf16[96,5120]{1,0:T(8,128)(2,1)S(1)} %add_convert_fusion.4), channel_id=1, source_target_pairs={{0,6},{1,7},{2,0},{3,1},{4,2},{5,3},{6,4},{7,5},{8,14},{9,15},{10,... | collective-permute-start | bytes 2949128 | tf_op jit(solution)/shard_map/ppermute | solution.py:27
  122.2 19.5 %shard_map.67 = (bf16[48,5120]{1,0:T(8,128)(2,1)S(1)}, bf16[48,5120]{1,0:T(8,128)(2,1)S(1)}, bf16[96,5120]{1,0:T(8,128)(2,1)S(1)}, bf16[96,5120]{1,0:T(8,128)(2,...) custom-call(s32[8]{0:T(128)S(1)} %get-tuple-element.109.ids, ...), custom_call_target="tpu_custom_call", output_to_operand_aliasing={{10}: (13, {}), {11}: (14, {})} | custom-call | flops 12079595520 | bytes 31457280 | tf_op jit(solution)/shard_map/pallas_call | solution.py:281
  141.7 1.3 collective-permute-start.26
  143.1 1.4 collective-permute-done.26
  144.5 0.7 collective-permute-done.27
  145.2 0.4 add_convert_fusion.7
  145.6 0.8 copy-done.18
  146.4 0.4 collective-permute-start.33
  146.8 2.0 %collective-permute-start.35 = (bf16[48,5120]{1,0:T(8,128)(2,1)S(1)}, bf16[48,5120]{1,0:T(8,128)(2,1)S(1)}, u32[]{:S(2)}, u32[]{:S(2)}) collective-permute-start(bf16[48,5120]{1,0:T(8,128)(2,1)S(1)} %get-tuple-element.121), channel_id=1, source_target_pairs={{0,6},{1,7},{2,0},{3,1},{4,2},{5,3},{6,4},{7,5},{8,14},{9,15},{10,... | collective-permute-start | bytes 1474568 | tf_op jit(solution)/shard_map/ppermute | solution.py:27
  148.8 0.3 collective-permute-start.31
  149.0 0.2 collective-permute-start.32
  149.3 0.6 add_convert_fusion.3
  149.9 1.5 collective-permute-done.31
  151.6 1.2 collective-permute-done.32
  152.7 0.2 convert_add_fusion.1
  153.0 6.4 %shard_map.68 = (bf16[96,5120]{1,0:T(8,128)(2,1)S(1)}, bf16[96,5120]{1,0:T(8,128)(2,1)S(1)}, bf16[4,5120,256]{2,1,0:T(8,128)(2,1)S(1)}, bf16[512,5120]{1,0:T(8,128)(2,1)S(1)}) custom-call(s32[8]{0:T(128)S(1)} %get-tuple-element.109.ids, s32[8]{0:T(128)S(1)} %get-tuple-element.123.sidx, ...), custom_call_target="tpu_custom_call", output_to_operand_aliasing={{2}: (5, {}), {3}: (6, {})} | custom-call | flops 3019898880 | bytes 19660800 | tf_op jit(solution)/shard_map/pallas_call | solution.py:281
  159.4 3.1 %collective-permute-done.34 = bf16[48,5120]{1,0:T(8,128)(2,1)S(1)} collective-permute-done((bf16[48,5120]{1,0:T(8,128)(2,1)S(1)}, bf16[48,5120]{1,0:T(8,128)(2,1)S(1)}, u32[]{:S(2)}, u32[]{:S(2)}) %collective-permute-start.34) | collective-permute-done | bytes 491552 | tf_op jit(solution)/shard_map/ppermute | solution.py:27
  162.8 1.2 collective-permute-start.36
  164.0 2.1 %collective-permute-start.37 = (bf16[96,5120]{1,0:T(8,128)(2,1)S(1)}, bf16[96,5120]{1,0:T(8,128)(2,1)S(1)}, u32[]{:S(2)}, u32[]{:S(2)}) collective-permute-start(bf16[96,5120]{1,0:T(8,128)(2,1)S(1)} %add_convert_fusion.3), channel_id=1, source_target_pairs={{0,8},{1,9},{2,10},{3,11},{4,12},{5,13},{6,14},{7,15},{8,0},{9,1},... | collective-permute-start | bytes 2949128 | tf_op jit(solution)/shard_map/ppermute | solution.py:27
  166.0 1.5 collective-permute-start.38
  167.5 21.3 %collective-permute-done.37 = bf16[96,5120]{1,0:T(8,128)(2,1)S(1)} collective-permute-done((bf16[96,5120]{1,0:T(8,128)(2,1)S(1)}, bf16[96,5120]{1,0:T(8,128)(2,1)S(1)}, u32[]{:S(2)}, u32[]{:S(2)}) %collective-permute-start.37) | collective-permute-done | bytes 983072 | tf_op jit(solution)/shard_map/ppermute | solution.py:27
  188.8 0.3 convert_add_fusion
  189.1 0.8 collective-permute-done.38
  189.9 1.2 add_convert_fusion
  (85 shorter events, 1.4 us)
Async XLA Ops:
  1.3 1.3 copy-start.1
  2.7 60.4 %copy-start = (bf16[5136,128]{1,0:T(8,128)(2,1)}, bf16[5136,128]{1,0:T(8,128)(2,1)S(1)}, u32[]{:S(2)}) copy-start(bf16[5136,128]{1,0:T(8,128)(2,1)S(1)} %shard_map.64.refs_0_) | copy-start | bytes 3944452
  2.8 33.0 %collective-permute-start = (bf16[5136,128]{1,0:T(8,128)(2,1)S(1)}, bf16[5136,128]{1,0:T(8,128)(2,1)S(1)}, u32[]{:S(2)}, u32[]{:S(2)}) collective-permute-start(bf16[5136,128]{1,0:T(8,128)(2,1)S(1)} %shard_map.64.refs_0_), channel_id=1, source_target_pairs={{0,32},{1,33},{2,34},{3,35},{4,36},{5,37},{6,38},{7,39},{8,40},{9,... | collective-permute-start | bytes 3944456 | tf_op jit(solution)/shard_map/ppermute | solution.py:27
  5.0 25.0 %collective-permute-start.2 = (bf16[96,5120]{1,0:T(8,128)(2,1)}, bf16[96,5120]{1,0:T(8,128)(2,1)S(1)}, u32[]{:S(2)}, u32[]{:S(2)}) collective-permute-start(bf16[96,5120]{1,0:T(8,128)(2,1)} %refs_0_.1), channel_id=1, source_target_pairs={{0,8},{1,9},{2,10},{3,11},{4,12},{5,13},{6,14},{7,15},{8,0},{9,1},... | collective-permute-start | bytes 2949128 | tf_op jit(solution)/shard_map/ppermute | solution.py:27
  8.5 22.6 %collective-permute-start.7 = (bf16[96,5120]{1,0:T(8,128)(2,1)}, bf16[96,5120]{1,0:T(8,128)(2,1)}, u32[]{:S(2)}, u32[]{:S(2)}) collective-permute-start(bf16[96,5120]{1,0:T(8,128)(2,1)} %refs_0_.1), channel_id=1, source_target_pairs={{0,6},{1,7},{2,0},{3,1},{4,2},{5,3},{6,4},{7,5},{8,14},{9,15},{10,... | collective-permute-start | bytes 2949128 | tf_op jit(solution)/shard_map/ppermute | solution.py:27
  11.0 23.3 %collective-permute-start.6 = (bf16[96,5120]{1,0:T(8,128)(2,1)}, bf16[96,5120]{1,0:T(8,128)(2,1)}, u32[]{:S(2)}, u32[]{:S(2)}) collective-permute-start(bf16[96,5120]{1,0:T(8,128)(2,1)} %refs_0_.1), channel_id=1, source_target_pairs={{0,2},{1,3},{2,4},{3,5},{4,6},{5,7},{6,0},{7,1},{8,10},{9,11},{10,... | collective-permute-start | bytes 2949128 | tf_op jit(solution)/shard_map/ppermute | solution.py:27
  11.0 28.8 %collective-permute-start.1 = (bf16[5136,128]{1,0:T(8,128)(2,1)S(1)}, bf16[5136,128]{1,0:T(8,128)(2,1)S(1)}, u32[]{:S(2)}, u32[]{:S(2)}) collective-permute-start(bf16[5136,128]{1,0:T(8,128)(2,1)S(1)} %shard_map.64.refs_0_), channel_id=1, source_target_pairs={{0,96},{1,97},{2,98},{3,99},{4,100},{5,101},{6,102},{7,103},{8,104... | collective-permute-start | bytes 3944456 | tf_op jit(solution)/shard_map/ppermute | solution.py:27
  29.9 10.0 %copy-start.14 = (bf16[96,5120]{1,0:T(8,128)(2,1)}, bf16[96,5120]{1,0:T(8,128)(2,1)S(1)}, u32[]{:S(2)}) copy-start(bf16[96,5120]{1,0:T(8,128)(2,1)S(1)} %collective-permute-done.2.refs_4_) | copy-start | bytes 2949124
  29.9 28.8 %collective-permute-start.3 = (bf16[5136,128]{1,0:T(8,128)(2,1)S(1)}, bf16[5136,128]{1,0:T(8,128)(2,1)S(1)}, u32[]{:S(2)}, u32[]{:S(2)}) collective-permute-start(bf16[5136,128]{1,0:T(8,128)(2,1)S(1)} %shard_map.64.refs_0_), channel_id=1, source_target_pairs={{0,16},{1,17},{2,18},{3,19},{4,20},{5,21},{6,22},{7,23},{8,24},{9,... | collective-permute-start | bytes 3944456 | tf_op jit(solution)/shard_map/ppermute | solution.py:27
  34.3 20.8 %collective-permute-start.9 = (bf16[96,5120]{1,0:T(8,128)(2,1)S(1)}, bf16[96,5120]{1,0:T(8,128)(2,1)S(1)}, u32[]{:S(2)}, u32[]{:S(2)}) collective-permute-start(bf16[96,5120]{1,0:T(8,128)(2,1)S(1)} %collective-permute-done.2.refs_4_), channel_id=1, source_target_pairs={{0,6},{1,7},{2,0},{3,1},{4,2},{5,3},{6,4},{7,5},{8,14},{9,15},{10,... | collective-permute-start | bytes 2949128 | tf_op jit(solution)/shard_map/ppermute | solution.py:27
  34.6 22.0 %collective-permute-start.8 = (bf16[96,5120]{1,0:T(8,128)(2,1)S(1)}, bf16[96,5120]{1,0:T(8,128)(2,1)S(1)}, u32[]{:S(2)}, u32[]{:S(2)}) collective-permute-start(bf16[96,5120]{1,0:T(8,128)(2,1)S(1)} %collective-permute-done.2.refs_4_), channel_id=1, source_target_pairs={{0,2},{1,3},{2,4},{3,5},{4,6},{5,7},{6,0},{7,1},{8,10},{9,11},{10,... | collective-permute-start | bytes 2949128 | tf_op jit(solution)/shard_map/ppermute | solution.py:27
  35.8 28.0 %copy-start.8 = (bf16[5136,128]{1,0:T(8,128)(2,1)}, bf16[5136,128]{1,0:T(8,128)(2,1)S(1)}, u32[]{:S(2)}) copy-start(bf16[5136,128]{1,0:T(8,128)(2,1)S(1)} %collective-permute-done.refs_1_) | copy-start | bytes 3944452
  35.9 20.7 %collective-permute-start.4 = (bf16[2576,128]{1,0:T(8,128)(2,1)S(1)}, bf16[2576,128]{1,0:T(8,128)(2,1)S(1)}, u32[]{:S(2)}, u32[]{:S(2)}) collective-permute-start(bf16[2576,128]{1,0:T(8,128)(2,1)S(1)} %pad_maximum_fusion), channel_id=1, source_target_pairs={{0,32},{1,33},{2,34},{3,35},{4,36},{5,37},{6,38},{7,39},{8,40},{9,... | collective-permute-start | bytes 1978376 | tf_op jit(solution)/shard_map/ppermute | solution.py:27
  39.9 23.9 %copy-start.9 = (bf16[5136,128]{1,0:T(8,128)(2,1)}, bf16[5136,128]{1,0:T(8,128)(2,1)S(1)}, u32[]{:S(2)}) copy-start(bf16[5136,128]{1,0:T(8,128)(2,1)S(1)} %collective-permute-done.1.refs_2_) | copy-start | bytes 3944452
  39.9 56.4 %copy-start.4 = (f32[64]{0:T(128)S(1)}, f32[64]{0:T(128)}, u32[]{:S(2)}) copy-start(f32[64]{0:T(128)} %table.5) | copy-start | bytes 772
  39.9 16.6 %collective-permute-start.5 = (bf16[2560,128]{1,0:T(8,128)(2,1)S(1)}, bf16[2560,128]{1,0:T(8,128)(2,1)S(1)}, u32[]{:S(2)}, u32[]{:S(2)}) collective-permute-start(bf16[2560,128]{1,0:T(8,128)(2,1)S(1)} %slice.66), channel_id=1, source_target_pairs={{0,96},{1,97},{2,98},{3,99},{4,100},{5,101},{6,102},{7,103},{8,104... | collective-permute-start | bytes 1966088 | tf_op jit(solution)/shard_map/ppermute | solution.py:27
  55.1 26.3 %copy-start.2 = (bf16[96,5120]{1,0:T(8,128)(2,1)}, bf16[96,5120]{1,0:T(8,128)(2,1)S(1)}, u32[]{:S(2)}) copy-start(bf16[96,5120]{1,0:T(8,128)(2,1)S(1)} %collective-permute-done.9.refs_5_.refs_10_) | copy-start | bytes 2949124
  56.6 34.4 %copy-start.3 = (bf16[96,5120]{1,0:T(8,128)(2,1)}, bf16[96,5120]{1,0:T(8,128)(2,1)S(1)}, u32[]{:S(2)}) copy-start(bf16[96,5120]{1,0:T(8,128)(2,1)S(1)} %collective-permute-done.8.refs_3_.refs_11_) | copy-start | bytes 2949124
  58.5 34.7 %copy-start.5 = (bf16[5136,128]{1,0:T(8,128)(2,1)}, bf16[5136,128]{1,0:T(8,128)(2,1)S(1)}, u32[]{:S(2)}) copy-start(bf16[5136,128]{1,0:T(8,128)(2,1)S(1)} %get-tuple-element.67.refs_4_) | copy-start | bytes 3944452
  58.7 34.4 %copy-start.10 = (bf16[5136,128]{1,0:T(8,128)(2,1)}, bf16[5136,128]{1,0:T(8,128)(2,1)S(1)}, u32[]{:S(2)}) copy-start(bf16[5136,128]{1,0:T(8,128)(2,1)S(1)} %collective-permute-done.3.refs_3_) | copy-start | bytes 3944452
  58.7 29.8 %collective-permute-start.11 = (bf16[5136,128]{1,0:T(8,128)(2,1)S(1)}, bf16[5136,128]{1,0:T(8,128)(2,1)S(1)}, u32[]{:S(2)}, u32[]{:S(2)}) collective-permute-start(bf16[5136,128]{1,0:T(8,128)(2,1)S(1)} %collective-permute-done.3.refs_3_), channel_id=1, source_target_pairs={{0,96},{1,97},{2,98},{3,99},{4,100},{5,101},{6,102},{7,103},{8,104... | collective-permute-start | bytes 3944456 | tf_op jit(solution)/shard_map/ppermute | solution.py:27
  60.6 30.3 %collective-permute-start.10 = (bf16[5136,128]{1,0:T(8,128)(2,1)S(1)}, bf16[5136,128]{1,0:T(8,128)(2,1)S(1)}, u32[]{:S(2)}, u32[]{:S(2)}) collective-permute-start(bf16[5136,128]{1,0:T(8,128)(2,1)S(1)} %collective-permute-done.3.refs_3_), channel_id=1, source_target_pairs={{0,32},{1,33},{2,34},{3,35},{4,36},{5,37},{6,38},{7,39},{8,40},{9,... | collective-permute-start | bytes 3944456 | tf_op jit(solution)/shard_map/ppermute | solution.py:27
  60.6 20.7 %collective-permute-start.14 = (bf16[96,5120]{1,0:T(8,128)(2,1)S(1)}, bf16[96,5120]{1,0:T(8,128)(2,1)}, u32[]{:S(2)}, u32[]{:S(2)}) collective-permute-start(bf16[96,5120]{1,0:T(8,128)(2,1)S(1)} %get-tuple-element.69), channel_id=1, source_target_pairs={{0,6},{1,7},{2,0},{3,1},{4,2},{5,3},{6,4},{7,5},{8,14},{9,15},{10,... | collective-permute-start | bytes 2949128 | tf_op jit(solution)/shard_map/ppermute | solution.py:27
  63.1 22.0 %collective-permute-start.13 = (bf16[96,5120]{1,0:T(8,128)(2,1)S(1)}, bf16[96,5120]{1,0:T(8,128)(2,1)S(1)}, u32[]{:S(2)}, u32[]{:S(2)}) collective-permute-start(bf16[96,5120]{1,0:T(8,128)(2,1)S(1)} %get-tuple-element.66), channel_id=1, source_target_pairs={{0,2},{1,3},{2,4},{3,5},{4,6},{5,7},{6,0},{7,1},{8,10},{9,11},{10,... | collective-permute-start | bytes 2949128 | tf_op jit(solution)/shard_map/ppermute | solution.py:27
  63.1 30.0 %collective-permute-start.12 = (bf16[5136,128]{1,0:T(8,128)(2,1)S(1)}, bf16[5136,128]{1,0:T(8,128)(2,1)S(1)}, u32[]{:S(2)}, u32[]{:S(2)}) collective-permute-start(bf16[5136,128]{1,0:T(8,128)(2,1)S(1)} %get-tuple-element.67.refs_4_), channel_id=1, source_target_pairs={{0,16},{1,17},{2,18},{3,19},{4,20},{5,21},{6,22},{7,23},{8,24},{9,... | collective-permute-start | bytes 3944456 | tf_op jit(solution)/shard_map/ppermute | solution.py:27
  81.4 14.9 %collective-permute-start.17 = (bf16[96,5120]{1,0:T(8,128)(2,1)S(1)}, bf16[96,5120]{1,0:T(8,128)(2,1)}, u32[]{:S(2)}, u32[]{:S(2)}) collective-permute-start(bf16[96,5120]{1,0:T(8,128)(2,1)S(1)} %collective-permute-done.9.refs_5_.refs_10_), channel_id=1, source_target_pairs={{0,1},{1,0},{2,3},{3,2},{4,5},{5,4},{6,7},{7,6},{8,9},{9,8},{10,11... | collective-permute-start | bytes 2949128 | tf_op jit(solution)/shard_map/ppermute | solution.py:27
  85.1 9.3 %collective-permute-start.16 = (bf16[96,5120]{1,0:T(8,128)(2,1)}, bf16[96,5120]{1,0:T(8,128)(2,1)}, u32[]{:S(2)}, u32[]{:S(2)}) collective-permute-start(bf16[96,5120]{1,0:T(8,128)(2,1)} %collective-permute-done.14.refs_9_.refs_1_), channel_id=1, source_target_pairs={{0,1},{1,0},{2,3},{3,2},{4,5},{5,4},{6,7},{7,6},{8,9},{9,8},{10,11... | collective-permute-start | bytes 2949128 | tf_op jit(solution)/shard_map/ppermute | solution.py:27
  88.5 4.7 %copy-start.11 = (bf16[5136,128]{1,0:T(8,128)(2,1)}, bf16[5136,128]{1,0:T(8,128)(2,1)S(1)}, u32[]{:S(2)}) copy-start(bf16[5136,128]{1,0:T(8,128)(2,1)S(1)} %collective-permute-done.11.refs_6_) | copy-start | bytes 3944452
  88.5 5.9 %collective-permute-start.15 = (bf16[96,5120]{1,0:T(8,128)(2,1)S(1)}, bf16[96,5120]{1,0:T(8,128)(2,1)}, u32[]{:S(2)}, u32[]{:S(2)}) collective-permute-start(bf16[96,5120]{1,0:T(8,128)(2,1)S(1)} %collective-permute-done.13.refs_8_.refs_0_), channel_id=1, source_target_pairs={{0,1},{1,0},{2,3},{3,2},{4,5},{5,4},{6,7},{7,6},{8,9},{9,8},{10,11... | collective-permute-start | bytes 2949128 | tf_op jit(solution)/shard_map/ppermute | solution.py:27
  90.0 0.9 copy-start.6
  91.0 2.2 %copy-start.12 = (bf16[5136,128]{1,0:T(8,128)(2,1)}, bf16[5136,128]{1,0:T(8,128)(2,1)S(1)}, u32[]{:S(2)}) copy-start(bf16[5136,128]{1,0:T(8,128)(2,1)S(1)} %collective-permute-done.10.refs_5_) | copy-start | bytes 3944452
  91.0 5.4 %collective-permute-start.18 = (bf16[96,5120]{1,0:T(8,128)(2,1)S(1)}, bf16[96,5120]{1,0:T(8,128)(2,1)}, u32[]{:S(2)}, u32[]{:S(2)}) collective-permute-start(bf16[96,5120]{1,0:T(8,128)(2,1)S(1)} %collective-permute-done.8.refs_3_.refs_11_), channel_id=1, source_target_pairs={{0,1},{1,0},{2,3},{3,2},{4,5},{5,4},{6,7},{7,6},{8,9},{9,8},{10,11... | collective-permute-start | bytes 2949128 | tf_op jit(solution)/shard_map/ppermute | solution.py:27
  93.2 1.1 copy-start.13
  94.4 18.9 %collective-permute-start.19 = (bf16[96,5120]{1,0:T(8,128)(2,1)}, bf16[96,5120]{1,0:T(8,128)(2,1)S(1)}, u32[]{:S(2)}, u32[]{:S(2)}) collective-permute-start(bf16[96,5120]{1,0:T(8,128)(2,1)} %collective-permute-done.7.refs_4_.refs_2_), channel_id=1, source_target_pairs={{0,1},{1,0},{2,3},{3,2},{4,5},{5,4},{6,7},{7,6},{8,9},{9,8},{10,11... | collective-permute-start | bytes 2949128 | tf_op jit(solution)/shard_map/ppermute | solution.py:27
  95.7 17.5 %collective-permute-start.20 = (bf16[96,5120]{1,0:T(8,128)(2,1)}, bf16[96,5120]{1,0:T(8,128)(2,1)S(1)}, u32[]{:S(2)}, u32[]{:S(2)}) collective-permute-start(bf16[96,5120]{1,0:T(8,128)(2,1)} %collective-permute-done.6.refs_2_.refs_3_), channel_id=1, source_target_pairs={{0,1},{1,0},{2,3},{3,2},{4,5},{5,4},{6,7},{7,6},{8,9},{9,8},{10,11... | collective-permute-start | bytes 2949128 | tf_op jit(solution)/shard_map/ppermute | solution.py:27
  95.8 17.4 %collective-permute-start.21 = (bf16[96,5120]{1,0:T(8,128)(2,1)}, bf16[96,5120]{1,0:T(8,128)(2,1)S(1)}, u32[]{:S(2)}, u32[]{:S(2)}) collective-permute-start(bf16[96,5120]{1,0:T(8,128)(2,1)} %copy-done.14), channel_id=1, source_target_pairs={{0,1},{1,0},{2,3},{3,2},{4,5},{5,4},{6,7},{7,6},{8,9},{9,8},{10,11... | collective-permute-start | bytes 2949128 | tf_op jit(solution)/shard_map/ppermute | solution.py:27
  96.3 17.0 %collective-permute-start.22 = (bf16[96,5120]{1,0:T(8,128)(2,1)}, bf16[96,5120]{1,0:T(8,128)(2,1)S(1)}, u32[]{:S(2)}, u32[]{:S(2)}) collective-permute-start(bf16[96,5120]{1,0:T(8,128)(2,1)} %refs_0_.1), channel_id=1, source_target_pairs={{0,1},{1,0},{2,3},{3,2},{4,5},{5,4},{6,7},{7,6},{8,9},{9,8},{10,11... | collective-permute-start | bytes 2949128 | tf_op jit(solution)/shard_map/ppermute | solution.py:27
  96.4 1.2 copy-start.7
  113.2 5.9 %copy-start.15 = (bf16[96,5120]{1,0:T(8,128)(2,1)}, bf16[96,5120]{1,0:T(8,128)(2,1)S(1)}, u32[]{:S(2)}) copy-start(bf16[96,5120]{1,0:T(8,128)(2,1)S(1)} %collective-permute-done.19.refs_7_) | copy-start | bytes 2949124
  113.2 1.1 copy-start.16
  113.3 2.7 %copy-start.17 = (bf16[96,5120]{1,0:T(8,128)(2,1)}, bf16[96,5120]{1,0:T(8,128)(2,1)S(1)}, u32[]{:S(2)}) copy-start(bf16[96,5120]{1,0:T(8,128)(2,1)S(1)} %collective-permute-done.21.refs_9_) | copy-start | bytes 2949124
  113.3 2.7 %collective-permute-start.23 = (bf16[96,5120]{1,0:T(8,128)(2,1)S(1)}, bf16[96,5120]{1,0:T(8,128)(2,1)S(1)}, u32[]{:S(2)}, u32[]{:S(2)}) collective-permute-start(bf16[96,5120]{1,0:T(8,128)(2,1)S(1)} %get-tuple-element.81), channel_id=1, source_target_pairs={{0,1},{1,0},{2,3},{3,2},{4,5},{5,4},{6,7},{7,6},{8,9},{9,8},{10,11... | collective-permute-start | bytes 2949128 | tf_op jit(solution)/shard_map/ppermute | solution.py:27
  113.8 5.1 %collective-permute-start.24 = (bf16[96,5120]{1,0:T(8,128)(2,1)S(1)}, bf16[96,5120]{1,0:T(8,128)(2,1)S(1)}, u32[]{:S(2)}, u32[]{:S(2)}) collective-permute-start(bf16[96,5120]{1,0:T(8,128)(2,1)S(1)} %get-tuple-element.83), channel_id=1, source_target_pairs={{0,1},{1,0},{2,3},{3,2},{4,5},{5,4},{6,7},{7,6},{8,9},{9,8},{10,11... | collective-permute-start | bytes 2949128 | tf_op jit(solution)/shard_map/ppermute | solution.py:27
  113.9 6.0 %collective-permute-start.25 = (bf16[96,5120]{1,0:T(8,128)(2,1)S(1)}, bf16[96,5120]{1,0:T(8,128)(2,1)S(1)}, u32[]{:S(2)}, u32[]{:S(2)}) collective-permute-start(bf16[96,5120]{1,0:T(8,128)(2,1)S(1)} %get-tuple-element.85), channel_id=1, source_target_pairs={{0,1},{1,0},{2,3},{3,2},{4,5},{5,4},{6,7},{7,6},{8,9},{9,8},{10,11... | collective-permute-start | bytes 2949128 | tf_op jit(solution)/shard_map/ppermute | solution.py:27
  116.2 28.9 %collective-permute-start.28 = (bf16[96,5120]{1,0:T(8,128)(2,1)S(1)}, bf16[96,5120]{1,0:T(8,128)(2,1)S(1)}, u32[]{:S(2)}, u32[]{:S(2)}) collective-permute-start(bf16[96,5120]{1,0:T(8,128)(2,1)S(1)} %add_convert_fusion.6), channel_id=1, source_target_pairs={{0,8},{1,9},{2,10},{3,11},{4,12},{5,13},{6,14},{7,15},{8,0},{9,1},... | collective-permute-start | bytes 2949128 | tf_op jit(solution)/shard_map/ppermute | solution.py:27
  119.1 26.1 %collective-permute-start.29 = (bf16[96,5120]{1,0:T(8,128)(2,1)S(1)}, bf16[96,5120]{1,0:T(8,128)(2,1)S(1)}, u32[]{:S(2)}, u32[]{:S(2)}) collective-permute-start(bf16[96,5120]{1,0:T(8,128)(2,1)S(1)} %add_convert_fusion.5), channel_id=1, source_target_pairs={{0,2},{1,3},{2,4},{3,5},{4,6},{5,7},{6,0},{7,1},{8,10},{9,11},{10,... | collective-permute-start | bytes 2949128 | tf_op jit(solution)/shard_map/ppermute | solution.py:27
  120.2 25.0 %collective-permute-start.30 = (bf16[96,5120]{1,0:T(8,128)(2,1)S(1)}, bf16[96,5120]{1,0:T(8,128)(2,1)S(1)}, u32[]{:S(2)}, u32[]{:S(2)}) collective-permute-start(bf16[96,5120]{1,0:T(8,128)(2,1)S(1)} %add_convert_fusion.4), channel_id=1, source_target_pairs={{0,6},{1,7},{2,0},{3,1},{4,2},{5,3},{6,4},{7,5},{8,14},{9,15},{10,... | collective-permute-start | bytes 2949128 | tf_op jit(solution)/shard_map/ppermute | solution.py:27
  141.7 2.8 %collective-permute-start.26 = (bf16[48,5120]{1,0:T(8,128)(2,1)S(1)}, bf16[48,5120]{1,0:T(8,128)(2,1)S(1)}, u32[]{:S(2)}, u32[]{:S(2)}) collective-permute-start(bf16[48,5120]{1,0:T(8,128)(2,1)S(1)} %get-tuple-element.95), channel_id=1, source_target_pairs={{0,1},{1,0},{2,3},{3,2},{4,5},{5,4},{6,7},{7,6},{8,9},{9,8},{10,11... | collective-permute-start | bytes 1474568 | tf_op jit(solution)/shard_map/ppermute | solution.py:27
  143.0 2.2 %collective-permute-start.27 = (bf16[48,5120]{1,0:T(8,128)(2,1)S(1)}, bf16[48,5120]{1,0:T(8,128)(2,1)S(1)}, u32[]{:S(2)}, u32[]{:S(2)}) collective-permute-start(bf16[48,5120]{1,0:T(8,128)(2,1)S(1)} %get-tuple-element.96), channel_id=1, source_target_pairs={{0,1},{1,0},{2,3},{3,2},{4,5},{5,4},{6,7},{7,6},{8,9},{9,8},{10,11... | collective-permute-start | bytes 1474568 | tf_op jit(solution)/shard_map/ppermute | solution.py:27
  145.2 1.2 copy-start.18
  146.4 2.9 %collective-permute-start.33 = (bf16[96,5120]{1,0:T(8,128)(2,1)S(1)}, bf16[96,5120]{1,0:T(8,128)(2,1)S(1)}, u32[]{:S(2)}, u32[]{:S(2)}) collective-permute-start(bf16[96,5120]{1,0:T(8,128)(2,1)S(1)} %copy-done.18), channel_id=1, source_target_pairs={{0,1},{1,0},{2,3},{3,2},{4,5},{5,4},{6,7},{7,6},{8,9},{9,8},{10,11... | collective-permute-start | bytes 2949128 | tf_op jit(solution)/shard_map/ppermute | solution.py:27
  146.8 12.7 %collective-permute-start.35 = (bf16[48,5120]{1,0:T(8,128)(2,1)S(1)}, bf16[48,5120]{1,0:T(8,128)(2,1)S(1)}, u32[]{:S(2)}, u32[]{:S(2)}) collective-permute-start(bf16[48,5120]{1,0:T(8,128)(2,1)S(1)} %get-tuple-element.121), channel_id=1, source_target_pairs={{0,6},{1,7},{2,0},{3,1},{4,2},{5,3},{6,4},{7,5},{8,14},{9,15},{10,... | collective-permute-start | bytes 1474568 | tf_op jit(solution)/shard_map/ppermute | solution.py:27
  148.8 13.7 %collective-permute-start.34 = (bf16[48,5120]{1,0:T(8,128)(2,1)S(1)}, bf16[48,5120]{1,0:T(8,128)(2,1)S(1)}, u32[]{:S(2)}, u32[]{:S(2)}) collective-permute-start(bf16[48,5120]{1,0:T(8,128)(2,1)S(1)} %get-tuple-element.122), channel_id=1, source_target_pairs={{0,2},{1,3},{2,4},{3,5},{4,6},{5,7},{6,0},{7,1},{8,10},{9,11},{10,... | collective-permute-start | bytes 1474568 | tf_op jit(solution)/shard_map/ppermute | solution.py:27
  148.8 2.6 %collective-permute-start.31 = (bf16[96,5120]{1,0:T(8,128)(2,1)S(1)}, bf16[96,5120]{1,0:T(8,128)(2,1)S(1)}, u32[]{:S(2)}, u32[]{:S(2)}) collective-permute-start(bf16[96,5120]{1,0:T(8,128)(2,1)S(1)} %get-tuple-element.102), channel_id=1, source_target_pairs={{0,1},{1,0},{2,3},{3,2},{4,5},{5,4},{6,7},{7,6},{8,9},{9,8},{10,11... | collective-permute-start | bytes 2949128 | tf_op jit(solution)/shard_map/ppermute | solution.py:27
  149.0 3.7 %collective-permute-start.32 = (bf16[96,5120]{1,0:T(8,128)(2,1)S(1)}, bf16[96,5120]{1,0:T(8,128)(2,1)S(1)}, u32[]{:S(2)}, u32[]{:S(2)}) collective-permute-start(bf16[96,5120]{1,0:T(8,128)(2,1)S(1)} %get-tuple-element.104), channel_id=1, source_target_pairs={{0,1},{1,0},{2,3},{3,2},{4,5},{5,4},{6,7},{7,6},{8,9},{9,8},{10,11... | collective-permute-start | bytes 2949128 | tf_op jit(solution)/shard_map/ppermute | solution.py:27
  162.8 4.7 %collective-permute-start.36 = (bf16[96,5120]{1,0:T(8,128)(2,1)S(1)}, bf16[96,5120]{1,0:T(8,128)(2,1)S(1)}, u32[]{:S(2)}, u32[]{:S(2)}) collective-permute-start(bf16[96,5120]{1,0:T(8,128)(2,1)S(1)} %get-tuple-element.120), channel_id=1, source_target_pairs={{0,1},{1,0},{2,3},{3,2},{4,5},{5,4},{6,7},{7,6},{8,9},{9,8},{10,11... | collective-permute-start | bytes 2949128 | tf_op jit(solution)/shard_map/ppermute | solution.py:27
  164.0 24.8 %collective-permute-start.37 = (bf16[96,5120]{1,0:T(8,128)(2,1)S(1)}, bf16[96,5120]{1,0:T(8,128)(2,1)S(1)}, u32[]{:S(2)}, u32[]{:S(2)}) collective-permute-start(bf16[96,5120]{1,0:T(8,128)(2,1)S(1)} %add_convert_fusion.3), channel_id=1, source_target_pairs={{0,8},{1,9},{2,10},{3,11},{4,12},{5,13},{6,14},{7,15},{8,0},{9,1},... | collective-permute-start | bytes 2949128 | tf_op jit(solution)/shard_map/ppermute | solution.py:27
  166.0 23.1 %collective-permute-start.39 = (bf16[96,5120]{1,0:T(8,128)(2,1)S(1)}, bf16[96,5120]{1,0:T(8,128)(2,1)S(1)}, u32[]{:S(2)}, u32[]{:S(2)}) collective-permute-start(bf16[96,5120]{1,0:T(8,128)(2,1)S(1)} %add_convert_fusion.1), channel_id=1, source_target_pairs={{0,6},{1,7},{2,0},{3,1},{4,2},{5,3},{6,4},{7,5},{8,14},{9,15},{10,... | collective-permute-start | bytes 2949128 | tf_op jit(solution)/shard_map/ppermute | solution.py:27
  166.0 23.9 %collective-permute-start.38 = (bf16[96,5120]{1,0:T(8,128)(2,1)S(1)}, bf16[96,5120]{1,0:T(8,128)(2,1)S(1)}, u32[]{:S(2)}, u32[]{:S(2)}) collective-permute-start(bf16[96,5120]{1,0:T(8,128)(2,1)S(1)} %add_convert_fusion.2), channel_id=1, source_target_pairs={{0,2},{1,3},{2,4},{3,5},{4,6},{5,7},{6,0},{7,1},{8,10},{9,11},{10,... | collective-permute-start | bytes 2949128 | tf_op jit(solution)/shard_map/ppermute | solution.py:27
